TPU v7x, 32 devices: a whole 2x2x4 slice. The times are simulated.
32 devices in a mesh: fsdp: 8 (over z, y), et: 4 (over x, core).
Axes of the slice: x: 2, y: 2, z: 4, core: 2. Of those that a mesh axis runs over, the one named last changes fastest.
Arguments:
- tokens: bfloat16 [4096, 3072], P(('fsdp', 'et')), may hold values from -6 to 6
- cotangent: bfloat16 [4096, 3072], P(('fsdp', 'et')), may hold values from -6 to 6
- route_experts: int32 [4096, 2], P('fsdp'), may hold values from 0 to 7, as said below
- route_gates: float32 [4096, 2], P('fsdp'), may hold values from 0.2 to 1
- w_gate: bfloat16 [3072, 8192], P('fsdp', 'et'), may hold values from -0.109375 to 0.109375
- w_up: bfloat16 [3072, 8192], P('fsdp', 'et'), may hold values from -0.109375 to 0.109375
- w_down: bfloat16 [8192, 3072], P('et', 'fsdp'), may hold values from -0.0625 to 0.0625
Outputs:
- moe_out: bfloat16 [4096, 3072], P(('fsdp', 'et'))
- grad_tokens: bfloat16 [4096, 3072], P(('fsdp', 'et'))
Inputs may be any that keep to these rules, and one draw needn't show every extreme that they name: `route_experts`: each row names two different experts. Among the 128 rows of one device (aligned blocks of rows) at most 16 name expert 0, so a group of 512 rows has at most 64 such rows; in every draw some device reaches 16 and some group reaches 64.
All inputs are finite; a program needn't handle non-finite values.
Results may differ from a plain program's by a relative error of at most 0.024.
Values may be sent and summed in bfloat16 or wider, within the bound.
No kernel may reach another device: no remote copies, remote signals or barrier semaphores. Data moves between devices by JAX's collectives and lax.ppermute only.
A program may use at most 128 MiB of HBM per device.

v0:
```python
import jax
import jax.numpy as jnp
from jax import lax
from jax.sharding import PartitionSpec as P


def contract_last(left, right):
    return lax.dot_general(
        left, right, (((1,), (1,)), ((), ())), preferred_element_type=jnp.float32
    )


def per_device(tokens, cotangent, route_experts, route_gates, w_gate, w_up, w_down):
    own_count = tokens.shape[0]
    most = own_count // 8
    own_start = lax.axis_index("et") * own_count
    own_experts = lax.dynamic_slice_in_dim(route_experts, own_start, own_count)
    own_gates = lax.dynamic_slice_in_dim(route_gates, own_start, own_count)
    is_first = own_experts[:, 0] == 0
    is_second = own_experts[:, 1] == 0
    own_chosen = jnp.logical_or(is_first, is_second)
    own_weight = jnp.where(is_first, own_gates[:, 0], 0.0) + jnp.where(
        is_second, own_gates[:, 1], 0.0
    )
    chosen_int = own_chosen.astype(jnp.int32)
    local_slot = jnp.cumsum(chosen_int) - chosen_int
    live_count = jnp.sum(chosen_int)
    target = jnp.where(own_chosen, local_slot, most)
    pack_source = (
        jnp.zeros((most,), jnp.int32)
        .at[target]
        .set(jnp.arange(own_count, dtype=jnp.int32), mode="drop")
    )
    live_rows = jnp.arange(most, dtype=jnp.int32) < live_count
    packed_rows = jnp.where(live_rows[:, None], jnp.take(tokens, pack_source, axis=0), 0.0)
    packed_weight = jnp.where(live_rows, jnp.take(own_weight, pack_source), 0.0)
    packed_cot = (
        packed_weight[:, None] * jnp.take(cotangent, pack_source, axis=0).astype(jnp.float32)
    ).astype(jnp.bfloat16)
    own_slot = jnp.where(own_chosen, local_slot, 0)
    expert_rows, slot_cot = (
        lax.all_gather(packed_rows, "et", axis=0, tiled=True),
        lax.all_gather(packed_cot, "et", axis=0, tiled=True),
    )
    gate_full, up_full = (
        lax.all_gather(w_gate, "fsdp", axis=0, tiled=True),
        lax.all_gather(w_up, "fsdp", axis=0, tiled=True),
    )
    down_full = lax.all_gather(w_down, "fsdp", axis=1, tiled=True)
    gate_pre = jnp.dot(expert_rows, gate_full, preferred_element_type=jnp.float32)
    up_pre = jnp.dot(expert_rows, up_full, preferred_element_type=jnp.float32)
    gate_sig = jax.nn.sigmoid(gate_pre)
    hidden = (gate_pre * gate_sig * up_pre).astype(jnp.bfloat16)
    out_part = jnp.dot(hidden, down_full, preferred_element_type=jnp.float32)
    grad_hidden = contract_last(slot_cot, down_full)
    gate_gradient = (grad_hidden * up_pre * gate_sig * (1.0 + gate_pre * (1.0 - gate_sig))).astype(
        jnp.bfloat16
    )
    up_gradient = (grad_hidden * gate_pre * gate_sig).astype(jnp.bfloat16)
    grad_part = contract_last(gate_gradient, gate_full) + contract_last(up_gradient, up_full)
    out_sum = lax.psum(out_part.astype(jnp.bfloat16), "et").astype(jnp.float32)
    grad_sum = lax.psum(grad_part.astype(jnp.bfloat16), "et").astype(jnp.float32)
    row_start = lax.axis_index("et") * most
    own_out = lax.dynamic_slice_in_dim(out_sum, row_start, most)
    own_grad = lax.dynamic_slice_in_dim(grad_sum, row_start, most)
    moe_out = (own_weight[:, None] * jnp.take(own_out, own_slot, axis=0)).astype(jnp.bfloat16)
    grad_tokens = jnp.where(own_chosen[:, None], jnp.take(own_grad, own_slot, axis=0), 0.0).astype(
        jnp.bfloat16
    )
    return (moe_out, grad_tokens)


def solution(mesh):
    in_specs = (
        P(("fsdp", "et"), None),
        P(("fsdp", "et"), None),
        P("fsdp", None),
        P("fsdp", None),
        P("fsdp", "et"),
        P("fsdp", "et"),
        P("et", "fsdp"),
    )
    out_specs = (P(("fsdp", "et"), None), P(("fsdp", "et"), None))
    return jax.shard_map(
        per_device, mesh=mesh, in_specs=in_specs, out_specs=out_specs, check_vma=False
    )
```

profile of v0, /device:TPU:0, one launch (start us, length us, event | category | flops | bytes accessed | tf_op | source)
XLA Modules:
  0.0 617.9 jit_solution(1295757873078999377)
XLA Ops:
  7.2 0.7 all-gather.4.cloned.1.call-update
  8.0 0.7 all-gather.6.cloned.1.call-update
  8.7 0.7 all-gather.8.cloned.1.call-update
  9.4 0.7 constant_dynamic-slice_fusion
  10.3 0.7 constant_dynamic-slice_fusion.1
  10.9 0.1 copy.14
  11.5 0.2 reduce-window.4
  11.7 0.1 fusion.13
  11.8 1.0 scatter_custom_fusion
  12.8 0.7 gather_fusion
  13.5 0.6 gather_fusion.3
  14.1 1.9 gather_fusion.1
  16.1 0.6 convert_reduce_fusion
  16.7 0.6 iota_compare_fusion
  17.4 0.7 select_select_fusion.2
  18.1 7.9 %all_gather.15 = bf16[64,3072]{1,0:T(8,128)(2,1)S(1)} all-gather(bf16[16,3072]{1,0:T(8,128)(2,1)S(1)} %select_select_fusion.1), channel_id=1, replica_groups=mesh['fsdp'=8,'et'=4] {'et'}, dimensions={0}, use_global_device_ids=true | all-gather | bytes 491520 | tf_op jit(solution)/shard_map/all_gather | solution.py:42
  26.1 6.6 %all_gather.19 = bf16[64,3072]{1,0:T(8,128)(2,1)S(1)} all-gather(bf16[16,3072]{1,0:T(8,128)(2,1)S(1)} %multiply_convert_fusion.6), channel_id=1, replica_groups=mesh['fsdp'=8,'et'=4] {'et'}, dimensions={0}, use_global_device_ids=true | all-gather | bytes 491520 | tf_op jit(solution)/shard_map/all_gather | solution.py:43
  32.7 156.7 %all-gather.4.cloned.1.call-done = bf16[3072,2048]{1,0:T(8,128)(2,1)} async-done(((bf16[384,2048]{1,0:T(8,128)(2,1)}), bf16[3072,2048]{1,0:T(8,128)(2,1)}) %all-gather.4.cloned.1.call-update) | async-done | bytes 12582928 | tf_op jit(solution)/shard_map/all_gather | solution.py:46
  189.4 6.9 %fusion.17 = f32[64,2048]{1,0:T(8,128)S(1)} fusion(bf16[64,3072]{1,0:T(8,128)(2,1)S(1)} %all_gather.15, bf16[3072,2048]{1,0:T(8,128)(2,1)} %all-gather.4.cloned.1.call-done), kind=kOutput, calls=%fused_computation.50 | convolution fusion | flops 805306368 | bytes 13500416 | tf_op jit(solution)/shard_map/dot_general | solution.py:50
  196.3 169.9 %all-gather.6.cloned.1.call-done = bf16[3072,2048]{1,0:T(8,128)(2,1)} async-done(((bf16[384,2048]{1,0:T(8,128)(2,1)}), bf16[3072,2048]{1,0:T(8,128)(2,1)}) %all-gather.6.cloned.1.call-update) | async-done | bytes 12582928 | tf_op jit(solution)/shard_map/all_gather | solution.py:47
  366.2 6.9 %fusion.18 = f32[64,2048]{1,0:T(8,128)S(1)} fusion(bf16[64,3072]{1,0:T(8,128)(2,1)S(1)} %all_gather.15, bf16[3072,2048]{1,0:T(8,128)(2,1)} %all-gather.6.cloned.1.call-done), kind=kOutput, calls=%fused_computation.51 | convolution fusion | flops 805306368 | bytes 13500416 | tf_op jit(solution)/shard_map/dot_general | solution.py:51
  373.1 170.0 %all-gather.8.cloned.1.call-done = bf16[2048,3072]{1,0:T(8,128)(2,1)} async-done(((bf16[2048,384]{1,0:T(8,128)(2,1)}), bf16[2048,3072]{1,0:T(8,128)(2,1)}) %all-gather.8.cloned.1.call-update) | async-done | bytes 12582928 | tf_op jit(solution)/shard_map/all_gather | solution.py:49
  543.1 8.6 %fusion.19 = f32[64,2048]{1,0:T(8,128)S(1)} fusion(bf16[64,3072]{1,0:T(8,128)(2,1)S(1)} %all_gather.19, bf16[2048,3072]{1,0:T(8,128)(2,1)} %all-gather.8.cloned.1.call-done), kind=kOutput, calls=%fused_computation.52 | convolution fusion | flops 805306368 | bytes 13500416 | tf_op jit(solution)/shard_map/dot_general | solution.py:8
  551.7 3.1 convolution_convert_fusion
  554.8 8.5 %fusion.3 = f32[64,3072]{1,0:T(8,128)S(1)} fusion(bf16[3072,2048]{1,0:T(8,128)(2,1)} %all-gather.4.cloned.1.call-done, f32[64,2048]{1,0:T(8,128)S(1)} %fusion.17, f32[64,2048]{1,0:T(8,128)S(1)} %fusion.19, f32[64,2048]{1,0:T(8,128)S(1)} %fusion.18), kind=kOutput, calls=%fused_computation.17 | convolution fusion | flops 806617088 | bytes 14942208 | tf_op jit(solution)/shard_map/dot_general | solution.py:8
  563.3 9.5 %fusion = bf16[64,3072]{1,0:T(8,128)(2,1)} fusion(f32[64,3072]{1,0:T(8,128)S(1)} %fusion.3, bf16[3072,2048]{1,0:T(8,128)(2,1)} %all-gather.6.cloned.1.call-done, f32[64,2048]{1,0:T(8,128)S(1)} %fusion.19, f32[64,2048]{1,0:T(8,128)S(1)} %fusion.17), kind=kOutput, calls=%fused_computation.7 | convolution fusion | flops 806486016 | bytes 14811136 | tf_op jit(solution)/shard_map/dot_general | solution.py:8
  572.9 33.1 %all-reduce.3.cloned.1.call-done = (bf16[64,3072]{1,0:T(8,128)(2,1)}, bf16[64,3072]{1,0:T(8,128)(2,1)}) async-done(((bf16[64,3072]{1,0:T(8,128)(2,1)}, bf16[64,3072]{1,0:T(8,128)(2,1)}), (bf16[64,3072]{1,0:T(8,128)(2,1)}, bf16[64,3072]{1,0:T(8,128)(2,1)})) %all-reduce.3.cloned.1.call-update) | async-done | bytes 786448 | tf_op jit(solution)/shard_map/psum | solution.py:61
  605.9 1.0 dynamic-slice_convert_fusion
  606.9 1.0 gather_fusion.4
  607.9 1.2 gather_fusion.2
  609.1 1.2 fusion.1
  610.3 1.1 fusion.2
  (24 shorter events, 1.0 us)
Async XLA Ops:
  7.2 6.3 %copy-start = (bf16[128,3072]{1,0:T(8,128)(2,1)S(1)}, bf16[128,3072]{1,0:T(8,128)(2,1)}, u32[]{:S(2)}) copy-start(bf16[128,3072]{1,0:T(8,128)(2,1)} %param.12) | copy-start | bytes 2359300
  7.2 182.2 %all-gather.4.cloned.1.call-start = ((), (), s32[]{:S(2)}) async-start(), calls=%async_computation | async-start | bytes 14155776 | tf_op jit(solution)/shard_map/all_gather | solution.py:46
  7.9 358.3 %all-gather.6.cloned.1.call-start = ((), (), s32[]{:S(2)}) async-start(), calls=%async_computation.1 | async-start | bytes 14155776 | tf_op jit(solution)/shard_map/all_gather | solution.py:47
  8.7 534.4 %all-gather.8.cloned.1.call-start = ((), (), s32[]{:S(2)}) async-start(), calls=%async_computation.2 | async-start | bytes 14155776 | tf_op jit(solution)/shard_map/all_gather | solution.py:49
  9.4 596.5 %all-reduce.3.cloned.1.call-start = ((), (), s32[]{:S(2)}) async-start(), calls=%async_computation.3 | async-start | bytes 1572864 | tf_op jit(solution)/shard_map/psum | solution.py:61
  543.1 8.7 %copy-start.1 = (bf16[2048,3072]{1,0:T(8,128)(2,1)S(1)}, bf16[2048,3072]{1,0:T(8,128)(2,1)}, u32[]{:S(2)}) copy-start(bf16[2048,3072]{1,0:T(8,128)(2,1)} %all-gather.8.cloned.1.call-done) | copy-start | bytes 37748740
Sparse Core Ops, SparseCore 0:
  10.2 179.1 all-gather.3
  191.6 174.6 all-gather.5
  368.3 174.7 all-gather.7
  572.9 32.9 all-reduce.2
where the time goes:
time: 618 us
  waiting for transfers between devices  532 us (86%)
  matrix products  43.5 us (7%)
  blocking collectives  14.5 us (2%)
  between operations  13.9 us (2%)
  local copies, waits for them, and re-layouts  8.24 us (1%)
    all_gather x1, waiting for transfers between devices, per_device(): down_full = lax.all_gather(w_down, 'fsdp', axis=1, tiled=True)  170 us
    all_gather x1, waiting for transfers between devices, per_device(): lax.all_gather(w_up, 'fsdp', axis=0, tiled=True)  170 us
    all_gather x1, waiting for transfers between devices, per_device(): lax.all_gather(w_gate, 'fsdp', axis=0, tiled=True)  157 us
    psum x1, waiting for transfers between devices, per_device(): out_sum = lax.psum(out_part.astype(jnp.bfloat16), 'et').astype(jnp.float32)  33.1 us
    dot_general x3, matrix products, contract_last(): lax.dot_general(left, right, (((1,), (1,)), ((), ())), preferred_element_...  26.6 us
  transfers between devices with their start and end apart: 4, of which 4 were waited for; matrix products, arithmetic and copies ran while one was open for 4% of the time, Pallas kernels for 0%

commit v1 on v0

v1 whole, which is shorter than its diff:
```python
import jax
import jax.numpy as jnp
from jax import lax
from jax.sharding import PartitionSpec as P

F32 = jnp.float32
BF16 = jnp.bfloat16
PAIR = 2
CUTS = (0, 4, 8, 12, 14, 16)


def dot(left, right):
    return jnp.dot(left, right, preferred_element_type=F32)


def dot_last(left, right):
    return lax.dot_general(left, right, (((1,), (1,)), ((), ())), preferred_element_type=F32)


def make_per_device(n_fsdp, n_et):
    n_z = n_fsdp // PAIR
    half_z = n_z // 2

    def over_z(pairs):
        return [(a * PAIR + y, b * PAIR + y) for a, b in pairs for y in range(PAIR)]

    def z_swap(values, step):
        return lax.ppermute(values, "fsdp", over_z([(z, z ^ step) for z in range(n_z)]))

    def y_swap(values):
        return lax.ppermute(values, "fsdp", [(f, f ^ 1) for f in range(n_fsdp)])

    def e_swap(values, step):
        return lax.ppermute(values, "et", [(e, e ^ step) for e in range(n_et)])

    def inward(values, step):
        last = n_z - 1
        pairs = [(step, step + 1), (last - step, last - step - 1)]
        return lax.ppermute(values, "fsdp", over_z(pairs))

    def outward(values, step):
        last = n_z - 1
        pairs = [(step + 1, step), (last - step - 1, last - step)]
        return lax.ppermute(values, "fsdp", over_z(pairs))

    def middle_swap(values):
        return lax.ppermute(
            values, "fsdp", over_z([(half_z - 1, half_z), (half_z, half_z - 1)])
        )

    steps_e = []
    step = n_et // 2
    while step >= 1:
        steps_e.append(step)
        step //= 2

    def per_device(tokens, cotangent, route_experts, route_gates, w_gate, w_up, w_down):
        own_count, width = tokens.shape
        most = own_count // 8
        own_width, hidden_units = w_gate.shape
        z_width = own_width * PAIR
        f_index = lax.axis_index("fsdp")
        z_index = f_index // PAIR
        y_index = f_index % PAIR
        depth = jnp.minimum(z_index, n_z - 1 - z_index)

        cuts = [hidden_units * c // CUTS[-1] for c in CUTS]
        own_w, far_w = [], []
        for lo, hi in zip(cuts[:-1], cuts[1:]):
            own = (w_gate[:, lo:hi], w_up[:, lo:hi], w_down[lo:hi, :])
            own_w.append(own)
            far_w.append(tuple(y_swap(v) for v in own))

        own_start = lax.axis_index("et") * own_count
        own_experts = lax.dynamic_slice_in_dim(route_experts, own_start, own_count)
        own_gates = lax.dynamic_slice_in_dim(route_gates, own_start, own_count)
        is_first = own_experts[:, 0] == 0
        is_second = own_experts[:, 1] == 0
        chosen = jnp.logical_or(is_first, is_second)
        weight = jnp.where(is_first, own_gates[:, 0], 0.0) + jnp.where(
            is_second, own_gates[:, 1], 0.0
        )
        chosen_int = chosen.astype(jnp.int32)
        slot = jnp.cumsum(chosen_int) - chosen_int
        picks = jnp.logical_and(
            chosen[None, :], slot[None, :] == jnp.arange(most, dtype=jnp.int32)[:, None]
        )
        one_hot = picks.astype(BF16)
        packed_weight = jnp.sum(jnp.where(picks, weight[None, :], 0.0), axis=1)
        packed_rows = dot(one_hot, tokens).astype(BF16)
        packed_cot = (packed_weight[:, None] * dot(one_hot, cotangent)).astype(BF16)
        packed = jnp.concatenate([packed_rows, packed_cot], axis=0)

        pieces = []
        for d in range(n_z):
            start = (z_index ^ d) * z_width
            piece = lax.dynamic_slice_in_dim(packed, start, z_width, axis=1)
            pieces.append(piece if d == 0 else z_swap(piece, d))
        stacked = jnp.stack(pieces)
        order = jnp.arange(n_z, dtype=jnp.int32) ^ (z_index & (half_z - 1))
        stacked = jnp.take(stacked, order, axis=0)[None]
        for step in steps_e:
            stacked = jnp.concatenate([stacked, e_swap(stacked, step)], axis=0)
        stacked = jnp.swapaxes(stacked, 0, 1)
        slots = n_z * n_et * most
        rows = stacked[:, :, :most].reshape(slots, z_width)
        cots = stacked[:, :, most:].reshape(slots, z_width)
        own_at = y_index * own_width
        far_at = (PAIR - 1 - y_index) * own_width
        rows_own = lax.dynamic_slice_in_dim(rows, own_at, own_width, axis=1)
        rows_far = lax.dynamic_slice_in_dim(rows, far_at, own_width, axis=1)
        cots_own = lax.dynamic_slice_in_dim(cots, own_at, own_width, axis=1)
        cots_far = lax.dynamic_slice_in_dim(cots, far_at, own_width, axis=1)

        half = slots // 2
        total = None
        for own, far in zip(own_w, far_w):
            units = own[0].shape[1]
            gate = dot(rows_own, own[0]) + dot(rows_far, far[0])
            up = dot(rows_own, own[1]) + dot(rows_far, far[1])
            grad = dot_last(cots_own, own[2]) + dot_last(cots_far, far[2])
            part = jnp.concatenate([gate, up, grad], axis=1).astype(BF16)
            for step in range(half_z - 1):
                part = (part.astype(F32) + inward(part, step).astype(F32)).astype(BF16)
            pre = part[:half].astype(F32) + middle_swap(part[half:]).astype(F32)
            gate, up, grad = pre[:, :units], pre[:, units : 2 * units], pre[:, 2 * units :]
            sig = jax.nn.sigmoid(gate)
            hidden = gate * sig * up
            grad_gate = grad * up * sig * (1.0 + gate * (1.0 - sig))
            grad_up = grad * gate * sig
            near = jnp.concatenate([hidden, grad_gate, grad_up], axis=1).astype(BF16)
            other = middle_swap(near)
            for step in reversed(range(half_z - 1)):
                near = jnp.where(depth == step, outward(near, step), near)
                other = jnp.where(depth == step, outward(other, step), other)
            full = jnp.concatenate([near, other], axis=0)
            hidden, grad_gate, grad_up = (
                full[:, :units],
                full[:, units : 2 * units],
                full[:, 2 * units :],
            )
            terms = (
                dot(hidden, own[2]),
                dot(hidden, far[2]),
                dot_last(grad_gate, own[0]) + dot_last(grad_up, own[1]),
                dot_last(grad_gate, far[0]) + dot_last(grad_up, far[1]),
            )
            total = terms if total is None else tuple(a + b for a, b in zip(total, terms))

        is_low = y_index == 0
        both = []
        for own_part, far_part in ((total[0], total[1]), (total[2], total[3])):
            left = jnp.where(is_low, own_part, far_part)
            right = jnp.where(is_low, far_part, own_part)
            both.append(jnp.concatenate([left, right], axis=1))
        sums = jnp.stack(both).reshape(2, n_z, n_et, most, z_width)
        sums = jnp.transpose(sums, (2, 1, 0, 3, 4))
        for step in reversed(steps_e):
            count = sums.shape[0] // 2
            sums = sums[:count] + e_swap(sums[count:].astype(BF16), step).astype(F32)
        sums = sums[0].astype(BF16)
        sums = jnp.take(sums, order, axis=0)
        blocks = [sums[0]] + [z_swap(sums[d], d) for d in range(1, n_z)]
        blocks = jnp.take(jnp.stack(blocks), jnp.arange(n_z, dtype=jnp.int32) ^ z_index, axis=0)
        own_sums = jnp.transpose(blocks, (1, 2, 0, 3)).reshape(2, most, width)
        spread = one_hot.T
        moe_out = (weight[:, None] * dot(spread, own_sums[0])).astype(BF16)
        grad_tokens = dot(spread, own_sums[1]).astype(BF16)
        return moe_out, grad_tokens

    return per_device


def solution(mesh):
    sizes = dict(mesh.shape)
    in_specs = (
        P(("fsdp", "et"), None),
        P(("fsdp", "et"), None),
        P("fsdp", None),
        P("fsdp", None),
        P("fsdp", "et"),
        P("fsdp", "et"),
        P("et", "fsdp"),
    )
    out_specs = (P(("fsdp", "et"), None), P(("fsdp", "et"), None))
    return jax.shard_map(
        make_per_device(sizes["fsdp"], sizes["et"]),
        mesh=mesh,
        in_specs=in_specs,
        out_specs=out_specs,
        check_vma=False,
    )
```

time: 618 us -> 255 us (0.41)
  waiting for transfers between devices: 532 us -> 139 us
  starting transfers between devices: 0.15 us -> 63.8 us
  matrix products: 43.5 us -> 28.1 us
  blocking collectives: 14.5 us -> 0 us
  between operations: 13.9 us -> 2.15 us
    all_gather x3 -> x0, waiting for transfers between devices: 497 us -> none  [the longest x1 170 us: per_device(): down_full = lax.all_gather(w_down, 'fsdp', axis=1, tiled=True)]
    ppermute x0 -> x50, waiting for transfers between devices: none -> 139 us  [the longest x10 61.9 us: outward(): return lax.ppermute(values, 'fsdp', over_z(pairs))]
    ppermute x0 -> x50, starting transfers between devices: none -> 63.8 us  [the longest x15 16.2 us: y_swap(): return lax.ppermute(values, 'fsdp', [(f, f ^ 1) for f in range(n_fsdp)])]
    psum x1 -> x0, waiting for transfers between devices: 33.1 us -> none  [per_device(): out_sum = lax.psum(out_part.astype(jnp.bfloat16), 'et').astype(jnp.float32)]
    dot_general x6 -> x64, matrix products: 43.5 us -> 28.1 us  [the longest x34 15.3 us: dot(): return jnp.dot(left, right, preferred_element_type=F32)]
    all_gather x2 -> x0, blocking collectives: 14.5 us -> none  [the longest x1 7.91 us: per_device(): lax.all_gather(packed_rows, 'et', axis=0, tiled=True)]
    slice x2 -> x20, local copies, waits for them, and re-layouts: 0.01 us -> 8.41 us  [the longest x6 7.97 us: per_device(): own = (w_gate[:, lo:hi], w_up[:, lo:hi], w_down[lo:hi, :])]
  transfers between devices with their start and end apart: 4 -> 50, of which waited for: 4 -> 20; matrix products, arithmetic and copies ran while one was open for 4% -> 14% of each run, Pallas kernels for 0% -> 0%
where the time goes in v1:
time: 255 us; the launch traced here: 254 us
  waiting for transfers between devices  139 us (55%)
  starting transfers between devices  63.8 us (25%)
  matrix products  28.1 us (11%)
  local copies, waits for them, and re-layouts  12.9 us (5%)
  other arithmetic  7.7 us (3%)
    ppermute x10, waiting for transfers between devices, outward(): return lax.ppermute(values, 'fsdp', over_z(pairs))  61.9 us
    ppermute x15, waiting for transfers between devices, y_swap(): return lax.ppermute(values, 'fsdp', [(f, f ^ 1) for f in range(n_fsdp)])  54 us
    ppermute x15, starting transfers between devices, y_swap(): return lax.ppermute(values, 'fsdp', [(f, f ^ 1) for f in range(n_fsdp)])  16.2 us
    ppermute x5, starting transfers between devices, inward(): return lax.ppermute(values, 'fsdp', over_z(pairs))  15.5 us
    dot_general x34, matrix products, dot(): return jnp.dot(left, right, preferred_element_type=F32)  15.3 us
    ppermute x10, starting transfers between devices, outward(): return lax.ppermute(values, 'fsdp', over_z(pairs))  12.9 us
    dot_general x30, matrix products, dot_last(): lax.dot_general(left, right, (((1,), (1,)), ((), ())), preferred_element_...  12.8 us
    ppermute x5, waiting for transfers between devices, inward(): return lax.ppermute(values, 'fsdp', over_z(pairs))  10.2 us
  transfers between devices with their start and end apart: 50, of which 20 were waited for; matrix products, arithmetic and copies ran while one was open for 14% of the time, Pallas kernels for 0%

profile of v1, /device:TPU:0, one launch (start us, length us, event | category | flops | bytes accessed | tf_op | source)
XLA Modules:
  0.0 253.7 jit_solution(3322118752359194468)
XLA Ops:
  0.7 1.9 fusion.167
  2.6 3.0 %collective-permute-start.38 = (bf16[384,256]{1,0:T(8,128)(2,1)}, bf16[384,256]{1,0:T(8,128)(2,1)}, u32[]{:S(2)}, u32[]{:S(2)}) collective-permute-start(bf16[384,256]{1,0:T(8,128)(2,1)} %get-tuple-element.19), channel_id=1, source_target_pairs={{0,4},{4,0},{8,12},{12,8},{16,20},{20,16},{24,28},{28,24},{1,5},{5... | collective-permute-start | bytes 589832 | tf_op jit(solution)/shard_map/ppermute | solution.py:31
  8.8 3.6 %collective-permute-start.2 = (bf16[32,768]{1,0:T(8,128)(2,1)}, bf16[32,768]{1,0:T(8,128)(2,1)S(1)}, u32[]{:S(2)}, u32[]{:S(2)}) collective-permute-start(bf16[32,768]{1,0:T(8,128)(2,1)} %get-tuple-element.50), channel_id=1, source_target_pairs={{0,24},{4,28},{8,16},{12,20},{16,8},{20,12},{24,0},{28,4},{1,25},{... | collective-permute-start | bytes 147464 | tf_op jit(solution)/shard_map/ppermute | solution.py:28
  14.3 1.8 fusion.165
  20.2 1.8 collective-permute-start.3
  23.0 2.9 %collective-permute-done.3 = bf16[1,4,32,768]{3,2,1,0:T(8,128)(2,1)S(1)} collective-permute-done((bf16[1,4,32,768]{3,2,1,0:T(8,128)(2,1)S(1)}, bf16[1,4,32,768]{3,2,1,0:T(8,128)(2,1)S(1)}, u32[]{:S(2)}, u32[]{:S(2)}) %collective-permute-start.3) | collective-permute-done | bytes 196640 | tf_op jit(solution)/shard_map/ppermute | solution.py:34
  29.1 1.8 collective-permute-start.31
  36.9 1.8 collective-permute-start.22
  42.1 16.9 %collective-permute-done.23 = bf16[512,384]{1,0:T(8,128)(2,1)S(1)} collective-permute-done((bf16[512,384]{1,0:T(8,128)(2,1)S(1)}, bf16[512,384]{1,0:T(8,128)(2,1)S(1)}, u32[]{:S(2)}, u32[]{:S(2)}) %collective-permute-start.23) | collective-permute-done | bytes 393248 | tf_op jit(solution)/shard_map/ppermute | solution.py:31
  59.9 1.8 collective-permute-start.14
  62.7 8.4 %collective-permute-done.21 = bf16[384,512]{1,0:T(8,128)(2,1)S(1)} collective-permute-done((bf16[384,512]{1,0:T(8,128)(2,1)S(1)}, bf16[384,512]{1,0:T(8,128)(2,1)S(1)}, u32[]{:S(2)}, u32[]{:S(2)}) %collective-permute-start.21) | collective-permute-done | bytes 393248 | tf_op jit(solution)/shard_map/ppermute | solution.py:31
  72.0 1.8 collective-permute-start.6
  75.0 12.9 %collective-permute-done.15 = bf16[512,384]{1,0:T(8,128)(2,1)S(1)} collective-permute-done((bf16[512,384]{1,0:T(8,128)(2,1)S(1)}, bf16[512,384]{1,0:T(8,128)(2,1)S(1)}, u32[]{:S(2)}, u32[]{:S(2)}) %collective-permute-start.15) | collective-permute-done | bytes 393248 | tf_op jit(solution)/shard_map/ppermute | solution.py:31
  88.9 1.8 collective-permute-start.5
  91.0 3.2 %collective-permute-start.40 = (bf16[256,768]{0,1:T(8,128)(2,1)S(1)}, bf16[256,768]{0,1:T(8,128)(2,1)S(1)}, u32[]{:S(2)}, u32[]{:S(2)}) collective-permute-start(bf16[256,768]{0,1:T(8,128)(2,1)S(1)} %pad_maximum_fusion.10), channel_id=1, source_target_pairs={{0,8},{4,12},{24,16},{28,20},{1,9},{5,13},{25,17},{29,21},{2,10},{... | collective-permute-start | bytes 1179656 | tf_op jit(solution)/shard_map/ppermute | solution.py:39
  94.5 1.8 collective-permute-done.13
  96.3 3.2 %collective-permute-start.32 = (bf16[256,768]{0,1:T(8,128)(2,1)S(1)}, bf16[256,768]{0,1:T(8,128)(2,1)S(1)}, u32[]{:S(2)}, u32[]{:S(2)}) collective-permute-start(bf16[256,768]{0,1:T(8,128)(2,1)S(1)} %pad_maximum_fusion.9), channel_id=1, source_target_pairs={{0,8},{4,12},{24,16},{28,20},{1,9},{5,13},{25,17},{29,21},{2,10},{... | collective-permute-start | bytes 1179656 | tf_op jit(solution)/shard_map/ppermute | solution.py:39
  100.2 13.0 %collective-permute-done.7 = bf16[512,384]{1,0:T(8,128)(2,1)S(1)} collective-permute-done((bf16[512,384]{1,0:T(8,128)(2,1)S(1)}, bf16[512,384]{1,0:T(8,128)(2,1)S(1)}, u32[]{:S(2)}, u32[]{:S(2)}) %collective-permute-start.7) | collective-permute-done | bytes 393248 | tf_op jit(solution)/shard_map/ppermute | solution.py:31
  113.2 3.2 %collective-permute-start.24 = (bf16[256,1536]{1,0:T(8,128)(2,1)S(1)}, bf16[256,1536]{1,0:T(8,128)(2,1)S(1)}, u32[]{:S(2)}, u32[]{:S(2)}) collective-permute-start(bf16[256,1536]{1,0:T(8,128)(2,1)S(1)} %pad_maximum_fusion.2), channel_id=1, source_target_pairs={{0,8},{4,12},{24,16},{28,20},{1,9},{5,13},{25,17},{29,21},{2,10},{... | collective-permute-start | bytes 2359304 | tf_op jit(solution)/shard_map/ppermute | solution.py:39
  125.0 15.7 %collective-permute-done.42 = bf16[128,768]{0,1:T(8,128)(2,1)S(1)} collective-permute-done((bf16[128,768]{0,1:T(8,128)(2,1)S(1)}, bf16[128,768]{0,1:T(8,128)(2,1)S(1)}, u32[]{:S(2)}, u32[]{:S(2)}) %collective-permute-start.42) | collective-permute-done | bytes 196640 | tf_op jit(solution)/shard_map/ppermute | solution.py:44
  142.1 4.6 %collective-permute-start.8 = (bf16[256,1536]{1,0:T(8,128)(2,1)S(1)}, bf16[256,1536]{1,0:T(8,128)(2,1)S(1)}, u32[]{:S(2)}, u32[]{:S(2)}) collective-permute-start(bf16[256,1536]{1,0:T(8,128)(2,1)S(1)} %pad_maximum_fusion), channel_id=1, source_target_pairs={{0,8},{4,12},{24,16},{28,20},{1,9},{5,13},{25,17},{29,21},{2,10},{... | collective-permute-start | bytes 2359304 | tf_op jit(solution)/shard_map/ppermute | solution.py:39
  148.0 2.4 collective-permute-done.34
  153.7 10.2 %collective-permute-done.8 = bf16[256,1536]{1,0:T(8,128)(2,1)S(1)} collective-permute-done((bf16[256,1536]{1,0:T(8,128)(2,1)S(1)}, bf16[256,1536]{1,0:T(8,128)(2,1)S(1)}, u32[]{:S(2)}, u32[]{:S(2)}) %collective-permute-start.8) | collective-permute-done | bytes 786464 | tf_op jit(solution)/shard_map/ppermute | solution.py:39
  178.2 9.2 %collective-permute-done.26 = bf16[128,1536]{1,0:T(8,128)(2,1)S(1)} collective-permute-done((bf16[128,1536]{1,0:T(8,128)(2,1)S(1)}, bf16[128,1536]{1,0:T(8,128)(2,1)S(1)}, u32[]{:S(2)}, u32[]{:S(2)}) %collective-permute-start.26) | collective-permute-done | bytes 393248 | tf_op jit(solution)/shard_map/ppermute | solution.py:44
  191.3 7.0 %collective-permute-done.18 = bf16[128,1536]{1,0:T(8,128)(2,1)S(1)} collective-permute-done((bf16[128,1536]{1,0:T(8,128)(2,1)S(1)}, bf16[128,1536]{1,0:T(8,128)(2,1)S(1)}, u32[]{:S(2)}, u32[]{:S(2)}) %collective-permute-start.18) | collective-permute-done | bytes 393248 | tf_op jit(solution)/shard_map/ppermute | solution.py:44
  198.4 8.3 %collective-permute-done.10 = bf16[128,1536]{1,0:T(8,128)(2,1)S(1)} collective-permute-done((bf16[128,1536]{1,0:T(8,128)(2,1)S(1)}, bf16[128,1536]{1,0:T(8,128)(2,1)S(1)}, u32[]{:S(2)}, u32[]{:S(2)}) %collective-permute-start.10) | collective-permute-done | bytes 393248 | tf_op jit(solution)/shard_map/ppermute | solution.py:44
  206.8 8.3 %collective-permute-done.28 = bf16[128,1536]{1,0:T(8,128)(2,1)S(1)} collective-permute-done((bf16[128,1536]{1,0:T(8,128)(2,1)S(1)}, bf16[128,1536]{1,0:T(8,128)(2,1)S(1)}, u32[]{:S(2)}, u32[]{:S(2)}) %collective-permute-start.28) | collective-permute-done | bytes 393248 | tf_op jit(solution)/shard_map/ppermute | solution.py:44
  215.9 7.7 %collective-permute-done.20 = bf16[128,1536]{1,0:T(8,128)(2,1)S(1)} collective-permute-done((bf16[128,1536]{1,0:T(8,128)(2,1)S(1)}, bf16[128,1536]{1,0:T(8,128)(2,1)S(1)}, u32[]{:S(2)}, u32[]{:S(2)}) %collective-permute-start.20) | collective-permute-done | bytes 393248 | tf_op jit(solution)/shard_map/ppermute | solution.py:44
  224.6 3.2 %collective-permute-done.12 = bf16[128,1536]{1,0:T(8,128)(2,1)S(1)} collective-permute-done((bf16[128,1536]{1,0:T(8,128)(2,1)S(1)}, bf16[128,1536]{1,0:T(8,128)(2,1)S(1)}, u32[]{:S(2)}, u32[]{:S(2)}) %collective-permute-start.12) | collective-permute-done | bytes 393248 | tf_op jit(solution)/shard_map/ppermute | solution.py:44
  236.6 5.5 %collective-permute-done.46 = bf16[1,4,2,16,768]{4,3,0,1,2:T(8,128)(2,1)S(1)} collective-permute-done((bf16[1,4,2,16,768]{4,3,0,1,2:T(8,128)(2,1)S(1)}, bf16[1,4,2,16,768]{4,3,0,1,2:T(8,128)(2,1)S(1)}, u32[]{:S(2)}, u32[]{:S(2)}) %collective-permute-start.46) | collective-permute-done | bytes 196640 | tf_op jit(solution)/shard_map/ppermute | solution.py:34
  242.8 2.4 collective-permute-start.49
  245.2 2.1 collective-permute-start.47
  (255 shorter events, 78.6 us)
Async XLA Ops:
  2.6 34.3 %collective-permute-start.38 = (bf16[384,256]{1,0:T(8,128)(2,1)}, bf16[384,256]{1,0:T(8,128)(2,1)}, u32[]{:S(2)}, u32[]{:S(2)}) collective-permute-start(bf16[384,256]{1,0:T(8,128)(2,1)} %get-tuple-element.19), channel_id=1, source_target_pairs={{0,4},{4,0},{8,12},{12,8},{16,20},{20,16},{24,28},{28,24},{1,5},{5... | collective-permute-start | bytes 589832 | tf_op jit(solution)/shard_map/ppermute | solution.py:31
  14.0 21.0 %collective-permute-start.39 = (bf16[256,384]{1,0:T(8,128)(2,1)}, bf16[256,384]{1,0:T(8,128)(2,1)}, u32[]{:S(2)}, u32[]{:S(2)}) collective-permute-start(bf16[256,384]{1,0:T(8,128)(2,1)} %get-tuple-element.17), channel_id=1, source_target_pairs={{0,4},{4,0},{8,12},{12,8},{16,20},{20,16},{24,28},{28,24},{1,5},{5... | collective-permute-start | bytes 589832 | tf_op jit(solution)/shard_map/ppermute | solution.py:31
  16.6 23.6 %collective-permute-start.37 = (bf16[384,256]{1,0:T(8,128)(2,1)}, bf16[384,256]{1,0:T(8,128)(2,1)}, u32[]{:S(2)}, u32[]{:S(2)}) collective-permute-start(bf16[384,256]{1,0:T(8,128)(2,1)} %get-tuple-element.15), channel_id=1, source_target_pairs={{0,4},{4,0},{8,12},{12,8},{16,20},{20,16},{24,28},{28,24},{1,5},{5... | collective-permute-start | bytes 589832 | tf_op jit(solution)/shard_map/ppermute | solution.py:31
  18.4 53.6 %collective-permute-start.30 = (bf16[384,256]{1,0:T(8,128)(2,1)}, bf16[384,256]{1,0:T(8,128)(2,1)}, u32[]{:S(2)}, u32[]{:S(2)}) collective-permute-start(bf16[384,256]{1,0:T(8,128)(2,1)} %get-tuple-element.18), channel_id=1, source_target_pairs={{0,4},{4,0},{8,12},{12,8},{16,20},{20,16},{24,28},{28,24},{1,5},{5... | collective-permute-start | bytes 589832 | tf_op jit(solution)/shard_map/ppermute | solution.py:31
  29.1 30.8 %collective-permute-start.31 = (bf16[256,384]{1,0:T(8,128)(2,1)S(1)}, bf16[256,384]{1,0:T(8,128)(2,1)S(1)}, u32[]{:S(2)}, u32[]{:S(2)}) collective-permute-start(bf16[256,384]{1,0:T(8,128)(2,1)S(1)} %copy-done.13), channel_id=1, source_target_pairs={{0,4},{4,0},{8,12},{12,8},{16,20},{20,16},{24,28},{28,24},{1,5},{5... | collective-permute-start | bytes 589832 | tf_op jit(solution)/shard_map/ppermute | solution.py:31
  35.0 53.8 %collective-permute-start.29 = (bf16[384,256]{1,0:T(8,128)(2,1)S(1)}, bf16[384,256]{1,0:T(8,128)(2,1)S(1)}, u32[]{:S(2)}, u32[]{:S(2)}) collective-permute-start(bf16[384,256]{1,0:T(8,128)(2,1)S(1)} %copy-done.12), channel_id=1, source_target_pairs={{0,4},{4,0},{8,12},{12,8},{16,20},{20,16},{24,28},{28,24},{1,5},{5... | collective-permute-start | bytes 589832 | tf_op jit(solution)/shard_map/ppermute | solution.py:31
  36.9 25.1 %collective-permute-start.22 = (bf16[384,512]{1,0:T(8,128)(2,1)S(1)}, bf16[384,512]{1,0:T(8,128)(2,1)S(1)}, u32[]{:S(2)}, u32[]{:S(2)}) collective-permute-start(bf16[384,512]{1,0:T(8,128)(2,1)S(1)} %copy-done.10), channel_id=1, source_target_pairs={{0,4},{4,0},{8,12},{12,8},{16,20},{20,16},{24,28},{28,24},{1,5},{5... | collective-permute-start | bytes 1179656 | tf_op jit(solution)/shard_map/ppermute | solution.py:31
  40.2 18.8 %collective-permute-start.23 = (bf16[512,384]{1,0:T(8,128)(2,1)S(1)}, bf16[512,384]{1,0:T(8,128)(2,1)S(1)}, u32[]{:S(2)}, u32[]{:S(2)}) collective-permute-start(bf16[512,384]{1,0:T(8,128)(2,1)S(1)} %copy-done.11), channel_id=1, source_target_pairs={{0,4},{4,0},{8,12},{12,8},{16,20},{20,16},{24,28},{28,24},{1,5},{5... | collective-permute-start | bytes 1179656 | tf_op jit(solution)/shard_map/ppermute | solution.py:31
  59.9 31.1 %collective-permute-start.14 = (bf16[384,512]{1,0:T(8,128)(2,1)S(1)}, bf16[384,512]{1,0:T(8,128)(2,1)S(1)}, u32[]{:S(2)}, u32[]{:S(2)}) collective-permute-start(bf16[384,512]{1,0:T(8,128)(2,1)S(1)} %copy-done.8), channel_id=1, source_target_pairs={{0,4},{4,0},{8,12},{12,8},{16,20},{20,16},{24,28},{28,24},{1,5},{5... | collective-permute-start | bytes 1179656 | tf_op jit(solution)/shard_map/ppermute | solution.py:31
  62.0 25.9 %collective-permute-start.15 = (bf16[512,384]{1,0:T(8,128)(2,1)S(1)}, bf16[512,384]{1,0:T(8,128)(2,1)S(1)}, u32[]{:S(2)}, u32[]{:S(2)}) collective-permute-start(bf16[512,384]{1,0:T(8,128)(2,1)S(1)} %copy-done.9), channel_id=1, source_target_pairs={{0,4},{4,0},{8,12},{12,8},{16,20},{20,16},{24,28},{28,24},{1,5},{5... | collective-permute-start | bytes 1179656 | tf_op jit(solution)/shard_map/ppermute | solution.py:31
  71.1 25.3 %collective-permute-start.13 = (bf16[384,512]{1,0:T(8,128)(2,1)S(1)}, bf16[384,512]{1,0:T(8,128)(2,1)S(1)}, u32[]{:S(2)}, u32[]{:S(2)}) collective-permute-start(bf16[384,512]{1,0:T(8,128)(2,1)S(1)} %get-tuple-element.7), channel_id=1, source_target_pairs={{0,4},{4,0},{8,12},{12,8},{16,20},{20,16},{24,28},{28,24},{1,5},{5... | collective-permute-start | bytes 1179656 | tf_op jit(solution)/shard_map/ppermute | solution.py:31
  72.0 45.3 %collective-permute-start.6 = (bf16[384,512]{1,0:T(8,128)(2,1)S(1)}, bf16[384,512]{1,0:T(8,128)(2,1)S(1)}, u32[]{:S(2)}, u32[]{:S(2)}) collective-permute-start(bf16[384,512]{1,0:T(8,128)(2,1)S(1)} %copy-done.6), channel_id=1, source_target_pairs={{0,4},{4,0},{8,12},{12,8},{16,20},{20,16},{24,28},{28,24},{1,5},{5... | collective-permute-start | bytes 1179656 | tf_op jit(solution)/shard_map/ppermute | solution.py:31
  87.9 25.3 %collective-permute-start.7 = (bf16[512,384]{1,0:T(8,128)(2,1)S(1)}, bf16[512,384]{1,0:T(8,128)(2,1)S(1)}, u32[]{:S(2)}, u32[]{:S(2)}) collective-permute-start(bf16[512,384]{1,0:T(8,128)(2,1)S(1)} %copy-done.7), channel_id=1, source_target_pairs={{0,4},{4,0},{8,12},{12,8},{16,20},{20,16},{24,28},{28,24},{1,5},{5... | collective-permute-start | bytes 1179656 | tf_op jit(solution)/shard_map/ppermute | solution.py:31
  88.9 31.1 %collective-permute-start.5 = (bf16[384,512]{1,0:T(8,128)(2,1)S(1)}, bf16[384,512]{1,0:T(8,128)(2,1)S(1)}, u32[]{:S(2)}, u32[]{:S(2)}) collective-permute-start(bf16[384,512]{1,0:T(8,128)(2,1)S(1)} %get-tuple-element.5), channel_id=1, source_target_pairs={{0,4},{4,0},{8,12},{12,8},{16,20},{20,16},{24,28},{28,24},{1,5},{5... | collective-permute-start | bytes 1179656 | tf_op jit(solution)/shard_map/ppermute | solution.py:31
  91.0 29.4 %collective-permute-start.40 = (bf16[256,768]{0,1:T(8,128)(2,1)S(1)}, bf16[256,768]{0,1:T(8,128)(2,1)S(1)}, u32[]{:S(2)}, u32[]{:S(2)}) collective-permute-start(bf16[256,768]{0,1:T(8,128)(2,1)S(1)} %pad_maximum_fusion.10), channel_id=1, source_target_pairs={{0,8},{4,12},{24,16},{28,20},{1,9},{5,13},{25,17},{29,21},{2,10},{... | collective-permute-start | bytes 1179656 | tf_op jit(solution)/shard_map/ppermute | solution.py:39
  96.3 24.8 %collective-permute-start.32 = (bf16[256,768]{0,1:T(8,128)(2,1)S(1)}, bf16[256,768]{0,1:T(8,128)(2,1)S(1)}, u32[]{:S(2)}, u32[]{:S(2)}) collective-permute-start(bf16[256,768]{0,1:T(8,128)(2,1)S(1)} %pad_maximum_fusion.9), channel_id=1, source_target_pairs={{0,8},{4,12},{24,16},{28,20},{1,9},{5,13},{25,17},{29,21},{2,10},{... | collective-permute-start | bytes 1179656 | tf_op jit(solution)/shard_map/ppermute | solution.py:39
  113.2 38.6 %collective-permute-start.24 = (bf16[256,1536]{1,0:T(8,128)(2,1)S(1)}, bf16[256,1536]{1,0:T(8,128)(2,1)S(1)}, u32[]{:S(2)}, u32[]{:S(2)}) collective-permute-start(bf16[256,1536]{1,0:T(8,128)(2,1)S(1)} %pad_maximum_fusion.2), channel_id=1, source_target_pairs={{0,8},{4,12},{24,16},{28,20},{1,9},{5,13},{25,17},{29,21},{2,10},{... | collective-permute-start | bytes 2359304 | tf_op jit(solution)/shard_map/ppermute | solution.py:39
  117.3 35.4 %collective-permute-start.16 = (bf16[256,1536]{1,0:T(8,128)(2,1)S(1)}, bf16[256,1536]{1,0:T(8,128)(2,1)S(1)}, u32[]{:S(2)}, u32[]{:S(2)}) collective-permute-start(bf16[256,1536]{1,0:T(8,128)(2,1)S(1)} %pad_maximum_fusion.1), channel_id=1, source_target_pairs={{0,8},{4,12},{24,16},{28,20},{1,9},{5,13},{25,17},{29,21},{2,10},{... | collective-permute-start | bytes 2359304 | tf_op jit(solution)/shard_map/ppermute | solution.py:39
  122.2 19.9 %collective-permute-start.43 = (bf16[128,768]{0,1:T(8,128)(2,1)S(1)}, bf16[128,768]{0,1:T(8,128)(2,1)S(1)}, u32[]{:S(2)}, u32[]{:S(2)}) collective-permute-start(bf16[128,768]{0,1:T(8,128)(2,1)S(1)} %pad_maximum_fusion.16), channel_id=1, source_target_pairs={{8,16},{12,20},{16,8},{20,12},{9,17},{13,21},{17,9},{21,13},{10,18... | collective-permute-start | bytes 589832 | tf_op jit(solution)/shard_map/ppermute | solution.py:47
  122.9 17.9 %collective-permute-start.42 = (bf16[128,768]{0,1:T(8,128)(2,1)S(1)}, bf16[128,768]{0,1:T(8,128)(2,1)S(1)}, u32[]{:S(2)}, u32[]{:S(2)}) collective-permute-start(bf16[128,768]{0,1:T(8,128)(2,1)S(1)} %pad_maximum_fusion.16), channel_id=1, source_target_pairs={{8,0},{12,4},{16,24},{20,28},{9,1},{13,5},{17,25},{21,29},{10,2},{... | collective-permute-start | bytes 589832 | tf_op jit(solution)/shard_map/ppermute | solution.py:44
  124.3 22.4 %collective-permute-start.35 = (bf16[128,768]{0,1:T(8,128)(2,1)S(1)}, bf16[128,768]{0,1:T(8,128)(2,1)S(1)}, u32[]{:S(2)}, u32[]{:S(2)}) collective-permute-start(bf16[128,768]{0,1:T(8,128)(2,1)S(1)} %pad_maximum_fusion.15), channel_id=1, source_target_pairs={{8,16},{12,20},{16,8},{20,12},{9,17},{13,21},{17,9},{21,13},{10,18... | collective-permute-start | bytes 589832 | tf_op jit(solution)/shard_map/ppermute | solution.py:47
  142.1 21.7 %collective-permute-start.8 = (bf16[256,1536]{1,0:T(8,128)(2,1)S(1)}, bf16[256,1536]{1,0:T(8,128)(2,1)S(1)}, u32[]{:S(2)}, u32[]{:S(2)}) collective-permute-start(bf16[256,1536]{1,0:T(8,128)(2,1)S(1)} %pad_maximum_fusion), channel_id=1, source_target_pairs={{0,8},{4,12},{24,16},{28,20},{1,9},{5,13},{25,17},{29,21},{2,10},{... | collective-permute-start | bytes 2359304 | tf_op jit(solution)/shard_map/ppermute | solution.py:39
  146.7 18.2 %collective-permute-start.44 = (bf16[128,768]{0,1:T(8,128)(2,1)S(1)}, bf16[128,768]{0,1:T(8,128)(2,1)S(1)}, u32[]{:S(2)}, u32[]{:S(2)}) collective-permute-start(bf16[128,768]{0,1:T(8,128)(2,1)S(1)} %collective-permute-done.43), channel_id=1, source_target_pairs={{8,0},{12,4},{16,24},{20,28},{9,1},{13,5},{17,25},{21,29},{10,2},{... | collective-permute-start | bytes 589832 | tf_op jit(solution)/shard_map/ppermute | solution.py:44
  152.1 18.6 %collective-permute-start.25 = (bf16[128,1536]{1,0:T(8,128)(2,1)S(1)}, bf16[128,1536]{1,0:T(8,128)(2,1)S(1)}, u32[]{:S(2)}, u32[]{:S(2)}) collective-permute-start(bf16[128,1536]{1,0:T(8,128)(2,1)S(1)} %slice.311), channel_id=1, source_target_pairs={{8,16},{12,20},{16,8},{20,12},{9,17},{13,21},{17,9},{21,13},{10,18... | collective-permute-start | bytes 1179656 | tf_op jit(solution)/shard_map/ppermute | solution.py:47
  153.0 20.0 %collective-permute-start.17 = (bf16[128,1536]{1,0:T(8,128)(2,1)S(1)}, bf16[128,1536]{1,0:T(8,128)(2,1)S(1)}, u32[]{:S(2)}, u32[]{:S(2)}) collective-permute-start(bf16[128,1536]{1,0:T(8,128)(2,1)S(1)} %slice.304), channel_id=1, source_target_pairs={{8,16},{12,20},{16,8},{20,12},{9,17},{13,21},{17,9},{21,13},{10,18... | collective-permute-start | bytes 1179656 | tf_op jit(solution)/shard_map/ppermute | solution.py:47
  171.7 15.7 %collective-permute-start.26 = (bf16[128,1536]{1,0:T(8,128)(2,1)S(1)}, bf16[128,1536]{1,0:T(8,128)(2,1)S(1)}, u32[]{:S(2)}, u32[]{:S(2)}) collective-permute-start(bf16[128,1536]{1,0:T(8,128)(2,1)S(1)} %pad_maximum_fusion.8), channel_id=1, source_target_pairs={{8,0},{12,4},{16,24},{20,28},{9,1},{13,5},{17,25},{21,29},{10,2},{... | collective-permute-start | bytes 1179656 | tf_op jit(solution)/shard_map/ppermute | solution.py:44
  174.3 15.6 %collective-permute-start.11 = (bf16[128,1536]{1,0:T(8,128)(2,1)S(1)}, bf16[128,1536]{1,0:T(8,128)(2,1)S(1)}, u32[]{:S(2)}, u32[]{:S(2)}) collective-permute-start(bf16[128,1536]{1,0:T(8,128)(2,1)S(1)} %pad_maximum_fusion.6), channel_id=1, source_target_pairs={{8,16},{12,20},{16,8},{20,12},{9,17},{13,21},{17,9},{21,13},{10,18... | collective-permute-start | bytes 1179656 | tf_op jit(solution)/shard_map/ppermute | solution.py:47
  175.5 22.8 %collective-permute-start.18 = (bf16[128,1536]{1,0:T(8,128)(2,1)S(1)}, bf16[128,1536]{1,0:T(8,128)(2,1)S(1)}, u32[]{:S(2)}, u32[]{:S(2)}) collective-permute-start(bf16[128,1536]{1,0:T(8,128)(2,1)S(1)} %pad_maximum_fusion.7), channel_id=1, source_target_pairs={{8,0},{12,4},{16,24},{20,28},{9,1},{13,5},{17,25},{21,29},{10,2},{... | collective-permute-start | bytes 1179656 | tf_op jit(solution)/shard_map/ppermute | solution.py:44
  176.9 29.9 %collective-permute-start.10 = (bf16[128,1536]{1,0:T(8,128)(2,1)S(1)}, bf16[128,1536]{1,0:T(8,128)(2,1)S(1)}, u32[]{:S(2)}, u32[]{:S(2)}) collective-permute-start(bf16[128,1536]{1,0:T(8,128)(2,1)S(1)} %pad_maximum_fusion.6), channel_id=1, source_target_pairs={{8,0},{12,4},{16,24},{20,28},{9,1},{13,5},{17,25},{21,29},{10,2},{... | collective-permute-start | bytes 1179656 | tf_op jit(solution)/shard_map/ppermute | solution.py:44
  187.3 27.8 %collective-permute-start.28 = (bf16[128,1536]{1,0:T(8,128)(2,1)S(1)}, bf16[128,1536]{1,0:T(8,128)(2,1)S(1)}, u32[]{:S(2)}, u32[]{:S(2)}) collective-permute-start(bf16[128,1536]{1,0:T(8,128)(2,1)S(1)} %collective-permute-done.27), channel_id=1, source_target_pairs={{8,0},{12,4},{16,24},{20,28},{9,1},{13,5},{17,25},{21,29},{10,2},{... | collective-permute-start | bytes 1179656 | tf_op jit(solution)/shard_map/ppermute | solution.py:44
  188.6 35.0 %collective-permute-start.20 = (bf16[128,1536]{1,0:T(8,128)(2,1)S(1)}, bf16[128,1536]{1,0:T(8,128)(2,1)S(1)}, u32[]{:S(2)}, u32[]{:S(2)}) collective-permute-start(bf16[128,1536]{1,0:T(8,128)(2,1)S(1)} %collective-permute-done.19), channel_id=1, source_target_pairs={{8,0},{12,4},{16,24},{20,28},{9,1},{13,5},{17,25},{21,29},{10,2},{... | collective-permute-start | bytes 1179656 | tf_op jit(solution)/shard_map/ppermute | solution.py:44
  189.9 37.9 %collective-permute-start.12 = (bf16[128,1536]{1,0:T(8,128)(2,1)S(1)}, bf16[128,1536]{1,0:T(8,128)(2,1)S(1)}, u32[]{:S(2)}, u32[]{:S(2)}) collective-permute-start(bf16[128,1536]{1,0:T(8,128)(2,1)S(1)} %collective-permute-done.11), channel_id=1, source_target_pairs={{8,0},{12,4},{16,24},{20,28},{9,1},{13,5},{17,25},{21,29},{10,2},{... | collective-permute-start | bytes 1179656 | tf_op jit(solution)/shard_map/ppermute | solution.py:44
  (35 other events, 269.4 us)

commit v2 on v1

v2 whole, which is shorter than its diff:
```python
import jax
import jax.numpy as jnp
from jax import lax
from jax.experimental import pallas as pl
from jax.experimental.pallas import tpu as pltpu
from jax.sharding import PartitionSpec as P

F32 = jnp.float32
BF16 = jnp.bfloat16
LANES = 128
AHEAD = 2


def dot(left, right):
    return jnp.dot(left, right, preferred_element_type=F32)


def dot_last(left, right):
    return lax.dot_general(left, right, (((1,), (1,)), ((), ())), preferred_element_type=F32)


def chunk_cuts(units):
    blocks = units // LANES
    if blocks < 8:
        sizes = [1] * blocks
    else:
        sizes = [2 * (blocks // 8)] * 3 + [blocks // 8] * 2
    cuts = [0]
    for size in sizes:
        cuts.append(cuts[-1] + size * LANES)
    return cuts


def make_plain(n_fsdp, n_et):
    n_half = n_fsdp // 4

    def f_swap(values, mask):
        return lax.ppermute(values, "fsdp", [(f, f ^ mask) for f in range(n_fsdp)])

    def e_swap(values, mask):
        return lax.ppermute(values, "et", [(e, e ^ mask) for e in range(n_et)])

    def zp_flip(values):
        return jnp.concatenate([values[..., 1:2, :], values[..., 0:1, :]], axis=-2)

    def zp_step(values):
        return f_swap(zp_flip(values), 2)

    steps = [zp_step]
    mask = n_et // 2
    while mask >= 1:
        steps.append(lambda values, mask=mask: e_swap(values, mask))
        mask //= 2

    def per_device(tokens, cotangent, route_experts, route_gates, w_gate, w_up, w_down):
        own_count, width = tokens.shape
        most = own_count // 8
        own_width, hidden_units = w_gate.shape
        half_units = hidden_units // 2
        f_index = lax.axis_index("fsdp")
        z_half = f_index // 4
        z_low = (f_index // 2) % 2
        y_index = f_index % 2

        cuts = chunk_cuts(half_units)
        keep_at = z_low * half_units
        give_at = (1 - z_low) * half_units

        def part_of(start, size):
            return jnp.stack(
                [
                    lax.dynamic_slice_in_dim(w_gate, start, size, axis=1),
                    lax.dynamic_slice_in_dim(w_up, start, size, axis=1),
                    lax.dynamic_slice_in_dim(w_down, start, size, axis=0).T,
                ]
            )

        count = len(cuts) - 1
        kept, given = [], []
        for lo, hi in zip(cuts[:-1], cuts[1:]):
            kept.append(part_of(keep_at + lo, hi - lo))
            given.append(part_of(give_at + lo, hi - lo))
        near, far = [None] * count, [None] * count

        def start_pair(k):
            near[k] = jnp.concatenate([kept[k], f_swap(given[k], 2)], axis=1)

        first_far = f_swap(kept[0], 1)
        first_pair = f_swap(given[0], 2)
        near[0] = jnp.concatenate([kept[0], first_pair], axis=1)
        far[0] = jnp.concatenate([first_far, f_swap(first_pair, 1)], axis=1)
        for k in range(1, min(AHEAD, count)):
            start_pair(k)
            far[k] = f_swap(near[k], 1)

        own_start = lax.axis_index("et") * own_count
        own_experts = lax.dynamic_slice_in_dim(route_experts, own_start, own_count)
        own_gates = lax.dynamic_slice_in_dim(route_gates, own_start, own_count)
        is_first = own_experts[:, 0] == 0
        is_second = own_experts[:, 1] == 0
        chosen = jnp.logical_or(is_first, is_second)
        weight = jnp.where(is_first, own_gates[:, 0], 0.0) + jnp.where(
            is_second, own_gates[:, 1], 0.0
        )
        chosen_int = chosen.astype(jnp.int32)
        slot = jnp.cumsum(chosen_int) - chosen_int
        picks = jnp.logical_and(
            chosen[None, :], slot[None, :] == jnp.arange(most, dtype=jnp.int32)[:, None]
        )
        one_hot = picks.astype(BF16)
        packed_weight = jnp.sum(jnp.where(picks, weight[None, :], 0.0), axis=1)
        packed_rows = dot(one_hot, tokens).astype(BF16)
        packed_cot = (packed_weight[:, None] * dot(one_hot, cotangent)).astype(BF16)
        packed = jnp.concatenate([packed_rows, packed_cot], axis=0)

        cols = packed.reshape(2 * most, n_half, 2, 2, own_width)
        cols = jnp.where(z_low == 0, cols, cols[:, :, ::-1])
        cols = jnp.where(y_index == 0, cols, cols[:, :, :, ::-1])
        cols = jnp.transpose(cols, (1, 0, 3, 2, 4))
        blocks = []
        for d in range(n_half):
            block = lax.dynamic_index_in_dim(cols, z_half ^ d, 0, keepdims=False)
            blocks.append(block if d == 0 else f_swap(block, 4 * d))
        rows = jnp.stack(blocks)[None]
        for step in steps:
            rows = jnp.concatenate([rows, step(rows)], axis=0)
        members = rows.shape[0]
        slots = n_half * members * most
        rows = rows.reshape(members, n_half, 2, most, 2, 2 * own_width)
        rows = jnp.transpose(rows, (2, 4, 1, 0, 3, 5)).reshape(2, 2, slots, 2 * own_width)
        x_near, x_far, cot_near, cot_far = rows[0, 0], rows[0, 1], rows[1, 0], rows[1, 1]

        own_slots = slots // n_half
        total = None
        for k in range(count):
            units = kept[k].shape[2]
            near_k, far_k = near[k], far[k]
            gate = dot(x_near, near_k[0]) + dot(x_far, far_k[0])
            up = dot(x_near, near_k[1]) + dot(x_far, far_k[1])
            grad = dot(cot_near, near_k[2]) + dot(cot_far, far_k[2])
            part = jnp.concatenate([gate, up, grad], axis=1)
            sent = part[own_slots:].astype(BF16).reshape(n_half - 1, own_slots, 3 * units)
            if k + AHEAD < count:
                held = lax.optimization_barrier((kept[k + AHEAD], given[k + AHEAD], sent))
                kept[k + AHEAD], given[k + AHEAD], sent = held
                start_pair(k + AHEAD)
                far[k + AHEAD] = f_swap(near[k + AHEAD], 1)
            pre = part[:own_slots]
            for d in range(1, n_half):
                pre = pre + f_swap(sent[d - 1], 4 * d).astype(F32)
            gate, up, grad = pre[:, :units], pre[:, units : 2 * units], pre[:, 2 * units :]
            sig = jax.nn.sigmoid(gate)
            hidden = gate * sig * up
            grad_gate = grad * up * sig * (1.0 + gate * (1.0 - sig))
            grad_up = grad * gate * sig
            mine = jnp.concatenate([hidden, grad_gate, grad_up], axis=1).astype(BF16)
            full = jnp.concatenate([mine] + [f_swap(mine, 4 * d) for d in range(1, n_half)], axis=0)
            hidden, grad_gate, grad_up = (
                full[:, :units],
                full[:, units : 2 * units],
                full[:, 2 * units :],
            )
            terms = (
                dot_last(hidden, near_k[2]),
                dot_last(hidden, far_k[2]),
                dot_last(grad_gate, near_k[0]) + dot_last(grad_up, near_k[1]),
                dot_last(grad_gate, far_k[0]) + dot_last(grad_up, far_k[1]),
            )
            total = terms if total is None else tuple(a + b for a, b in zip(total, terms))

        sums = jnp.stack([jnp.stack(total[:2]), jnp.stack(total[2:])])
        sums = sums.reshape(2, 2, n_half, members, most, 2, own_width)
        sums = jnp.transpose(sums, (3, 2, 0, 4, 1, 5, 6))
        for step in reversed(steps):
            rest = sums.shape[0] // 2
            sums = sums[:rest] + step(sums[rest:].astype(BF16)).astype(F32)
        sums = sums[0].astype(BF16)
        back = [sums[0]] + [f_swap(sums[d], 4 * d) for d in range(1, n_half)]
        back = jnp.stack(back)
        order = jnp.arange(n_half, dtype=jnp.int32) ^ z_half
        back = jnp.take(back, order, axis=0)
        back = jnp.transpose(back, (1, 2, 0, 4, 3, 5))
        back = jnp.where(z_low == 0, back, back[:, :, :, ::-1])
        back = jnp.where(y_index == 0, back, back[:, :, :, :, ::-1])
        own_sums = back.reshape(2, most, width)
        spread = one_hot.T
        moe_out = (weight[:, None] * dot(spread, own_sums[0])).astype(BF16)
        grad_tokens = dot(spread, own_sums[1]).astype(BF16)
        return moe_out, grad_tokens

    return per_device


def call(body, outs, *args, scratch=(), flops=0):
    moved = sum(v.size * v.dtype.itemsize for v in list(args) + list(outs))
    return pl.pallas_call(
        body,
        out_shape=list(outs),
        scratch_shapes=list(scratch),
        compiler_params=pltpu.CompilerParams(vmem_limit_bytes=40 * 1024 * 1024),
        cost_estimate=pl.CostEstimate(flops=flops, bytes_accessed=moved, transcendentals=0),
    )(*args)


def shaped(shape, kind):
    return jax.ShapeDtypeStruct(shape, kind)


def flip_pairs(values, own_width):
    parts = [values[..., i * own_width : (i + 1) * own_width] for i in (1, 0, 3, 2)]
    return jnp.concatenate(parts, axis=-1)


def route_columns(experts_ref, gates_ref):
    count = experts_ref.shape[0] // 4
    start = pl.multiple_of(lax.axis_index("et") * count, count)
    experts = experts_ref[pl.ds(start, count), :]
    gates = gates_ref[pl.ds(start, count), :]
    hits = (experts == 0).astype(F32)
    chosen = jnp.sum(hits, axis=1, keepdims=True)
    weight = jnp.sum(hits * gates, axis=1, keepdims=True)
    return chosen, weight


def as_row(column, keep):
    return jnp.sum(jnp.where(keep, column, 0.0), axis=0, keepdims=True)


def weight_chunk_body(low_ref, *refs):
    for gate, up, down, out in (refs[0:3] + refs[6:7], refs[3:6] + refs[7:8]):
        out[0] = gate[...]
        out[1] = up[...]
        out[2] = down[...].T


def weight_chunk(low, w_gate, w_up, w_down, lo, size):
    own_width, hidden_units = w_gate.shape
    half = hidden_units // 2 // size
    at = lo // size

    def spec(kept, rows):
        def index(i, low_ref):
            block = at + half * (low_ref[0] if kept else 1 - low_ref[0])
            return (block, 0) if rows else (0, block)

        return pl.BlockSpec((size, own_width) if rows else (own_width, size), index)

    out = shaped((3, own_width, size), BF16)
    specs = [spec(kept, rows) for kept in (True, False) for rows in (False, False, True)]
    whole = pl.BlockSpec((3, own_width, size), lambda i, low_ref: (0, 0, 0))
    return pl.pallas_call(
        weight_chunk_body,
        out_shape=[out, out],
        grid_spec=pltpu.PrefetchScalarGridSpec(
            num_scalar_prefetch=1, grid=(1,), in_specs=specs, out_specs=[whole, whole]
        ),
        compiler_params=pltpu.CompilerParams(vmem_limit_bytes=40 * 1024 * 1024),
        cost_estimate=pl.CostEstimate(
            flops=0, bytes_accessed=12 * out.size * 2, transcendentals=0
        ),
    )(low, w_gate, w_up, w_down, w_gate, w_up, w_down)


def make_fused(n_fsdp, n_et):
    world = n_fsdp * n_et

    def swap(values, mask):
        pairs = [(i, i ^ mask) for i in range(world)]
        return lax.ppermute(values, ("fsdp", "et"), pairs)

    at_y, at_zp, at_zh = n_et, 2 * n_et, 4 * n_et
    at_core, at_x = 1, 2

    def per_device(tokens, cotangent, route_experts, route_gates, w_gate, w_up, w_down):
        own_count, width = tokens.shape
        most = own_count // 8
        own_width, hidden_units = w_gate.shape
        half_units = hidden_units // 2
        z_width = 4 * own_width
        block_shape = (2, most, z_width)
        low = ((lax.axis_index("fsdp") // 2) % 2).astype(jnp.int32).reshape(1)

        cuts = chunk_cuts(half_units)
        count = len(cuts) - 1
        own_w, zp_w, far_own, far_zp = ([None] * count for _ in range(4))
        given = [None] * count

        def make_chunk(k):
            own_w[k], given[k] = weight_chunk(
                low, w_gate, w_up, w_down, cuts[k], cuts[k + 1] - cuts[k]
            )

        def send_chunk(k):
            zp_w[k] = swap(given[k], at_zp)
            far_own[k] = swap(own_w[k], at_y)
            far_zp[k] = swap(zp_w[k], at_y)

        make_chunk(0)
        send_chunk(0)
        tokens, cotangent, own_w[0] = lax.optimization_barrier((tokens, cotangent, own_w[0]))

        def pack_body(tokens_ref, cot_ref, experts_ref, gates_ref, keep_ref, send_ref, packed_ref):
            chosen, weight = route_columns(experts_ref, gates_ref)
            shape = (own_count, own_count)
            down = lax.broadcasted_iota(jnp.int32, shape, 0)
            across = lax.broadcasted_iota(jnp.int32, shape, 1)
            chosen_row = as_row(chosen, down == across)
            weight_row = as_row(weight, down == across)
            slot_row = as_row(chosen, down < across)
            places = lax.broadcasted_iota(jnp.int32, (most, own_count), 0).astype(F32)
            picks = jnp.logical_and(slot_row == places, chosen_row > 0.0)
            one_hot = jnp.where(picks, 1.0, 0.0).astype(BF16)
            slot_weight = jnp.sum(jnp.where(picks, weight_row, 0.0), axis=1, keepdims=True)
            packed_ref[0] = dot(one_hot, tokens_ref[...]).astype(BF16)
            packed_ref[1] = (slot_weight * dot(one_hot, cot_ref[...])).astype(BF16)
            f_index = lax.axis_index("fsdp")
            for d, out in enumerate((keep_ref, send_ref)):
                for i in range(4):
                    mask = 4 * d + 2 * (i % 2) + i // 2
                    start = pl.multiple_of((f_index ^ mask) * own_width, LANES)
                    columns = slice(i * own_width, (i + 1) * own_width)
                    out[:, :, columns] = packed_ref[:, :, pl.ds(start, own_width)]

        block = shaped(block_shape, BF16)
        mine, sent = call(
            pack_body,
            [block, block],
            tokens,
            cotangent,
            route_experts,
            route_gates,
            scratch=[pltpu.VMEM((2, most, width), BF16)],
            flops=4 * most * own_count * width,
        )
        other = swap(sent, at_zh)
        if count > 1:
            make_chunk(1)
            send_chunk(1)

        def join_body(mine_ref, other_ref, plain_ref, flipped_ref):
            for j, ref in enumerate((mine_ref, other_ref)):
                values = ref[...]
                plain_ref[j] = values
                flipped_ref[j] = flip_pairs(values, own_width)

        pair = shaped((2,) + block_shape, BF16)
        plain, flipped = call(join_body, [pair, pair], mine, other)
        near_rows = jnp.stack(
            [plain, swap(plain, at_x), swap(flipped, at_zp), swap(flipped, at_zp + at_x)]
        )
        far_rows = swap(near_rows, at_core)

        slots = 16 * most
        own_slots = slots // 2

        def rows_of(near_ref, far_ref, which):
            parts = [ref[:, :, which].reshape(own_slots, z_width) for ref in (near_ref, far_ref)]
            return jnp.concatenate(parts, axis=0)

        def first_body(near_ref, far_ref, a_ref, b_ref, c_ref, d_ref, keep_ref, send_ref):
            units = a_ref.shape[2]
            rows = rows_of(near_ref, far_ref, 0)
            cots = rows_of(near_ref, far_ref, 1)
            for j in range(3):
                left = cots if j == 2 else rows
                value = None
                for i, ref in enumerate((a_ref, b_ref, c_ref, d_ref)):
                    term = dot(left[:, i * own_width : (i + 1) * own_width], ref[j])
                    value = term if value is None else value + term
                value = value.reshape(8, 2, most, units)
                columns = slice(j * units, (j + 1) * units)
                keep_ref[:, columns] = value[:, 0].reshape(own_slots, units)
                send_ref[:, columns] = value[:, 1].reshape(own_slots, units).astype(BF16)

        def middle_body(keep_ref, recv_ref, out_ref):
            units = keep_ref.shape[1] // 3
            pre = keep_ref[...] + recv_ref[...].astype(F32)
            gate, up, grad = pre[:, :units], pre[:, units : 2 * units], pre[:, 2 * units :]
            sig = 1.0 / (1.0 + jnp.exp(-gate))
            out_ref[:, :units] = (gate * sig * up).astype(BF16)
            out_ref[:, units : 2 * units] = (
                grad * up * sig * (1.0 + gate * (1.0 - sig))
            ).astype(BF16)
            out_ref[:, 2 * units :] = (grad * gate * sig).astype(BF16)

        def second_terms(mine_ref, recv_ref, refs):
            units = refs[0].shape[2]
            full = jnp.concatenate([mine_ref[...], recv_ref[...]], axis=0)
            hidden, grad_gate, grad_up = (
                full[:, j * units : (j + 1) * units] for j in range(3)
            )
            outs = [dot_last(hidden, ref[2]) for ref in refs]
            grads = [dot_last(grad_gate, ref[0]) + dot_last(grad_up, ref[1]) for ref in refs]
            return outs, grads

        def second_body(first, last, mine_ref, recv_ref, a_ref, b_ref, c_ref, d_ref, *rest):
            terms = second_terms(mine_ref, recv_ref, (a_ref, b_ref, c_ref, d_ref))
            rest = list(rest)
            held = None if first else rest.pop(0)
            for which in range(2):
                for i in range(4):
                    columns = slice(i * own_width, (i + 1) * own_width)
                    value = terms[which][i]
                    if held is not None:
                        value = value + held[which, :, columns]
                    if not last:
                        rest[0][which, :, columns] = value
                        continue
                    value = value.reshape(2, 2, 4, most, own_width)
                    for j in range(2):
                        rest[0][:, j, which, :, columns] = value[j, 0]
                        rest[1][:, j, which, :, columns] = value[j, 1].astype(BF16)

        total = None
        quad = (4, 2) + block_shape
        for k in range(count):
            units = cuts[k + 1] - cuts[k]
            work = 2 * slots * z_width * units * 3
            weights = (own_w[k], zp_w[k], far_own[k], far_zp[k])
            keep, sent = call(
                first_body,
                [shaped((own_slots, 3 * units), F32), shaped((own_slots, 3 * units), BF16)],
                near_rows,
                far_rows,
                *weights,
                flops=work,
            )
            if k + AHEAD < count:
                make_chunk(k + AHEAD)
                own_w[k + AHEAD], given[k + AHEAD], sent = lax.optimization_barrier(
                    (own_w[k + AHEAD], given[k + AHEAD], sent)
                )
                send_chunk(k + AHEAD)
            (mine,) = call(
                middle_body,
                [shaped((own_slots, 3 * units), BF16)],
                keep,
                swap(sent, at_zh),
            )
            first, last = k == 0, k == count - 1
            outs = (
                [shaped(quad, F32), shaped(quad, BF16)]
                if last
                else [shaped((2, slots, z_width), F32)]
            )
            held = () if first else (total,)
            total = call(
                lambda *refs, first=first, last=last: second_body(first, last, *refs),
                outs,
                mine,
                swap(mine, at_zh),
                *weights,
                *held,
                flops=work,
            )
            if not last:
                (total,) = total

        def spread_body(keep_ref, recv_ref, own_ref, *outs):
            value = keep_ref[...] + recv_ref[...].astype(F32)
            own_ref[...] = value[0]
            for i in range(1, 4):
                part = value[i].astype(BF16)
                outs[i - 1][...] = flip_pairs(part, own_width) if i >= 2 else part

        keep, sent = total
        own, by_x, by_zp, by_both = call(
            spread_body,
            [shaped(pair.shape, F32), pair, pair, pair],
            keep,
            swap(sent, at_core),
        )

        def gather_body(own_ref, x_ref, zp_ref, both_ref, keep_ref, send_ref):
            value = own_ref[...] + x_ref[...].astype(F32)
            value = value + (zp_ref[...].astype(F32) + both_ref[...].astype(F32))
            keep_ref[...] = value[0].astype(BF16)
            send_ref[...] = value[1].astype(BF16)

        mine, sent = call(
            gather_body,
            [block, block],
            own,
            swap(by_x, at_x),
            swap(by_zp, at_zp),
            swap(by_both, at_zp + at_x),
        )

        def unpack_body(mine_ref, other_ref, experts_ref, gates_ref, out_ref, grad_ref, sums_ref):
            f_index = lax.axis_index("fsdp")
            for d, ref in enumerate((mine_ref, other_ref)):
                for i in range(4):
                    mask = 4 * d + 2 * (i % 2) + i // 2
                    start = pl.multiple_of((f_index ^ mask) * own_width, LANES)
                    columns = slice(i * own_width, (i + 1) * own_width)
                    sums_ref[:, :, pl.ds(start, own_width)] = ref[:, :, columns]
            chosen, weight = route_columns(experts_ref, gates_ref)
            shape = (own_count, own_count)
            down = lax.broadcasted_iota(jnp.int32, shape, 0)
            across = lax.broadcasted_iota(jnp.int32, shape, 1)
            chosen_row = as_row(chosen, down == across)
            slot = jnp.sum(jnp.where(across < down, chosen_row, 0.0), axis=1, keepdims=True)
            places = lax.broadcasted_iota(jnp.int32, (own_count, most), 1).astype(F32)
            picks = jnp.logical_and(slot == places, chosen > 0.0)
            spread = jnp.where(picks, 1.0, 0.0).astype(BF16)
            out_ref[...] = (weight * dot(spread, sums_ref[0])).astype(BF16)
            grad_ref[...] = dot(spread, sums_ref[1]).astype(BF16)

        result = shaped(tokens.shape, BF16)
        return tuple(
            call(
                unpack_body,
                [result, result],
                mine,
                swap(sent, at_zh),
                route_experts,
                route_gates,
                scratch=[pltpu.VMEM((2, most, width), BF16)],
                flops=4 * most * own_count * width,
            )
        )

    return per_device


def solution(mesh):
    sizes = dict(mesh.shape)
    make = make_fused if sizes["fsdp"] == 8 and sizes["et"] == 4 else make_plain
    in_specs = (
        P(("fsdp", "et"), None),
        P(("fsdp", "et"), None),
        P("fsdp", None),
        P("fsdp", None),
        P("fsdp", "et"),
        P("fsdp", "et"),
        P("et", "fsdp"),
    )
    out_specs = (P(("fsdp", "et"), None), P(("fsdp", "et"), None))
    return jax.shard_map(
        make(sizes["fsdp"], sizes["et"]),
        mesh=mesh,
        in_specs=in_specs,
        out_specs=out_specs,
        check_vma=False,
    )
```

time: 255 us -> 216 us (0.85)
  matrix products: 28.1 us -> 0 us
  starting transfers between devices: 63.8 us -> 44.3 us
  Pallas kernels: 0 us -> 12.6 us
  other arithmetic: 7.7 us -> 0.1 us
  waiting for transfers between devices: 139 us -> 146 us
    dot_general x64 -> x0, matrix products: 28.1 us -> none  [the longest x34 15.3 us: dot(): return jnp.dot(left, right, preferred_element_type=F32)]
    ppermute x50 -> x35, starting transfers between devices: 63.8 us -> 44.3 us  [swap(): return lax.ppermute(values, ('fsdp', 'et'), pairs)]
    pallas_call x0 -> x25, Pallas kernels: none -> 12.6 us  [the longest x20 11.7 us: call(): pl.pallas_call(body, out_shape=list(outs), scratch_shapes=list(scratch),...]
    unnamed x36 -> x34, local copies, waits for them, and re-layouts: 1.3 us -> 11.5 us
    slice x20 -> x0, local copies, waits for them, and re-layouts: 8.41 us -> none  [the longest x6 7.97 us: per_device(): own = (w_gate[:, lo:hi], w_up[:, lo:hi], w_down[lo:hi, :])]
    ppermute x50 -> x35, waiting for transfers between devices: 139 us -> 146 us  [swap(): return lax.ppermute(values, ('fsdp', 'et'), pairs)]
  transfers between devices with their start and end apart: 50 -> 35, of which waited for: 20 -> 25; matrix products, arithmetic and copies ran while one was open for 14% -> 0% of each run, Pallas kernels for 0% -> 4%
where the time goes in v2:
time: 216 us
  waiting for transfers between devices  146 us (68%)
  starting transfers between devices  44.3 us (21%)
  Pallas kernels  12.6 us (6%)
  local copies, waits for them, and re-layouts  11.5 us (5%)
    ppermute x35, waiting for transfers between devices, swap(): return lax.ppermute(values, ('fsdp', 'et'), pairs)  146 us
    ppermute x35, starting transfers between devices, swap(): return lax.ppermute(values, ('fsdp', 'et'), pairs)  44.3 us
    pallas_call x20, Pallas kernels, call(): pl.pallas_call(body, out_shape=list(outs), scratch_shapes=list(scratch),...  11.7 us
    unnamed x34, local copies, waits for them, and re-layouts  11.5 us
  transfers between devices with their start and end apart: 35, of which 25 were waited for; matrix products, arithmetic and copies ran while one was open for 0% of the time, Pallas kernels for 4%

profile of v2, /device:TPU:0, one launch (start us, length us, event | category | flops | bytes accessed | tf_op | source)
XLA Modules:
  0.0 215.8 jit_solution(15892560850628966043)
XLA Ops:
  11.4 4.1 %collective-permute-start = (bf16[2,16,1536]{2,1,0:T(8,128)(2,1)S(1)}, bf16[2,16,1536]{2,1,0:T(8,128)(2,1)S(1)}, u32[]{:S(2)}, u32[]{:S(2)}) collective-permute-start(bf16[2,16,1536]{2,1,0:T(8,128)(2,1)S(1)} %get-tuple-element.50), channel_id=1, source_target_pairs={{0,16},{1,17},{2,18},{3,19},{4,20},{5,21},{6,22},{7,23},{8,24},{9,... | collective-permute-start | bytes 294920 | tf_op jit(solution)/shard_map/ppermute | solution.py:269
  15.5 4.9 %collective-permute-done.other_ref = bf16[2,16,1536]{2,1,0:T(8,128)(2,1)S(1)} collective-permute-done((bf16[2,16,1536]{2,1,0:T(8,128)(2,1)S(1)}, bf16[2,16,1536]{2,1,0:T(8,128)(2,1)S(1)}, u32[]{:S(2)}, u32[]{:S(2)}) %collective-permute-start) | collective-permute-done | bytes 98336 | tf_op jit(solution)/shard_map/ppermute | solution.py:269
  20.4 1.6 collective-permute-start.1
  24.7 2.7 %collective-permute-done.1 = bf16[2,2,16,1536]{3,2,1,0:T(8,128)(2,1)S(1)} collective-permute-done((bf16[2,2,16,1536]{3,2,1,0:T(8,128)(2,1)S(1)}, bf16[2,2,16,1536]{3,2,1,0:T(8,128)(2,1)S(1)}, u32[]{:S(2)}, u32[]{:S(2)}) %collective-permute-start.1) | collective-permute-done | bytes 196640 | tf_op jit(solution)/shard_map/ppermute | solution.py:269
  27.4 2.5 %collective-permute-done.2 = bf16[2,2,16,1536]{3,2,1,0:T(8,128)(2,1)S(1)} collective-permute-done((bf16[2,2,16,1536]{3,2,1,0:T(8,128)(2,1)S(1)}, bf16[2,2,16,1536]{3,2,1,0:T(8,128)(2,1)S(1)}, u32[]{:S(2)}, u32[]{:S(2)}) %collective-permute-start.2) | collective-permute-done | bytes 196640 | tf_op jit(solution)/shard_map/ppermute | solution.py:269
  29.9 4.1 %collective-permute-done.3 = bf16[2,2,16,1536]{3,2,1,0:T(8,128)(2,1)S(1)} collective-permute-done((bf16[2,2,16,1536]{3,2,1,0:T(8,128)(2,1)S(1)}, bf16[2,2,16,1536]{3,2,1,0:T(8,128)(2,1)S(1)}, u32[]{:S(2)}, u32[]{:S(2)}) %collective-permute-start.3) | collective-permute-done | bytes 196640 | tf_op jit(solution)/shard_map/ppermute | solution.py:269
  35.7 8.7 %collective-permute-done.5.b_ref.refs_3_ = bf16[3,384,256]{2,1,0:T(8,128)(2,1)S(1)} collective-permute-done((bf16[3,384,256]{2,1,0:T(8,128)(2,1)}, bf16[3,384,256]{2,1,0:T(8,128)(2,1)S(1)}, u32[]{:S(2)}, u32[]{:S(2)}) %collective-permute-start.5) | collective-permute-done | bytes 589856 | tf_op jit(solution)/shard_map/ppermute | solution.py:269
  47.5 1.8 collective-permute-start.16
  50.4 12.2 %collective-permute-done.7.d_ref.refs_5_ = bf16[3,384,256]{2,1,0:T(8,128)(2,1)S(1)} collective-permute-done((bf16[3,384,256]{2,1,0:T(8,128)(2,1)S(1)}, bf16[3,384,256]{2,1,0:T(8,128)(2,1)S(1)}, u32[]{:S(2)}, u32[]{:S(2)}) %collective-permute-start.7) | collective-permute-done | bytes 589856 | tf_op jit(solution)/shard_map/ppermute | solution.py:269
  67.9 10.6 %collective-permute-done.8.b_ref.refs_3_ = bf16[3,384,256]{2,1,0:T(8,128)(2,1)S(1)} collective-permute-done((bf16[3,384,256]{2,1,0:T(8,128)(2,1)S(1)}, bf16[3,384,256]{2,1,0:T(8,128)(2,1)S(1)}, u32[]{:S(2)}, u32[]{:S(2)}) %collective-permute-start.8) | collective-permute-done | bytes 589856 | tf_op jit(solution)/shard_map/ppermute | solution.py:269
  80.6 12.6 %collective-permute-done.18.d_ref.refs_5_ = bf16[3,384,256]{2,1,0:T(8,128)(2,1)S(1)} collective-permute-done((bf16[3,384,256]{2,1,0:T(8,128)(2,1)S(1)}, bf16[3,384,256]{2,1,0:T(8,128)(2,1)S(1)}, u32[]{:S(2)}, u32[]{:S(2)}) %collective-permute-start.18) | collective-permute-done | bytes 589856 | tf_op jit(solution)/shard_map/ppermute | solution.py:269
  95.6 10.3 %collective-permute-done.9.c_ref.refs_4_ = bf16[3,384,256]{2,1,0:T(8,128)(2,1)S(1)} collective-permute-done((bf16[3,384,256]{2,1,0:T(8,128)(2,1)S(1)}, bf16[3,384,256]{2,1,0:T(8,128)(2,1)S(1)}, u32[]{:S(2)}, u32[]{:S(2)}) %collective-permute-start.9) | collective-permute-done | bytes 589856 | tf_op jit(solution)/shard_map/ppermute | solution.py:269
  105.9 11.0 %collective-permute-done.10.d_ref.refs_5_ = bf16[3,384,256]{2,1,0:T(8,128)(2,1)S(1)} collective-permute-done((bf16[3,384,256]{2,1,0:T(8,128)(2,1)S(1)}, bf16[3,384,256]{2,1,0:T(8,128)(2,1)S(1)}, u32[]{:S(2)}, u32[]{:S(2)}) %collective-permute-start.10) | collective-permute-done | bytes 589856 | tf_op jit(solution)/shard_map/ppermute | solution.py:269
  119.2 2.4 %collective-permute-start.28 = (bf16[128,768]{1,0:T(8,128)(2,1)S(1)}, bf16[128,768]{1,0:T(8,128)(2,1)S(1)}, u32[]{:S(2)}, u32[]{:S(2)}) collective-permute-start(bf16[128,768]{1,0:T(8,128)(2,1)S(1)} %get-tuple-element.81), channel_id=1, source_target_pairs={{0,16},{1,17},{2,18},{3,19},{4,20},{5,21},{6,22},{7,23},{8,24},{9,... | collective-permute-start | bytes 589832 | tf_op jit(solution)/shard_map/ppermute | solution.py:269
  124.2 6.3 %collective-permute-done.28.recv_ref = bf16[128,768]{1,0:T(8,128)(2,1)S(1)} collective-permute-done((bf16[128,768]{1,0:T(8,128)(2,1)S(1)}, bf16[128,768]{1,0:T(8,128)(2,1)S(1)}, u32[]{:S(2)}, u32[]{:S(2)}) %collective-permute-start.28) | collective-permute-done | bytes 196640 | tf_op jit(solution)/shard_map/ppermute | solution.py:269
  132.2 1.5 collective-permute-start.13
  133.7 5.7 %collective-permute-done.26.recv_ref = bf16[128,768]{1,0:T(8,128)(2,1)S(1)} collective-permute-done((bf16[128,768]{1,0:T(8,128)(2,1)S(1)}, bf16[128,768]{1,0:T(8,128)(2,1)S(1)}, u32[]{:S(2)}, u32[]{:S(2)}) %collective-permute-start.26) | collective-permute-done | bytes 196640 | tf_op jit(solution)/shard_map/ppermute | solution.py:269
  139.6 3.0 %collective-permute-start.29 = (bf16[128,768]{1,0:T(8,128)(2,1)S(1)}, bf16[128,768]{1,0:T(8,128)(2,1)S(1)}, u32[]{:S(2)}, u32[]{:S(2)}) collective-permute-start(bf16[128,768]{1,0:T(8,128)(2,1)S(1)} %shard_map.102.refs_0_), channel_id=1, source_target_pairs={{0,16},{1,17},{2,18},{3,19},{4,20},{5,21},{6,22},{7,23},{8,24},{9,... | collective-permute-start | bytes 589832 | tf_op jit(solution)/shard_map/ppermute | solution.py:269
  142.6 9.6 %collective-permute-done.24.recv_ref = bf16[128,768]{1,0:T(8,128)(2,1)S(1)} collective-permute-done((bf16[128,768]{1,0:T(8,128)(2,1)S(1)}, bf16[128,768]{1,0:T(8,128)(2,1)S(1)}, u32[]{:S(2)}, u32[]{:S(2)}) %collective-permute-start.24) | collective-permute-done | bytes 196640 | tf_op jit(solution)/shard_map/ppermute | solution.py:269
  152.4 3.0 %collective-permute-start.25 = (bf16[128,768]{1,0:T(8,128)(2,1)S(1)}, bf16[128,768]{1,0:T(8,128)(2,1)S(1)}, u32[]{:S(2)}, u32[]{:S(2)}) collective-permute-start(bf16[128,768]{1,0:T(8,128)(2,1)S(1)} %shard_map.100.refs_0_), channel_id=1, source_target_pairs={{0,16},{1,17},{2,18},{3,19},{4,20},{5,21},{6,22},{7,23},{8,24},{9,... | collective-permute-start | bytes 589832 | tf_op jit(solution)/shard_map/ppermute | solution.py:269
  157.0 3.0 %collective-permute-start.14 = (bf16[128,384]{1,0:T(8,128)(2,1)S(1)}, bf16[128,384]{1,0:T(8,128)(2,1)S(1)}, u32[]{:S(2)}, u32[]{:S(2)}) collective-permute-start(bf16[128,384]{1,0:T(8,128)(2,1)S(1)} %get-tuple-element.66), channel_id=1, source_target_pairs={{0,16},{1,17},{2,18},{3,19},{4,20},{5,21},{6,22},{7,23},{8,24},{9,... | collective-permute-start | bytes 294920 | tf_op jit(solution)/shard_map/ppermute | solution.py:269
  161.0 22.5 %collective-permute-done.22.recv_ref = bf16[128,384]{1,0:T(8,128)(2,1)S(1)} collective-permute-done((bf16[128,384]{1,0:T(8,128)(2,1)S(1)}, bf16[128,384]{1,0:T(8,128)(2,1)S(1)}, u32[]{:S(2)}, u32[]{:S(2)}) %collective-permute-start.22) | collective-permute-done | bytes 98336 | tf_op jit(solution)/shard_map/ppermute | solution.py:269
  183.6 2.0 collective-permute-done.14.recv_ref
  189.9 1.7 collective-permute-done.15.refs_1_
  192.5 2.3 %collective-permute-done.30.recv_ref = bf16[4,2,2,16,1536]{4,3,2,1,0:T(8,128)(2,1)S(1)} collective-permute-done((bf16[4,2,2,16,1536]{4,3,2,1,0:T(8,128)(2,1)S(1)}, bf16[4,2,2,16,1536]{4,3,2,1,0:T(8,128)(2,1)S(1)}, u32[]{:S(2)}, u32[]{:S(2)}) %collective-permute-start.30) | collective-permute-done | bytes 786464 | tf_op jit(solution)/shard_map/ppermute | solution.py:269
  194.9 1.5 collective-permute-start.31
  196.4 2.0 collective-permute-start.33
  198.4 3.5 %collective-permute-done.31.x_ref = bf16[2,2,16,1536]{3,2,1,0:T(8,128)(2,1)S(1)} collective-permute-done((bf16[2,2,16,1536]{3,2,1,0:T(8,128)(2,1)S(1)}, bf16[2,2,16,1536]{3,2,1,0:T(8,128)(2,1)S(1)}, u32[]{:S(2)}, u32[]{:S(2)}) %collective-permute-start.31) | collective-permute-done | bytes 196640 | tf_op jit(solution)/shard_map/ppermute | solution.py:269
  201.9 2.3 %collective-permute-done.32.zp_ref = bf16[2,2,16,1536]{3,2,1,0:T(8,128)(2,1)S(1)} collective-permute-done((bf16[2,2,16,1536]{3,2,1,0:T(8,128)(2,1)S(1)}, bf16[2,2,16,1536]{3,2,1,0:T(8,128)(2,1)S(1)}, u32[]{:S(2)}, u32[]{:S(2)}) %collective-permute-start.32) | collective-permute-done | bytes 196640 | tf_op jit(solution)/shard_map/ppermute | solution.py:269
  204.2 3.1 %collective-permute-done.33.both_ref = bf16[2,2,16,1536]{3,2,1,0:T(8,128)(2,1)S(1)} collective-permute-done((bf16[2,2,16,1536]{3,2,1,0:T(8,128)(2,1)S(1)}, bf16[2,2,16,1536]{3,2,1,0:T(8,128)(2,1)S(1)}, u32[]{:S(2)}, u32[]{:S(2)}) %collective-permute-start.33) | collective-permute-done | bytes 196640 | tf_op jit(solution)/shard_map/ppermute | solution.py:269
  208.2 5.9 %collective-permute-done.34.other_ref = bf16[2,16,1536]{2,1,0:T(8,128)(2,1)S(1)} collective-permute-done((bf16[2,16,1536]{2,1,0:T(8,128)(2,1)S(1)}, bf16[2,16,1536]{2,1,0:T(8,128)(2,1)S(1)}, u32[]{:S(2)}, u32[]{:S(2)}) %collective-permute-start.34) | collective-permute-done | bytes 98336 | tf_op jit(solution)/shard_map/ppermute | solution.py:269
  214.1 1.7 shard_map.110
  (98 shorter events, 44.9 us)
Async XLA Ops:
  11.4 9.0 %collective-permute-start = (bf16[2,16,1536]{2,1,0:T(8,128)(2,1)S(1)}, bf16[2,16,1536]{2,1,0:T(8,128)(2,1)S(1)}, u32[]{:S(2)}, u32[]{:S(2)}) collective-permute-start(bf16[2,16,1536]{2,1,0:T(8,128)(2,1)S(1)} %get-tuple-element.50), channel_id=1, source_target_pairs={{0,16},{1,17},{2,18},{3,19},{4,20},{5,21},{6,22},{7,23},{8,24},{9,... | collective-permute-start | bytes 294920 | tf_op jit(solution)/shard_map/ppermute | solution.py:269
  20.4 7.0 %collective-permute-start.1 = (bf16[2,2,16,1536]{3,2,1,0:T(8,128)(2,1)S(1)}, bf16[2,2,16,1536]{3,2,1,0:T(8,128)(2,1)S(1)}, u32[]{:S(2)}, u32[]{:S(2)}) collective-permute-start(bf16[2,2,16,1536]{3,2,1,0:T(8,128)(2,1)S(1)} %get-tuple-element.51), channel_id=1, source_target_pairs={{0,2},{1,3},{2,0},{3,1},{4,6},{5,7},{6,4},{7,5},{8,10},{9,11},{10,... | collective-permute-start | bytes 589832 | tf_op jit(solution)/shard_map/ppermute | solution.py:269
  22.0 7.9 %collective-permute-start.2 = (bf16[2,2,16,1536]{3,2,1,0:T(8,128)(2,1)S(1)}, bf16[2,2,16,1536]{3,2,1,0:T(8,128)(2,1)S(1)}, u32[]{:S(2)}, u32[]{:S(2)}) collective-permute-start(bf16[2,2,16,1536]{3,2,1,0:T(8,128)(2,1)S(1)} %get-tuple-element.52), channel_id=1, source_target_pairs={{0,8},{1,9},{2,10},{3,11},{4,12},{5,13},{6,14},{7,15},{8,0},{9,1},... | collective-permute-start | bytes 589832 | tf_op jit(solution)/shard_map/ppermute | solution.py:269
  22.7 11.3 %collective-permute-start.3 = (bf16[2,2,16,1536]{3,2,1,0:T(8,128)(2,1)S(1)}, bf16[2,2,16,1536]{3,2,1,0:T(8,128)(2,1)S(1)}, u32[]{:S(2)}, u32[]{:S(2)}) collective-permute-start(bf16[2,2,16,1536]{3,2,1,0:T(8,128)(2,1)S(1)} %get-tuple-element.52), channel_id=1, source_target_pairs={{0,10},{1,11},{2,8},{3,9},{4,14},{5,15},{6,12},{7,13},{8,2},{9,3},... | collective-permute-start | bytes 589832 | tf_op jit(solution)/shard_map/ppermute | solution.py:269
  24.0 20.4 %collective-permute-start.5 = (bf16[3,384,256]{2,1,0:T(8,128)(2,1)}, bf16[3,384,256]{2,1,0:T(8,128)(2,1)S(1)}, u32[]{:S(2)}, u32[]{:S(2)}) collective-permute-start(bf16[3,384,256]{2,1,0:T(8,128)(2,1)} %copy-done.13), channel_id=1, source_target_pairs={{0,8},{1,9},{2,10},{3,11},{4,12},{5,13},{6,14},{7,15},{8,0},{9,1},... | collective-permute-start | bytes 1769480 | tf_op jit(solution)/shard_map/ppermute | solution.py:269
  34.1 16.3 %collective-permute-start.4 = (bf16[4,2,2,16,1536]{4,3,2,1,0:T(8,128)(2,1)S(1)}, bf16[4,2,2,16,1536]{4,3,2,1,0:T(8,128)(2,1)S(1)}, u32[]{:S(2)}, u32[]{:S(2)}) collective-permute-start(bf16[4,2,2,16,1536]{4,3,2,1,0:T(8,128)(2,1)S(1)} %pad_maximum_fusion.near_ref), channel_id=1, source_target_pairs={{0,1},{1,0},{2,3},{3,2},{4,5},{5,4},{6,7},{7,6},{8,9},{9,8},{10,11... | collective-permute-start | bytes 2359304 | tf_op jit(solution)/shard_map/ppermute | solution.py:269
  34.2 16.2 %collective-permute-start.6 = (bf16[3,384,256]{2,1,0:T(8,128)(2,1)S(1)}, bf16[3,384,256]{2,1,0:T(8,128)(2,1)S(1)}, u32[]{:S(2)}, u32[]{:S(2)}) collective-permute-start(bf16[3,384,256]{2,1,0:T(8,128)(2,1)S(1)} %copy-done.8), channel_id=1, source_target_pairs={{0,4},{1,5},{2,6},{3,7},{4,0},{5,1},{6,2},{7,3},{8,12},{9,13},{10,... | collective-permute-start | bytes 1769480 | tf_op jit(solution)/shard_map/ppermute | solution.py:269
  44.4 18.2 %collective-permute-start.7 = (bf16[3,384,256]{2,1,0:T(8,128)(2,1)S(1)}, bf16[3,384,256]{2,1,0:T(8,128)(2,1)S(1)}, u32[]{:S(2)}, u32[]{:S(2)}) collective-permute-start(bf16[3,384,256]{2,1,0:T(8,128)(2,1)S(1)} %collective-permute-done.5.b_ref.refs_3_), channel_id=1, source_target_pairs={{0,4},{1,5},{2,6},{3,7},{4,0},{5,1},{6,2},{7,3},{8,12},{9,13},{10,... | collective-permute-start | bytes 1769480 | tf_op jit(solution)/shard_map/ppermute | solution.py:269
  47.5 18.3 %collective-permute-start.16 = (bf16[3,384,256]{2,1,0:T(8,128)(2,1)S(1)}, bf16[3,384,256]{2,1,0:T(8,128)(2,1)S(1)}, u32[]{:S(2)}, u32[]{:S(2)}) collective-permute-start(bf16[3,384,256]{2,1,0:T(8,128)(2,1)S(1)} %get-tuple-element.70), channel_id=1, source_target_pairs={{0,8},{1,9},{2,10},{3,11},{4,12},{5,13},{6,14},{7,15},{8,0},{9,1},... | collective-permute-start | bytes 1769480 | tf_op jit(solution)/shard_map/ppermute | solution.py:269
  63.6 14.9 %collective-permute-start.8 = (bf16[3,384,256]{2,1,0:T(8,128)(2,1)S(1)}, bf16[3,384,256]{2,1,0:T(8,128)(2,1)S(1)}, u32[]{:S(2)}, u32[]{:S(2)}) collective-permute-start(bf16[3,384,256]{2,1,0:T(8,128)(2,1)S(1)} %get-tuple-element.61), channel_id=1, source_target_pairs={{0,8},{1,9},{2,10},{3,11},{4,12},{5,13},{6,14},{7,15},{8,0},{9,1},... | collective-permute-start | bytes 1769480 | tf_op jit(solution)/shard_map/ppermute | solution.py:269
  64.3 16.3 %collective-permute-start.17 = (bf16[3,384,256]{2,1,0:T(8,128)(2,1)S(1)}, bf16[3,384,256]{2,1,0:T(8,128)(2,1)S(1)}, u32[]{:S(2)}, u32[]{:S(2)}) collective-permute-start(bf16[3,384,256]{2,1,0:T(8,128)(2,1)S(1)} %get-tuple-element.69.a_ref.refs_2_), channel_id=1, source_target_pairs={{0,4},{1,5},{2,6},{3,7},{4,0},{5,1},{6,2},{7,3},{8,12},{9,13},{10,... | collective-permute-start | bytes 1769480 | tf_op jit(solution)/shard_map/ppermute | solution.py:269
  65.8 27.4 %collective-permute-start.18 = (bf16[3,384,256]{2,1,0:T(8,128)(2,1)S(1)}, bf16[3,384,256]{2,1,0:T(8,128)(2,1)S(1)}, u32[]{:S(2)}, u32[]{:S(2)}) collective-permute-start(bf16[3,384,256]{2,1,0:T(8,128)(2,1)S(1)} %collective-permute-done.16.b_ref.refs_3_), channel_id=1, source_target_pairs={{0,4},{1,5},{2,6},{3,7},{4,0},{5,1},{6,2},{7,3},{8,12},{9,13},{10,... | collective-permute-start | bytes 1769480 | tf_op jit(solution)/shard_map/ppermute | solution.py:269
  66.3 39.5 %collective-permute-start.9 = (bf16[3,384,256]{2,1,0:T(8,128)(2,1)S(1)}, bf16[3,384,256]{2,1,0:T(8,128)(2,1)S(1)}, u32[]{:S(2)}, u32[]{:S(2)}) collective-permute-start(bf16[3,384,256]{2,1,0:T(8,128)(2,1)S(1)} %get-tuple-element.60.a_ref.refs_2_), channel_id=1, source_target_pairs={{0,4},{1,5},{2,6},{3,7},{4,0},{5,1},{6,2},{7,3},{8,12},{9,13},{10,... | collective-permute-start | bytes 1769480 | tf_op jit(solution)/shard_map/ppermute | solution.py:269
  78.5 38.3 %collective-permute-start.10 = (bf16[3,384,256]{2,1,0:T(8,128)(2,1)S(1)}, bf16[3,384,256]{2,1,0:T(8,128)(2,1)S(1)}, u32[]{:S(2)}, u32[]{:S(2)}) collective-permute-start(bf16[3,384,256]{2,1,0:T(8,128)(2,1)S(1)} %collective-permute-done.8.b_ref.refs_3_), channel_id=1, source_target_pairs={{0,4},{1,5},{2,6},{3,7},{4,0},{5,1},{6,2},{7,3},{8,12},{9,13},{10,... | collective-permute-start | bytes 1769480 | tf_op jit(solution)/shard_map/ppermute | solution.py:269
  94.2 29.4 %collective-permute-start.19 = (bf16[3,384,128]{2,1,0:T(8,128)(2,1)S(1)}, bf16[3,384,128]{2,1,0:T(8,128)(2,1)S(1)}, u32[]{:S(2)}, u32[]{:S(2)}) collective-permute-start(bf16[3,384,128]{2,1,0:T(8,128)(2,1)S(1)} %get-tuple-element.73), channel_id=1, source_target_pairs={{0,8},{1,9},{2,10},{3,11},{4,12},{5,13},{6,14},{7,15},{8,0},{9,1},... | collective-permute-start | bytes 884744 | tf_op jit(solution)/shard_map/ppermute | solution.py:269
  117.8 14.4 %collective-permute-start.11 = (bf16[3,384,128]{2,1,0:T(8,128)(2,1)S(1)}, bf16[3,384,128]{2,1,0:T(8,128)(2,1)S(1)}, u32[]{:S(2)}, u32[]{:S(2)}) collective-permute-start(bf16[3,384,128]{2,1,0:T(8,128)(2,1)S(1)} %get-tuple-element.64), channel_id=1, source_target_pairs={{0,8},{1,9},{2,10},{3,11},{4,12},{5,13},{6,14},{7,15},{8,0},{9,1},... | collective-permute-start | bytes 884744 | tf_op jit(solution)/shard_map/ppermute | solution.py:269
  119.2 11.2 %collective-permute-start.28 = (bf16[128,768]{1,0:T(8,128)(2,1)S(1)}, bf16[128,768]{1,0:T(8,128)(2,1)S(1)}, u32[]{:S(2)}, u32[]{:S(2)}) collective-permute-start(bf16[128,768]{1,0:T(8,128)(2,1)S(1)} %get-tuple-element.81), channel_id=1, source_target_pairs={{0,16},{1,17},{2,18},{3,19},{4,20},{5,21},{6,22},{7,23},{8,24},{9,... | collective-permute-start | bytes 589832 | tf_op jit(solution)/shard_map/ppermute | solution.py:269
  121.6 17.8 %collective-permute-start.26 = (bf16[128,768]{1,0:T(8,128)(2,1)S(1)}, bf16[128,768]{1,0:T(8,128)(2,1)S(1)}, u32[]{:S(2)}, u32[]{:S(2)}) collective-permute-start(bf16[128,768]{1,0:T(8,128)(2,1)S(1)} %get-tuple-element.79), channel_id=1, source_target_pairs={{0,16},{1,17},{2,18},{3,19},{4,20},{5,21},{6,22},{7,23},{8,24},{9,... | collective-permute-start | bytes 589832 | tf_op jit(solution)/shard_map/ppermute | solution.py:269
  122.1 17.4 %collective-permute-start.20 = (bf16[3,384,128]{2,1,0:T(8,128)(2,1)S(1)}, bf16[3,384,128]{2,1,0:T(8,128)(2,1)S(1)}, u32[]{:S(2)}, u32[]{:S(2)}) collective-permute-start(bf16[3,384,128]{2,1,0:T(8,128)(2,1)S(1)} %get-tuple-element.72.a_ref.refs_2_), channel_id=1, source_target_pairs={{0,4},{1,5},{2,6},{3,7},{4,0},{5,1},{6,2},{7,3},{8,12},{9,13},{10,... | collective-permute-start | bytes 884744 | tf_op jit(solution)/shard_map/ppermute | solution.py:269
  123.6 28.8 %collective-permute-start.21 = (bf16[3,384,128]{2,1,0:T(8,128)(2,1)S(1)}, bf16[3,384,128]{2,1,0:T(8,128)(2,1)S(1)}, u32[]{:S(2)}, u32[]{:S(2)}) collective-permute-start(bf16[3,384,128]{2,1,0:T(8,128)(2,1)S(1)} %collective-permute-done.19.b_ref.refs_3_), channel_id=1, source_target_pairs={{0,4},{1,5},{2,6},{3,7},{4,0},{5,1},{6,2},{7,3},{8,12},{9,13},{10,... | collective-permute-start | bytes 884744 | tf_op jit(solution)/shard_map/ppermute | solution.py:269
  130.5 25.7 %collective-permute-start.12 = (bf16[3,384,128]{2,1,0:T(8,128)(2,1)S(1)}, bf16[3,384,128]{2,1,0:T(8,128)(2,1)S(1)}, u32[]{:S(2)}, u32[]{:S(2)}) collective-permute-start(bf16[3,384,128]{2,1,0:T(8,128)(2,1)S(1)} %get-tuple-element.63.a_ref.refs_2_), channel_id=1, source_target_pairs={{0,4},{1,5},{2,6},{3,7},{4,0},{5,1},{6,2},{7,3},{8,12},{9,13},{10,... | collective-permute-start | bytes 884744 | tf_op jit(solution)/shard_map/ppermute | solution.py:269
  132.2 24.0 %collective-permute-start.13 = (bf16[3,384,128]{2,1,0:T(8,128)(2,1)S(1)}, bf16[3,384,128]{2,1,0:T(8,128)(2,1)S(1)}, u32[]{:S(2)}, u32[]{:S(2)}) collective-permute-start(bf16[3,384,128]{2,1,0:T(8,128)(2,1)S(1)} %collective-permute-done.11.b_ref.refs_3_), channel_id=1, source_target_pairs={{0,4},{1,5},{2,6},{3,7},{4,0},{5,1},{6,2},{7,3},{8,12},{9,13},{10,... | collective-permute-start | bytes 884744 | tf_op jit(solution)/shard_map/ppermute | solution.py:269
  139.4 12.8 %collective-permute-start.24 = (bf16[128,768]{1,0:T(8,128)(2,1)S(1)}, bf16[128,768]{1,0:T(8,128)(2,1)S(1)}, u32[]{:S(2)}, u32[]{:S(2)}) collective-permute-start(bf16[128,768]{1,0:T(8,128)(2,1)S(1)} %get-tuple-element.77), channel_id=1, source_target_pairs={{0,16},{1,17},{2,18},{3,19},{4,20},{5,21},{6,22},{7,23},{8,24},{9,... | collective-permute-start | bytes 589832 | tf_op jit(solution)/shard_map/ppermute | solution.py:269
  139.6 20.4 %collective-permute-start.29 = (bf16[128,768]{1,0:T(8,128)(2,1)S(1)}, bf16[128,768]{1,0:T(8,128)(2,1)S(1)}, u32[]{:S(2)}, u32[]{:S(2)}) collective-permute-start(bf16[128,768]{1,0:T(8,128)(2,1)S(1)} %shard_map.102.refs_0_), channel_id=1, source_target_pairs={{0,16},{1,17},{2,18},{3,19},{4,20},{5,21},{6,22},{7,23},{8,24},{9,... | collective-permute-start | bytes 589832 | tf_op jit(solution)/shard_map/ppermute | solution.py:269
  152.2 34.4 %collective-permute-start.27 = (bf16[128,768]{1,0:T(8,128)(2,1)S(1)}, bf16[128,768]{1,0:T(8,128)(2,1)S(1)}, u32[]{:S(2)}, u32[]{:S(2)}) collective-permute-start(bf16[128,768]{1,0:T(8,128)(2,1)S(1)} %shard_map.101.refs_0_), channel_id=1, source_target_pairs={{0,16},{1,17},{2,18},{3,19},{4,20},{5,21},{6,22},{7,23},{8,24},{9,... | collective-permute-start | bytes 589832 | tf_op jit(solution)/shard_map/ppermute | solution.py:269
  152.4 35.3 %collective-permute-start.25 = (bf16[128,768]{1,0:T(8,128)(2,1)S(1)}, bf16[128,768]{1,0:T(8,128)(2,1)S(1)}, u32[]{:S(2)}, u32[]{:S(2)}) collective-permute-start(bf16[128,768]{1,0:T(8,128)(2,1)S(1)} %shard_map.100.refs_0_), channel_id=1, source_target_pairs={{0,16},{1,17},{2,18},{3,19},{4,20},{5,21},{6,22},{7,23},{8,24},{9,... | collective-permute-start | bytes 589832 | tf_op jit(solution)/shard_map/ppermute | solution.py:269
  156.1 27.3 %collective-permute-start.22 = (bf16[128,384]{1,0:T(8,128)(2,1)S(1)}, bf16[128,384]{1,0:T(8,128)(2,1)S(1)}, u32[]{:S(2)}, u32[]{:S(2)}) collective-permute-start(bf16[128,384]{1,0:T(8,128)(2,1)S(1)} %get-tuple-element.75), channel_id=1, source_target_pairs={{0,16},{1,17},{2,18},{3,19},{4,20},{5,21},{6,22},{7,23},{8,24},{9,... | collective-permute-start | bytes 294920 | tf_op jit(solution)/shard_map/ppermute | solution.py:269
  157.0 28.6 %collective-permute-start.14 = (bf16[128,384]{1,0:T(8,128)(2,1)S(1)}, bf16[128,384]{1,0:T(8,128)(2,1)S(1)}, u32[]{:S(2)}, u32[]{:S(2)}) collective-permute-start(bf16[128,384]{1,0:T(8,128)(2,1)S(1)} %get-tuple-element.66), channel_id=1, source_target_pairs={{0,16},{1,17},{2,18},{3,19},{4,20},{5,21},{6,22},{7,23},{8,24},{9,... | collective-permute-start | bytes 294920 | tf_op jit(solution)/shard_map/ppermute | solution.py:269
  194.9 7.0 %collective-permute-start.31 = (bf16[2,2,16,1536]{3,2,1,0:T(8,128)(2,1)S(1)}, bf16[2,2,16,1536]{3,2,1,0:T(8,128)(2,1)S(1)}, u32[]{:S(2)}, u32[]{:S(2)}) collective-permute-start(bf16[2,2,16,1536]{3,2,1,0:T(8,128)(2,1)S(1)} %get-tuple-element.85), channel_id=1, source_target_pairs={{0,2},{1,3},{2,0},{3,1},{4,6},{5,7},{6,4},{7,5},{8,10},{9,11},{10,... | collective-permute-start | bytes 589832 | tf_op jit(solution)/shard_map/ppermute | solution.py:269
  196.4 7.8 %collective-permute-start.32 = (bf16[2,2,16,1536]{3,2,1,0:T(8,128)(2,1)S(1)}, bf16[2,2,16,1536]{3,2,1,0:T(8,128)(2,1)S(1)}, u32[]{:S(2)}, u32[]{:S(2)}) collective-permute-start(bf16[2,2,16,1536]{3,2,1,0:T(8,128)(2,1)S(1)} %get-tuple-element.86), channel_id=1, source_target_pairs={{0,8},{1,9},{2,10},{3,11},{4,12},{5,13},{6,14},{7,15},{8,0},{9,1},... | collective-permute-start | bytes 589832 | tf_op jit(solution)/shard_map/ppermute | solution.py:269
  196.4 10.9 %collective-permute-start.33 = (bf16[2,2,16,1536]{3,2,1,0:T(8,128)(2,1)S(1)}, bf16[2,2,16,1536]{3,2,1,0:T(8,128)(2,1)S(1)}, u32[]{:S(2)}, u32[]{:S(2)}) collective-permute-start(bf16[2,2,16,1536]{3,2,1,0:T(8,128)(2,1)S(1)} %get-tuple-element.87), channel_id=1, source_target_pairs={{0,10},{1,11},{2,8},{3,9},{4,14},{5,15},{6,12},{7,13},{8,2},{9,3},... | collective-permute-start | bytes 589832 | tf_op jit(solution)/shard_map/ppermute | solution.py:269
  207.4 6.8 %collective-permute-start.34 = (bf16[2,16,1536]{2,1,0:T(8,128)(2,1)S(1)}, bf16[2,16,1536]{2,1,0:T(8,128)(2,1)S(1)}, u32[]{:S(2)}, u32[]{:S(2)}) collective-permute-start(bf16[2,16,1536]{2,1,0:T(8,128)(2,1)S(1)} %get-tuple-element.89), channel_id=1, source_target_pairs={{0,16},{1,17},{2,18},{3,19},{4,20},{5,21},{6,22},{7,23},{8,24},{9,... | collective-permute-start | bytes 294920 | tf_op jit(solution)/shard_map/ppermute | solution.py:269
  (19 other events, 184.4 us)

commit v3 on v2

--- a/solution.py
+++ b/solution.py
@@ -9,6 +9,7 @@
 BF16 = jnp.bfloat16
 LANES = 128
 AHEAD = 2
+IN_FLIGHT = 2
 
 
 def dot(left, right):
@@ -198,7 +199,7 @@
         out_shape=list(outs),
         scratch_shapes=list(scratch),
         compiler_params=pltpu.CompilerParams(vmem_limit_bytes=40 * 1024 * 1024),
-        cost_estimate=pl.CostEstimate(flops=flops, bytes_accessed=moved, transcendentals=0),
+        cost_estimate=pl.CostEstimate(flops=0, bytes_accessed=1024, transcendentals=0),
     )(*args)
 
 
@@ -254,9 +255,9 @@
         grid_spec=pltpu.PrefetchScalarGridSpec(
             num_scalar_prefetch=1, grid=(1,), in_specs=specs, out_specs=[whole, whole]
         ),
-        compiler_params=pltpu.CompilerParams(vmem_limit_bytes=40 * 1024 * 1024),
+        compiler_params=pltpu.CompilerParams(vmem_limit_bytes=60 * 1024 * 1024),
         cost_estimate=pl.CostEstimate(
-            flops=0, bytes_accessed=12 * out.size * 2, transcendentals=0
+            flops=0, bytes_accessed=1024, transcendentals=0
         ),
     )(low, w_gate, w_up, w_down, w_gate, w_up, w_down)
 
@@ -282,22 +283,33 @@
 
         cuts = chunk_cuts(half_units)
         count = len(cuts) - 1
-        own_w, zp_w, far_own, far_zp = ([None] * count for _ in range(4))
+        own_w, zp_w = [None] * count, [None] * count
         given = [None] * count
 
-        def make_chunk(k):
+        stream = []
+
+        def over_y(values, *after):
+            after = list(after)
+            if len(stream) >= IN_FLIGHT:
+                after.append(stream[-IN_FLIGHT])
+            if after:
+                values, *after = lax.optimization_barrier((values, *after))
+            if len(stream) >= IN_FLIGHT:
+                stream[-IN_FLIGHT] = after.pop()
+            stream.append(swap(values, at_y))
+            return after
+
+        def stream_chunk(k, *after):
             own_w[k], given[k] = weight_chunk(
                 low, w_gate, w_up, w_down, cuts[k], cuts[k + 1] - cuts[k]
             )
-
-        def send_chunk(k):
             zp_w[k] = swap(given[k], at_zp)
-            far_own[k] = swap(own_w[k], at_y)
-            far_zp[k] = swap(zp_w[k], at_y)
-
-        make_chunk(0)
-        send_chunk(0)
-        tokens, cotangent, own_w[0] = lax.optimization_barrier((tokens, cotangent, own_w[0]))
+            after = over_y(own_w[k], *after)
+            over_y(zp_w[k])
+            return after
+
+        for k in range(min(AHEAD, count)):
+            stream_chunk(k)
 
         def pack_body(tokens_ref, cot_ref, experts_ref, gates_ref, keep_ref, send_ref, packed_ref):
             chosen, weight = route_columns(experts_ref, gates_ref)
@@ -333,9 +345,6 @@
             flops=4 * most * own_count * width,
         )
         other = swap(sent, at_zh)
-        if count > 1:
-            make_chunk(1)
-            send_chunk(1)
 
         def join_body(mine_ref, other_ref, plain_ref, flipped_ref):
             for j, ref in enumerate((mine_ref, other_ref)):
@@ -411,50 +420,80 @@
                         rest[0][:, j, which, :, columns] = value[j, 0]
                         rest[1][:, j, which, :, columns] = value[j, 1].astype(BF16)
 
-        total = None
         quad = (4, 2) + block_shape
-        for k in range(count):
+        pre, mine, total = [None] * count, [None] * count, [None] * count
+
+        def weights_of(k):
+            return own_w[k], zp_w[k], stream[2 * k], stream[2 * k + 1]
+
+        def first(k, near_rows, far_rows):
             units = cuts[k + 1] - cuts[k]
-            work = 2 * slots * z_width * units * 3
-            weights = (own_w[k], zp_w[k], far_own[k], far_zp[k])
-            keep, sent = call(
+            pre[k] = call(
                 first_body,
                 [shaped((own_slots, 3 * units), F32), shaped((own_slots, 3 * units), BF16)],
                 near_rows,
                 far_rows,
-                *weights,
-                flops=work,
-            )
-            if k + AHEAD < count:
-                make_chunk(k + AHEAD)
-                own_w[k + AHEAD], given[k + AHEAD], sent = lax.optimization_barrier(
-                    (own_w[k + AHEAD], given[k + AHEAD], sent)
-                )
-                send_chunk(k + AHEAD)
-            (mine,) = call(
+                *weights_of(k),
+            )
+
+        def middle(k):
+            units = cuts[k + 1] - cuts[k]
+            keep, sent = pre[k]
+            (mine[k],) = call(
                 middle_body,
                 [shaped((own_slots, 3 * units), BF16)],
                 keep,
                 swap(sent, at_zh),
             )
-            first, last = k == 0, k == count - 1
+
+        def second(k):
+            is_first, is_last = k == 0, k == count - 1
             outs = (
                 [shaped(quad, F32), shaped(quad, BF16)]
-                if last
+                if is_last
                 else [shaped((2, slots, z_width), F32)]
             )
-            held = () if first else (total,)
-            total = call(
-                lambda *refs, first=first, last=last: second_body(first, last, *refs),
+            held = () if is_first else total[k - 1]
+            total[k] = call(
+                lambda *refs: second_body(is_first, is_last, *refs),
                 outs,
-                mine,
-                swap(mine, at_zh),
-                *weights,
+                mine[k],
+                swap(mine[k], at_zh),
+                *weights_of(k),
                 *held,
-                flops=work,
-            )
-            if not last:
-                (total,) = total
+            )
+
+        for k in range(count):
+            if k == count - 1:
+                after = [near_rows]
+                if k >= 1:
+                    after.append(mine[k - 1])
+                if k >= 2:
+                    after.append(total[k - 2][0])
+                after = lax.optimization_barrier(tuple(after))
+                near_rows = after[0]
+                if k >= 1:
+                    mine[k - 1] = after[1]
+                if k >= 2:
+                    total[k - 2] = [after[2]]
+            first(k, near_rows, far_rows)
+            if k + AHEAD < count:
+                after = [pre[k][1]]
+                if k >= 1:
+                    after.append(mine[k - 1])
+                if k >= 2:
+                    after.append(total[k - 2][0])
+                after = stream_chunk(k + AHEAD, *after)
+                pre[k] = [pre[k][0], after[0]]
+                if k >= 1:
+                    mine[k - 1] = after[1]
+                if k >= 2:
+                    total[k - 2] = [after[2]]
+            middle(k)
+            if k >= 1:
+                second(k - 1)
+        second(count - 1)
+        total = total[-1]
 
         def spread_body(keep_ref, recv_ref, own_ref, *outs):
             value = keep_ref[...] + recv_ref[...].astype(F32)

time: 216 us -> 185 us (0.86)
  waiting for transfers between devices: 146 us -> 91.8 us
  Pallas kernels: 12.6 us -> 35.3 us
    ppermute x35, waiting for transfers between devices: 146 us -> 91.8 us  [swap(): return lax.ppermute(values, ('fsdp', 'et'), pairs)]
    pallas_call x20, Pallas kernels: 11.7 us -> 23.6 us  [call(): pl.pallas_call(body, out_shape=list(outs), scratch_shapes=list(scratch),...]
    pallas_call x5, Pallas kernels: 0.91 us -> 11.7 us  [weight_chunk(): pl.pallas_call(weight_chunk_body, out_shape=[out, out], grid_spec=pltpu.P...]
    unnamed x34 -> x54, local copies, waits for them, and re-layouts: 11.5 us -> 10.3 us
  transfers between devices with their start and end apart: 35 -> 35, of which waited for: 25 -> 20; matrix products, arithmetic and copies ran while one was open for 0% -> 0% of each run, Pallas kernels for 4% -> 16%
where the time goes in v3:
time: 185 us
  waiting for transfers between devices  91.8 us (50%)
  starting transfers between devices  46.1 us (25%)
  Pallas kernels  35.3 us (19%)
  local copies, waits for them, and re-layouts  10.3 us (6%)
    ppermute x35, waiting for transfers between devices, swap(): return lax.ppermute(values, ('fsdp', 'et'), pairs)  91.8 us
    ppermute x35, starting transfers between devices, swap(): return lax.ppermute(values, ('fsdp', 'et'), pairs)  46.1 us
    pallas_call x20, Pallas kernels, call(): pl.pallas_call(body, out_shape=list(outs), scratch_shapes=list(scratch),...  23.6 us
    pallas_call x5, Pallas kernels, weight_chunk(): pl.pallas_call(weight_chunk_body, out_shape=[out, out], grid_spec=pltpu.P...  11.7 us
    unnamed x54, local copies, waits for them, and re-layouts  10.3 us
  transfers between devices with their start and end apart: 35, of which 20 were waited for; matrix products, arithmetic and copies ran while one was open for 0% of the time, Pallas kernels for 16%

profile of v3, /device:TPU:0, one launch (start us, length us, event | category | flops | bytes accessed | tf_op | source)
XLA Modules:
  0.0 184.6 jit_solution(12765928521556259449)
XLA Ops:
  0.7 2.6 %shard_map.92 = (bf16[3,384,256]{2,1,0:T(8,128)(2,1)}, bf16[3,384,256]{2,1,0:T(8,128)(2,1)}) custom-call(s32[1]{0:T(128)} %bitcast.4.low_ref, bf16[384,2048]{1,0:T(8,128)(2,1)} %refs_3_.9, bf16[384,2048]{1,0:T(8,128)(2,1)} %refs_4_.9, bf16[2048,384]{1,0:T(8,128)(2,1)} %refs_5_.9, bf16[384,2048]{1,0:T(8,128)(2,1)} %refs_3_.9, bf16[384,2048]{1,0:T(8,128)(2,1)} %refs_4_.9, ...), custom_call_target="tpu_custom_call" | custom-call | bytes 1024 | tf_op jit(solution)/shard_map/pallas_call | solution.py:252
  3.3 3.0 %collective-permute-start.8 = (bf16[3,384,256]{2,1,0:T(8,128)(2,1)}, bf16[3,384,256]{2,1,0:T(8,128)(2,1)S(1)}, u32[]{:S(2)}, u32[]{:S(2)}) collective-permute-start(bf16[3,384,256]{2,1,0:T(8,128)(2,1)} %get-tuple-element.71), channel_id=1, source_target_pairs={{0,8},{1,9},{2,10},{3,11},{4,12},{5,13},{6,14},{7,15},{8,0},{9,1},... | collective-permute-start | bytes 1769480 | tf_op jit(solution)/shard_map/ppermute | solution.py:270
  7.1 2.7 %collective-permute-start = (bf16[2,16,1536]{2,1,0:T(8,128)(2,1)S(1)}, bf16[2,16,1536]{2,1,0:T(8,128)(2,1)S(1)}, u32[]{:S(2)}, u32[]{:S(2)}) collective-permute-start(bf16[2,16,1536]{2,1,0:T(8,128)(2,1)S(1)} %get-tuple-element.60), channel_id=1, source_target_pairs={{0,16},{1,17},{2,18},{3,19},{4,20},{5,21},{6,22},{7,23},{8,24},{9,... | collective-permute-start | bytes 294920 | tf_op jit(solution)/shard_map/ppermute | solution.py:270
  9.8 11.5 %collective-permute-done.other_ref = bf16[2,16,1536]{2,1,0:T(8,128)(2,1)S(1)} collective-permute-done((bf16[2,16,1536]{2,1,0:T(8,128)(2,1)S(1)}, bf16[2,16,1536]{2,1,0:T(8,128)(2,1)S(1)}, u32[]{:S(2)}, u32[]{:S(2)}) %collective-permute-start) | collective-permute-done | bytes 98336 | tf_op jit(solution)/shard_map/ppermute | solution.py:270
  22.8 3.5 %collective-permute-start.2 = (bf16[2,2,16,1536]{3,2,1,0:T(8,128)(2,1)S(1)}, bf16[2,2,16,1536]{3,2,1,0:T(8,128)(2,1)S(1)}, u32[]{:S(2)}, u32[]{:S(2)}) collective-permute-start(bf16[2,2,16,1536]{3,2,1,0:T(8,128)(2,1)S(1)} %get-tuple-element.62), channel_id=1, source_target_pairs={{0,8},{1,9},{2,10},{3,11},{4,12},{5,13},{6,14},{7,15},{8,0},{9,1},... | collective-permute-start | bytes 589832 | tf_op jit(solution)/shard_map/ppermute | solution.py:270
  27.8 2.5 %shard_map.91 = (bf16[3,384,256]{2,1,0:T(8,128)(2,1)}, bf16[3,384,256]{2,1,0:T(8,128)(2,1)}) custom-call(s32[1]{0:T(128)} %bitcast.4.low_ref, bf16[384,2048]{1,0:T(8,128)(2,1)} %refs_3_.9, bf16[384,2048]{1,0:T(8,128)(2,1)} %refs_4_.9, bf16[2048,384]{1,0:T(8,128)(2,1)} %refs_5_.9, bf16[384,2048]{1,0:T(8,128)(2,1)} %refs_3_.9, bf16[384,2048]{1,0:T(8,128)(2,1)} %refs_4_.9, ...), custom_call_target="tpu_custom_call" | custom-call | bytes 1024 | tf_op jit(solution)/shard_map/pallas_call | solution.py:252
  33.7 2.5 %collective-permute-done.3 = bf16[2,2,16,1536]{3,2,1,0:T(8,128)(2,1)S(1)} collective-permute-done((bf16[2,2,16,1536]{3,2,1,0:T(8,128)(2,1)S(1)}, bf16[2,2,16,1536]{3,2,1,0:T(8,128)(2,1)S(1)}, u32[]{:S(2)}, u32[]{:S(2)}) %collective-permute-start.3) | collective-permute-done | bytes 196640 | tf_op jit(solution)/shard_map/ppermute | solution.py:270
  36.3 6.5 %collective-permute-done.9.c_ref.refs_4_ = bf16[3,384,256]{2,1,0:T(8,128)(2,1)S(1)} collective-permute-done((bf16[3,384,256]{2,1,0:T(8,128)(2,1)}, bf16[3,384,256]{2,1,0:T(8,128)(2,1)S(1)}, u32[]{:S(2)}, u32[]{:S(2)}) %collective-permute-start.9) | collective-permute-done | bytes 589856 | tf_op jit(solution)/shard_map/ppermute | solution.py:270
  45.1 2.5 %shard_map.90 = (bf16[3,384,256]{2,1,0:T(8,128)(2,1)}, bf16[3,384,256]{2,1,0:T(8,128)(2,1)}) custom-call(s32[1]{0:T(128)} %bitcast.4.low_ref, bf16[384,2048]{1,0:T(8,128)(2,1)} %refs_3_.9, bf16[384,2048]{1,0:T(8,128)(2,1)} %refs_4_.9, bf16[2048,384]{1,0:T(8,128)(2,1)} %refs_5_.9, bf16[384,2048]{1,0:T(8,128)(2,1)} %refs_3_.9, bf16[384,2048]{1,0:T(8,128)(2,1)} %refs_4_.9, ...), custom_call_target="tpu_custom_call" | custom-call | bytes 1024 | tf_op jit(solution)/shard_map/pallas_call | solution.py:252
  49.6 5.9 %collective-permute-done.10.d_ref.refs_5_ = bf16[3,384,256]{2,1,0:T(8,128)(2,1)} collective-permute-done((bf16[3,384,256]{2,1,0:T(8,128)(2,1)S(1)}, bf16[3,384,256]{2,1,0:T(8,128)(2,1)}, u32[]{:S(2)}, u32[]{:S(2)}) %collective-permute-start.10) | collective-permute-done | bytes 589856 | tf_op jit(solution)/shard_map/ppermute | solution.py:270
  58.1 2.7 %shard_map.93 = (f32[128,768]{1,0:T(8,128)S(1)}, bf16[128,768]{1,0:T(8,128)(2,1)}) custom-call(bf16[4,2,2,16,1536]{4,3,2,1,0:T(8,128)(2,1)S(1)} %pad_maximum_fusion.near_ref, bf16[4,2,2,16,1536]{4,3,2,1,0:T(8,128)(2,1)S(1)} %collective-permute-done.4.far_ref, bf16[3,384,256]{2,1,0:T(8,128)(2,1)S(1)} %copy-done.1, ...), custom_call_target="tpu_custom_call" | custom-call | bytes 1024 | tf_op jit(solution)/shard_map/pallas_call | solution.py:197
  61.6 6.6 %collective-permute-done.11.c_ref.refs_4_ = bf16[3,384,256]{2,1,0:T(8,128)(2,1)} collective-permute-done((bf16[3,384,256]{2,1,0:T(8,128)(2,1)}, bf16[3,384,256]{2,1,0:T(8,128)(2,1)}, u32[]{:S(2)}, u32[]{:S(2)}) %collective-permute-start.11) | collective-permute-done | bytes 589856 | tf_op jit(solution)/shard_map/ppermute | solution.py:270
  69.7 11.0 %collective-permute-done.12.d_ref.refs_5_ = bf16[3,384,256]{2,1,0:T(8,128)(2,1)S(1)} collective-permute-done((bf16[3,384,256]{2,1,0:T(8,128)(2,1)S(1)}, bf16[3,384,256]{2,1,0:T(8,128)(2,1)S(1)}, u32[]{:S(2)}, u32[]{:S(2)}) %collective-permute-start.12) | collective-permute-done | bytes 589856 | tf_op jit(solution)/shard_map/ppermute | solution.py:270
  87.1 4.9 %collective-permute-done.13.recv_ref = bf16[128,768]{1,0:T(8,128)(2,1)S(1)} collective-permute-done((bf16[128,768]{1,0:T(8,128)(2,1)}, bf16[128,768]{1,0:T(8,128)(2,1)S(1)}, u32[]{:S(2)}, u32[]{:S(2)}) %collective-permute-start.13) | collective-permute-done | bytes 196640 | tf_op jit(solution)/shard_map/ppermute | solution.py:270
  95.8 2.7 %shard_map.94 = (f32[128,768]{1,0:T(8,128)S(1)}, bf16[128,768]{1,0:T(8,128)(2,1)}) custom-call(bf16[4,2,2,16,1536]{4,3,2,1,0:T(8,128)(2,1)S(1)} %pad_maximum_fusion.near_ref, bf16[4,2,2,16,1536]{4,3,2,1,0:T(8,128)(2,1)S(1)} %collective-permute-done.4.far_ref, bf16[3,384,256]{2,1,0:T(8,128)(2,1)S(1)} %copy-done, ...), custom_call_target="tpu_custom_call" | custom-call | bytes 1024 | tf_op jit(solution)/shard_map/pallas_call | solution.py:197
  99.8 2.9 %collective-permute-start.16 = (bf16[128,768]{1,0:T(8,128)(2,1)}, bf16[128,768]{1,0:T(8,128)(2,1)}, u32[]{:S(2)}, u32[]{:S(2)}) collective-permute-start(bf16[128,768]{1,0:T(8,128)(2,1)} %get-tuple-element.88), channel_id=1, source_target_pairs={{0,16},{1,17},{2,18},{3,19},{4,20},{5,21},{6,22},{7,23},{8,24},{9,... | collective-permute-start | bytes 589832 | tf_op jit(solution)/shard_map/ppermute | solution.py:270
  107.6 2.5 %collective-permute-done.17.refs_1_ = bf16[128,768]{1,0:T(8,128)(2,1)} collective-permute-done((bf16[128,768]{1,0:T(8,128)(2,1)S(1)}, bf16[128,768]{1,0:T(8,128)(2,1)}, u32[]{:S(2)}, u32[]{:S(2)}) %collective-permute-start.17) | collective-permute-done | bytes 196640 | tf_op jit(solution)/shard_map/ppermute | solution.py:270
  112.2 2.2 %shard_map.98.refs_6_ = f32[2,256,1536]{2,1,0:T(8,128)S(1)} custom-call(bf16[128,768]{1,0:T(8,128)(2,1)S(1)} %shard_map.95.refs_0_, bf16[128,768]{1,0:T(8,128)(2,1)} %collective-permute-done.17.refs_1_, bf16[3,384,256]{2,1,0:T(8,128)(2,1)S(1)} %copy-done.1, bf16[3,384,256]{2,1,0:T(8,128)(2,1)S(1)} %copy-done.4, bf16[3,384,256]{2,1,0:T(8,128)(2,1)S(1)} %copy-done.10, ...), custom_call_target="tpu_custom_call" | custom-call | bytes 1024 | tf_op jit(solution)/shard_map/pallas_call | solution.py:197
  115.5 2.4 %shard_map.96 = (f32[128,768]{1,0:T(8,128)S(1)}, bf16[128,768]{1,0:T(8,128)(2,1)S(1)}) custom-call(bf16[4,2,2,16,1536]{4,3,2,1,0:T(8,128)(2,1)S(1)} %pad_maximum_fusion.near_ref, bf16[4,2,2,16,1536]{4,3,2,1,0:T(8,128)(2,1)S(1)} %collective-permute-done.4.far_ref, bf16[3,384,256]{2,1,0:T(8,128)(2,1)S(1)} %copy-done.2, ...), custom_call_target="tpu_custom_call" | custom-call | bytes 1024 | tf_op jit(solution)/shard_map/pallas_call | solution.py:197
  120.2 2.8 %collective-permute-start.24 = (bf16[128,768]{1,0:T(8,128)(2,1)S(1)}, bf16[128,768]{1,0:T(8,128)(2,1)S(1)}, u32[]{:S(2)}, u32[]{:S(2)}) collective-permute-start(bf16[128,768]{1,0:T(8,128)(2,1)S(1)} %shard_map.97.refs_0_), channel_id=1, source_target_pairs={{0,16},{1,17},{2,18},{3,19},{4,20},{5,21},{6,22},{7,23},{8,24},{9,... | collective-permute-start | bytes 589832 | tf_op jit(solution)/shard_map/ppermute | solution.py:270
  123.0 9.4 %collective-permute-done.22.recv_ref = bf16[128,768]{1,0:T(8,128)(2,1)S(1)} collective-permute-done((bf16[128,768]{1,0:T(8,128)(2,1)S(1)}, bf16[128,768]{1,0:T(8,128)(2,1)S(1)}, u32[]{:S(2)}, u32[]{:S(2)}) %collective-permute-start.22) | collective-permute-done | bytes 196640 | tf_op jit(solution)/shard_map/ppermute | solution.py:270
  134.5 3.0 %collective-permute-start.21 = (bf16[128,384]{1,0:T(8,128)(2,1)S(1)}, bf16[128,384]{1,0:T(8,128)(2,1)S(1)}, u32[]{:S(2)}, u32[]{:S(2)}) collective-permute-start(bf16[128,384]{1,0:T(8,128)(2,1)S(1)} %get-tuple-element.96), channel_id=1, source_target_pairs={{0,16},{1,17},{2,18},{3,19},{4,20},{5,21},{6,22},{7,23},{8,24},{9,... | collective-permute-start | bytes 294920 | tf_op jit(solution)/shard_map/ppermute | solution.py:270
  140.7 2.2 %collective-permute-done.21.recv_ref = bf16[128,384]{1,0:T(8,128)(2,1)S(1)} collective-permute-done((bf16[128,384]{1,0:T(8,128)(2,1)S(1)}, bf16[128,384]{1,0:T(8,128)(2,1)S(1)}, u32[]{:S(2)}, u32[]{:S(2)}) %collective-permute-start.21) | collective-permute-done | bytes 98336 | tf_op jit(solution)/shard_map/ppermute | solution.py:270
  143.0 2.4 %shard_map.103.refs_6_ = f32[2,256,1536]{2,1,0:T(8,128)S(1)} custom-call(bf16[128,768]{1,0:T(8,128)(2,1)S(1)} %shard_map.101.refs_0_, bf16[128,768]{1,0:T(8,128)(2,1)S(1)} %collective-permute-done.23.refs_1_, bf16[3,384,256]{2,1,0:T(8,128)(2,1)S(1)} %copy-done.2, bf16[3,384,256]{2,1,0:T(8,128)(2,1)} %collective-permute-done.6.b_ref.refs_3_, ...), custom_call_target="tpu_custom_call" | custom-call | bytes 1024 | tf_op jit(solution)/shard_map/pallas_call | solution.py:197
  146.5 2.7 %collective-permute-start.29 = (bf16[128,384]{1,0:T(8,128)(2,1)S(1)}, bf16[128,384]{1,0:T(8,128)(2,1)S(1)}, u32[]{:S(2)}, u32[]{:S(2)}) collective-permute-start(bf16[128,384]{1,0:T(8,128)(2,1)S(1)} %shard_map.100.refs_0_), channel_id=1, source_target_pairs={{0,16},{1,17},{2,18},{3,19},{4,20},{5,21},{6,22},{7,23},{8,24},{9,... | collective-permute-start | bytes 294920 | tf_op jit(solution)/shard_map/ppermute | solution.py:270
  149.2 5.5 %collective-permute-done.27.recv_ref = bf16[128,384]{1,0:T(8,128)(2,1)S(1)} collective-permute-done((bf16[128,384]{1,0:T(8,128)(2,1)S(1)}, bf16[128,384]{1,0:T(8,128)(2,1)S(1)}, u32[]{:S(2)}, u32[]{:S(2)}) %collective-permute-start.27) | collective-permute-done | bytes 98336 | tf_op jit(solution)/shard_map/ppermute | solution.py:270
  157.7 2.8 %collective-permute-done.28.refs_1_ = bf16[128,384]{1,0:T(8,128)(2,1)S(1)} collective-permute-done((bf16[128,384]{1,0:T(8,128)(2,1)S(1)}, bf16[128,384]{1,0:T(8,128)(2,1)S(1)}, u32[]{:S(2)}, u32[]{:S(2)}) %collective-permute-start.28) | collective-permute-done | bytes 98336 | tf_op jit(solution)/shard_map/ppermute | solution.py:270
  161.3 2.3 %collective-permute-done.30.recv_ref = bf16[4,2,2,16,1536]{4,3,2,1,0:T(8,128)(2,1)S(1)} collective-permute-done((bf16[4,2,2,16,1536]{4,3,2,1,0:T(8,128)(2,1)S(1)}, bf16[4,2,2,16,1536]{4,3,2,1,0:T(8,128)(2,1)S(1)}, u32[]{:S(2)}, u32[]{:S(2)}) %collective-permute-start.30) | collective-permute-done | bytes 786464 | tf_op jit(solution)/shard_map/ppermute | solution.py:270
  167.3 3.5 %collective-permute-done.31.x_ref = bf16[2,2,16,1536]{3,2,1,0:T(8,128)(2,1)S(1)} collective-permute-done((bf16[2,2,16,1536]{3,2,1,0:T(8,128)(2,1)S(1)}, bf16[2,2,16,1536]{3,2,1,0:T(8,128)(2,1)S(1)}, u32[]{:S(2)}, u32[]{:S(2)}) %collective-permute-start.31) | collective-permute-done | bytes 196640 | tf_op jit(solution)/shard_map/ppermute | solution.py:270
  170.7 2.3 %collective-permute-done.32.zp_ref = bf16[2,2,16,1536]{3,2,1,0:T(8,128)(2,1)S(1)} collective-permute-done((bf16[2,2,16,1536]{3,2,1,0:T(8,128)(2,1)S(1)}, bf16[2,2,16,1536]{3,2,1,0:T(8,128)(2,1)S(1)}, u32[]{:S(2)}, u32[]{:S(2)}) %collective-permute-start.32) | collective-permute-done | bytes 196640 | tf_op jit(solution)/shard_map/ppermute | solution.py:270
  173.0 3.1 %collective-permute-done.33.both_ref = bf16[2,2,16,1536]{3,2,1,0:T(8,128)(2,1)S(1)} collective-permute-done((bf16[2,2,16,1536]{3,2,1,0:T(8,128)(2,1)S(1)}, bf16[2,2,16,1536]{3,2,1,0:T(8,128)(2,1)S(1)}, u32[]{:S(2)}, u32[]{:S(2)}) %collective-permute-start.33) | collective-permute-done | bytes 196640 | tf_op jit(solution)/shard_map/ppermute | solution.py:270
  177.0 6.0 %collective-permute-done.34.other_ref = bf16[2,16,1536]{2,1,0:T(8,128)(2,1)S(1)} collective-permute-done((bf16[2,16,1536]{2,1,0:T(8,128)(2,1)S(1)}, bf16[2,16,1536]{2,1,0:T(8,128)(2,1)S(1)}, u32[]{:S(2)}, u32[]{:S(2)}) %collective-permute-start.34) | collective-permute-done | bytes 98336 | tf_op jit(solution)/shard_map/ppermute | solution.py:270
  (118 shorter events, 54.6 us)
Async XLA Ops:
  3.3 29.2 %collective-permute-start.8 = (bf16[3,384,256]{2,1,0:T(8,128)(2,1)}, bf16[3,384,256]{2,1,0:T(8,128)(2,1)S(1)}, u32[]{:S(2)}, u32[]{:S(2)}) collective-permute-start(bf16[3,384,256]{2,1,0:T(8,128)(2,1)} %get-tuple-element.71), channel_id=1, source_target_pairs={{0,8},{1,9},{2,10},{3,11},{4,12},{5,13},{6,14},{7,15},{8,0},{9,1},... | collective-permute-start | bytes 1769480 | tf_op jit(solution)/shard_map/ppermute | solution.py:270
  7.1 14.1 %collective-permute-start = (bf16[2,16,1536]{2,1,0:T(8,128)(2,1)S(1)}, bf16[2,16,1536]{2,1,0:T(8,128)(2,1)S(1)}, u32[]{:S(2)}, u32[]{:S(2)}) collective-permute-start(bf16[2,16,1536]{2,1,0:T(8,128)(2,1)S(1)} %get-tuple-element.60), channel_id=1, source_target_pairs={{0,16},{1,17},{2,18},{3,19},{4,20},{5,21},{6,22},{7,23},{8,24},{9,... | collective-permute-start | bytes 294920 | tf_op jit(solution)/shard_map/ppermute | solution.py:270
  21.2 9.1 %collective-permute-start.1 = (bf16[2,2,16,1536]{3,2,1,0:T(8,128)(2,1)S(1)}, bf16[2,2,16,1536]{3,2,1,0:T(8,128)(2,1)S(1)}, u32[]{:S(2)}, u32[]{:S(2)}) collective-permute-start(bf16[2,2,16,1536]{3,2,1,0:T(8,128)(2,1)S(1)} %get-tuple-element.61), channel_id=1, source_target_pairs={{0,2},{1,3},{2,0},{3,1},{4,6},{5,7},{6,4},{7,5},{8,10},{9,11},{10,... | collective-permute-start | bytes 589832 | tf_op jit(solution)/shard_map/ppermute | solution.py:270
  22.8 10.9 %collective-permute-start.2 = (bf16[2,2,16,1536]{3,2,1,0:T(8,128)(2,1)S(1)}, bf16[2,2,16,1536]{3,2,1,0:T(8,128)(2,1)S(1)}, u32[]{:S(2)}, u32[]{:S(2)}) collective-permute-start(bf16[2,2,16,1536]{3,2,1,0:T(8,128)(2,1)S(1)} %get-tuple-element.62), channel_id=1, source_target_pairs={{0,8},{1,9},{2,10},{3,11},{4,12},{5,13},{6,14},{7,15},{8,0},{9,1},... | collective-permute-start | bytes 589832 | tf_op jit(solution)/shard_map/ppermute | solution.py:270
  26.3 9.8 %collective-permute-start.3 = (bf16[2,2,16,1536]{3,2,1,0:T(8,128)(2,1)S(1)}, bf16[2,2,16,1536]{3,2,1,0:T(8,128)(2,1)S(1)}, u32[]{:S(2)}, u32[]{:S(2)}) collective-permute-start(bf16[2,2,16,1536]{3,2,1,0:T(8,128)(2,1)S(1)} %get-tuple-element.62), channel_id=1, source_target_pairs={{0,10},{1,11},{2,8},{3,9},{4,14},{5,15},{6,12},{7,13},{8,2},{9,3},... | collective-permute-start | bytes 589832 | tf_op jit(solution)/shard_map/ppermute | solution.py:270
  26.3 16.5 %collective-permute-start.9 = (bf16[3,384,256]{2,1,0:T(8,128)(2,1)}, bf16[3,384,256]{2,1,0:T(8,128)(2,1)S(1)}, u32[]{:S(2)}, u32[]{:S(2)}) collective-permute-start(bf16[3,384,256]{2,1,0:T(8,128)(2,1)} %get-tuple-element.70.a_ref.refs_2_), channel_id=1, source_target_pairs={{0,4},{1,5},{2,6},{3,7},{4,0},{5,1},{6,2},{7,3},{8,12},{9,13},{10,... | collective-permute-start | bytes 1769480 | tf_op jit(solution)/shard_map/ppermute | solution.py:270
  30.4 19.2 %collective-permute-start.7 = (bf16[3,384,256]{2,1,0:T(8,128)(2,1)}, bf16[3,384,256]{2,1,0:T(8,128)(2,1)S(1)}, u32[]{:S(2)}, u32[]{:S(2)}) collective-permute-start(bf16[3,384,256]{2,1,0:T(8,128)(2,1)} %get-tuple-element.69), channel_id=1, source_target_pairs={{0,8},{1,9},{2,10},{3,11},{4,12},{5,13},{6,14},{7,15},{8,0},{9,1},... | collective-permute-start | bytes 1769480 | tf_op jit(solution)/shard_map/ppermute | solution.py:270
  32.4 23.1 %collective-permute-start.10 = (bf16[3,384,256]{2,1,0:T(8,128)(2,1)S(1)}, bf16[3,384,256]{2,1,0:T(8,128)(2,1)}, u32[]{:S(2)}, u32[]{:S(2)}) collective-permute-start(bf16[3,384,256]{2,1,0:T(8,128)(2,1)S(1)} %collective-permute-done.8.b_ref.refs_3_), channel_id=1, source_target_pairs={{0,4},{1,5},{2,6},{3,7},{4,0},{5,1},{6,2},{7,3},{8,12},{9,13},{10,... | collective-permute-start | bytes 1769480 | tf_op jit(solution)/shard_map/ppermute | solution.py:270
  36.2 20.8 %collective-permute-start.4 = (bf16[4,2,2,16,1536]{4,3,2,1,0:T(8,128)(2,1)S(1)}, bf16[4,2,2,16,1536]{4,3,2,1,0:T(8,128)(2,1)S(1)}, u32[]{:S(2)}, u32[]{:S(2)}) collective-permute-start(bf16[4,2,2,16,1536]{4,3,2,1,0:T(8,128)(2,1)S(1)} %pad_maximum_fusion.near_ref), channel_id=1, source_target_pairs={{0,1},{1,0},{2,3},{3,2},{4,5},{5,4},{6,7},{7,6},{8,9},{9,8},{10,11... | collective-permute-start | bytes 2359304 | tf_op jit(solution)/shard_map/ppermute | solution.py:270
  43.6 24.6 %collective-permute-start.11 = (bf16[3,384,256]{2,1,0:T(8,128)(2,1)}, bf16[3,384,256]{2,1,0:T(8,128)(2,1)}, u32[]{:S(2)}, u32[]{:S(2)}) collective-permute-start(bf16[3,384,256]{2,1,0:T(8,128)(2,1)} %get-tuple-element.75.a_ref.refs_2_), channel_id=1, source_target_pairs={{0,4},{1,5},{2,6},{3,7},{4,0},{5,1},{6,2},{7,3},{8,12},{9,13},{10,... | collective-permute-start | bytes 1769480 | tf_op jit(solution)/shard_map/ppermute | solution.py:270
  47.6 22.1 %collective-permute-start.6 = (bf16[3,384,256]{2,1,0:T(8,128)(2,1)}, bf16[3,384,256]{2,1,0:T(8,128)(2,1)}, u32[]{:S(2)}, u32[]{:S(2)}) collective-permute-start(bf16[3,384,256]{2,1,0:T(8,128)(2,1)} %get-tuple-element.67), channel_id=1, source_target_pairs={{0,8},{1,9},{2,10},{3,11},{4,12},{5,13},{6,14},{7,15},{8,0},{9,1},... | collective-permute-start | bytes 1769480 | tf_op jit(solution)/shard_map/ppermute | solution.py:270
  55.5 25.2 %collective-permute-start.12 = (bf16[3,384,256]{2,1,0:T(8,128)(2,1)S(1)}, bf16[3,384,256]{2,1,0:T(8,128)(2,1)S(1)}, u32[]{:S(2)}, u32[]{:S(2)}) collective-permute-start(bf16[3,384,256]{2,1,0:T(8,128)(2,1)S(1)} %collective-permute-done.7.b_ref.refs_3_), channel_id=1, source_target_pairs={{0,4},{1,5},{2,6},{3,7},{4,0},{5,1},{6,2},{7,3},{8,12},{9,13},{10,... | collective-permute-start | bytes 1769480 | tf_op jit(solution)/shard_map/ppermute | solution.py:270
  68.2 31.1 %collective-permute-start.14 = (bf16[3,384,256]{2,1,0:T(8,128)(2,1)S(1)}, bf16[3,384,256]{2,1,0:T(8,128)(2,1)}, u32[]{:S(2)}, u32[]{:S(2)}) collective-permute-start(bf16[3,384,256]{2,1,0:T(8,128)(2,1)S(1)} %copy-done.2), channel_id=1, source_target_pairs={{0,4},{1,5},{2,6},{3,7},{4,0},{5,1},{6,2},{7,3},{8,12},{9,13},{10,... | collective-permute-start | bytes 1769480 | tf_op jit(solution)/shard_map/ppermute | solution.py:270
  81.5 24.6 %collective-permute-start.15 = (bf16[3,384,256]{2,1,0:T(8,128)(2,1)}, bf16[3,384,256]{2,1,0:T(8,128)(2,1)}, u32[]{:S(2)}, u32[]{:S(2)}) collective-permute-start(bf16[3,384,256]{2,1,0:T(8,128)(2,1)} %collective-permute-done.6.b_ref.refs_3_), channel_id=1, source_target_pairs={{0,4},{1,5},{2,6},{3,7},{4,0},{5,1},{6,2},{7,3},{8,12},{9,13},{10,... | collective-permute-start | bytes 1769480 | tf_op jit(solution)/shard_map/ppermute | solution.py:270
  83.0 9.0 %collective-permute-start.13 = (bf16[128,768]{1,0:T(8,128)(2,1)}, bf16[128,768]{1,0:T(8,128)(2,1)S(1)}, u32[]{:S(2)}, u32[]{:S(2)}) collective-permute-start(bf16[128,768]{1,0:T(8,128)(2,1)} %get-tuple-element.81), channel_id=1, source_target_pairs={{0,16},{1,17},{2,18},{3,19},{4,20},{5,21},{6,22},{7,23},{8,24},{9,... | collective-permute-start | bytes 589832 | tf_op jit(solution)/shard_map/ppermute | solution.py:270
  87.0 17.8 %collective-permute-start.5 = (bf16[3,384,128]{2,1,0:T(8,128)(2,1)}, bf16[3,384,128]{2,1,0:T(8,128)(2,1)}, u32[]{:S(2)}, u32[]{:S(2)}) collective-permute-start(bf16[3,384,128]{2,1,0:T(8,128)(2,1)} %get-tuple-element.64), channel_id=1, source_target_pairs={{0,8},{1,9},{2,10},{3,11},{4,12},{5,13},{6,14},{7,15},{8,0},{9,1},... | collective-permute-start | bytes 884744 | tf_op jit(solution)/shard_map/ppermute | solution.py:270
  99.3 18.7 %collective-permute-start.18 = (bf16[3,384,128]{2,1,0:T(8,128)(2,1)}, bf16[3,384,128]{2,1,0:T(8,128)(2,1)}, u32[]{:S(2)}, u32[]{:S(2)}) collective-permute-start(bf16[3,384,128]{2,1,0:T(8,128)(2,1)} %get-tuple-element.90.a_ref.refs_2_), channel_id=1, source_target_pairs={{0,4},{1,5},{2,6},{3,7},{4,0},{5,1},{6,2},{7,3},{8,12},{9,13},{10,... | collective-permute-start | bytes 884744 | tf_op jit(solution)/shard_map/ppermute | solution.py:270
  99.8 10.3 %collective-permute-start.17 = (bf16[128,768]{1,0:T(8,128)(2,1)S(1)}, bf16[128,768]{1,0:T(8,128)(2,1)}, u32[]{:S(2)}, u32[]{:S(2)}) collective-permute-start(bf16[128,768]{1,0:T(8,128)(2,1)S(1)} %shard_map.95.refs_0_), channel_id=1, source_target_pairs={{0,16},{1,17},{2,18},{3,19},{4,20},{5,21},{6,22},{7,23},{8,24},{9,... | collective-permute-start | bytes 589832 | tf_op jit(solution)/shard_map/ppermute | solution.py:270
  99.8 14.6 %collective-permute-start.16 = (bf16[128,768]{1,0:T(8,128)(2,1)}, bf16[128,768]{1,0:T(8,128)(2,1)}, u32[]{:S(2)}, u32[]{:S(2)}) collective-permute-start(bf16[128,768]{1,0:T(8,128)(2,1)} %get-tuple-element.88), channel_id=1, source_target_pairs={{0,16},{1,17},{2,18},{3,19},{4,20},{5,21},{6,22},{7,23},{8,24},{9,... | collective-permute-start | bytes 589832 | tf_op jit(solution)/shard_map/ppermute | solution.py:270
  104.8 14.9 %collective-permute-start.19 = (bf16[3,384,128]{2,1,0:T(8,128)(2,1)}, bf16[3,384,128]{2,1,0:T(8,128)(2,1)S(1)}, u32[]{:S(2)}, u32[]{:S(2)}) collective-permute-start(bf16[3,384,128]{2,1,0:T(8,128)(2,1)} %get-tuple-element.92), channel_id=1, source_target_pairs={{0,8},{1,9},{2,10},{3,11},{4,12},{5,13},{6,14},{7,15},{8,0},{9,1},... | collective-permute-start | bytes 884744 | tf_op jit(solution)/shard_map/ppermute | solution.py:270
  106.1 13.6 %collective-permute-start.20 = (bf16[3,384,128]{2,1,0:T(8,128)(2,1)}, bf16[3,384,128]{2,1,0:T(8,128)(2,1)S(1)}, u32[]{:S(2)}, u32[]{:S(2)}) collective-permute-start(bf16[3,384,128]{2,1,0:T(8,128)(2,1)} %collective-permute-done.5.b_ref.refs_3_), channel_id=1, source_target_pairs={{0,4},{1,5},{2,6},{3,7},{4,0},{5,1},{6,2},{7,3},{8,12},{9,13},{10,... | collective-permute-start | bytes 884744 | tf_op jit(solution)/shard_map/ppermute | solution.py:270
  118.0 14.5 %collective-permute-start.22 = (bf16[128,768]{1,0:T(8,128)(2,1)S(1)}, bf16[128,768]{1,0:T(8,128)(2,1)S(1)}, u32[]{:S(2)}, u32[]{:S(2)}) collective-permute-start(bf16[128,768]{1,0:T(8,128)(2,1)S(1)} %get-tuple-element.98), channel_id=1, source_target_pairs={{0,16},{1,17},{2,18},{3,19},{4,20},{5,21},{6,22},{7,23},{8,24},{9,... | collective-permute-start | bytes 589832 | tf_op jit(solution)/shard_map/ppermute | solution.py:270
  118.1 27.3 %collective-permute-start.25 = (bf16[3,384,128]{2,1,0:T(8,128)(2,1)S(1)}, bf16[3,384,128]{2,1,0:T(8,128)(2,1)S(1)}, u32[]{:S(2)}, u32[]{:S(2)}) collective-permute-start(bf16[3,384,128]{2,1,0:T(8,128)(2,1)S(1)} %copy-done.15), channel_id=1, source_target_pairs={{0,4},{1,5},{2,6},{3,7},{4,0},{5,1},{6,2},{7,3},{8,12},{9,13},{10,... | collective-permute-start | bytes 884744 | tf_op jit(solution)/shard_map/ppermute | solution.py:270
  119.7 25.7 %collective-permute-start.26 = (bf16[3,384,128]{2,1,0:T(8,128)(2,1)S(1)}, bf16[3,384,128]{2,1,0:T(8,128)(2,1)S(1)}, u32[]{:S(2)}, u32[]{:S(2)}) collective-permute-start(bf16[3,384,128]{2,1,0:T(8,128)(2,1)S(1)} %collective-permute-done.19.b_ref.refs_3_), channel_id=1, source_target_pairs={{0,4},{1,5},{2,6},{3,7},{4,0},{5,1},{6,2},{7,3},{8,12},{9,13},{10,... | collective-permute-start | bytes 884744 | tf_op jit(solution)/shard_map/ppermute | solution.py:270
  120.2 18.5 %collective-permute-start.24 = (bf16[128,768]{1,0:T(8,128)(2,1)S(1)}, bf16[128,768]{1,0:T(8,128)(2,1)S(1)}, u32[]{:S(2)}, u32[]{:S(2)}) collective-permute-start(bf16[128,768]{1,0:T(8,128)(2,1)S(1)} %shard_map.97.refs_0_), channel_id=1, source_target_pairs={{0,16},{1,17},{2,18},{3,19},{4,20},{5,21},{6,22},{7,23},{8,24},{9,... | collective-permute-start | bytes 589832 | tf_op jit(solution)/shard_map/ppermute | solution.py:270
  132.5 10.4 %collective-permute-start.23 = (bf16[128,768]{1,0:T(8,128)(2,1)S(1)}, bf16[128,768]{1,0:T(8,128)(2,1)S(1)}, u32[]{:S(2)}, u32[]{:S(2)}) collective-permute-start(bf16[128,768]{1,0:T(8,128)(2,1)S(1)} %shard_map.101.refs_0_), channel_id=1, source_target_pairs={{0,16},{1,17},{2,18},{3,19},{4,20},{5,21},{6,22},{7,23},{8,24},{9,... | collective-permute-start | bytes 589832 | tf_op jit(solution)/shard_map/ppermute | solution.py:270
  134.5 8.4 %collective-permute-start.21 = (bf16[128,384]{1,0:T(8,128)(2,1)S(1)}, bf16[128,384]{1,0:T(8,128)(2,1)S(1)}, u32[]{:S(2)}, u32[]{:S(2)}) collective-permute-start(bf16[128,384]{1,0:T(8,128)(2,1)S(1)} %get-tuple-element.96), channel_id=1, source_target_pairs={{0,16},{1,17},{2,18},{3,19},{4,20},{5,21},{6,22},{7,23},{8,24},{9,... | collective-permute-start | bytes 294920 | tf_op jit(solution)/shard_map/ppermute | solution.py:270
  146.2 8.5 %collective-permute-start.27 = (bf16[128,384]{1,0:T(8,128)(2,1)S(1)}, bf16[128,384]{1,0:T(8,128)(2,1)S(1)}, u32[]{:S(2)}, u32[]{:S(2)}) collective-permute-start(bf16[128,384]{1,0:T(8,128)(2,1)S(1)} %get-tuple-element.105), channel_id=1, source_target_pairs={{0,16},{1,17},{2,18},{3,19},{4,20},{5,21},{6,22},{7,23},{8,24},{9,... | collective-permute-start | bytes 294920 | tf_op jit(solution)/shard_map/ppermute | solution.py:270
  146.5 9.3 %collective-permute-start.29 = (bf16[128,384]{1,0:T(8,128)(2,1)S(1)}, bf16[128,384]{1,0:T(8,128)(2,1)S(1)}, u32[]{:S(2)}, u32[]{:S(2)}) collective-permute-start(bf16[128,384]{1,0:T(8,128)(2,1)S(1)} %shard_map.100.refs_0_), channel_id=1, source_target_pairs={{0,16},{1,17},{2,18},{3,19},{4,20},{5,21},{6,22},{7,23},{8,24},{9,... | collective-permute-start | bytes 294920 | tf_op jit(solution)/shard_map/ppermute | solution.py:270
  163.7 7.0 %collective-permute-start.31 = (bf16[2,2,16,1536]{3,2,1,0:T(8,128)(2,1)S(1)}, bf16[2,2,16,1536]{3,2,1,0:T(8,128)(2,1)S(1)}, u32[]{:S(2)}, u32[]{:S(2)}) collective-permute-start(bf16[2,2,16,1536]{3,2,1,0:T(8,128)(2,1)S(1)} %get-tuple-element.111), channel_id=1, source_target_pairs={{0,2},{1,3},{2,0},{3,1},{4,6},{5,7},{6,4},{7,5},{8,10},{9,11},{10,... | collective-permute-start | bytes 589832 | tf_op jit(solution)/shard_map/ppermute | solution.py:270
  165.2 7.8 %collective-permute-start.32 = (bf16[2,2,16,1536]{3,2,1,0:T(8,128)(2,1)S(1)}, bf16[2,2,16,1536]{3,2,1,0:T(8,128)(2,1)S(1)}, u32[]{:S(2)}, u32[]{:S(2)}) collective-permute-start(bf16[2,2,16,1536]{3,2,1,0:T(8,128)(2,1)S(1)} %get-tuple-element.112), channel_id=1, source_target_pairs={{0,8},{1,9},{2,10},{3,11},{4,12},{5,13},{6,14},{7,15},{8,0},{9,1},... | collective-permute-start | bytes 589832 | tf_op jit(solution)/shard_map/ppermute | solution.py:270
  165.2 10.9 %collective-permute-start.33 = (bf16[2,2,16,1536]{3,2,1,0:T(8,128)(2,1)S(1)}, bf16[2,2,16,1536]{3,2,1,0:T(8,128)(2,1)S(1)}, u32[]{:S(2)}, u32[]{:S(2)}) collective-permute-start(bf16[2,2,16,1536]{3,2,1,0:T(8,128)(2,1)S(1)} %get-tuple-element.113), channel_id=1, source_target_pairs={{0,10},{1,11},{2,8},{3,9},{4,14},{5,15},{6,12},{7,13},{8,2},{9,3},... | collective-permute-start | bytes 589832 | tf_op jit(solution)/shard_map/ppermute | solution.py:270
  (29 other events, 260.7 us)

commit v4 on v3

--- a/solution.py
+++ b/solution.py
@@ -9,7 +9,6 @@
 BF16 = jnp.bfloat16
 LANES = 128
 AHEAD = 2
-IN_FLIGHT = 2
 
 
 def dot(left, right):
@@ -20,16 +19,12 @@
     return lax.dot_general(left, right, (((1,), (1,)), ((), ())), preferred_element_type=F32)
 
 
-def chunk_cuts(units):
+def chunk_list(units):
     blocks = units // LANES
-    if blocks < 8:
-        sizes = [1] * blocks
-    else:
-        sizes = [2 * (blocks // 8)] * 3 + [blocks // 8] * 2
-    cuts = [0]
-    for size in sizes:
-        cuts.append(cuts[-1] + size * LANES)
-    return cuts
+    if blocks != 8:
+        return [(i * LANES, LANES) for i in range(blocks)]
+    shape = ((0, 1), (2, 2), (4, 2), (6, 2), (1, 1))
+    return [(start * LANES, size * LANES) for start, size in shape]
 
 
 def make_plain(n_fsdp, n_et):
@@ -63,7 +58,7 @@
         z_low = (f_index // 2) % 2
         y_index = f_index % 2
 
-        cuts = chunk_cuts(half_units)
+        chunks = chunk_list(half_units)
         keep_at = z_low * half_units
         give_at = (1 - z_low) * half_units
 
@@ -76,11 +71,11 @@
                 ]
             )
 
-        count = len(cuts) - 1
+        count = len(chunks)
         kept, given = [], []
-        for lo, hi in zip(cuts[:-1], cuts[1:]):
-            kept.append(part_of(keep_at + lo, hi - lo))
-            given.append(part_of(give_at + lo, hi - lo))
+        for lo, size in chunks:
+            kept.append(part_of(keep_at + lo, size))
+            given.append(part_of(give_at + lo, size))
         near, far = [None] * count, [None] * count
 
         def start_pair(k):
@@ -203,6 +198,10 @@
     )(*args)
 
 
+def after(values, *others):
+    return lax.optimization_barrier((values, *others))
+
+
 def shaped(shape, kind):
     return jax.ShapeDtypeStruct(shape, kind)
 
@@ -281,35 +280,23 @@
         block_shape = (2, most, z_width)
         low = ((lax.axis_index("fsdp") // 2) % 2).astype(jnp.int32).reshape(1)
 
-        cuts = chunk_cuts(half_units)
-        count = len(cuts) - 1
+        chunks = chunk_list(half_units)
+        count = len(chunks)
         own_w, zp_w = [None] * count, [None] * count
         given = [None] * count
 
         stream = []
 
-        def over_y(values, *after):
-            after = list(after)
-            if len(stream) >= IN_FLIGHT:
-                after.append(stream[-IN_FLIGHT])
-            if after:
-                values, *after = lax.optimization_barrier((values, *after))
-            if len(stream) >= IN_FLIGHT:
-                stream[-IN_FLIGHT] = after.pop()
+        def over_y(values):
             stream.append(swap(values, at_y))
-            return after
-
-        def stream_chunk(k, *after):
+
+        for k in range(count):
             own_w[k], given[k] = weight_chunk(
-                low, w_gate, w_up, w_down, cuts[k], cuts[k + 1] - cuts[k]
-            )
-            zp_w[k] = swap(given[k], at_zp)
-            after = over_y(own_w[k], *after)
-            over_y(zp_w[k])
-            return after
-
-        for k in range(min(AHEAD, count)):
-            stream_chunk(k)
+                low, w_gate, w_up, w_down, *chunks[k]
+            )
+        over_y(own_w[0])
+        zp_w[0] = swap(given[0], at_zp)
+        over_y(own_w[1])
 
         def pack_body(tokens_ref, cot_ref, experts_ref, gates_ref, keep_ref, send_ref, packed_ref):
             chosen, weight = route_columns(experts_ref, gates_ref)
@@ -353,11 +340,24 @@
                 flipped_ref[j] = flip_pairs(values, own_width)
 
         pair = shaped((2,) + block_shape, BF16)
+        mine, zp_w[0], stream[0] = after(mine, zp_w[0], stream[0])
         plain, flipped = call(join_body, [pair, pair], mine, other)
+        own_w[2], _ = after(own_w[2], plain)
+        over_y(own_w[2])
+        over_y(zp_w[0])
+        for k in range(1, count):
+            if k <= 2:
+                given[k], _ = after(given[k], plain)
+            else:
+                given[k], zp_w[k - 2] = after(given[k], zp_w[k - 2])
+            zp_w[k] = swap(given[k], at_zp)
         near_rows = jnp.stack(
             [plain, swap(plain, at_x), swap(flipped, at_zp), swap(flipped, at_zp + at_x)]
         )
+        near_rows, stream[1] = after(near_rows, stream[1])
         far_rows = swap(near_rows, at_core)
+        near_rows, stream[2], zp_w[1] = after(near_rows, stream[2], zp_w[1])
+        over_y(zp_w[1])
 
         slots = 16 * most
         own_slots = slots // 2
@@ -424,10 +424,11 @@
         pre, mine, total = [None] * count, [None] * count, [None] * count
 
         def weights_of(k):
-            return own_w[k], zp_w[k], stream[2 * k], stream[2 * k + 1]
+            at = (k, k + 3) if k < 3 else (2 * k, 2 * k + 1)
+            return own_w[k], zp_w[k], stream[at[0]], stream[at[1]]
 
         def first(k, near_rows, far_rows):
-            units = cuts[k + 1] - cuts[k]
+            units = chunks[k][1]
             pre[k] = call(
                 first_body,
                 [shaped((own_slots, 3 * units), F32), shaped((own_slots, 3 * units), BF16)],
@@ -437,7 +438,7 @@
             )
 
         def middle(k):
-            units = cuts[k + 1] - cuts[k]
+            units = chunks[k][1]
             keep, sent = pre[k]
             (mine[k],) = call(
                 middle_body,
@@ -463,36 +464,50 @@
                 *held,
             )
 
-        for k in range(count):
-            if k == count - 1:
-                after = [near_rows]
-                if k >= 1:
-                    after.append(mine[k - 1])
-                if k >= 2:
-                    after.append(total[k - 2][0])
-                after = lax.optimization_barrier(tuple(after))
-                near_rows = after[0]
-                if k >= 1:
-                    mine[k - 1] = after[1]
-                if k >= 2:
-                    total[k - 2] = [after[2]]
-            first(k, near_rows, far_rows)
-            if k + AHEAD < count:
-                after = [pre[k][1]]
-                if k >= 1:
-                    after.append(mine[k - 1])
-                if k >= 2:
-                    after.append(total[k - 2][0])
-                after = stream_chunk(k + AHEAD, *after)
-                pre[k] = [pre[k][0], after[0]]
-                if k >= 1:
-                    mine[k - 1] = after[1]
-                if k >= 2:
-                    total[k - 2] = [after[2]]
-            middle(k)
-            if k >= 1:
-                second(k - 1)
-        second(count - 1)
+        def held_back(values, firsts=(), middles=(), seconds=()):
+            middles = [k for k in middles if k >= 0]
+            seconds = [k for k in seconds if k >= 0]
+            done = [pre[k][1] for k in firsts] + [mine[k] for k in middles]
+            done += [total[k][0] for k in seconds]
+            values, *done = after(values, *done)
+            for k in firsts:
+                pre[k] = [pre[k][0], done.pop(0)]
+            for k in middles:
+                mine[k] = done.pop(0)
+            for k in seconds:
+                total[k] = [done.pop(0)]
+            return values
+
+        def own_over_y(k, *steps):
+            own_w[k] = held_back(own_w[k], *steps)
+            over_y(own_w[k])
+
+        def pair_over_y(k, *steps):
+            zp_w[k] = held_back(zp_w[k], *steps)
+            over_y(zp_w[k])
+
+        first(0, near_rows, far_rows)
+        pair_over_y(2, [0])
+        first(1, near_rows, far_rows)
+        own_over_y(3, [1])
+        pair_over_y(3, [1])
+        middle(0)
+        second(0)
+        first(2, held_back(near_rows, [], [0]), far_rows)
+        own_over_y(4, [2])
+        pair_over_y(4, [2])
+        middle(1)
+        second(1)
+        pre[2] = [held_back(pre[2][0], [], [1], [0]), pre[2][1]]
+        middle(2)
+        second(2)
+        first(3, held_back(near_rows, [], [2], [1]), far_rows)
+        first(4, held_back(near_rows, [3], [], [2]), far_rows)
+        pre[3] = [held_back(pre[3][0], [4]), pre[3][1]]
+        middle(3)
+        second(3)
+        middle(4)
+        second(4)
         total = total[-1]
 
         def spread_body(keep_ref, recv_ref, own_ref, *outs):

time: 185 us -> 171 us (0.924)
  local copies, waits for them, and re-layouts: 10.3 us -> 2.36 us
  Pallas kernels: 35.3 us -> 29.5 us
  starting transfers between devices: 46.1 us -> 41.4 us
  waiting for transfers between devices: 91.8 us -> 96 us
    unnamed x54 -> x36, local copies, waits for them, and re-layouts: 10.3 us -> 2.36 us
    pallas_call x20, Pallas kernels: 23.6 us -> 18 us  [call(): pl.pallas_call(body, out_shape=list(outs), scratch_shapes=list(scratch),...]
    ppermute x35, starting transfers between devices: 46.1 us -> 41.4 us  [swap(): return lax.ppermute(values, ('fsdp', 'et'), pairs)]
    ppermute x35, waiting for transfers between devices: 91.8 us -> 96 us  [swap(): return lax.ppermute(values, ('fsdp', 'et'), pairs)]
  transfers between devices with their start and end apart: 35 -> 35, of which waited for: 20 -> 25; matrix products, arithmetic and copies ran while one was open for 0% -> 0% of each run, Pallas kernels for 16% -> 15%
where the time goes in v4:
time: 171 us; the launch traced here: 170 us
  waiting for transfers between devices  96 us (56%)
  starting transfers between devices  41.4 us (24%)
  Pallas kernels  29.5 us (17%)
  local copies, waits for them, and re-layouts  2.36 us (1%)
    ppermute x35, waiting for transfers between devices, swap(): return lax.ppermute(values, ('fsdp', 'et'), pairs)  96 us
    ppermute x35, starting transfers between devices, swap(): return lax.ppermute(values, ('fsdp', 'et'), pairs)  41.4 us
    pallas_call x20, Pallas kernels, call(): pl.pallas_call(body, out_shape=list(outs), scratch_shapes=list(scratch),...  18 us
    pallas_call x5, Pallas kernels, weight_chunk(): pl.pallas_call(weight_chunk_body, out_shape=[out, out], grid_spec=pltpu.P...  11.5 us
  transfers between devices with their start and end apart: 35, of which 25 were waited for; matrix products, arithmetic and copies ran while one was open for 0% of the time, Pallas kernels for 15%

profile of v4, /device:TPU:0, one launch (start us, length us, event | category | flops | bytes accessed | tf_op | source)
XLA Modules:
  0.0 170.4 jit_solution(16466217657730528894)
XLA Ops:
  0.7 2.1 %shard_map.87 = (bf16[3,384,128]{2,1,0:T(8,128)(2,1)}, bf16[3,384,128]{2,1,0:T(8,128)(2,1)}) custom-call(s32[1]{0:T(128)} %bitcast.low_ref, bf16[384,2048]{1,0:T(8,128)(2,1)} %refs_3_.9, bf16[384,2048]{1,0:T(8,128)(2,1)} %refs_4_.9, bf16[2048,384]{1,0:T(8,128)(2,1)} %refs_5_.9, bf16[384,2048]{1,0:T(8,128)(2,1)} %refs_3_.9, bf16[384,2048]{1,0:T(8,128)(2,1)} %refs_4_.9, ...), custom_call_target="tpu_custom_call" | custom-call | bytes 1024 | tf_op jit(solution)/shard_map/pallas_call | solution.py:251
  2.7 3.0 %collective-permute-start = (bf16[3,384,128]{2,1,0:T(8,128)(2,1)}, bf16[3,384,128]{2,1,0:T(8,128)(2,1)}, u32[]{:S(2)}, u32[]{:S(2)}) collective-permute-start(bf16[3,384,128]{2,1,0:T(8,128)(2,1)} %get-tuple-element.68), channel_id=1, source_target_pairs={{0,8},{1,9},{2,10},{3,11},{4,12},{5,13},{6,14},{7,15},{8,0},{9,1},... | collective-permute-start | bytes 884744 | tf_op jit(solution)/shard_map/ppermute | solution.py:269
  7.3 2.5 %shard_map.89 = (bf16[3,384,256]{2,1,0:T(8,128)(2,1)}, bf16[3,384,256]{2,1,0:T(8,128)(2,1)}) custom-call(s32[1]{0:T(128)} %bitcast.low_ref, bf16[384,2048]{1,0:T(8,128)(2,1)} %refs_3_.9, bf16[384,2048]{1,0:T(8,128)(2,1)} %refs_4_.9, bf16[2048,384]{1,0:T(8,128)(2,1)} %refs_5_.9, bf16[384,2048]{1,0:T(8,128)(2,1)} %refs_3_.9, bf16[384,2048]{1,0:T(8,128)(2,1)} %refs_4_.9, ...), custom_call_target="tpu_custom_call" | custom-call | bytes 1024 | tf_op jit(solution)/shard_map/pallas_call | solution.py:251
  11.1 2.7 %collective-permute-start.2 = (bf16[2,16,1536]{2,1,0:T(8,128)(2,1)S(1)}, bf16[2,16,1536]{2,1,0:T(8,128)(2,1)S(1)}, u32[]{:S(2)}, u32[]{:S(2)}) collective-permute-start(bf16[2,16,1536]{2,1,0:T(8,128)(2,1)S(1)} %get-tuple-element.71), channel_id=1, source_target_pairs={{0,16},{1,17},{2,18},{3,19},{4,20},{5,21},{6,22},{7,23},{8,24},{9,... | collective-permute-start | bytes 294920 | tf_op jit(solution)/shard_map/ppermute | solution.py:269
  13.8 2.2 %collective-permute-done.1.c_ref.refs_4_ = bf16[3,384,128]{2,1,0:T(8,128)(2,1)S(1)} collective-permute-done((bf16[3,384,128]{2,1,0:T(8,128)(2,1)}, bf16[3,384,128]{2,1,0:T(8,128)(2,1)S(1)}, u32[]{:S(2)}, u32[]{:S(2)}) %collective-permute-start.1) | collective-permute-done | bytes 294944 | tf_op jit(solution)/shard_map/ppermute | solution.py:269
  16.0 2.1 %collective-permute-done.2.other_ref = bf16[2,16,1536]{2,1,0:T(8,128)(2,1)S(1)} collective-permute-done((bf16[2,16,1536]{2,1,0:T(8,128)(2,1)S(1)}, bf16[2,16,1536]{2,1,0:T(8,128)(2,1)S(1)}, u32[]{:S(2)}, u32[]{:S(2)}) %collective-permute-start.2) | collective-permute-done | bytes 98336 | tf_op jit(solution)/shard_map/ppermute | solution.py:269
  19.6 2.0 %collective-permute-start.5 = (bf16[2,2,16,1536]{3,2,1,0:T(8,128)(2,1)S(1)}, bf16[2,2,16,1536]{3,2,1,0:T(8,128)(2,1)S(1)}, u32[]{:S(2)}, u32[]{:S(2)}) collective-permute-start(bf16[2,2,16,1536]{3,2,1,0:T(8,128)(2,1)S(1)} %get-tuple-element.73), channel_id=1, source_target_pairs={{0,10},{1,11},{2,8},{3,9},{4,14},{5,15},{6,12},{7,13},{8,2},{9,3},... | collective-permute-start | bytes 589832 | tf_op jit(solution)/shard_map/ppermute | solution.py:269
  21.6 2.5 %shard_map.90 = (bf16[3,384,256]{2,1,0:T(8,128)(2,1)}, bf16[3,384,256]{2,1,0:T(8,128)(2,1)}) custom-call(s32[1]{0:T(128)} %bitcast.low_ref, bf16[384,2048]{1,0:T(8,128)(2,1)} %refs_3_.9, bf16[384,2048]{1,0:T(8,128)(2,1)} %refs_4_.9, bf16[2048,384]{1,0:T(8,128)(2,1)} %refs_5_.9, bf16[384,2048]{1,0:T(8,128)(2,1)} %refs_3_.9, bf16[384,2048]{1,0:T(8,128)(2,1)} %refs_4_.9, ...), custom_call_target="tpu_custom_call" | custom-call | bytes 1024 | tf_op jit(solution)/shard_map/pallas_call | solution.py:251
  27.5 3.6 %collective-permute-done.5 = bf16[2,2,16,1536]{3,2,1,0:T(8,128)(2,1)S(1)} collective-permute-done((bf16[2,2,16,1536]{3,2,1,0:T(8,128)(2,1)S(1)}, bf16[2,2,16,1536]{3,2,1,0:T(8,128)(2,1)S(1)}, u32[]{:S(2)}, u32[]{:S(2)}) %collective-permute-start.5) | collective-permute-done | bytes 196640 | tf_op jit(solution)/shard_map/ppermute | solution.py:269
  33.9 2.5 %shard_map.91 = (bf16[3,384,256]{2,1,0:T(8,128)(2,1)}, bf16[3,384,256]{2,1,0:T(8,128)(2,1)}) custom-call(s32[1]{0:T(128)} %bitcast.low_ref, bf16[384,2048]{1,0:T(8,128)(2,1)} %refs_3_.9, bf16[384,2048]{1,0:T(8,128)(2,1)} %refs_4_.9, bf16[2048,384]{1,0:T(8,128)(2,1)} %refs_5_.9, bf16[384,2048]{1,0:T(8,128)(2,1)} %refs_3_.9, bf16[384,2048]{1,0:T(8,128)(2,1)} %refs_4_.9, ...), custom_call_target="tpu_custom_call" | custom-call | bytes 1024 | tf_op jit(solution)/shard_map/pallas_call | solution.py:251
  36.4 7.9 %collective-permute-done.8.b_ref.refs_3_ = bf16[3,384,256]{2,1,0:T(8,128)(2,1)S(1)} collective-permute-done((bf16[3,384,256]{2,1,0:T(8,128)(2,1)}, bf16[3,384,256]{2,1,0:T(8,128)(2,1)S(1)}, u32[]{:S(2)}, u32[]{:S(2)}) %collective-permute-start.8) | collective-permute-done | bytes 589856 | tf_op jit(solution)/shard_map/ppermute | solution.py:269
  44.3 3.4 %collective-permute-done.7.c_ref.refs_4_ = bf16[3,384,256]{2,1,0:T(8,128)(2,1)S(1)} collective-permute-done((bf16[3,384,256]{2,1,0:T(8,128)(2,1)}, bf16[3,384,256]{2,1,0:T(8,128)(2,1)S(1)}, u32[]{:S(2)}, u32[]{:S(2)}) %collective-permute-start.7) | collective-permute-done | bytes 589856 | tf_op jit(solution)/shard_map/ppermute | solution.py:269
  49.7 2.1 %shard_map.93 = (bf16[3,384,128]{2,1,0:T(8,128)(2,1)}, bf16[3,384,128]{2,1,0:T(8,128)(2,1)}) custom-call(s32[1]{0:T(128)} %bitcast.low_ref, bf16[384,2048]{1,0:T(8,128)(2,1)} %refs_3_.9, bf16[384,2048]{1,0:T(8,128)(2,1)} %refs_4_.9, bf16[2048,384]{1,0:T(8,128)(2,1)} %refs_5_.9, bf16[384,2048]{1,0:T(8,128)(2,1)} %refs_3_.9, bf16[384,2048]{1,0:T(8,128)(2,1)} %refs_4_.9, ...), custom_call_target="tpu_custom_call" | custom-call | bytes 1024 | tf_op jit(solution)/shard_map/pallas_call | solution.py:251
  51.8 3.9 %collective-permute-done.11.b_ref.refs_3_ = bf16[3,384,256]{2,1,0:T(8,128)(2,1)} collective-permute-done((bf16[3,384,256]{2,1,0:T(8,128)(2,1)}, bf16[3,384,256]{2,1,0:T(8,128)(2,1)}, u32[]{:S(2)}, u32[]{:S(2)}) %collective-permute-start.11) | collective-permute-done | bytes 589856 | tf_op jit(solution)/shard_map/ppermute | solution.py:269
  63.3 3.5 %collective-permute-done.14.d_ref.refs_5_ = bf16[3,384,256]{2,1,0:T(8,128)(2,1)} collective-permute-done((bf16[3,384,256]{2,1,0:T(8,128)(2,1)S(1)}, bf16[3,384,256]{2,1,0:T(8,128)(2,1)}, u32[]{:S(2)}, u32[]{:S(2)}) %collective-permute-start.14) | collective-permute-done | bytes 589856 | tf_op jit(solution)/shard_map/ppermute | solution.py:269
  66.8 2.0 %shard_map.96 = (f32[128,768]{1,0:T(8,128)S(1)}, bf16[128,768]{1,0:T(8,128)(2,1)S(1)}) custom-call(bf16[4,2,2,16,1536]{4,3,2,1,0:T(8,128)(2,1)S(1)} %pad_maximum_fusion.near_ref, bf16[4,2,2,16,1536]{4,3,2,1,0:T(8,128)(2,1)S(1)} %collective-permute-done.9.far_ref, bf16[3,384,256]{2,1,0:T(8,128)(2,1)S(1)} %copy-done, ...), custom_call_target="tpu_custom_call" | custom-call | bytes 1024 | tf_op jit(solution)/shard_map/pallas_call | solution.py:192
  72.7 3.4 %collective-permute-start.16 = (bf16[128,768]{1,0:T(8,128)(2,1)S(1)}, bf16[128,768]{1,0:T(8,128)(2,1)S(1)}, u32[]{:S(2)}, u32[]{:S(2)}) collective-permute-start(bf16[128,768]{1,0:T(8,128)(2,1)S(1)} %get-tuple-element.103), channel_id=1, source_target_pairs={{0,16},{1,17},{2,18},{3,19},{4,20},{5,21},{6,22},{7,23},{8,24},{9,... | collective-permute-start | bytes 589832 | tf_op jit(solution)/shard_map/ppermute | solution.py:269
  76.1 3.2 %collective-permute-done.13.d_ref.refs_5_ = bf16[3,384,256]{2,1,0:T(8,128)(2,1)S(1)} collective-permute-done((bf16[3,384,256]{2,1,0:T(8,128)(2,1)}, bf16[3,384,256]{2,1,0:T(8,128)(2,1)S(1)}, u32[]{:S(2)}, u32[]{:S(2)}) %collective-permute-start.13) | collective-permute-done | bytes 589856 | tf_op jit(solution)/shard_map/ppermute | solution.py:269
  79.3 2.0 %shard_map.95 = (f32[128,768]{1,0:T(8,128)S(1)}, bf16[128,768]{1,0:T(8,128)(2,1)S(1)}) custom-call(bf16[4,2,2,16,1536]{4,3,2,1,0:T(8,128)(2,1)S(1)} %pad_maximum_fusion.near_ref, bf16[4,2,2,16,1536]{4,3,2,1,0:T(8,128)(2,1)S(1)} %collective-permute-done.9.far_ref, bf16[3,384,256]{2,1,0:T(8,128)(2,1)S(1)} %copy-done.2, ...), custom_call_target="tpu_custom_call" | custom-call | bytes 1024 | tf_op jit(solution)/shard_map/pallas_call | solution.py:192
  86.4 14.7 %collective-permute-done.17.refs_1_ = bf16[128,384]{1,0:T(8,128)(2,1)S(1)} collective-permute-done((bf16[128,384]{1,0:T(8,128)(2,1)S(1)}, bf16[128,384]{1,0:T(8,128)(2,1)S(1)}, u32[]{:S(2)}, u32[]{:S(2)}) %collective-permute-start.17) | collective-permute-done | bytes 98336 | tf_op jit(solution)/shard_map/ppermute | solution.py:269
  106.4 2.0 %shard_map.100.refs_6_ = f32[2,256,1536]{2,1,0:T(8,128)S(1)} custom-call(bf16[128,768]{1,0:T(8,128)(2,1)S(1)} %shard_map.97.refs_0_, bf16[128,768]{1,0:T(8,128)(2,1)S(1)} %collective-permute-done.20.refs_1_, bf16[3,384,256]{2,1,0:T(8,128)(2,1)S(1)} %copy-done, bf16[3,384,256]{2,1,0:T(8,128)(2,1)S(1)} %collective-permute-done.8.b_ref.refs_3_, ...), custom_call_target="tpu_custom_call" | custom-call | bytes 1024 | tf_op jit(solution)/shard_map/pallas_call | solution.py:192
  109.5 4.9 %collective-permute-done.23.refs_1_ = bf16[128,768]{1,0:T(8,128)(2,1)S(1)} collective-permute-done((bf16[128,768]{1,0:T(8,128)(2,1)S(1)}, bf16[128,768]{1,0:T(8,128)(2,1)S(1)}, u32[]{:S(2)}, u32[]{:S(2)}) %collective-permute-start.23) | collective-permute-done | bytes 196640 | tf_op jit(solution)/shard_map/ppermute | solution.py:269
  114.3 2.0 %shard_map.102.refs_6_ = f32[2,256,1536]{2,1,0:T(8,128)S(1)} custom-call(bf16[128,768]{1,0:T(8,128)(2,1)S(1)} %shard_map.99.refs_0_, bf16[128,768]{1,0:T(8,128)(2,1)S(1)} %collective-permute-done.23.refs_1_, bf16[3,384,256]{2,1,0:T(8,128)(2,1)S(1)} %copy-done.2, bf16[3,384,256]{2,1,0:T(8,128)(2,1)} %collective-permute-done.11.b_ref.refs_3_, ...), custom_call_target="tpu_custom_call" | custom-call | bytes 1024 | tf_op jit(solution)/shard_map/pallas_call | solution.py:192
  119.1 2.6 %collective-permute-start.26 = (bf16[128,384]{1,0:T(8,128)(2,1)S(1)}, bf16[128,384]{1,0:T(8,128)(2,1)S(1)}, u32[]{:S(2)}, u32[]{:S(2)}) collective-permute-start(bf16[128,384]{1,0:T(8,128)(2,1)S(1)} %get-tuple-element.120), channel_id=1, source_target_pairs={{0,16},{1,17},{2,18},{3,19},{4,20},{5,21},{6,22},{7,23},{8,24},{9,... | collective-permute-start | bytes 294920 | tf_op jit(solution)/shard_map/ppermute | solution.py:269
  121.7 8.0 %collective-permute-done.28.recv_ref = bf16[128,768]{1,0:T(8,128)(2,1)S(1)} collective-permute-done((bf16[128,768]{1,0:T(8,128)(2,1)S(1)}, bf16[128,768]{1,0:T(8,128)(2,1)S(1)}, u32[]{:S(2)}, u32[]{:S(2)}) %collective-permute-start.28) | collective-permute-done | bytes 196640 | tf_op jit(solution)/shard_map/ppermute | solution.py:269
  132.9 10.4 %collective-permute-done.29.refs_1_ = bf16[128,768]{1,0:T(8,128)(2,1)S(1)} collective-permute-done((bf16[128,768]{1,0:T(8,128)(2,1)S(1)}, bf16[128,768]{1,0:T(8,128)(2,1)S(1)}, u32[]{:S(2)}, u32[]{:S(2)}) %collective-permute-start.29) | collective-permute-done | bytes 196640 | tf_op jit(solution)/shard_map/ppermute | solution.py:269
  146.2 2.3 %collective-permute-done.30.recv_ref = bf16[4,2,2,16,1536]{4,3,2,1,0:T(8,128)(2,1)S(1)} collective-permute-done((bf16[4,2,2,16,1536]{4,3,2,1,0:T(8,128)(2,1)S(1)}, bf16[4,2,2,16,1536]{4,3,2,1,0:T(8,128)(2,1)S(1)}, u32[]{:S(2)}, u32[]{:S(2)}) %collective-permute-start.30) | collective-permute-done | bytes 786464 | tf_op jit(solution)/shard_map/ppermute | solution.py:269
  148.6 2.3 %collective-permute-start.31 = (bf16[2,2,16,1536]{3,2,1,0:T(8,128)(2,1)S(1)}, bf16[2,2,16,1536]{3,2,1,0:T(8,128)(2,1)S(1)}, u32[]{:S(2)}, u32[]{:S(2)}) collective-permute-start(bf16[2,2,16,1536]{3,2,1,0:T(8,128)(2,1)S(1)} %get-tuple-element.127), channel_id=1, source_target_pairs={{0,2},{1,3},{2,0},{3,1},{4,6},{5,7},{6,4},{7,5},{8,10},{9,11},{10,... | collective-permute-start | bytes 589832 | tf_op jit(solution)/shard_map/ppermute | solution.py:269
  152.5 3.7 %collective-permute-done.31.x_ref = bf16[2,2,16,1536]{3,2,1,0:T(8,128)(2,1)S(1)} collective-permute-done((bf16[2,2,16,1536]{3,2,1,0:T(8,128)(2,1)S(1)}, bf16[2,2,16,1536]{3,2,1,0:T(8,128)(2,1)S(1)}, u32[]{:S(2)}, u32[]{:S(2)}) %collective-permute-start.31) | collective-permute-done | bytes 196640 | tf_op jit(solution)/shard_map/ppermute | solution.py:269
  156.1 2.6 %collective-permute-done.32.zp_ref = bf16[2,2,16,1536]{3,2,1,0:T(8,128)(2,1)S(1)} collective-permute-done((bf16[2,2,16,1536]{3,2,1,0:T(8,128)(2,1)S(1)}, bf16[2,2,16,1536]{3,2,1,0:T(8,128)(2,1)S(1)}, u32[]{:S(2)}, u32[]{:S(2)}) %collective-permute-start.32) | collective-permute-done | bytes 196640 | tf_op jit(solution)/shard_map/ppermute | solution.py:269
  158.7 2.9 %collective-permute-done.33.both_ref = bf16[2,2,16,1536]{3,2,1,0:T(8,128)(2,1)S(1)} collective-permute-done((bf16[2,2,16,1536]{3,2,1,0:T(8,128)(2,1)S(1)}, bf16[2,2,16,1536]{3,2,1,0:T(8,128)(2,1)S(1)}, u32[]{:S(2)}, u32[]{:S(2)}) %collective-permute-start.33) | collective-permute-done | bytes 196640 | tf_op jit(solution)/shard_map/ppermute | solution.py:269
  162.2 6.6 %collective-permute-done.34.other_ref = bf16[2,16,1536]{2,1,0:T(8,128)(2,1)S(1)} collective-permute-done((bf16[2,16,1536]{2,1,0:T(8,128)(2,1)S(1)}, bf16[2,16,1536]{2,1,0:T(8,128)(2,1)S(1)}, u32[]{:S(2)}, u32[]{:S(2)}) %collective-permute-start.34) | collective-permute-done | bytes 98336 | tf_op jit(solution)/shard_map/ppermute | solution.py:269
  (100 shorter events, 48.1 us)
Async XLA Ops:
  2.7 11.1 %collective-permute-start = (bf16[3,384,128]{2,1,0:T(8,128)(2,1)}, bf16[3,384,128]{2,1,0:T(8,128)(2,1)}, u32[]{:S(2)}, u32[]{:S(2)}) collective-permute-start(bf16[3,384,128]{2,1,0:T(8,128)(2,1)} %get-tuple-element.68), channel_id=1, source_target_pairs={{0,8},{1,9},{2,10},{3,11},{4,12},{5,13},{6,14},{7,15},{8,0},{9,1},... | collective-permute-start | bytes 884744 | tf_op jit(solution)/shard_map/ppermute | solution.py:269
  5.7 10.2 %collective-permute-start.1 = (bf16[3,384,128]{2,1,0:T(8,128)(2,1)}, bf16[3,384,128]{2,1,0:T(8,128)(2,1)S(1)}, u32[]{:S(2)}, u32[]{:S(2)}) collective-permute-start(bf16[3,384,128]{2,1,0:T(8,128)(2,1)} %get-tuple-element.69.a_ref.refs_2_), channel_id=1, source_target_pairs={{0,4},{1,5},{2,6},{3,7},{4,0},{5,1},{6,2},{7,3},{8,12},{9,13},{10,... | collective-permute-start | bytes 884744 | tf_op jit(solution)/shard_map/ppermute | solution.py:269
  9.8 21.4 %collective-permute-start.6 = (bf16[3,384,256]{2,1,0:T(8,128)(2,1)}, bf16[3,384,256]{2,1,0:T(8,128)(2,1)S(1)}, u32[]{:S(2)}, u32[]{:S(2)}) collective-permute-start(bf16[3,384,256]{2,1,0:T(8,128)(2,1)} %get-tuple-element.74.a_ref.refs_2_), channel_id=1, source_target_pairs={{0,4},{1,5},{2,6},{3,7},{4,0},{5,1},{6,2},{7,3},{8,12},{9,13},{10,... | collective-permute-start | bytes 1769480 | tf_op jit(solution)/shard_map/ppermute | solution.py:269
  18.1 7.7 %collective-permute-start.3 = (bf16[2,2,16,1536]{3,2,1,0:T(8,128)(2,1)S(1)}, bf16[2,2,16,1536]{3,2,1,0:T(8,128)(2,1)S(1)}, u32[]{:S(2)}, u32[]{:S(2)}) collective-permute-start(bf16[2,2,16,1536]{3,2,1,0:T(8,128)(2,1)S(1)} %get-tuple-element.72), channel_id=1, source_target_pairs={{0,2},{1,3},{2,0},{3,1},{4,6},{5,7},{6,4},{7,5},{8,10},{9,11},{10,... | collective-permute-start | bytes 589832 | tf_op jit(solution)/shard_map/ppermute | solution.py:269
  19.6 7.8 %collective-permute-start.4 = (bf16[2,2,16,1536]{3,2,1,0:T(8,128)(2,1)S(1)}, bf16[2,2,16,1536]{3,2,1,0:T(8,128)(2,1)S(1)}, u32[]{:S(2)}, u32[]{:S(2)}) collective-permute-start(bf16[2,2,16,1536]{3,2,1,0:T(8,128)(2,1)S(1)} %get-tuple-element.73), channel_id=1, source_target_pairs={{0,8},{1,9},{2,10},{3,11},{4,12},{5,13},{6,14},{7,15},{8,0},{9,1},... | collective-permute-start | bytes 589832 | tf_op jit(solution)/shard_map/ppermute | solution.py:269
  19.6 11.5 %collective-permute-start.5 = (bf16[2,2,16,1536]{3,2,1,0:T(8,128)(2,1)S(1)}, bf16[2,2,16,1536]{3,2,1,0:T(8,128)(2,1)S(1)}, u32[]{:S(2)}, u32[]{:S(2)}) collective-permute-start(bf16[2,2,16,1536]{3,2,1,0:T(8,128)(2,1)S(1)} %get-tuple-element.73), channel_id=1, source_target_pairs={{0,10},{1,11},{2,8},{3,9},{4,14},{5,15},{6,12},{7,13},{8,2},{9,3},... | collective-permute-start | bytes 589832 | tf_op jit(solution)/shard_map/ppermute | solution.py:269
  24.1 20.2 %collective-permute-start.8 = (bf16[3,384,256]{2,1,0:T(8,128)(2,1)}, bf16[3,384,256]{2,1,0:T(8,128)(2,1)S(1)}, u32[]{:S(2)}, u32[]{:S(2)}) collective-permute-start(bf16[3,384,256]{2,1,0:T(8,128)(2,1)} %get-tuple-element.80), channel_id=1, source_target_pairs={{0,8},{1,9},{2,10},{3,11},{4,12},{5,13},{6,14},{7,15},{8,0},{9,1},... | collective-permute-start | bytes 1769480 | tf_op jit(solution)/shard_map/ppermute | solution.py:269
  31.2 24.4 %collective-permute-start.9 = (bf16[4,2,2,16,1536]{4,3,2,1,0:T(8,128)(2,1)S(1)}, bf16[4,2,2,16,1536]{4,3,2,1,0:T(8,128)(2,1)S(1)}, u32[]{:S(2)}, u32[]{:S(2)}) collective-permute-start(bf16[4,2,2,16,1536]{4,3,2,1,0:T(8,128)(2,1)S(1)} %pad_maximum_fusion.near_ref), channel_id=1, source_target_pairs={{0,1},{1,0},{2,3},{3,2},{4,5},{5,4},{6,7},{7,6},{8,9},{9,8},{10,11... | collective-permute-start | bytes 2359304 | tf_op jit(solution)/shard_map/ppermute | solution.py:269
  31.3 16.4 %collective-permute-start.7 = (bf16[3,384,256]{2,1,0:T(8,128)(2,1)}, bf16[3,384,256]{2,1,0:T(8,128)(2,1)S(1)}, u32[]{:S(2)}, u32[]{:S(2)}) collective-permute-start(bf16[3,384,256]{2,1,0:T(8,128)(2,1)} %get-tuple-element.77.a_ref.refs_2_), channel_id=1, source_target_pairs={{0,4},{1,5},{2,6},{3,7},{4,0},{5,1},{6,2},{7,3},{8,12},{9,13},{10,... | collective-permute-start | bytes 1769480 | tf_op jit(solution)/shard_map/ppermute | solution.py:269
  32.6 23.1 %collective-permute-start.11 = (bf16[3,384,256]{2,1,0:T(8,128)(2,1)}, bf16[3,384,256]{2,1,0:T(8,128)(2,1)}, u32[]{:S(2)}, u32[]{:S(2)}) collective-permute-start(bf16[3,384,256]{2,1,0:T(8,128)(2,1)} %get-tuple-element.88), channel_id=1, source_target_pairs={{0,8},{1,9},{2,10},{3,11},{4,12},{5,13},{6,14},{7,15},{8,0},{9,1},... | collective-permute-start | bytes 1769480 | tf_op jit(solution)/shard_map/ppermute | solution.py:269
  33.4 22.3 %collective-permute-start.10 = (bf16[3,384,128]{2,1,0:T(8,128)(2,1)}, bf16[3,384,128]{2,1,0:T(8,128)(2,1)}, u32[]{:S(2)}, u32[]{:S(2)}) collective-permute-start(bf16[3,384,128]{2,1,0:T(8,128)(2,1)} %collective-permute-done.b_ref.refs_3_), channel_id=1, source_target_pairs={{0,4},{1,5},{2,6},{3,7},{4,0},{5,1},{6,2},{7,3},{8,12},{9,13},{10,... | collective-permute-start | bytes 884744 | tf_op jit(solution)/shard_map/ppermute | solution.py:269
  47.7 19.1 %collective-permute-start.14 = (bf16[3,384,256]{2,1,0:T(8,128)(2,1)S(1)}, bf16[3,384,256]{2,1,0:T(8,128)(2,1)}, u32[]{:S(2)}, u32[]{:S(2)}) collective-permute-start(bf16[3,384,256]{2,1,0:T(8,128)(2,1)S(1)} %collective-permute-done.8.b_ref.refs_3_), channel_id=1, source_target_pairs={{0,4},{1,5},{2,6},{3,7},{4,0},{5,1},{6,2},{7,3},{8,12},{9,13},{10,... | collective-permute-start | bytes 1769480 | tf_op jit(solution)/shard_map/ppermute | solution.py:269
  48.9 21.4 %collective-permute-start.15 = (bf16[3,384,256]{2,1,0:T(8,128)(2,1)}, bf16[3,384,256]{2,1,0:T(8,128)(2,1)S(1)}, u32[]{:S(2)}, u32[]{:S(2)}) collective-permute-start(bf16[3,384,256]{2,1,0:T(8,128)(2,1)} %get-tuple-element.99), channel_id=1, source_target_pairs={{0,8},{1,9},{2,10},{3,11},{4,12},{5,13},{6,14},{7,15},{8,0},{9,1},... | collective-permute-start | bytes 1769480 | tf_op jit(solution)/shard_map/ppermute | solution.py:269
  59.5 19.8 %collective-permute-start.13 = (bf16[3,384,256]{2,1,0:T(8,128)(2,1)}, bf16[3,384,256]{2,1,0:T(8,128)(2,1)S(1)}, u32[]{:S(2)}, u32[]{:S(2)}) collective-permute-start(bf16[3,384,256]{2,1,0:T(8,128)(2,1)} %collective-permute-done.11.b_ref.refs_3_), channel_id=1, source_target_pairs={{0,4},{1,5},{2,6},{3,7},{4,0},{5,1},{6,2},{7,3},{8,12},{9,13},{10,... | collective-permute-start | bytes 1769480 | tf_op jit(solution)/shard_map/ppermute | solution.py:269
  61.1 20.2 %collective-permute-start.18 = (bf16[3,384,128]{2,1,0:T(8,128)(2,1)}, bf16[3,384,128]{2,1,0:T(8,128)(2,1)S(1)}, u32[]{:S(2)}, u32[]{:S(2)}) collective-permute-start(bf16[3,384,128]{2,1,0:T(8,128)(2,1)} %get-tuple-element.105), channel_id=1, source_target_pairs={{0,8},{1,9},{2,10},{3,11},{4,12},{5,13},{6,14},{7,15},{8,0},{9,1},... | collective-permute-start | bytes 884744 | tf_op jit(solution)/shard_map/ppermute | solution.py:269
  62.4 10.2 %collective-permute-start.12 = (bf16[128,384]{1,0:T(8,128)(2,1)S(1)}, bf16[128,384]{1,0:T(8,128)(2,1)S(1)}, u32[]{:S(2)}, u32[]{:S(2)}) collective-permute-start(bf16[128,384]{1,0:T(8,128)(2,1)S(1)} %get-tuple-element.91), channel_id=1, source_target_pairs={{0,16},{1,17},{2,18},{3,19},{4,20},{5,21},{6,22},{7,23},{8,24},{9,... | collective-permute-start | bytes 294920 | tf_op jit(solution)/shard_map/ppermute | solution.py:269
  70.3 38.2 %collective-permute-start.22 = (bf16[3,384,256]{2,1,0:T(8,128)(2,1)S(1)}, bf16[3,384,256]{2,1,0:T(8,128)(2,1)S(1)}, u32[]{:S(2)}, u32[]{:S(2)}) collective-permute-start(bf16[3,384,256]{2,1,0:T(8,128)(2,1)S(1)} %collective-permute-done.15.b_ref.refs_3_), channel_id=1, source_target_pairs={{0,4},{1,5},{2,6},{3,7},{4,0},{5,1},{6,2},{7,3},{8,12},{9,13},{10,... | collective-permute-start | bytes 1769480 | tf_op jit(solution)/shard_map/ppermute | solution.py:269
  71.9 36.6 %collective-permute-start.21 = (bf16[3,384,256]{2,1,0:T(8,128)(2,1)S(1)}, bf16[3,384,256]{2,1,0:T(8,128)(2,1)S(1)}, u32[]{:S(2)}, u32[]{:S(2)}) collective-permute-start(bf16[3,384,256]{2,1,0:T(8,128)(2,1)S(1)} %copy-done.1), channel_id=1, source_target_pairs={{0,4},{1,5},{2,6},{3,7},{4,0},{5,1},{6,2},{7,3},{8,12},{9,13},{10,... | collective-permute-start | bytes 1769480 | tf_op jit(solution)/shard_map/ppermute | solution.py:269
  72.7 11.7 %collective-permute-start.16 = (bf16[128,768]{1,0:T(8,128)(2,1)S(1)}, bf16[128,768]{1,0:T(8,128)(2,1)S(1)}, u32[]{:S(2)}, u32[]{:S(2)}) collective-permute-start(bf16[128,768]{1,0:T(8,128)(2,1)S(1)} %get-tuple-element.103), channel_id=1, source_target_pairs={{0,16},{1,17},{2,18},{3,19},{4,20},{5,21},{6,22},{7,23},{8,24},{9,... | collective-permute-start | bytes 589832 | tf_op jit(solution)/shard_map/ppermute | solution.py:269
  81.4 21.5 %collective-permute-start.19 = (bf16[128,768]{1,0:T(8,128)(2,1)S(1)}, bf16[128,768]{1,0:T(8,128)(2,1)S(1)}, u32[]{:S(2)}, u32[]{:S(2)}) collective-permute-start(bf16[128,768]{1,0:T(8,128)(2,1)S(1)} %get-tuple-element.109), channel_id=1, source_target_pairs={{0,16},{1,17},{2,18},{3,19},{4,20},{5,21},{6,22},{7,23},{8,24},{9,... | collective-permute-start | bytes 589832 | tf_op jit(solution)/shard_map/ppermute | solution.py:269
  83.3 17.8 %collective-permute-start.17 = (bf16[128,384]{1,0:T(8,128)(2,1)S(1)}, bf16[128,384]{1,0:T(8,128)(2,1)S(1)}, u32[]{:S(2)}, u32[]{:S(2)}) collective-permute-start(bf16[128,384]{1,0:T(8,128)(2,1)S(1)} %shard_map.94.refs_0_), channel_id=1, source_target_pairs={{0,16},{1,17},{2,18},{3,19},{4,20},{5,21},{6,22},{7,23},{8,24},{9,... | collective-permute-start | bytes 294920 | tf_op jit(solution)/shard_map/ppermute | solution.py:269
  84.5 20.7 %collective-permute-start.20 = (bf16[128,768]{1,0:T(8,128)(2,1)S(1)}, bf16[128,768]{1,0:T(8,128)(2,1)S(1)}, u32[]{:S(2)}, u32[]{:S(2)}) collective-permute-start(bf16[128,768]{1,0:T(8,128)(2,1)S(1)} %shard_map.97.refs_0_), channel_id=1, source_target_pairs={{0,16},{1,17},{2,18},{3,19},{4,20},{5,21},{6,22},{7,23},{8,24},{9,... | collective-permute-start | bytes 589832 | tf_op jit(solution)/shard_map/ppermute | solution.py:269
  103.0 11.3 %collective-permute-start.23 = (bf16[128,768]{1,0:T(8,128)(2,1)S(1)}, bf16[128,768]{1,0:T(8,128)(2,1)S(1)}, u32[]{:S(2)}, u32[]{:S(2)}) collective-permute-start(bf16[128,768]{1,0:T(8,128)(2,1)S(1)} %shard_map.99.refs_0_), channel_id=1, source_target_pairs={{0,16},{1,17},{2,18},{3,19},{4,20},{5,21},{6,22},{7,23},{8,24},{9,... | collective-permute-start | bytes 589832 | tf_op jit(solution)/shard_map/ppermute | solution.py:269
  103.1 13.4 %collective-permute-start.25 = (bf16[3,384,128]{2,1,0:T(8,128)(2,1)S(1)}, bf16[3,384,128]{2,1,0:T(8,128)(2,1)S(1)}, u32[]{:S(2)}, u32[]{:S(2)}) collective-permute-start(bf16[3,384,128]{2,1,0:T(8,128)(2,1)S(1)} %collective-permute-done.18.b_ref.refs_3_), channel_id=1, source_target_pairs={{0,4},{1,5},{2,6},{3,7},{4,0},{5,1},{6,2},{7,3},{8,12},{9,13},{10,... | collective-permute-start | bytes 884744 | tf_op jit(solution)/shard_map/ppermute | solution.py:269
  105.2 13.1 %collective-permute-start.24 = (bf16[3,384,128]{2,1,0:T(8,128)(2,1)S(1)}, bf16[3,384,128]{2,1,0:T(8,128)(2,1)S(1)}, u32[]{:S(2)}, u32[]{:S(2)}) collective-permute-start(bf16[3,384,128]{2,1,0:T(8,128)(2,1)S(1)} %copy-done.9), channel_id=1, source_target_pairs={{0,4},{1,5},{2,6},{3,7},{4,0},{5,1},{6,2},{7,3},{8,12},{9,13},{10,... | collective-permute-start | bytes 884744 | tf_op jit(solution)/shard_map/ppermute | solution.py:269
  116.4 13.3 %collective-permute-start.28 = (bf16[128,768]{1,0:T(8,128)(2,1)S(1)}, bf16[128,768]{1,0:T(8,128)(2,1)S(1)}, u32[]{:S(2)}, u32[]{:S(2)}) collective-permute-start(bf16[128,768]{1,0:T(8,128)(2,1)S(1)} %get-tuple-element.122), channel_id=1, source_target_pairs={{0,16},{1,17},{2,18},{3,19},{4,20},{5,21},{6,22},{7,23},{8,24},{9,... | collective-permute-start | bytes 589832 | tf_op jit(solution)/shard_map/ppermute | solution.py:269
  119.1 12.7 %collective-permute-start.26 = (bf16[128,384]{1,0:T(8,128)(2,1)S(1)}, bf16[128,384]{1,0:T(8,128)(2,1)S(1)}, u32[]{:S(2)}, u32[]{:S(2)}) collective-permute-start(bf16[128,384]{1,0:T(8,128)(2,1)S(1)} %get-tuple-element.120), channel_id=1, source_target_pairs={{0,16},{1,17},{2,18},{3,19},{4,20},{5,21},{6,22},{7,23},{8,24},{9,... | collective-permute-start | bytes 294920 | tf_op jit(solution)/shard_map/ppermute | solution.py:269
  129.8 13.5 %collective-permute-start.29 = (bf16[128,768]{1,0:T(8,128)(2,1)S(1)}, bf16[128,768]{1,0:T(8,128)(2,1)S(1)}, u32[]{:S(2)}, u32[]{:S(2)}) collective-permute-start(bf16[128,768]{1,0:T(8,128)(2,1)S(1)} %shard_map.105.refs_0_), channel_id=1, source_target_pairs={{0,16},{1,17},{2,18},{3,19},{4,20},{5,21},{6,22},{7,23},{8,24},{9,... | collective-permute-start | bytes 589832 | tf_op jit(solution)/shard_map/ppermute | solution.py:269
  131.8 13.6 %collective-permute-start.27 = (bf16[128,384]{1,0:T(8,128)(2,1)S(1)}, bf16[128,384]{1,0:T(8,128)(2,1)S(1)}, u32[]{:S(2)}, u32[]{:S(2)}) collective-permute-start(bf16[128,384]{1,0:T(8,128)(2,1)S(1)} %shard_map.104.refs_0_), channel_id=1, source_target_pairs={{0,16},{1,17},{2,18},{3,19},{4,20},{5,21},{6,22},{7,23},{8,24},{9,... | collective-permute-start | bytes 294920 | tf_op jit(solution)/shard_map/ppermute | solution.py:269
  148.6 7.5 %collective-permute-start.31 = (bf16[2,2,16,1536]{3,2,1,0:T(8,128)(2,1)S(1)}, bf16[2,2,16,1536]{3,2,1,0:T(8,128)(2,1)S(1)}, u32[]{:S(2)}, u32[]{:S(2)}) collective-permute-start(bf16[2,2,16,1536]{3,2,1,0:T(8,128)(2,1)S(1)} %get-tuple-element.127), channel_id=1, source_target_pairs={{0,2},{1,3},{2,0},{3,1},{4,6},{5,7},{6,4},{7,5},{8,10},{9,11},{10,... | collective-permute-start | bytes 589832 | tf_op jit(solution)/shard_map/ppermute | solution.py:269
  150.9 7.8 %collective-permute-start.32 = (bf16[2,2,16,1536]{3,2,1,0:T(8,128)(2,1)S(1)}, bf16[2,2,16,1536]{3,2,1,0:T(8,128)(2,1)S(1)}, u32[]{:S(2)}, u32[]{:S(2)}) collective-permute-start(bf16[2,2,16,1536]{3,2,1,0:T(8,128)(2,1)S(1)} %get-tuple-element.128), channel_id=1, source_target_pairs={{0,8},{1,9},{2,10},{3,11},{4,12},{5,13},{6,14},{7,15},{8,0},{9,1},... | collective-permute-start | bytes 589832 | tf_op jit(solution)/shard_map/ppermute | solution.py:269
  150.9 10.7 %collective-permute-start.33 = (bf16[2,2,16,1536]{3,2,1,0:T(8,128)(2,1)S(1)}, bf16[2,2,16,1536]{3,2,1,0:T(8,128)(2,1)S(1)}, u32[]{:S(2)}, u32[]{:S(2)}) collective-permute-start(bf16[2,2,16,1536]{3,2,1,0:T(8,128)(2,1)S(1)} %get-tuple-element.129), channel_id=1, source_target_pairs={{0,10},{1,11},{2,8},{3,9},{4,14},{5,15},{6,12},{7,13},{8,2},{9,3},... | collective-permute-start | bytes 589832 | tf_op jit(solution)/shard_map/ppermute | solution.py:269
  (20 other events, 264.8 us)

commit v5 on v4

--- a/solution.py
+++ b/solution.py
@@ -6,6 +6,8 @@
 from jax.sharding import PartitionSpec as P
 
 F32 = jnp.float32
+SHAPE = ((0, 1), (2, 2), (4, 2), (6, 2), (1, 1))
+CFG = {'us': [8, 0], 'flags': {'join_y0': True, 'join_zp0': True, 'own2_plain': True, 'near_y1': True, 'near_y2': False, 'near_y3': False, 'near_zp1': False, 'first_y2': True, 'first_zp1': True}, 'order': [('F', 0), ('F', 1), ('S', 0), ('F', 2), ('S', 1), ('F', 3), ('S', 2), ('F', 4), ('S', 3), ('S', 4)], 'ties': {('F', 1): [('F', 0)], ('F', 2): [('F', 1)], ('S', 0): [('F', 1)], ('F', 3): [('S', 0)], ('S', 1): [('F', 2)], ('F', 4): [('S', 1), ('F', 3)], ('S', 2): [('F', 3)], ('S', 3): [('F', 4)]}, 'y': {5: [('F', 0)], 6: [('F', 1)], 7: [('F', 1)], 8: [('F', 2)], 9: [('F', 2)]}, 'arrive': {}}
 BF16 = jnp.bfloat16
 LANES = 128
 AHEAD = 2
@@ -23,7 +25,7 @@
     blocks = units // LANES
     if blocks != 8:
         return [(i * LANES, LANES) for i in range(blocks)]
-    shape = ((0, 1), (2, 2), (4, 2), (6, 2), (1, 1))
+    shape = SHAPE
     return [(start * LANES, size * LANES) for start, size in shape]
 
 
@@ -187,14 +189,14 @@
     return per_device
 
 
-def call(body, outs, *args, scratch=(), flops=0):
+def call(body, outs, *args, scratch=(), flops=0, us=0):
     moved = sum(v.size * v.dtype.itemsize for v in list(args) + list(outs))
     return pl.pallas_call(
         body,
         out_shape=list(outs),
         scratch_shapes=list(scratch),
         compiler_params=pltpu.CompilerParams(vmem_limit_bytes=40 * 1024 * 1024),
-        cost_estimate=pl.CostEstimate(flops=0, bytes_accessed=1024, transcendentals=0),
+        cost_estimate=pl.CostEstimate(flops=us * 1000000000, bytes_accessed=1024, transcendentals=0),
     )(*args)
 
 
@@ -340,9 +342,13 @@
                 flipped_ref[j] = flip_pairs(values, own_width)
 
         pair = shaped((2,) + block_shape, BF16)
-        mine, zp_w[0], stream[0] = after(mine, zp_w[0], stream[0])
+        if CFG["flags"]["join_y0"]:
+            mine, stream[0] = after(mine, stream[0])
+        if CFG["flags"]["join_zp0"]:
+            mine, zp_w[0] = after(mine, zp_w[0])
         plain, flipped = call(join_body, [pair, pair], mine, other)
-        own_w[2], _ = after(own_w[2], plain)
+        if CFG["flags"]["own2_plain"]:
+            own_w[2], _ = after(own_w[2], plain)
         over_y(own_w[2])
         over_y(zp_w[0])
         for k in range(1, count):
@@ -354,9 +360,17 @@
         near_rows = jnp.stack(
             [plain, swap(plain, at_x), swap(flipped, at_zp), swap(flipped, at_zp + at_x)]
         )
-        near_rows, stream[1] = after(near_rows, stream[1])
+        for at in (1, 2, 3):
+            if CFG["flags"][f"near_y{at}"]:
+                near_rows, stream[at] = after(near_rows, stream[at])
+        if CFG["flags"]["near_zp1"]:
+            near_rows, zp_w[1] = after(near_rows, zp_w[1])
         far_rows = swap(near_rows, at_core)
-        near_rows, stream[2], zp_w[1] = after(near_rows, stream[2], zp_w[1])
+        for at in (2,):
+            if CFG["flags"]["first_y2"]:
+                near_rows, stream[at] = after(near_rows, stream[at])
+        if CFG["flags"]["first_zp1"]:
+            near_rows, zp_w[1] = after(near_rows, zp_w[1])
         over_y(zp_w[1])
 
         slots = 16 * most
@@ -376,34 +390,26 @@
                 for i, ref in enumerate((a_ref, b_ref, c_ref, d_ref)):
                     term = dot(left[:, i * own_width : (i + 1) * own_width], ref[j])
                     value = term if value is None else value + term
-                value = value.reshape(8, 2, most, units)
                 columns = slice(j * units, (j + 1) * units)
-                keep_ref[:, columns] = value[:, 0].reshape(own_slots, units)
-                send_ref[:, columns] = value[:, 1].reshape(own_slots, units).astype(BF16)
-
-        def middle_body(keep_ref, recv_ref, out_ref):
-            units = keep_ref.shape[1] // 3
+                keep_ref[:, columns] = value
+                value = value.astype(BF16).reshape(8, 2, most, units)
+                value = jnp.concatenate([value[:, 1:2], value[:, 0:1]], axis=1)
+                send_ref[:, columns] = value.reshape(slots, units)
+
+        def second_terms(keep_ref, recv_ref, refs):
+            units = refs[0].shape[2]
             pre = keep_ref[...] + recv_ref[...].astype(F32)
             gate, up, grad = pre[:, :units], pre[:, units : 2 * units], pre[:, 2 * units :]
             sig = 1.0 / (1.0 + jnp.exp(-gate))
-            out_ref[:, :units] = (gate * sig * up).astype(BF16)
-            out_ref[:, units : 2 * units] = (
-                grad * up * sig * (1.0 + gate * (1.0 - sig))
-            ).astype(BF16)
-            out_ref[:, 2 * units :] = (grad * gate * sig).astype(BF16)
-
-        def second_terms(mine_ref, recv_ref, refs):
-            units = refs[0].shape[2]
-            full = jnp.concatenate([mine_ref[...], recv_ref[...]], axis=0)
-            hidden, grad_gate, grad_up = (
-                full[:, j * units : (j + 1) * units] for j in range(3)
-            )
+            hidden = (gate * sig * up).astype(BF16)
+            grad_gate = (grad * up * sig * (1.0 + gate * (1.0 - sig))).astype(BF16)
+            grad_up = (grad * gate * sig).astype(BF16)
             outs = [dot_last(hidden, ref[2]) for ref in refs]
             grads = [dot_last(grad_gate, ref[0]) + dot_last(grad_up, ref[1]) for ref in refs]
             return outs, grads
 
-        def second_body(first, last, mine_ref, recv_ref, a_ref, b_ref, c_ref, d_ref, *rest):
-            terms = second_terms(mine_ref, recv_ref, (a_ref, b_ref, c_ref, d_ref))
+        def second_body(first, last, keep_ref, recv_ref, a_ref, b_ref, c_ref, d_ref, *rest):
+            terms = second_terms(keep_ref, recv_ref, (a_ref, b_ref, c_ref, d_ref))
             rest = list(rest)
             held = None if first else rest.pop(0)
             for which in range(2):
@@ -415,13 +421,13 @@
                     if not last:
                         rest[0][which, :, columns] = value
                         continue
-                    value = value.reshape(2, 2, 4, most, own_width)
+                    value = value.reshape(2, 4, 2, most, own_width)
                     for j in range(2):
-                        rest[0][:, j, which, :, columns] = value[j, 0]
-                        rest[1][:, j, which, :, columns] = value[j, 1].astype(BF16)
+                        rest[0][:, j, which, :, columns] = value[0, :, j]
+                        rest[1][:, j, which, :, columns] = value[1, :, j].astype(BF16)
 
         quad = (4, 2) + block_shape
-        pre, mine, total = [None] * count, [None] * count, [None] * count
+        pre, total = [None] * count, [None] * count
 
         def weights_of(k):
             at = (k, k + 3) if k < 3 else (2 * k, 2 * k + 1)
@@ -431,20 +437,11 @@
             units = chunks[k][1]
             pre[k] = call(
                 first_body,
-                [shaped((own_slots, 3 * units), F32), shaped((own_slots, 3 * units), BF16)],
+                [shaped((slots, 3 * units), F32), shaped((slots, 3 * units), BF16)],
                 near_rows,
                 far_rows,
                 *weights_of(k),
-            )
-
-        def middle(k):
-            units = chunks[k][1]
-            keep, sent = pre[k]
-            (mine[k],) = call(
-                middle_body,
-                [shaped((own_slots, 3 * units), BF16)],
-                keep,
-                swap(sent, at_zh),
+                us=CFG["us"][0] * units // 256,
             )
 
         def second(k):
@@ -455,59 +452,58 @@
                 else [shaped((2, slots, z_width), F32)]
             )
             held = () if is_first else total[k - 1]
+            keep, sent = pre[k]
             total[k] = call(
                 lambda *refs: second_body(is_first, is_last, *refs),
                 outs,
-                mine[k],
-                swap(mine[k], at_zh),
+                keep,
+                swap(sent, at_zh),
                 *weights_of(k),
                 *held,
-            )
-
-        def held_back(values, firsts=(), middles=(), seconds=()):
-            middles = [k for k in middles if k >= 0]
-            seconds = [k for k in seconds if k >= 0]
-            done = [pre[k][1] for k in firsts] + [mine[k] for k in middles]
-            done += [total[k][0] for k in seconds]
+                us=CFG["us"][1],
+            )
+
+        def held_back(values, firsts=(), seconds=()):
+            done = [pre[k][1] for k in firsts] + [total[k][0] for k in seconds]
+            if not done:
+                return values
             values, *done = after(values, *done)
             for k in firsts:
                 pre[k] = [pre[k][0], done.pop(0)]
-            for k in middles:
-                mine[k] = done.pop(0)
             for k in seconds:
                 total[k] = [done.pop(0)]
             return values
 
-        def own_over_y(k, *steps):
-            own_w[k] = held_back(own_w[k], *steps)
-            over_y(own_w[k])
-
-        def pair_over_y(k, *steps):
-            zp_w[k] = held_back(zp_w[k], *steps)
-            over_y(zp_w[k])
-
-        first(0, near_rows, far_rows)
-        pair_over_y(2, [0])
-        first(1, near_rows, far_rows)
-        own_over_y(3, [1])
-        pair_over_y(3, [1])
-        middle(0)
-        second(0)
-        first(2, held_back(near_rows, [], [0]), far_rows)
-        own_over_y(4, [2])
-        pair_over_y(4, [2])
-        middle(1)
-        second(1)
-        pre[2] = [held_back(pre[2][0], [], [1], [0]), pre[2][1]]
-        middle(2)
-        second(2)
-        first(3, held_back(near_rows, [], [2], [1]), far_rows)
-        first(4, held_back(near_rows, [3], [], [2]), far_rows)
-        pre[3] = [held_back(pre[3][0], [4]), pre[3][1]]
-        middle(3)
-        second(3)
-        middle(4)
-        second(4)
+        def steps_of(names):
+            return [[k for kind, k in names if kind == want] for want in "FS"]
+
+        def emit_y(j):
+            k = j // 2
+            values = zp_w if (j % 2 or k < 3) else own_w
+            k = j - 3 if j < 6 else k
+            values[k] = held_back(values[k], *steps_of(CFG["y"][j]))
+            over_y(values[k])
+
+        pending = [5, 6, 7, 8, 9]
+        done_ops = []
+        while pending and not CFG["y"][pending[0]]:
+            emit_y(pending.pop(0))
+        for kind, k in CFG["order"]:
+            ties = steps_of(CFG["ties"].get((kind, k), []))
+            late = CFG["arrive"].get((kind, k), [])
+            values = near_rows if kind == "F" else pre[k][0]
+            if any(ties):
+                values = held_back(values, *ties)
+            for at in late:
+                values, stream[at] = after(values, stream[at])
+            if kind == "F":
+                first(k, values, far_rows)
+            else:
+                pre[k] = [values, pre[k][1]]
+                second(k)
+            done_ops.append((kind, k))
+            while pending and all(op in done_ops for op in CFG["y"][pending[0]]):
+                emit_y(pending.pop(0))
         total = total[-1]
 
         def spread_body(keep_ref, recv_ref, own_ref, *outs):

time: 171 us -> 158 us (0.924)
  waiting for transfers between devices: 96 us -> 83 us
  Pallas kernels: 29.5 us -> 32.1 us
  starting transfers between devices: 41.4 us -> 38.8 us
    ppermute x35 -> x30, waiting for transfers between devices: 96 us -> 83 us  [swap(): return lax.ppermute(values, ('fsdp', 'et'), pairs)]
    ppermute x35 -> x30, starting transfers between devices: 41.4 us -> 38.8 us  [swap(): return lax.ppermute(values, ('fsdp', 'et'), pairs)]
    pallas_call x20 -> x15, Pallas kernels: 18 us -> 20.6 us  [call(): pl.pallas_call(body, out_shape=list(outs), scratch_shapes=list(scratch),...]
  transfers between devices with their start and end apart: 35 -> 30, of which waited for: 25 -> 18; matrix products, arithmetic and copies ran while one was open for 0% -> 1% of each run, Pallas kernels for 15% -> 17%
where the time goes in v5:
time: 158 us; the launch traced here: 157 us
  waiting for transfers between devices  83 us (53%)
  starting transfers between devices  38.8 us (25%)
  Pallas kernels  32.1 us (20%)
    ppermute x30, waiting for transfers between devices, swap(): return lax.ppermute(values, ('fsdp', 'et'), pairs)  83 us
    ppermute x30, starting transfers between devices, swap(): return lax.ppermute(values, ('fsdp', 'et'), pairs)  38.8 us
    pallas_call x15, Pallas kernels, call(): pl.pallas_call(body, out_shape=list(outs), scratch_shapes=list(scratch),...  20.6 us
    pallas_call x5, Pallas kernels, weight_chunk(): pl.pallas_call(weight_chunk_body, out_shape=[out, out], grid_spec=pltpu.P...  11.5 us
  transfers between devices with their start and end apart: 30, of which 18 were waited for; matrix products, arithmetic and copies ran while one was open for 1% of the time, Pallas kernels for 17%

profile of v5, /device:TPU:0, one launch (start us, length us, event | category | flops | bytes accessed | tf_op | source)
XLA Modules:
  0.0 157.4 jit_solution(2412387674883739811)
XLA Ops:
  0.7 2.1 %shard_map.87 = (bf16[3,384,128]{2,1,0:T(8,128)(2,1)}, bf16[3,384,128]{2,1,0:T(8,128)(2,1)}) custom-call(s32[1]{0:T(128)} %bitcast.low_ref, bf16[384,2048]{1,0:T(8,128)(2,1)} %refs_3_.9, bf16[384,2048]{1,0:T(8,128)(2,1)} %refs_4_.9, bf16[2048,384]{1,0:T(8,128)(2,1)} %refs_5_.9, bf16[384,2048]{1,0:T(8,128)(2,1)} %refs_3_.9, bf16[384,2048]{1,0:T(8,128)(2,1)} %refs_4_.9, ...), custom_call_target="tpu_custom_call" | custom-call | bytes 1024 | tf_op jit(solution)/shard_map/pallas_call | solution.py:253
  2.7 3.0 %collective-permute-start = (bf16[3,384,128]{2,1,0:T(8,128)(2,1)}, bf16[3,384,128]{2,1,0:T(8,128)(2,1)S(1)}, u32[]{:S(2)}, u32[]{:S(2)}) collective-permute-start(bf16[3,384,128]{2,1,0:T(8,128)(2,1)} %get-tuple-element.77.a_ref.refs_2_), channel_id=1, source_target_pairs={{0,4},{1,5},{2,6},{3,7},{4,0},{5,1},{6,2},{7,3},{8,12},{9,13},{10,... | collective-permute-start | bytes 884744 | tf_op jit(solution)/shard_map/ppermute | solution.py:271
  7.3 2.5 %shard_map.89 = (bf16[3,384,256]{2,1,0:T(8,128)(2,1)}, bf16[3,384,256]{2,1,0:T(8,128)(2,1)}) custom-call(s32[1]{0:T(128)} %bitcast.low_ref, bf16[384,2048]{1,0:T(8,128)(2,1)} %refs_3_.9, bf16[384,2048]{1,0:T(8,128)(2,1)} %refs_4_.9, bf16[2048,384]{1,0:T(8,128)(2,1)} %refs_5_.9, bf16[384,2048]{1,0:T(8,128)(2,1)} %refs_3_.9, bf16[384,2048]{1,0:T(8,128)(2,1)} %refs_4_.9, ...), custom_call_target="tpu_custom_call" | custom-call | bytes 1024 | tf_op jit(solution)/shard_map/pallas_call | solution.py:253
  11.1 2.7 %collective-permute-start.2 = (bf16[2,16,1536]{2,1,0:T(8,128)(2,1)S(1)}, bf16[2,16,1536]{2,1,0:T(8,128)(2,1)S(1)}, u32[]{:S(2)}, u32[]{:S(2)}) collective-permute-start(bf16[2,16,1536]{2,1,0:T(8,128)(2,1)S(1)} %get-tuple-element.81), channel_id=1, source_target_pairs={{0,16},{1,17},{2,18},{3,19},{4,20},{5,21},{6,22},{7,23},{8,24},{9,... | collective-permute-start | bytes 294920 | tf_op jit(solution)/shard_map/ppermute | solution.py:271
  15.5 1.9 %collective-permute-done.2.other_ref = bf16[2,16,1536]{2,1,0:T(8,128)(2,1)S(1)} collective-permute-done((bf16[2,16,1536]{2,1,0:T(8,128)(2,1)S(1)}, bf16[2,16,1536]{2,1,0:T(8,128)(2,1)S(1)}, u32[]{:S(2)}, u32[]{:S(2)}) %collective-permute-start.2) | collective-permute-done | bytes 98336 | tf_op jit(solution)/shard_map/ppermute | solution.py:271
  21.0 2.5 %shard_map.90 = (bf16[3,384,256]{2,1,0:T(8,128)(2,1)}, bf16[3,384,256]{2,1,0:T(8,128)(2,1)}) custom-call(s32[1]{0:T(128)} %bitcast.low_ref, bf16[384,2048]{1,0:T(8,128)(2,1)} %refs_3_.9, bf16[384,2048]{1,0:T(8,128)(2,1)} %refs_4_.9, bf16[2048,384]{1,0:T(8,128)(2,1)} %refs_5_.9, bf16[384,2048]{1,0:T(8,128)(2,1)} %refs_3_.9, bf16[384,2048]{1,0:T(8,128)(2,1)} %refs_4_.9, ...), custom_call_target="tpu_custom_call" | custom-call | bytes 1024 | tf_op jit(solution)/shard_map/pallas_call | solution.py:253
  23.5 2.1 %collective-permute-start.7 = (bf16[3,384,256]{2,1,0:T(8,128)(2,1)}, bf16[3,384,256]{2,1,0:T(8,128)(2,1)S(1)}, u32[]{:S(2)}, u32[]{:S(2)}) collective-permute-start(bf16[3,384,256]{2,1,0:T(8,128)(2,1)} %get-tuple-element.87.a_ref.refs_2_), channel_id=1, source_target_pairs={{0,4},{1,5},{2,6},{3,7},{4,0},{5,1},{6,2},{7,3},{8,12},{9,13},{10,... | collective-permute-start | bytes 1769480 | tf_op jit(solution)/shard_map/ppermute | solution.py:271
  27.1 3.9 %collective-permute-done.5 = bf16[2,2,16,1536]{3,2,1,0:T(8,128)(2,1)} collective-permute-done((bf16[2,2,16,1536]{3,2,1,0:T(8,128)(2,1)S(1)}, bf16[2,2,16,1536]{3,2,1,0:T(8,128)(2,1)}, u32[]{:S(2)}, u32[]{:S(2)}) %collective-permute-start.5) | collective-permute-done | bytes 196640 | tf_op jit(solution)/shard_map/ppermute | solution.py:271
  32.3 1.9 %collective-permute-start.12 = (bf16[3,384,256]{2,1,0:T(8,128)(2,1)}, bf16[3,384,256]{2,1,0:T(8,128)(2,1)}, u32[]{:S(2)}, u32[]{:S(2)}) collective-permute-start(bf16[3,384,256]{2,1,0:T(8,128)(2,1)} %get-tuple-element.101), channel_id=1, source_target_pairs={{0,8},{1,9},{2,10},{3,11},{4,12},{5,13},{6,14},{7,15},{8,0},{9,1},... | collective-permute-start | bytes 1769480 | tf_op jit(solution)/shard_map/ppermute | solution.py:271
  34.2 2.5 %shard_map.91 = (bf16[3,384,256]{2,1,0:T(8,128)(2,1)}, bf16[3,384,256]{2,1,0:T(8,128)(2,1)}) custom-call(s32[1]{0:T(128)} %bitcast.low_ref, bf16[384,2048]{1,0:T(8,128)(2,1)} %refs_3_.9, bf16[384,2048]{1,0:T(8,128)(2,1)} %refs_4_.9, bf16[2048,384]{1,0:T(8,128)(2,1)} %refs_5_.9, bf16[384,2048]{1,0:T(8,128)(2,1)} %refs_3_.9, bf16[384,2048]{1,0:T(8,128)(2,1)} %refs_4_.9, ...), custom_call_target="tpu_custom_call" | custom-call | bytes 1024 | tf_op jit(solution)/shard_map/pallas_call | solution.py:253
  36.7 3.0 %collective-permute-done.7.c_ref.refs_4_ = bf16[3,384,256]{2,1,0:T(8,128)(2,1)S(1)} collective-permute-done((bf16[3,384,256]{2,1,0:T(8,128)(2,1)}, bf16[3,384,256]{2,1,0:T(8,128)(2,1)S(1)}, u32[]{:S(2)}, u32[]{:S(2)}) %collective-permute-start.7) | collective-permute-done | bytes 589856 | tf_op jit(solution)/shard_map/ppermute | solution.py:271
  39.6 4.0 %collective-permute-done.8.b_ref.refs_3_ = bf16[3,384,256]{2,1,0:T(8,128)(2,1)S(1)} collective-permute-done((bf16[3,384,256]{2,1,0:T(8,128)(2,1)}, bf16[3,384,256]{2,1,0:T(8,128)(2,1)S(1)}, u32[]{:S(2)}, u32[]{:S(2)}) %collective-permute-start.8) | collective-permute-done | bytes 589856 | tf_op jit(solution)/shard_map/ppermute | solution.py:271
  45.3 2.1 %shard_map.93 = (bf16[3,384,128]{2,1,0:T(8,128)(2,1)}, bf16[3,384,128]{2,1,0:T(8,128)(2,1)}) custom-call(s32[1]{0:T(128)} %bitcast.low_ref, bf16[384,2048]{1,0:T(8,128)(2,1)} %refs_3_.9, bf16[384,2048]{1,0:T(8,128)(2,1)} %refs_4_.9, bf16[2048,384]{1,0:T(8,128)(2,1)} %refs_5_.9, bf16[384,2048]{1,0:T(8,128)(2,1)} %refs_3_.9, bf16[384,2048]{1,0:T(8,128)(2,1)} %refs_4_.9, ...), custom_call_target="tpu_custom_call" | custom-call | bytes 1024 | tf_op jit(solution)/shard_map/pallas_call | solution.py:253
  47.3 6.1 %collective-permute-done.12.b_ref.refs_3_ = bf16[3,384,256]{2,1,0:T(8,128)(2,1)} collective-permute-done((bf16[3,384,256]{2,1,0:T(8,128)(2,1)}, bf16[3,384,256]{2,1,0:T(8,128)(2,1)}, u32[]{:S(2)}, u32[]{:S(2)}) %collective-permute-start.12) | collective-permute-done | bytes 589856 | tf_op jit(solution)/shard_map/ppermute | solution.py:271
  56.5 2.0 %shard_map.92 = (f32[256,384]{1,0:T(8,128)S(1)}, bf16[256,384]{1,0:T(8,128)(2,1)S(1)}) custom-call(bf16[4,2,2,16,1536]{4,3,2,1,0:T(8,128)(2,1)S(1)} %pad_maximum_fusion.near_ref, bf16[4,2,2,16,1536]{4,3,2,1,0:T(8,128)(2,1)} %collective-permute-done.9.far_ref, bf16[3,384,128]{2,1,0:T(8,128)(2,1)S(1)} %copy-done.7, ...), custom_call_target="tpu_custom_call" | custom-call | flops 4000000000 | bytes 1024 | tf_op jit(solution)/shard_map/pallas_call | solution.py:194
  61.8 2.3 %shard_map.94 = (f32[256,768]{1,0:T(8,128)S(1)}, bf16[256,768]{1,0:T(8,128)(2,1)S(1)}) custom-call(bf16[4,2,2,16,1536]{4,3,2,1,0:T(8,128)(2,1)S(1)} %pad_maximum_fusion.near_ref, bf16[4,2,2,16,1536]{4,3,2,1,0:T(8,128)(2,1)} %collective-permute-done.9.far_ref, bf16[3,384,256]{2,1,0:T(8,128)(2,1)S(1)} %copy-done.2, ...), custom_call_target="tpu_custom_call" | custom-call | flops 8000000000 | bytes 1024 | tf_op jit(solution)/shard_map/pallas_call | solution.py:194
  64.1 13.5 %collective-permute-done.11.b_ref.refs_3_ = bf16[3,384,256]{2,1,0:T(8,128)(2,1)S(1)} collective-permute-done((bf16[3,384,256]{2,1,0:T(8,128)(2,1)}, bf16[3,384,256]{2,1,0:T(8,128)(2,1)S(1)}, u32[]{:S(2)}, u32[]{:S(2)}) %collective-permute-start.11) | collective-permute-done | bytes 589856 | tf_op jit(solution)/shard_map/ppermute | solution.py:271
  82.1 2.3 %shard_map.95 = (f32[256,768]{1,0:T(8,128)S(1)}, bf16[256,768]{1,0:T(8,128)(2,1)S(1)}) custom-call(bf16[4,2,2,16,1536]{4,3,2,1,0:T(8,128)(2,1)S(1)} %pad_maximum_fusion.near_ref, bf16[4,2,2,16,1536]{4,3,2,1,0:T(8,128)(2,1)} %collective-permute-done.9.far_ref, bf16[3,384,256]{2,1,0:T(8,128)(2,1)S(1)} %copy-done.3, ...), custom_call_target="tpu_custom_call" | custom-call | flops 8000000000 | bytes 1024 | tf_op jit(solution)/shard_map/pallas_call | solution.py:194
  84.5 3.5 %collective-permute-start.24 = (bf16[256,768]{1,0:T(8,128)(2,1)S(1)}, bf16[256,768]{1,0:T(8,128)(2,1)S(1)}, u32[]{:S(2)}, u32[]{:S(2)}) collective-permute-start(bf16[256,768]{1,0:T(8,128)(2,1)S(1)} %get-tuple-element.141), channel_id=1, source_target_pairs={{0,16},{1,17},{2,18},{3,19},{4,20},{5,21},{6,22},{7,23},{8,24},{9,... | collective-permute-start | bytes 1179656 | tf_op jit(solution)/shard_map/ppermute | solution.py:271
  89.4 14.1 %collective-permute-done.19.refs_1_ = bf16[256,768]{1,0:T(8,128)(2,1)S(1)} collective-permute-done((bf16[256,768]{1,0:T(8,128)(2,1)S(1)}, bf16[256,768]{1,0:T(8,128)(2,1)S(1)}, u32[]{:S(2)}, u32[]{:S(2)}) %collective-permute-start.19) | collective-permute-done | bytes 393248 | tf_op jit(solution)/shard_map/ppermute | solution.py:271
  104.5 2.1 %shard_map.98.refs_6_ = f32[2,256,1536]{2,1,0:T(8,128)S(1)} custom-call(f32[256,768]{1,0:T(8,128)S(1)} %get-tuple-element.129.refs_0_, bf16[256,768]{1,0:T(8,128)(2,1)S(1)} %collective-permute-done.19.refs_1_, bf16[3,384,256]{2,1,0:T(8,128)(2,1)S(1)} %copy-done.2, bf16[3,384,256]{2,1,0:T(8,128)(2,1)S(1)} %copy-done.6, ...), custom_call_target="tpu_custom_call" | custom-call | bytes 1024 | tf_op jit(solution)/shard_map/pallas_call | solution.py:194
  106.6 2.1 %shard_map.97 = (f32[256,768]{1,0:T(8,128)S(1)}, bf16[256,768]{1,0:T(8,128)(2,1)S(1)}) custom-call(bf16[4,2,2,16,1536]{4,3,2,1,0:T(8,128)(2,1)S(1)} %pad_maximum_fusion.near_ref, bf16[4,2,2,16,1536]{4,3,2,1,0:T(8,128)(2,1)} %collective-permute-done.9.far_ref, bf16[3,384,256]{2,1,0:T(8,128)(2,1)S(1)} %copy-done.4, ...), custom_call_target="tpu_custom_call" | custom-call | flops 8000000000 | bytes 1024 | tf_op jit(solution)/shard_map/pallas_call | solution.py:194
  110.2 1.9 %shard_map.99 = (f32[256,384]{1,0:T(8,128)S(1)}, bf16[256,384]{1,0:T(8,128)(2,1)S(1)}) custom-call(bf16[4,2,2,16,1536]{4,3,2,1,0:T(8,128)(2,1)S(1)} %pad_maximum_fusion.near_ref, bf16[4,2,2,16,1536]{4,3,2,1,0:T(8,128)(2,1)} %collective-permute-done.9.far_ref, bf16[3,384,128]{2,1,0:T(8,128)(2,1)S(1)} %copy-done.11, ...), custom_call_target="tpu_custom_call" | custom-call | flops 4000000000 | bytes 1024 | tf_op jit(solution)/shard_map/pallas_call | solution.py:194
  113.6 4.6 %collective-permute-done.24.refs_1_ = bf16[256,768]{1,0:T(8,128)(2,1)S(1)} collective-permute-done((bf16[256,768]{1,0:T(8,128)(2,1)S(1)}, bf16[256,768]{1,0:T(8,128)(2,1)S(1)}, u32[]{:S(2)}, u32[]{:S(2)}) %collective-permute-start.24) | collective-permute-done | bytes 393248 | tf_op jit(solution)/shard_map/ppermute | solution.py:271
  118.3 2.1 %shard_map.100.refs_6_ = f32[2,256,1536]{2,1,0:T(8,128)S(1)} custom-call(f32[256,768]{1,0:T(8,128)S(1)} %get-tuple-element.140.refs_0_, bf16[256,768]{1,0:T(8,128)(2,1)S(1)} %collective-permute-done.24.refs_1_, bf16[3,384,256]{2,1,0:T(8,128)(2,1)S(1)} %copy-done.3, bf16[3,384,256]{2,1,0:T(8,128)(2,1)} %collective-permute-done.12.b_ref.refs_3_, ...), custom_call_target="tpu_custom_call" | custom-call | bytes 1024 | tf_op jit(solution)/shard_map/pallas_call | solution.py:194
  120.4 10.5 %collective-permute-done.23.refs_1_ = bf16[256,768]{1,0:T(8,128)(2,1)S(1)} collective-permute-done((bf16[256,768]{1,0:T(8,128)(2,1)S(1)}, bf16[256,768]{1,0:T(8,128)(2,1)S(1)}, u32[]{:S(2)}, u32[]{:S(2)}) %collective-permute-start.23) | collective-permute-done | bytes 393248 | tf_op jit(solution)/shard_map/ppermute | solution.py:271
  133.8 2.3 %collective-permute-done.25.recv_ref = bf16[4,2,2,16,1536]{4,3,2,1,0:T(8,128)(2,1)S(1)} collective-permute-done((bf16[4,2,2,16,1536]{4,3,2,1,0:T(8,128)(2,1)S(1)}, bf16[4,2,2,16,1536]{4,3,2,1,0:T(8,128)(2,1)S(1)}, u32[]{:S(2)}, u32[]{:S(2)}) %collective-permute-start.25) | collective-permute-done | bytes 786464 | tf_op jit(solution)/shard_map/ppermute | solution.py:271
  136.2 1.9 %collective-permute-start.26 = (bf16[2,2,16,1536]{3,2,1,0:T(8,128)(2,1)S(1)}, bf16[2,2,16,1536]{3,2,1,0:T(8,128)(2,1)S(1)}, u32[]{:S(2)}, u32[]{:S(2)}) collective-permute-start(bf16[2,2,16,1536]{3,2,1,0:T(8,128)(2,1)S(1)} %get-tuple-element.145), channel_id=1, source_target_pairs={{0,2},{1,3},{2,0},{3,1},{4,6},{5,7},{6,4},{7,5},{8,10},{9,11},{10,... | collective-permute-start | bytes 589832 | tf_op jit(solution)/shard_map/ppermute | solution.py:271
  139.7 3.5 %collective-permute-done.26.x_ref = bf16[2,2,16,1536]{3,2,1,0:T(8,128)(2,1)S(1)} collective-permute-done((bf16[2,2,16,1536]{3,2,1,0:T(8,128)(2,1)S(1)}, bf16[2,2,16,1536]{3,2,1,0:T(8,128)(2,1)S(1)}, u32[]{:S(2)}, u32[]{:S(2)}) %collective-permute-start.26) | collective-permute-done | bytes 196640 | tf_op jit(solution)/shard_map/ppermute | solution.py:271
  143.3 2.6 %collective-permute-done.27.zp_ref = bf16[2,2,16,1536]{3,2,1,0:T(8,128)(2,1)S(1)} collective-permute-done((bf16[2,2,16,1536]{3,2,1,0:T(8,128)(2,1)S(1)}, bf16[2,2,16,1536]{3,2,1,0:T(8,128)(2,1)S(1)}, u32[]{:S(2)}, u32[]{:S(2)}) %collective-permute-start.27) | collective-permute-done | bytes 196640 | tf_op jit(solution)/shard_map/ppermute | solution.py:271
  145.8 2.9 %collective-permute-done.28.both_ref = bf16[2,2,16,1536]{3,2,1,0:T(8,128)(2,1)S(1)} collective-permute-done((bf16[2,2,16,1536]{3,2,1,0:T(8,128)(2,1)S(1)}, bf16[2,2,16,1536]{3,2,1,0:T(8,128)(2,1)S(1)}, u32[]{:S(2)}, u32[]{:S(2)}) %collective-permute-start.28) | collective-permute-done | bytes 196640 | tf_op jit(solution)/shard_map/ppermute | solution.py:271
  150.5 5.2 %collective-permute-done.29.other_ref = bf16[2,16,1536]{2,1,0:T(8,128)(2,1)S(1)} collective-permute-done((bf16[2,16,1536]{2,1,0:T(8,128)(2,1)S(1)}, bf16[2,16,1536]{2,1,0:T(8,128)(2,1)S(1)}, u32[]{:S(2)}, u32[]{:S(2)}) %collective-permute-start.29) | collective-permute-done | bytes 98336 | tf_op jit(solution)/shard_map/ppermute | solution.py:271
  (79 shorter events, 37.2 us)
Async XLA Ops:
  2.7 11.0 %collective-permute-start = (bf16[3,384,128]{2,1,0:T(8,128)(2,1)}, bf16[3,384,128]{2,1,0:T(8,128)(2,1)S(1)}, u32[]{:S(2)}, u32[]{:S(2)}) collective-permute-start(bf16[3,384,128]{2,1,0:T(8,128)(2,1)} %get-tuple-element.77.a_ref.refs_2_), channel_id=1, source_target_pairs={{0,4},{1,5},{2,6},{3,7},{4,0},{5,1},{6,2},{7,3},{8,12},{9,13},{10,... | collective-permute-start | bytes 884744 | tf_op jit(solution)/shard_map/ppermute | solution.py:271
  5.7 9.8 %collective-permute-start.1 = (bf16[3,384,128]{2,1,0:T(8,128)(2,1)}, bf16[3,384,128]{2,1,0:T(8,128)(2,1)S(1)}, u32[]{:S(2)}, u32[]{:S(2)}) collective-permute-start(bf16[3,384,128]{2,1,0:T(8,128)(2,1)} %get-tuple-element.79), channel_id=1, source_target_pairs={{0,8},{1,9},{2,10},{3,11},{4,12},{5,13},{6,14},{7,15},{8,0},{9,1},... | collective-permute-start | bytes 884744 | tf_op jit(solution)/shard_map/ppermute | solution.py:271
  9.8 22.4 %collective-permute-start.6 = (bf16[3,384,256]{2,1,0:T(8,128)(2,1)}, bf16[3,384,256]{2,1,0:T(8,128)(2,1)S(1)}, u32[]{:S(2)}, u32[]{:S(2)}) collective-permute-start(bf16[3,384,256]{2,1,0:T(8,128)(2,1)} %get-tuple-element.84.a_ref.refs_2_), channel_id=1, source_target_pairs={{0,4},{1,5},{2,6},{3,7},{4,0},{5,1},{6,2},{7,3},{8,12},{9,13},{10,... | collective-permute-start | bytes 1769480 | tf_op jit(solution)/shard_map/ppermute | solution.py:271
  11.1 6.3 %collective-permute-start.2 = (bf16[2,16,1536]{2,1,0:T(8,128)(2,1)S(1)}, bf16[2,16,1536]{2,1,0:T(8,128)(2,1)S(1)}, u32[]{:S(2)}, u32[]{:S(2)}) collective-permute-start(bf16[2,16,1536]{2,1,0:T(8,128)(2,1)S(1)} %get-tuple-element.81), channel_id=1, source_target_pairs={{0,16},{1,17},{2,18},{3,19},{4,20},{5,21},{6,22},{7,23},{8,24},{9,... | collective-permute-start | bytes 294920 | tf_op jit(solution)/shard_map/ppermute | solution.py:271
  17.4 8.1 %collective-permute-start.3 = (bf16[2,2,16,1536]{3,2,1,0:T(8,128)(2,1)S(1)}, bf16[2,2,16,1536]{3,2,1,0:T(8,128)(2,1)}, u32[]{:S(2)}, u32[]{:S(2)}) collective-permute-start(bf16[2,2,16,1536]{3,2,1,0:T(8,128)(2,1)S(1)} %get-tuple-element.82), channel_id=1, source_target_pairs={{0,2},{1,3},{2,0},{3,1},{4,6},{5,7},{6,4},{7,5},{8,10},{9,11},{10,... | collective-permute-start | bytes 589832 | tf_op jit(solution)/shard_map/ppermute | solution.py:271
  19.0 8.1 %collective-permute-start.4 = (bf16[2,2,16,1536]{3,2,1,0:T(8,128)(2,1)S(1)}, bf16[2,2,16,1536]{3,2,1,0:T(8,128)(2,1)}, u32[]{:S(2)}, u32[]{:S(2)}) collective-permute-start(bf16[2,2,16,1536]{3,2,1,0:T(8,128)(2,1)S(1)} %get-tuple-element.83), channel_id=1, source_target_pairs={{0,8},{1,9},{2,10},{3,11},{4,12},{5,13},{6,14},{7,15},{8,0},{9,1},... | collective-permute-start | bytes 589832 | tf_op jit(solution)/shard_map/ppermute | solution.py:271
  20.7 10.3 %collective-permute-start.5 = (bf16[2,2,16,1536]{3,2,1,0:T(8,128)(2,1)S(1)}, bf16[2,2,16,1536]{3,2,1,0:T(8,128)(2,1)}, u32[]{:S(2)}, u32[]{:S(2)}) collective-permute-start(bf16[2,2,16,1536]{3,2,1,0:T(8,128)(2,1)S(1)} %get-tuple-element.83), channel_id=1, source_target_pairs={{0,10},{1,11},{2,8},{3,9},{4,14},{5,15},{6,12},{7,13},{8,2},{9,3},... | collective-permute-start | bytes 589832 | tf_op jit(solution)/shard_map/ppermute | solution.py:271
  23.5 16.2 %collective-permute-start.7 = (bf16[3,384,256]{2,1,0:T(8,128)(2,1)}, bf16[3,384,256]{2,1,0:T(8,128)(2,1)S(1)}, u32[]{:S(2)}, u32[]{:S(2)}) collective-permute-start(bf16[3,384,256]{2,1,0:T(8,128)(2,1)} %get-tuple-element.87.a_ref.refs_2_), channel_id=1, source_target_pairs={{0,4},{1,5},{2,6},{3,7},{4,0},{5,1},{6,2},{7,3},{8,12},{9,13},{10,... | collective-permute-start | bytes 1769480 | tf_op jit(solution)/shard_map/ppermute | solution.py:271
  25.6 18.1 %collective-permute-start.8 = (bf16[3,384,256]{2,1,0:T(8,128)(2,1)}, bf16[3,384,256]{2,1,0:T(8,128)(2,1)S(1)}, u32[]{:S(2)}, u32[]{:S(2)}) collective-permute-start(bf16[3,384,256]{2,1,0:T(8,128)(2,1)} %get-tuple-element.91), channel_id=1, source_target_pairs={{0,8},{1,9},{2,10},{3,11},{4,12},{5,13},{6,14},{7,15},{8,0},{9,1},... | collective-permute-start | bytes 1769480 | tf_op jit(solution)/shard_map/ppermute | solution.py:271
  32.2 23.3 %collective-permute-start.9 = (bf16[4,2,2,16,1536]{4,3,2,1,0:T(8,128)(2,1)S(1)}, bf16[4,2,2,16,1536]{4,3,2,1,0:T(8,128)(2,1)}, u32[]{:S(2)}, u32[]{:S(2)}) collective-permute-start(bf16[4,2,2,16,1536]{4,3,2,1,0:T(8,128)(2,1)S(1)} %pad_maximum_fusion.near_ref), channel_id=1, source_target_pairs={{0,1},{1,0},{2,3},{3,2},{4,5},{5,4},{6,7},{7,6},{8,9},{9,8},{10,11... | collective-permute-start | bytes 2359304 | tf_op jit(solution)/shard_map/ppermute | solution.py:271
  32.3 21.1 %collective-permute-start.12 = (bf16[3,384,256]{2,1,0:T(8,128)(2,1)}, bf16[3,384,256]{2,1,0:T(8,128)(2,1)}, u32[]{:S(2)}, u32[]{:S(2)}) collective-permute-start(bf16[3,384,256]{2,1,0:T(8,128)(2,1)} %get-tuple-element.101), channel_id=1, source_target_pairs={{0,8},{1,9},{2,10},{3,11},{4,12},{5,13},{6,14},{7,15},{8,0},{9,1},... | collective-permute-start | bytes 1769480 | tf_op jit(solution)/shard_map/ppermute | solution.py:271
  34.2 21.3 %collective-permute-start.10 = (bf16[3,384,128]{2,1,0:T(8,128)(2,1)S(1)}, bf16[3,384,128]{2,1,0:T(8,128)(2,1)}, u32[]{:S(2)}, u32[]{:S(2)}) collective-permute-start(bf16[3,384,128]{2,1,0:T(8,128)(2,1)S(1)} %collective-permute-done.1.b_ref.refs_3_), channel_id=1, source_target_pairs={{0,4},{1,5},{2,6},{3,7},{4,0},{5,1},{6,2},{7,3},{8,12},{9,13},{10,... | collective-permute-start | bytes 884744 | tf_op jit(solution)/shard_map/ppermute | solution.py:271
  43.7 18.1 %collective-permute-start.13 = (bf16[3,384,256]{2,1,0:T(8,128)(2,1)S(1)}, bf16[3,384,256]{2,1,0:T(8,128)(2,1)}, u32[]{:S(2)}, u32[]{:S(2)}) collective-permute-start(bf16[3,384,256]{2,1,0:T(8,128)(2,1)S(1)} %collective-permute-done.8.b_ref.refs_3_), channel_id=1, source_target_pairs={{0,4},{1,5},{2,6},{3,7},{4,0},{5,1},{6,2},{7,3},{8,12},{9,13},{10,... | collective-permute-start | bytes 1769480 | tf_op jit(solution)/shard_map/ppermute | solution.py:271
  53.5 24.2 %collective-permute-start.11 = (bf16[3,384,256]{2,1,0:T(8,128)(2,1)}, bf16[3,384,256]{2,1,0:T(8,128)(2,1)S(1)}, u32[]{:S(2)}, u32[]{:S(2)}) collective-permute-start(bf16[3,384,256]{2,1,0:T(8,128)(2,1)} %get-tuple-element.97), channel_id=1, source_target_pairs={{0,8},{1,9},{2,10},{3,11},{4,12},{5,13},{6,14},{7,15},{8,0},{9,1},... | collective-permute-start | bytes 1769480 | tf_op jit(solution)/shard_map/ppermute | solution.py:271
  55.2 29.3 %collective-permute-start.18 = (bf16[3,384,128]{2,1,0:T(8,128)(2,1)}, bf16[3,384,128]{2,1,0:T(8,128)(2,1)S(1)}, u32[]{:S(2)}, u32[]{:S(2)}) collective-permute-start(bf16[3,384,128]{2,1,0:T(8,128)(2,1)} %get-tuple-element.124), channel_id=1, source_target_pairs={{0,8},{1,9},{2,10},{3,11},{4,12},{5,13},{6,14},{7,15},{8,0},{9,1},... | collective-permute-start | bytes 884744 | tf_op jit(solution)/shard_map/ppermute | solution.py:271
  58.4 21.9 %copy-start.10 = (bf16[3,384,128]{2,1,0:T(8,128)(2,1)S(1)}, bf16[3,384,128]{2,1,0:T(8,128)(2,1)}, u32[]{:S(2)}) copy-start(bf16[3,384,128]{2,1,0:T(8,128)(2,1)} %copy-done.8) | copy-start | bytes 884740
  58.5 23.6 %collective-permute-start.14 = (bf16[3,384,256]{2,1,0:T(8,128)(2,1)}, bf16[3,384,256]{2,1,0:T(8,128)(2,1)S(1)}, u32[]{:S(2)}, u32[]{:S(2)}) collective-permute-start(bf16[3,384,256]{2,1,0:T(8,128)(2,1)} %collective-permute-done.12.b_ref.refs_3_), channel_id=1, source_target_pairs={{0,4},{1,5},{2,6},{3,7},{4,0},{5,1},{6,2},{7,3},{8,12},{9,13},{10,... | collective-permute-start | bytes 1769480 | tf_op jit(solution)/shard_map/ppermute | solution.py:271
  60.0 19.8 %collective-permute-start.15 = (bf16[256,384]{1,0:T(8,128)(2,1)S(1)}, bf16[256,384]{1,0:T(8,128)(2,1)S(1)}, u32[]{:S(2)}, u32[]{:S(2)}) collective-permute-start(bf16[256,384]{1,0:T(8,128)(2,1)S(1)} %get-tuple-element.117), channel_id=1, source_target_pairs={{0,16},{1,17},{2,18},{3,19},{4,20},{5,21},{6,22},{7,23},{8,24},{9,... | collective-permute-start | bytes 589832 | tf_op jit(solution)/shard_map/ppermute | solution.py:271
  77.6 25.9 %collective-permute-start.19 = (bf16[256,768]{1,0:T(8,128)(2,1)S(1)}, bf16[256,768]{1,0:T(8,128)(2,1)S(1)}, u32[]{:S(2)}, u32[]{:S(2)}) collective-permute-start(bf16[256,768]{1,0:T(8,128)(2,1)S(1)} %get-tuple-element.130), channel_id=1, source_target_pairs={{0,16},{1,17},{2,18},{3,19},{4,20},{5,21},{6,22},{7,23},{8,24},{9,... | collective-permute-start | bytes 1179656 | tf_op jit(solution)/shard_map/ppermute | solution.py:271
  77.6 28.9 %collective-permute-start.17 = (bf16[3,384,256]{2,1,0:T(8,128)(2,1)S(1)}, bf16[3,384,256]{2,1,0:T(8,128)(2,1)S(1)}, u32[]{:S(2)}, u32[]{:S(2)}) collective-permute-start(bf16[3,384,256]{2,1,0:T(8,128)(2,1)S(1)} %collective-permute-done.11.b_ref.refs_3_), channel_id=1, source_target_pairs={{0,4},{1,5},{2,6},{3,7},{4,0},{5,1},{6,2},{7,3},{8,12},{9,13},{10,... | collective-permute-start | bytes 1769480 | tf_op jit(solution)/shard_map/ppermute | solution.py:271
  79.8 26.8 %collective-permute-start.16 = (bf16[3,384,256]{2,1,0:T(8,128)(2,1)S(1)}, bf16[3,384,256]{2,1,0:T(8,128)(2,1)S(1)}, u32[]{:S(2)}, u32[]{:S(2)}) collective-permute-start(bf16[3,384,256]{2,1,0:T(8,128)(2,1)S(1)} %copy-done.4), channel_id=1, source_target_pairs={{0,4},{1,5},{2,6},{3,7},{4,0},{5,1},{6,2},{7,3},{8,12},{9,13},{10,... | collective-permute-start | bytes 1769480 | tf_op jit(solution)/shard_map/ppermute | solution.py:271
  82.1 22.4 %copy-start.6 = (bf16[3,384,256]{2,1,0:T(8,128)(2,1)S(1)}, bf16[3,384,256]{2,1,0:T(8,128)(2,1)}, u32[]{:S(2)}) copy-start(bf16[3,384,256]{2,1,0:T(8,128)(2,1)} %copy-done.5) | copy-start | bytes 1769476
  84.5 33.8 %collective-permute-start.24 = (bf16[256,768]{1,0:T(8,128)(2,1)S(1)}, bf16[256,768]{1,0:T(8,128)(2,1)S(1)}, u32[]{:S(2)}, u32[]{:S(2)}) collective-permute-start(bf16[256,768]{1,0:T(8,128)(2,1)S(1)} %get-tuple-element.141), channel_id=1, source_target_pairs={{0,16},{1,17},{2,18},{3,19},{4,20},{5,21},{6,22},{7,23},{8,24},{9,... | collective-permute-start | bytes 1179656 | tf_op jit(solution)/shard_map/ppermute | solution.py:271
  88.0 20.8 %collective-permute-start.21 = (bf16[3,384,128]{2,1,0:T(8,128)(2,1)S(1)}, bf16[3,384,128]{2,1,0:T(8,128)(2,1)S(1)}, u32[]{:S(2)}, u32[]{:S(2)}) collective-permute-start(bf16[3,384,128]{2,1,0:T(8,128)(2,1)S(1)} %collective-permute-done.18.b_ref.refs_3_), channel_id=1, source_target_pairs={{0,4},{1,5},{2,6},{3,7},{4,0},{5,1},{6,2},{7,3},{8,12},{9,13},{10,... | collective-permute-start | bytes 884744 | tf_op jit(solution)/shard_map/ppermute | solution.py:271
  103.5 6.7 %collective-permute-start.20 = (bf16[3,384,128]{2,1,0:T(8,128)(2,1)S(1)}, bf16[3,384,128]{2,1,0:T(8,128)(2,1)S(1)}, u32[]{:S(2)}, u32[]{:S(2)}) collective-permute-start(bf16[3,384,128]{2,1,0:T(8,128)(2,1)S(1)} %copy-done.11), channel_id=1, source_target_pairs={{0,4},{1,5},{2,6},{3,7},{4,0},{5,1},{6,2},{7,3},{8,12},{9,13},{10,... | collective-permute-start | bytes 884744 | tf_op jit(solution)/shard_map/ppermute | solution.py:271
  108.7 22.1 %collective-permute-start.23 = (bf16[256,768]{1,0:T(8,128)(2,1)S(1)}, bf16[256,768]{1,0:T(8,128)(2,1)S(1)}, u32[]{:S(2)}, u32[]{:S(2)}) collective-permute-start(bf16[256,768]{1,0:T(8,128)(2,1)S(1)} %get-tuple-element.139), channel_id=1, source_target_pairs={{0,16},{1,17},{2,18},{3,19},{4,20},{5,21},{6,22},{7,23},{8,24},{9,... | collective-permute-start | bytes 1179656 | tf_op jit(solution)/shard_map/ppermute | solution.py:271
  112.1 20.8 %collective-permute-start.22 = (bf16[256,384]{1,0:T(8,128)(2,1)S(1)}, bf16[256,384]{1,0:T(8,128)(2,1)S(1)}, u32[]{:S(2)}, u32[]{:S(2)}) collective-permute-start(bf16[256,384]{1,0:T(8,128)(2,1)S(1)} %get-tuple-element.137), channel_id=1, source_target_pairs={{0,16},{1,17},{2,18},{3,19},{4,20},{5,21},{6,22},{7,23},{8,24},{9,... | collective-permute-start | bytes 589832 | tf_op jit(solution)/shard_map/ppermute | solution.py:271
  133.7 2.4 %collective-permute-start.25 = (bf16[4,2,2,16,1536]{4,3,2,1,0:T(8,128)(2,1)S(1)}, bf16[4,2,2,16,1536]{4,3,2,1,0:T(8,128)(2,1)S(1)}, u32[]{:S(2)}, u32[]{:S(2)}) collective-permute-start(bf16[4,2,2,16,1536]{4,3,2,1,0:T(8,128)(2,1)S(1)} %get-tuple-element.143), channel_id=1, source_target_pairs={{0,1},{1,0},{2,3},{3,2},{4,5},{5,4},{6,7},{7,6},{8,9},{9,8},{10,11... | collective-permute-start | bytes 2359304 | tf_op jit(solution)/shard_map/ppermute | solution.py:271
  136.2 7.1 %collective-permute-start.26 = (bf16[2,2,16,1536]{3,2,1,0:T(8,128)(2,1)S(1)}, bf16[2,2,16,1536]{3,2,1,0:T(8,128)(2,1)S(1)}, u32[]{:S(2)}, u32[]{:S(2)}) collective-permute-start(bf16[2,2,16,1536]{3,2,1,0:T(8,128)(2,1)S(1)} %get-tuple-element.145), channel_id=1, source_target_pairs={{0,2},{1,3},{2,0},{3,1},{4,6},{5,7},{6,4},{7,5},{8,10},{9,11},{10,... | collective-permute-start | bytes 589832 | tf_op jit(solution)/shard_map/ppermute | solution.py:271
  138.1 7.8 %collective-permute-start.27 = (bf16[2,2,16,1536]{3,2,1,0:T(8,128)(2,1)S(1)}, bf16[2,2,16,1536]{3,2,1,0:T(8,128)(2,1)S(1)}, u32[]{:S(2)}, u32[]{:S(2)}) collective-permute-start(bf16[2,2,16,1536]{3,2,1,0:T(8,128)(2,1)S(1)} %get-tuple-element.146), channel_id=1, source_target_pairs={{0,8},{1,9},{2,10},{3,11},{4,12},{5,13},{6,14},{7,15},{8,0},{9,1},... | collective-permute-start | bytes 589832 | tf_op jit(solution)/shard_map/ppermute | solution.py:271
  138.1 10.7 %collective-permute-start.28 = (bf16[2,2,16,1536]{3,2,1,0:T(8,128)(2,1)S(1)}, bf16[2,2,16,1536]{3,2,1,0:T(8,128)(2,1)S(1)}, u32[]{:S(2)}, u32[]{:S(2)}) collective-permute-start(bf16[2,2,16,1536]{3,2,1,0:T(8,128)(2,1)S(1)} %get-tuple-element.147), channel_id=1, source_target_pairs={{0,10},{1,11},{2,8},{3,9},{4,14},{5,15},{6,12},{7,13},{8,2},{9,3},... | collective-permute-start | bytes 589832 | tf_op jit(solution)/shard_map/ppermute | solution.py:271
  148.8 6.9 %collective-permute-start.29 = (bf16[2,16,1536]{2,1,0:T(8,128)(2,1)S(1)}, bf16[2,16,1536]{2,1,0:T(8,128)(2,1)S(1)}, u32[]{:S(2)}, u32[]{:S(2)}) collective-permute-start(bf16[2,16,1536]{2,1,0:T(8,128)(2,1)S(1)} %get-tuple-element.149), channel_id=1, source_target_pairs={{0,16},{1,17},{2,18},{3,19},{4,20},{5,21},{6,22},{7,23},{8,24},{9,... | collective-permute-start | bytes 294920 | tf_op jit(solution)/shard_map/ppermute | solution.py:271
  (12 other events, 129.1 us)

commit v6 on v5

--- a/solution.py
+++ b/solution.py
@@ -6,8 +6,8 @@
 from jax.sharding import PartitionSpec as P
 
 F32 = jnp.float32
-SHAPE = ((0, 1), (2, 2), (4, 2), (6, 2), (1, 1))
-CFG = {'us': [8, 0], 'flags': {'join_y0': True, 'join_zp0': True, 'own2_plain': True, 'near_y1': True, 'near_y2': False, 'near_y3': False, 'near_zp1': False, 'first_y2': True, 'first_zp1': True}, 'order': [('F', 0), ('F', 1), ('S', 0), ('F', 2), ('S', 1), ('F', 3), ('S', 2), ('F', 4), ('S', 3), ('S', 4)], 'ties': {('F', 1): [('F', 0)], ('F', 2): [('F', 1)], ('S', 0): [('F', 1)], ('F', 3): [('S', 0)], ('S', 1): [('F', 2)], ('F', 4): [('S', 1), ('F', 3)], ('S', 2): [('F', 3)], ('S', 3): [('F', 4)]}, 'y': {5: [('F', 0)], 6: [('F', 1)], 7: [('F', 1)], 8: [('F', 2)], 9: [('F', 2)]}, 'arrive': {}}
+SHAPE = ((0, 1), (2, 2), (4, 2), (1, 1), (6, 1), (7, 1))
+CFG = {'us': [8, 0], 'flags': {'join_y0': True, 'join_zp0': True, 'own2_plain': True, 'near_y1': True, 'near_y2': False, 'near_y3': False, 'near_zp1': False, 'first_y2': True, 'first_zp1': True, 'zp0_early': True}, 'order': [('F', 0), ('F', 1), ('S', 0), ('F', 2), ('S', 1), ('F', 3), ('S', 2), ('F', 4), ('S', 3), ('F', 5), ('S', 4), ('S', 5)], 'ties': {('F', 1): [('F', 0)], ('F', 2): [('F', 1)], ('S', 0): [('F', 1)], ('F', 3): [('S', 0)], ('S', 1): [('F', 2)], ('F', 4): [('S', 1), ('F', 3)], ('F', 5): [('S', 3), ('F', 4)], ('S', 3): [('F', 4)], ('S', 4): [('F', 5)]}, 'y': {5: [('F', 0)], 6: [('F', 1)], 7: [('F', 1)], 8: [('F', 2)], 9: [('F', 2)], 10: [('F', 3)], 11: [('F', 3)]}, 'zp': {3: [('F', 0)], 4: [('F', 1)], 5: [('F', 2)]}, 'arrive': {}}
 BF16 = jnp.bfloat16
 LANES = 128
 AHEAD = 2
@@ -349,17 +349,20 @@
         plain, flipped = call(join_body, [pair, pair], mine, other)
         if CFG["flags"]["own2_plain"]:
             own_w[2], _ = after(own_w[2], plain)
+        early = CFG["flags"]["zp0_early"]
+        if early:
+            over_y(zp_w[0])
         over_y(own_w[2])
-        over_y(zp_w[0])
-        for k in range(1, count):
-            if k <= 2:
-                given[k], _ = after(given[k], plain)
-            else:
-                given[k], zp_w[k - 2] = after(given[k], zp_w[k - 2])
+        if not early:
+            over_y(zp_w[0])
+        for k in range(1, 3):
+            given[k], _ = after(given[k], plain)
             zp_w[k] = swap(given[k], at_zp)
         near_rows = jnp.stack(
             [plain, swap(plain, at_x), swap(flipped, at_zp), swap(flipped, at_zp + at_x)]
         )
+        if early:
+            stream[2], stream[3] = stream[3], stream[2]
         for at in (1, 2, 3):
             if CFG["flags"][f"near_y{at}"]:
                 near_rows, stream[at] = after(near_rows, stream[at])
@@ -484,8 +487,15 @@
             values[k] = held_back(values[k], *steps_of(CFG["y"][j]))
             over_y(values[k])
 
-        pending = [5, 6, 7, 8, 9]
+        def give(k):
+            given[k] = held_back(given[k], *steps_of(CFG["zp"][k]))
+            zp_w[k] = swap(given[k], at_zp)
+
+        to_give = list(range(3, count))
+        pending = list(range(5, 2 * count))
         done_ops = []
+        while to_give and not CFG["zp"][to_give[0]]:
+            give(to_give.pop(0))
         while pending and not CFG["y"][pending[0]]:
             emit_y(pending.pop(0))
         for kind, k in CFG["order"]:
@@ -502,6 +512,8 @@
                 pre[k] = [values, pre[k][1]]
                 second(k)
             done_ops.append((kind, k))
+            while to_give and all(op in done_ops for op in CFG["zp"][to_give[0]]):
+                give(to_give.pop(0))
             while pending and all(op in done_ops for op in CFG["y"][pending[0]]):
                 emit_y(pending.pop(0))
         total = total[-1]

time: 158 us -> 151 us (0.956)
  waiting for transfers between devices: 83 us -> 64.1 us
  starting transfers between devices: 38.8 us -> 46 us
  Pallas kernels: 32.1 us -> 36.1 us
    ppermute x30 -> x34, waiting for transfers between devices: 83 us -> 64.1 us  [swap(): return lax.ppermute(values, ('fsdp', 'et'), pairs)]
    ppermute x30 -> x34, starting transfers between devices: 38.8 us -> 46 us  [swap(): return lax.ppermute(values, ('fsdp', 'et'), pairs)]
    pallas_call x15 -> x17, Pallas kernels: 20.6 us -> 22.8 us  [call(): pl.pallas_call(body, out_shape=list(outs), scratch_shapes=list(scratch),...]
    pallas_call x5 -> x6, Pallas kernels: 11.5 us -> 13.3 us  [weight_chunk(): pl.pallas_call(weight_chunk_body, out_shape=[out, out], grid_spec=pltpu.P...]
  transfers between devices with their start and end apart: 30 -> 34, of which waited for: 18 -> 19; matrix products, arithmetic and copies ran while one was open for 1% -> 1% of each run, Pallas kernels for 17% -> 21%
where the time goes in v6:
time: 151 us; the launch traced here: 150 us
  waiting for transfers between devices  64.1 us (42%)
  starting transfers between devices  46 us (30%)
  Pallas kernels  36.1 us (24%)
    ppermute x34, waiting for transfers between devices, swap(): return lax.ppermute(values, ('fsdp', 'et'), pairs)  64.1 us
    ppermute x34, starting transfers between devices, swap(): return lax.ppermute(values, ('fsdp', 'et'), pairs)  46 us
    pallas_call x17, Pallas kernels, call(): pl.pallas_call(body, out_shape=list(outs), scratch_shapes=list(scratch),...  22.8 us
    pallas_call x6, Pallas kernels, weight_chunk(): pl.pallas_call(weight_chunk_body, out_shape=[out, out], grid_spec=pltpu.P...  13.3 us
  transfers between devices with their start and end apart: 34, of which 19 were waited for; matrix products, arithmetic and copies ran while one was open for 1% of the time, Pallas kernels for 21%

profile of v6, /device:TPU:0, one launch (start us, length us, event | category | flops | bytes accessed | tf_op | source)
XLA Modules:
  0.0 149.7 jit_solution(11495192954304260209)
XLA Ops:
  0.7 2.1 %shard_map.87 = (bf16[3,384,128]{2,1,0:T(8,128)(2,1)}, bf16[3,384,128]{2,1,0:T(8,128)(2,1)}) custom-call(s32[1]{0:T(128)} %bitcast.low_ref, bf16[384,2048]{1,0:T(8,128)(2,1)} %refs_3_.11, bf16[384,2048]{1,0:T(8,128)(2,1)} %refs_4_.11, bf16[2048,384]{1,0:T(8,128)(2,1)} %refs_5_.11, bf16[384,2048]{1,0:T(8,128)(2,1)} %refs_3_.11, bf16[384,2048]{1,0:T(8,128)(2,1)} %refs_4_.11, ...), custom_call_target="tpu_custom_call" | custom-call | bytes 1024 | tf_op jit(solution)/shard_map/pallas_call | solution.py:253
  2.7 3.0 %collective-permute-start = (bf16[3,384,128]{2,1,0:T(8,128)(2,1)}, bf16[3,384,128]{2,1,0:T(8,128)(2,1)S(1)}, u32[]{:S(2)}, u32[]{:S(2)}) collective-permute-start(bf16[3,384,128]{2,1,0:T(8,128)(2,1)} %get-tuple-element.90.a_ref.refs_2_), channel_id=1, source_target_pairs={{0,4},{1,5},{2,6},{3,7},{4,0},{5,1},{6,2},{7,3},{8,12},{9,13},{10,... | collective-permute-start | bytes 884744 | tf_op jit(solution)/shard_map/ppermute | solution.py:271
  7.3 2.5 %shard_map.89 = (bf16[3,384,256]{2,1,0:T(8,128)(2,1)}, bf16[3,384,256]{2,1,0:T(8,128)(2,1)}) custom-call(s32[1]{0:T(128)} %bitcast.low_ref, bf16[384,2048]{1,0:T(8,128)(2,1)} %refs_3_.11, bf16[384,2048]{1,0:T(8,128)(2,1)} %refs_4_.11, bf16[2048,384]{1,0:T(8,128)(2,1)} %refs_5_.11, bf16[384,2048]{1,0:T(8,128)(2,1)} %refs_3_.11, bf16[384,2048]{1,0:T(8,128)(2,1)} %refs_4_.11, ...), custom_call_target="tpu_custom_call" | custom-call | bytes 1024 | tf_op jit(solution)/shard_map/pallas_call | solution.py:253
  11.1 2.7 %collective-permute-start.2 = (bf16[2,16,1536]{2,1,0:T(8,128)(2,1)S(1)}, bf16[2,16,1536]{2,1,0:T(8,128)(2,1)S(1)}, u32[]{:S(2)}, u32[]{:S(2)}) collective-permute-start(bf16[2,16,1536]{2,1,0:T(8,128)(2,1)S(1)} %get-tuple-element.94), channel_id=1, source_target_pairs={{0,16},{1,17},{2,18},{3,19},{4,20},{5,21},{6,22},{7,23},{8,24},{9,... | collective-permute-start | bytes 294920 | tf_op jit(solution)/shard_map/ppermute | solution.py:271
  21.0 2.5 %shard_map.90 = (bf16[3,384,256]{2,1,0:T(8,128)(2,1)}, bf16[3,384,256]{2,1,0:T(8,128)(2,1)}) custom-call(s32[1]{0:T(128)} %bitcast.low_ref, bf16[384,2048]{1,0:T(8,128)(2,1)} %refs_3_.11, bf16[384,2048]{1,0:T(8,128)(2,1)} %refs_4_.11, bf16[2048,384]{1,0:T(8,128)(2,1)} %refs_5_.11, bf16[384,2048]{1,0:T(8,128)(2,1)} %refs_3_.11, bf16[384,2048]{1,0:T(8,128)(2,1)} %refs_4_.11, ...), custom_call_target="tpu_custom_call" | custom-call | bytes 1024 | tf_op jit(solution)/shard_map/pallas_call | solution.py:253
  23.5 2.1 %collective-permute-start.7 = (bf16[3,384,256]{2,1,0:T(8,128)(2,1)}, bf16[3,384,256]{2,1,0:T(8,128)(2,1)S(1)}, u32[]{:S(2)}, u32[]{:S(2)}) collective-permute-start(bf16[3,384,256]{2,1,0:T(8,128)(2,1)} %get-tuple-element.100.a_ref.refs_2_), channel_id=1, source_target_pairs={{0,4},{1,5},{2,6},{3,7},{4,0},{5,1},{6,2},{7,3},{8,12},{9,13},{10,... | collective-permute-start | bytes 1769480 | tf_op jit(solution)/shard_map/ppermute | solution.py:271
  27.1 3.9 %collective-permute-done.5 = bf16[2,2,16,1536]{3,2,1,0:T(8,128)(2,1)} collective-permute-done((bf16[2,2,16,1536]{3,2,1,0:T(8,128)(2,1)S(1)}, bf16[2,2,16,1536]{3,2,1,0:T(8,128)(2,1)}, u32[]{:S(2)}, u32[]{:S(2)}) %collective-permute-start.5) | collective-permute-done | bytes 196640 | tf_op jit(solution)/shard_map/ppermute | solution.py:271
  34.3 5.7 %collective-permute-done.7.c_ref.refs_4_ = bf16[3,384,256]{2,1,0:T(8,128)(2,1)S(1)} collective-permute-done((bf16[3,384,256]{2,1,0:T(8,128)(2,1)}, bf16[3,384,256]{2,1,0:T(8,128)(2,1)S(1)}, u32[]{:S(2)}, u32[]{:S(2)}) %collective-permute-start.7) | collective-permute-done | bytes 589856 | tf_op jit(solution)/shard_map/ppermute | solution.py:271
  40.0 3.7 %collective-permute-done.8.b_ref.refs_3_ = bf16[3,384,256]{2,1,0:T(8,128)(2,1)S(1)} collective-permute-done((bf16[3,384,256]{2,1,0:T(8,128)(2,1)}, bf16[3,384,256]{2,1,0:T(8,128)(2,1)S(1)}, u32[]{:S(2)}, u32[]{:S(2)}) %collective-permute-start.8) | collective-permute-done | bytes 589856 | tf_op jit(solution)/shard_map/ppermute | solution.py:271
  45.3 2.1 %shard_map.92 = (bf16[3,384,128]{2,1,0:T(8,128)(2,1)}, bf16[3,384,128]{2,1,0:T(8,128)(2,1)}) custom-call(s32[1]{0:T(128)} %bitcast.low_ref, bf16[384,2048]{1,0:T(8,128)(2,1)} %refs_3_.11, bf16[384,2048]{1,0:T(8,128)(2,1)} %refs_4_.11, bf16[2048,384]{1,0:T(8,128)(2,1)} %refs_5_.11, bf16[384,2048]{1,0:T(8,128)(2,1)} %refs_3_.11, bf16[384,2048]{1,0:T(8,128)(2,1)} %refs_4_.11, ...), custom_call_target="tpu_custom_call" | custom-call | bytes 1024 | tf_op jit(solution)/shard_map/pallas_call | solution.py:253
  47.4 2.1 %shard_map.93 = (bf16[3,384,128]{2,1,0:T(8,128)(2,1)}, bf16[3,384,128]{2,1,0:T(8,128)(2,1)}) custom-call(s32[1]{0:T(128)} %bitcast.low_ref, bf16[384,2048]{1,0:T(8,128)(2,1)} %refs_3_.11, bf16[384,2048]{1,0:T(8,128)(2,1)} %refs_4_.11, bf16[2048,384]{1,0:T(8,128)(2,1)} %refs_5_.11, bf16[384,2048]{1,0:T(8,128)(2,1)} %refs_3_.11, bf16[384,2048]{1,0:T(8,128)(2,1)} %refs_4_.11, ...), custom_call_target="tpu_custom_call" | custom-call | bytes 1024 | tf_op jit(solution)/shard_map/pallas_call | solution.py:253
  49.5 2.1 %shard_map.97 = (bf16[3,384,128]{2,1,0:T(8,128)(2,1)}, bf16[3,384,128]{2,1,0:T(8,128)(2,1)}) custom-call(s32[1]{0:T(128)} %bitcast.low_ref, bf16[384,2048]{1,0:T(8,128)(2,1)} %refs_3_.11, bf16[384,2048]{1,0:T(8,128)(2,1)} %refs_4_.11, bf16[2048,384]{1,0:T(8,128)(2,1)} %refs_5_.11, bf16[384,2048]{1,0:T(8,128)(2,1)} %refs_3_.11, bf16[384,2048]{1,0:T(8,128)(2,1)} %refs_4_.11, ...), custom_call_target="tpu_custom_call" | custom-call | bytes 1024 | tf_op jit(solution)/shard_map/pallas_call | solution.py:253
  59.4 2.3 %shard_map.94 = (f32[256,768]{1,0:T(8,128)S(1)}, bf16[256,768]{1,0:T(8,128)(2,1)S(1)}) custom-call(bf16[4,2,2,16,1536]{4,3,2,1,0:T(8,128)(2,1)S(1)} %pad_maximum_fusion.near_ref, bf16[4,2,2,16,1536]{4,3,2,1,0:T(8,128)(2,1)} %collective-permute-done.9.far_ref, bf16[3,384,256]{2,1,0:T(8,128)(2,1)S(1)} %copy-done.2, ...), custom_call_target="tpu_custom_call" | custom-call | flops 8000000000 | bytes 1024 | tf_op jit(solution)/shard_map/pallas_call | solution.py:194
  61.7 2.4 %collective-permute-start.19 = (bf16[3,384,128]{2,1,0:T(8,128)(2,1)S(1)}, bf16[3,384,128]{2,1,0:T(8,128)(2,1)S(1)}, u32[]{:S(2)}, u32[]{:S(2)}) collective-permute-start(bf16[3,384,128]{2,1,0:T(8,128)(2,1)S(1)} %copy-done.16), channel_id=1, source_target_pairs={{0,8},{1,9},{2,10},{3,11},{4,12},{5,13},{6,14},{7,15},{8,0},{9,1},... | collective-permute-start | bytes 884744 | tf_op jit(solution)/shard_map/ppermute | solution.py:271
  64.8 3.1 %collective-permute-done.11.b_ref.refs_3_ = bf16[3,384,128]{2,1,0:T(8,128)(2,1)S(1)} collective-permute-done((bf16[3,384,128]{2,1,0:T(8,128)(2,1)S(1)}, bf16[3,384,128]{2,1,0:T(8,128)(2,1)S(1)}, u32[]{:S(2)}, u32[]{:S(2)}) %collective-permute-start.11) | collective-permute-done | bytes 294944 | tf_op jit(solution)/shard_map/ppermute | solution.py:271
  69.7 3.2 %collective-permute-start.16 = (bf16[3,384,128]{2,1,0:T(8,128)(2,1)S(1)}, bf16[3,384,128]{2,1,0:T(8,128)(2,1)S(1)}, u32[]{:S(2)}, u32[]{:S(2)}) collective-permute-start(bf16[3,384,128]{2,1,0:T(8,128)(2,1)S(1)} %collective-permute-done.11.b_ref.refs_3_), channel_id=1, source_target_pairs={{0,4},{1,5},{2,6},{3,7},{4,0},{5,1},{6,2},{7,3},{8,12},{9,13},{10,... | collective-permute-start | bytes 884744 | tf_op jit(solution)/shard_map/ppermute | solution.py:271
  72.8 2.3 %shard_map.98 = (f32[256,768]{1,0:T(8,128)S(1)}, bf16[256,768]{1,0:T(8,128)(2,1)S(1)}) custom-call(bf16[4,2,2,16,1536]{4,3,2,1,0:T(8,128)(2,1)S(1)} %pad_maximum_fusion.near_ref, bf16[4,2,2,16,1536]{4,3,2,1,0:T(8,128)(2,1)} %collective-permute-done.9.far_ref, bf16[3,384,256]{2,1,0:T(8,128)(2,1)S(1)} %copy-done.3, ...), custom_call_target="tpu_custom_call" | custom-call | flops 8000000000 | bytes 1024 | tf_op jit(solution)/shard_map/pallas_call | solution.py:194
  80.6 4.0 %collective-permute-done.16.d_ref.refs_5_ = bf16[3,384,128]{2,1,0:T(8,128)(2,1)S(1)} collective-permute-done((bf16[3,384,128]{2,1,0:T(8,128)(2,1)S(1)}, bf16[3,384,128]{2,1,0:T(8,128)(2,1)S(1)}, u32[]{:S(2)}, u32[]{:S(2)}) %collective-permute-start.16) | collective-permute-done | bytes 294944 | tf_op jit(solution)/shard_map/ppermute | solution.py:271
  84.6 2.3 %collective-permute-start.21 = (bf16[3,384,128]{2,1,0:T(8,128)(2,1)S(1)}, bf16[3,384,128]{2,1,0:T(8,128)(2,1)S(1)}, u32[]{:S(2)}, u32[]{:S(2)}) collective-permute-start(bf16[3,384,128]{2,1,0:T(8,128)(2,1)S(1)} %copy-done.7), channel_id=1, source_target_pairs={{0,4},{1,5},{2,6},{3,7},{4,0},{5,1},{6,2},{7,3},{8,12},{9,13},{10,... | collective-permute-start | bytes 884744 | tf_op jit(solution)/shard_map/ppermute | solution.py:271
  88.8 6.7 %collective-permute-done.20.refs_1_ = bf16[256,768]{1,0:T(8,128)(2,1)S(1)} collective-permute-done((bf16[256,768]{1,0:T(8,128)(2,1)S(1)}, bf16[256,768]{1,0:T(8,128)(2,1)S(1)}, u32[]{:S(2)}, u32[]{:S(2)}) %collective-permute-start.20) | collective-permute-done | bytes 393248 | tf_op jit(solution)/shard_map/ppermute | solution.py:271
  95.5 2.1 %shard_map.99.refs_6_ = f32[2,256,1536]{2,1,0:T(8,128)S(1)} custom-call(f32[256,768]{1,0:T(8,128)S(1)} %get-tuple-element.147.refs_0_, bf16[256,768]{1,0:T(8,128)(2,1)S(1)} %collective-permute-done.20.refs_1_, bf16[3,384,256]{2,1,0:T(8,128)(2,1)S(1)} %copy-done.2, bf16[3,384,256]{2,1,0:T(8,128)(2,1)S(1)} %copy-done.5, ...), custom_call_target="tpu_custom_call" | custom-call | bytes 1024 | tf_op jit(solution)/shard_map/pallas_call | solution.py:194
  97.6 2.1 %collective-permute-start.26 = (bf16[3,384,128]{2,1,0:T(8,128)(2,1)S(1)}, bf16[3,384,128]{2,1,0:T(8,128)(2,1)S(1)}, u32[]{:S(2)}, u32[]{:S(2)}) collective-permute-start(bf16[3,384,128]{2,1,0:T(8,128)(2,1)S(1)} %collective-permute-done.18.b_ref.refs_3_), channel_id=1, source_target_pairs={{0,4},{1,5},{2,6},{3,7},{4,0},{5,1},{6,2},{7,3},{8,12},{9,13},{10,... | collective-permute-start | bytes 884744 | tf_op jit(solution)/shard_map/ppermute | solution.py:271
  101.6 2.9 %collective-permute-done.24.refs_1_ = bf16[256,768]{1,0:T(8,128)(2,1)S(1)} collective-permute-done((bf16[256,768]{1,0:T(8,128)(2,1)S(1)}, bf16[256,768]{1,0:T(8,128)(2,1)S(1)}, u32[]{:S(2)}, u32[]{:S(2)}) %collective-permute-start.24) | collective-permute-done | bytes 393248 | tf_op jit(solution)/shard_map/ppermute | solution.py:271
  104.5 2.1 %shard_map.101.refs_6_ = f32[2,256,1536]{2,1,0:T(8,128)S(1)} custom-call(f32[256,768]{1,0:T(8,128)S(1)} %get-tuple-element.156.refs_0_, bf16[256,768]{1,0:T(8,128)(2,1)S(1)} %collective-permute-done.24.refs_1_, bf16[3,384,256]{2,1,0:T(8,128)(2,1)S(1)} %copy-done.3, bf16[3,384,256]{2,1,0:T(8,128)(2,1)} %collective-permute-done.12.b_ref.refs_3_, ...), custom_call_target="tpu_custom_call" | custom-call | bytes 1024 | tf_op jit(solution)/shard_map/pallas_call | solution.py:194
  106.6 2.9 %collective-permute-done.23.refs_1_ = bf16[256,384]{1,0:T(8,128)(2,1)S(1)} collective-permute-done((bf16[256,384]{1,0:T(8,128)(2,1)S(1)}, bf16[256,384]{1,0:T(8,128)(2,1)S(1)}, u32[]{:S(2)}, u32[]{:S(2)}) %collective-permute-start.23) | collective-permute-done | bytes 196640 | tf_op jit(solution)/shard_map/ppermute | solution.py:271
  112.2 3.0 %collective-permute-start.27 = (bf16[256,384]{1,0:T(8,128)(2,1)S(1)}, bf16[256,384]{1,0:T(8,128)(2,1)S(1)}, u32[]{:S(2)}, u32[]{:S(2)}) collective-permute-start(bf16[256,384]{1,0:T(8,128)(2,1)S(1)} %get-tuple-element.164), channel_id=1, source_target_pairs={{0,16},{1,17},{2,18},{3,19},{4,20},{5,21},{6,22},{7,23},{8,24},{9,... | collective-permute-start | bytes 589832 | tf_op jit(solution)/shard_map/ppermute | solution.py:271
  115.2 8.3 %collective-permute-done.28.refs_1_ = bf16[256,384]{1,0:T(8,128)(2,1)S(1)} collective-permute-done((bf16[256,384]{1,0:T(8,128)(2,1)S(1)}, bf16[256,384]{1,0:T(8,128)(2,1)S(1)}, u32[]{:S(2)}, u32[]{:S(2)}) %collective-permute-start.28) | collective-permute-done | bytes 196640 | tf_op jit(solution)/shard_map/ppermute | solution.py:271
  126.4 2.3 %collective-permute-done.29.recv_ref = bf16[4,2,2,16,1536]{4,3,2,1,0:T(8,128)(2,1)S(1)} collective-permute-done((bf16[4,2,2,16,1536]{4,3,2,1,0:T(8,128)(2,1)S(1)}, bf16[4,2,2,16,1536]{4,3,2,1,0:T(8,128)(2,1)S(1)}, u32[]{:S(2)}, u32[]{:S(2)}) %collective-permute-start.29) | collective-permute-done | bytes 786464 | tf_op jit(solution)/shard_map/ppermute | solution.py:271
  132.4 3.5 %collective-permute-done.30.x_ref = bf16[2,2,16,1536]{3,2,1,0:T(8,128)(2,1)S(1)} collective-permute-done((bf16[2,2,16,1536]{3,2,1,0:T(8,128)(2,1)S(1)}, bf16[2,2,16,1536]{3,2,1,0:T(8,128)(2,1)S(1)}, u32[]{:S(2)}, u32[]{:S(2)}) %collective-permute-start.30) | collective-permute-done | bytes 196640 | tf_op jit(solution)/shard_map/ppermute | solution.py:271
  135.8 2.4 %collective-permute-done.31.zp_ref = bf16[2,2,16,1536]{3,2,1,0:T(8,128)(2,1)S(1)} collective-permute-done((bf16[2,2,16,1536]{3,2,1,0:T(8,128)(2,1)S(1)}, bf16[2,2,16,1536]{3,2,1,0:T(8,128)(2,1)S(1)}, u32[]{:S(2)}, u32[]{:S(2)}) %collective-permute-start.31) | collective-permute-done | bytes 196640 | tf_op jit(solution)/shard_map/ppermute | solution.py:271
  138.3 3.0 %collective-permute-done.32.both_ref = bf16[2,2,16,1536]{3,2,1,0:T(8,128)(2,1)S(1)} collective-permute-done((bf16[2,2,16,1536]{3,2,1,0:T(8,128)(2,1)S(1)}, bf16[2,2,16,1536]{3,2,1,0:T(8,128)(2,1)S(1)}, u32[]{:S(2)}, u32[]{:S(2)}) %collective-permute-start.32) | collective-permute-done | bytes 196640 | tf_op jit(solution)/shard_map/ppermute | solution.py:271
  142.2 5.9 %collective-permute-done.33.other_ref = bf16[2,16,1536]{2,1,0:T(8,128)(2,1)S(1)} collective-permute-done((bf16[2,16,1536]{2,1,0:T(8,128)(2,1)S(1)}, bf16[2,16,1536]{2,1,0:T(8,128)(2,1)S(1)}, u32[]{:S(2)}, u32[]{:S(2)}) %collective-permute-start.33) | collective-permute-done | bytes 98336 | tf_op jit(solution)/shard_map/ppermute | solution.py:271
  (98 shorter events, 48.2 us)
Async XLA Ops:
  2.7 11.1 %collective-permute-start = (bf16[3,384,128]{2,1,0:T(8,128)(2,1)}, bf16[3,384,128]{2,1,0:T(8,128)(2,1)S(1)}, u32[]{:S(2)}, u32[]{:S(2)}) collective-permute-start(bf16[3,384,128]{2,1,0:T(8,128)(2,1)} %get-tuple-element.90.a_ref.refs_2_), channel_id=1, source_target_pairs={{0,4},{1,5},{2,6},{3,7},{4,0},{5,1},{6,2},{7,3},{8,12},{9,13},{10,... | collective-permute-start | bytes 884744 | tf_op jit(solution)/shard_map/ppermute | solution.py:271
  5.7 9.8 %collective-permute-start.1 = (bf16[3,384,128]{2,1,0:T(8,128)(2,1)}, bf16[3,384,128]{2,1,0:T(8,128)(2,1)S(1)}, u32[]{:S(2)}, u32[]{:S(2)}) collective-permute-start(bf16[3,384,128]{2,1,0:T(8,128)(2,1)} %get-tuple-element.92), channel_id=1, source_target_pairs={{0,8},{1,9},{2,10},{3,11},{4,12},{5,13},{6,14},{7,15},{8,0},{9,1},... | collective-permute-start | bytes 884744 | tf_op jit(solution)/shard_map/ppermute | solution.py:271
  9.8 22.4 %collective-permute-start.6 = (bf16[3,384,256]{2,1,0:T(8,128)(2,1)}, bf16[3,384,256]{2,1,0:T(8,128)(2,1)S(1)}, u32[]{:S(2)}, u32[]{:S(2)}) collective-permute-start(bf16[3,384,256]{2,1,0:T(8,128)(2,1)} %get-tuple-element.97.a_ref.refs_2_), channel_id=1, source_target_pairs={{0,4},{1,5},{2,6},{3,7},{4,0},{5,1},{6,2},{7,3},{8,12},{9,13},{10,... | collective-permute-start | bytes 1769480 | tf_op jit(solution)/shard_map/ppermute | solution.py:271
  17.5 8.1 %collective-permute-start.3 = (bf16[2,2,16,1536]{3,2,1,0:T(8,128)(2,1)S(1)}, bf16[2,2,16,1536]{3,2,1,0:T(8,128)(2,1)}, u32[]{:S(2)}, u32[]{:S(2)}) collective-permute-start(bf16[2,2,16,1536]{3,2,1,0:T(8,128)(2,1)S(1)} %get-tuple-element.95), channel_id=1, source_target_pairs={{0,2},{1,3},{2,0},{3,1},{4,6},{5,7},{6,4},{7,5},{8,10},{9,11},{10,... | collective-permute-start | bytes 589832 | tf_op jit(solution)/shard_map/ppermute | solution.py:271
  19.0 8.1 %collective-permute-start.4 = (bf16[2,2,16,1536]{3,2,1,0:T(8,128)(2,1)S(1)}, bf16[2,2,16,1536]{3,2,1,0:T(8,128)(2,1)}, u32[]{:S(2)}, u32[]{:S(2)}) collective-permute-start(bf16[2,2,16,1536]{3,2,1,0:T(8,128)(2,1)S(1)} %get-tuple-element.96), channel_id=1, source_target_pairs={{0,8},{1,9},{2,10},{3,11},{4,12},{5,13},{6,14},{7,15},{8,0},{9,1},... | collective-permute-start | bytes 589832 | tf_op jit(solution)/shard_map/ppermute | solution.py:271
  20.7 10.3 %collective-permute-start.5 = (bf16[2,2,16,1536]{3,2,1,0:T(8,128)(2,1)S(1)}, bf16[2,2,16,1536]{3,2,1,0:T(8,128)(2,1)}, u32[]{:S(2)}, u32[]{:S(2)}) collective-permute-start(bf16[2,2,16,1536]{3,2,1,0:T(8,128)(2,1)S(1)} %get-tuple-element.96), channel_id=1, source_target_pairs={{0,10},{1,11},{2,8},{3,9},{4,14},{5,15},{6,12},{7,13},{8,2},{9,3},... | collective-permute-start | bytes 589832 | tf_op jit(solution)/shard_map/ppermute | solution.py:271
  23.5 16.5 %collective-permute-start.7 = (bf16[3,384,256]{2,1,0:T(8,128)(2,1)}, bf16[3,384,256]{2,1,0:T(8,128)(2,1)S(1)}, u32[]{:S(2)}, u32[]{:S(2)}) collective-permute-start(bf16[3,384,256]{2,1,0:T(8,128)(2,1)} %get-tuple-element.100.a_ref.refs_2_), channel_id=1, source_target_pairs={{0,4},{1,5},{2,6},{3,7},{4,0},{5,1},{6,2},{7,3},{8,12},{9,13},{10,... | collective-permute-start | bytes 1769480 | tf_op jit(solution)/shard_map/ppermute | solution.py:271
  25.5 18.2 %collective-permute-start.8 = (bf16[3,384,256]{2,1,0:T(8,128)(2,1)}, bf16[3,384,256]{2,1,0:T(8,128)(2,1)S(1)}, u32[]{:S(2)}, u32[]{:S(2)}) collective-permute-start(bf16[3,384,256]{2,1,0:T(8,128)(2,1)} %get-tuple-element.103), channel_id=1, source_target_pairs={{0,8},{1,9},{2,10},{3,11},{4,12},{5,13},{6,14},{7,15},{8,0},{9,1},... | collective-permute-start | bytes 1769480 | tf_op jit(solution)/shard_map/ppermute | solution.py:271
  32.2 19.4 %collective-permute-start.9 = (bf16[4,2,2,16,1536]{4,3,2,1,0:T(8,128)(2,1)S(1)}, bf16[4,2,2,16,1536]{4,3,2,1,0:T(8,128)(2,1)}, u32[]{:S(2)}, u32[]{:S(2)}) collective-permute-start(bf16[4,2,2,16,1536]{4,3,2,1,0:T(8,128)(2,1)S(1)} %pad_maximum_fusion.near_ref), channel_id=1, source_target_pairs={{0,1},{1,0},{2,3},{3,2},{4,5},{5,4},{6,7},{7,6},{8,9},{9,8},{10,11... | collective-permute-start | bytes 2359304 | tf_op jit(solution)/shard_map/ppermute | solution.py:271
  32.3 19.3 %collective-permute-start.10 = (bf16[3,384,128]{2,1,0:T(8,128)(2,1)S(1)}, bf16[3,384,128]{2,1,0:T(8,128)(2,1)}, u32[]{:S(2)}, u32[]{:S(2)}) collective-permute-start(bf16[3,384,128]{2,1,0:T(8,128)(2,1)S(1)} %collective-permute-done.1.b_ref.refs_3_), channel_id=1, source_target_pairs={{0,4},{1,5},{2,6},{3,7},{4,0},{5,1},{6,2},{7,3},{8,12},{9,13},{10,... | collective-permute-start | bytes 884744 | tf_op jit(solution)/shard_map/ppermute | solution.py:271
  33.1 21.5 %collective-permute-start.12 = (bf16[3,384,256]{2,1,0:T(8,128)(2,1)}, bf16[3,384,256]{2,1,0:T(8,128)(2,1)}, u32[]{:S(2)}, u32[]{:S(2)}) collective-permute-start(bf16[3,384,256]{2,1,0:T(8,128)(2,1)} %get-tuple-element.114), channel_id=1, source_target_pairs={{0,8},{1,9},{2,10},{3,11},{4,12},{5,13},{6,14},{7,15},{8,0},{9,1},... | collective-permute-start | bytes 1769480 | tf_op jit(solution)/shard_map/ppermute | solution.py:271
  43.7 15.7 %collective-permute-start.13 = (bf16[3,384,256]{2,1,0:T(8,128)(2,1)S(1)}, bf16[3,384,256]{2,1,0:T(8,128)(2,1)}, u32[]{:S(2)}, u32[]{:S(2)}) collective-permute-start(bf16[3,384,256]{2,1,0:T(8,128)(2,1)S(1)} %collective-permute-done.8.b_ref.refs_3_), channel_id=1, source_target_pairs={{0,4},{1,5},{2,6},{3,7},{4,0},{5,1},{6,2},{7,3},{8,12},{9,13},{10,... | collective-permute-start | bytes 1769480 | tf_op jit(solution)/shard_map/ppermute | solution.py:271
  54.7 13.2 %collective-permute-start.11 = (bf16[3,384,128]{2,1,0:T(8,128)(2,1)S(1)}, bf16[3,384,128]{2,1,0:T(8,128)(2,1)S(1)}, u32[]{:S(2)}, u32[]{:S(2)}) collective-permute-start(bf16[3,384,128]{2,1,0:T(8,128)(2,1)S(1)} %copy-done.17), channel_id=1, source_target_pairs={{0,8},{1,9},{2,10},{3,11},{4,12},{5,13},{6,14},{7,15},{8,0},{9,1},... | collective-permute-start | bytes 884744 | tf_op jit(solution)/shard_map/ppermute | solution.py:271
  55.5 17.3 %collective-permute-start.17 = (bf16[3,384,256]{2,1,0:T(8,128)(2,1)}, bf16[3,384,256]{2,1,0:T(8,128)(2,1)S(1)}, u32[]{:S(2)}, u32[]{:S(2)}) collective-permute-start(bf16[3,384,256]{2,1,0:T(8,128)(2,1)} %collective-permute-done.12.b_ref.refs_3_), channel_id=1, source_target_pairs={{0,4},{1,5},{2,6},{3,7},{4,0},{5,1},{6,2},{7,3},{8,12},{9,13},{10,... | collective-permute-start | bytes 1769480 | tf_op jit(solution)/shard_map/ppermute | solution.py:271
  56.9 11.0 %collective-permute-start.14 = (bf16[256,384]{1,0:T(8,128)(2,1)S(1)}, bf16[256,384]{1,0:T(8,128)(2,1)S(1)}, u32[]{:S(2)}, u32[]{:S(2)}) collective-permute-start(bf16[256,384]{1,0:T(8,128)(2,1)S(1)} %get-tuple-element.125), channel_id=1, source_target_pairs={{0,16},{1,17},{2,18},{3,19},{4,20},{5,21},{6,22},{7,23},{8,24},{9,... | collective-permute-start | bytes 589832 | tf_op jit(solution)/shard_map/ppermute | solution.py:271
  61.7 13.7 %collective-permute-start.19 = (bf16[3,384,128]{2,1,0:T(8,128)(2,1)S(1)}, bf16[3,384,128]{2,1,0:T(8,128)(2,1)S(1)}, u32[]{:S(2)}, u32[]{:S(2)}) collective-permute-start(bf16[3,384,128]{2,1,0:T(8,128)(2,1)S(1)} %copy-done.16), channel_id=1, source_target_pairs={{0,8},{1,9},{2,10},{3,11},{4,12},{5,13},{6,14},{7,15},{8,0},{9,1},... | collective-permute-start | bytes 884744 | tf_op jit(solution)/shard_map/ppermute | solution.py:271
  64.2 14.5 %collective-permute-start.15 = (bf16[3,384,128]{2,1,0:T(8,128)(2,1)S(1)}, bf16[3,384,128]{2,1,0:T(8,128)(2,1)S(1)}, u32[]{:S(2)}, u32[]{:S(2)}) collective-permute-start(bf16[3,384,128]{2,1,0:T(8,128)(2,1)S(1)} %copy-done.12), channel_id=1, source_target_pairs={{0,4},{1,5},{2,6},{3,7},{4,0},{5,1},{6,2},{7,3},{8,12},{9,13},{10,... | collective-permute-start | bytes 884744 | tf_op jit(solution)/shard_map/ppermute | solution.py:271
  67.9 27.6 %collective-permute-start.20 = (bf16[256,768]{1,0:T(8,128)(2,1)S(1)}, bf16[256,768]{1,0:T(8,128)(2,1)S(1)}, u32[]{:S(2)}, u32[]{:S(2)}) collective-permute-start(bf16[256,768]{1,0:T(8,128)(2,1)S(1)} %get-tuple-element.148), channel_id=1, source_target_pairs={{0,16},{1,17},{2,18},{3,19},{4,20},{5,21},{6,22},{7,23},{8,24},{9,... | collective-permute-start | bytes 1179656 | tf_op jit(solution)/shard_map/ppermute | solution.py:271
  69.7 14.9 %collective-permute-start.16 = (bf16[3,384,128]{2,1,0:T(8,128)(2,1)S(1)}, bf16[3,384,128]{2,1,0:T(8,128)(2,1)S(1)}, u32[]{:S(2)}, u32[]{:S(2)}) collective-permute-start(bf16[3,384,128]{2,1,0:T(8,128)(2,1)S(1)} %collective-permute-done.11.b_ref.refs_3_), channel_id=1, source_target_pairs={{0,4},{1,5},{2,6},{3,7},{4,0},{5,1},{6,2},{7,3},{8,12},{9,13},{10,... | collective-permute-start | bytes 884744 | tf_op jit(solution)/shard_map/ppermute | solution.py:271
  75.4 29.1 %collective-permute-start.24 = (bf16[256,768]{1,0:T(8,128)(2,1)S(1)}, bf16[256,768]{1,0:T(8,128)(2,1)S(1)}, u32[]{:S(2)}, u32[]{:S(2)}) collective-permute-start(bf16[256,768]{1,0:T(8,128)(2,1)S(1)} %get-tuple-element.157), channel_id=1, source_target_pairs={{0,16},{1,17},{2,18},{3,19},{4,20},{5,21},{6,22},{7,23},{8,24},{9,... | collective-permute-start | bytes 1179656 | tf_op jit(solution)/shard_map/ppermute | solution.py:271
  77.1 20.4 %collective-permute-start.18 = (bf16[3,384,128]{2,1,0:T(8,128)(2,1)S(1)}, bf16[3,384,128]{2,1,0:T(8,128)(2,1)S(1)}, u32[]{:S(2)}, u32[]{:S(2)}) collective-permute-start(bf16[3,384,128]{2,1,0:T(8,128)(2,1)S(1)} %copy-done.15), channel_id=1, source_target_pairs={{0,8},{1,9},{2,10},{3,11},{4,12},{5,13},{6,14},{7,15},{8,0},{9,1},... | collective-permute-start | bytes 884744 | tf_op jit(solution)/shard_map/ppermute | solution.py:271
  78.7 19.0 %collective-permute-start.22 = (bf16[3,384,128]{2,1,0:T(8,128)(2,1)S(1)}, bf16[3,384,128]{2,1,0:T(8,128)(2,1)S(1)}, u32[]{:S(2)}, u32[]{:S(2)}) collective-permute-start(bf16[3,384,128]{2,1,0:T(8,128)(2,1)S(1)} %collective-permute-done.19.b_ref.refs_3_), channel_id=1, source_target_pairs={{0,4},{1,5},{2,6},{3,7},{4,0},{5,1},{6,2},{7,3},{8,12},{9,13},{10,... | collective-permute-start | bytes 884744 | tf_op jit(solution)/shard_map/ppermute | solution.py:271
  84.6 15.1 %collective-permute-start.21 = (bf16[3,384,128]{2,1,0:T(8,128)(2,1)S(1)}, bf16[3,384,128]{2,1,0:T(8,128)(2,1)S(1)}, u32[]{:S(2)}, u32[]{:S(2)}) collective-permute-start(bf16[3,384,128]{2,1,0:T(8,128)(2,1)S(1)} %copy-done.7), channel_id=1, source_target_pairs={{0,4},{1,5},{2,6},{3,7},{4,0},{5,1},{6,2},{7,3},{8,12},{9,13},{10,... | collective-permute-start | bytes 884744 | tf_op jit(solution)/shard_map/ppermute | solution.py:271
  95.5 14.8 %collective-permute-start.25 = (bf16[3,384,128]{2,1,0:T(8,128)(2,1)S(1)}, bf16[3,384,128]{2,1,0:T(8,128)(2,1)S(1)}, u32[]{:S(2)}, u32[]{:S(2)}) collective-permute-start(bf16[3,384,128]{2,1,0:T(8,128)(2,1)S(1)} %copy-done.6), channel_id=1, source_target_pairs={{0,4},{1,5},{2,6},{3,7},{4,0},{5,1},{6,2},{7,3},{8,12},{9,13},{10,... | collective-permute-start | bytes 884744 | tf_op jit(solution)/shard_map/ppermute | solution.py:271
  97.6 11.9 %collective-permute-start.23 = (bf16[256,384]{1,0:T(8,128)(2,1)S(1)}, bf16[256,384]{1,0:T(8,128)(2,1)S(1)}, u32[]{:S(2)}, u32[]{:S(2)}) collective-permute-start(bf16[256,384]{1,0:T(8,128)(2,1)S(1)} %get-tuple-element.155), channel_id=1, source_target_pairs={{0,16},{1,17},{2,18},{3,19},{4,20},{5,21},{6,22},{7,23},{8,24},{9,... | collective-permute-start | bytes 589832 | tf_op jit(solution)/shard_map/ppermute | solution.py:271
  97.6 12.7 %collective-permute-start.26 = (bf16[3,384,128]{2,1,0:T(8,128)(2,1)S(1)}, bf16[3,384,128]{2,1,0:T(8,128)(2,1)S(1)}, u32[]{:S(2)}, u32[]{:S(2)}) collective-permute-start(bf16[3,384,128]{2,1,0:T(8,128)(2,1)S(1)} %collective-permute-done.18.b_ref.refs_3_), channel_id=1, source_target_pairs={{0,4},{1,5},{2,6},{3,7},{4,0},{5,1},{6,2},{7,3},{8,12},{9,13},{10,... | collective-permute-start | bytes 884744 | tf_op jit(solution)/shard_map/ppermute | solution.py:271
  110.2 13.2 %collective-permute-start.28 = (bf16[256,384]{1,0:T(8,128)(2,1)S(1)}, bf16[256,384]{1,0:T(8,128)(2,1)S(1)}, u32[]{:S(2)}, u32[]{:S(2)}) collective-permute-start(bf16[256,384]{1,0:T(8,128)(2,1)S(1)} %get-tuple-element.166), channel_id=1, source_target_pairs={{0,16},{1,17},{2,18},{3,19},{4,20},{5,21},{6,22},{7,23},{8,24},{9,... | collective-permute-start | bytes 589832 | tf_op jit(solution)/shard_map/ppermute | solution.py:271
  112.2 13.3 %collective-permute-start.27 = (bf16[256,384]{1,0:T(8,128)(2,1)S(1)}, bf16[256,384]{1,0:T(8,128)(2,1)S(1)}, u32[]{:S(2)}, u32[]{:S(2)}) collective-permute-start(bf16[256,384]{1,0:T(8,128)(2,1)S(1)} %get-tuple-element.164), channel_id=1, source_target_pairs={{0,16},{1,17},{2,18},{3,19},{4,20},{5,21},{6,22},{7,23},{8,24},{9,... | collective-permute-start | bytes 589832 | tf_op jit(solution)/shard_map/ppermute | solution.py:271
  128.8 7.0 %collective-permute-start.30 = (bf16[2,2,16,1536]{3,2,1,0:T(8,128)(2,1)S(1)}, bf16[2,2,16,1536]{3,2,1,0:T(8,128)(2,1)S(1)}, u32[]{:S(2)}, u32[]{:S(2)}) collective-permute-start(bf16[2,2,16,1536]{3,2,1,0:T(8,128)(2,1)S(1)} %get-tuple-element.171), channel_id=1, source_target_pairs={{0,2},{1,3},{2,0},{3,1},{4,6},{5,7},{6,4},{7,5},{8,10},{9,11},{10,... | collective-permute-start | bytes 589832 | tf_op jit(solution)/shard_map/ppermute | solution.py:271
  130.5 7.8 %collective-permute-start.31 = (bf16[2,2,16,1536]{3,2,1,0:T(8,128)(2,1)S(1)}, bf16[2,2,16,1536]{3,2,1,0:T(8,128)(2,1)S(1)}, u32[]{:S(2)}, u32[]{:S(2)}) collective-permute-start(bf16[2,2,16,1536]{3,2,1,0:T(8,128)(2,1)S(1)} %get-tuple-element.172), channel_id=1, source_target_pairs={{0,8},{1,9},{2,10},{3,11},{4,12},{5,13},{6,14},{7,15},{8,0},{9,1},... | collective-permute-start | bytes 589832 | tf_op jit(solution)/shard_map/ppermute | solution.py:271
  130.5 10.7 %collective-permute-start.32 = (bf16[2,2,16,1536]{3,2,1,0:T(8,128)(2,1)S(1)}, bf16[2,2,16,1536]{3,2,1,0:T(8,128)(2,1)S(1)}, u32[]{:S(2)}, u32[]{:S(2)}) collective-permute-start(bf16[2,2,16,1536]{3,2,1,0:T(8,128)(2,1)S(1)} %get-tuple-element.173), channel_id=1, source_target_pairs={{0,10},{1,11},{2,8},{3,9},{4,14},{5,15},{6,12},{7,13},{8,2},{9,3},... | collective-permute-start | bytes 589832 | tf_op jit(solution)/shard_map/ppermute | solution.py:271
  141.3 6.8 %collective-permute-start.33 = (bf16[2,16,1536]{2,1,0:T(8,128)(2,1)S(1)}, bf16[2,16,1536]{2,1,0:T(8,128)(2,1)S(1)}, u32[]{:S(2)}, u32[]{:S(2)}) collective-permute-start(bf16[2,16,1536]{2,1,0:T(8,128)(2,1)S(1)} %get-tuple-element.175), channel_id=1, source_target_pairs={{0,16},{1,17},{2,18},{3,19},{4,20},{5,21},{6,22},{7,23},{8,24},{9,... | collective-permute-start | bytes 294920 | tf_op jit(solution)/shard_map/ppermute | solution.py:271
  (20 other events, 170.0 us)

commit v7 on v5

--- a/solution.py
+++ b/solution.py
@@ -6,8 +6,6 @@
 from jax.sharding import PartitionSpec as P
 
 F32 = jnp.float32
-SHAPE = ((0, 1), (2, 2), (4, 2), (6, 2), (1, 1))
-CFG = {'us': [8, 0], 'flags': {'join_y0': True, 'join_zp0': True, 'own2_plain': True, 'near_y1': True, 'near_y2': False, 'near_y3': False, 'near_zp1': False, 'first_y2': True, 'first_zp1': True}, 'order': [('F', 0), ('F', 1), ('S', 0), ('F', 2), ('S', 1), ('F', 3), ('S', 2), ('F', 4), ('S', 3), ('S', 4)], 'ties': {('F', 1): [('F', 0)], ('F', 2): [('F', 1)], ('S', 0): [('F', 1)], ('F', 3): [('S', 0)], ('S', 1): [('F', 2)], ('F', 4): [('S', 1), ('F', 3)], ('S', 2): [('F', 3)], ('S', 3): [('F', 4)]}, 'y': {5: [('F', 0)], 6: [('F', 1)], 7: [('F', 1)], 8: [('F', 2)], 9: [('F', 2)]}, 'arrive': {}}
 BF16 = jnp.bfloat16
 LANES = 128
 AHEAD = 2
@@ -25,7 +23,7 @@
     blocks = units // LANES
     if blocks != 8:
         return [(i * LANES, LANES) for i in range(blocks)]
-    shape = SHAPE
+    shape = ((0, 1), (2, 2), (4, 2), (1, 1), (6, 1), (7, 1))
     return [(start * LANES, size * LANES) for start, size in shape]
 
 
@@ -189,8 +187,7 @@
     return per_device
 
 
-def call(body, outs, *args, scratch=(), flops=0, us=0):
-    moved = sum(v.size * v.dtype.itemsize for v in list(args) + list(outs))
+def call(body, outs, *args, scratch=(), us=0):
     return pl.pallas_call(
         body,
         out_shape=list(outs),
@@ -293,9 +290,7 @@
             stream.append(swap(values, at_y))
 
         for k in range(count):
-            own_w[k], given[k] = weight_chunk(
-                low, w_gate, w_up, w_down, *chunks[k]
-            )
+            own_w[k], given[k] = weight_chunk(low, w_gate, w_up, w_down, *chunks[k])
         over_y(own_w[0])
         zp_w[0] = swap(given[0], at_zp)
         over_y(own_w[1])
@@ -331,7 +326,6 @@
             route_experts,
             route_gates,
             scratch=[pltpu.VMEM((2, most, width), BF16)],
-            flops=4 * most * own_count * width,
         )
         other = swap(sent, at_zh)
 
@@ -342,35 +336,22 @@
                 flipped_ref[j] = flip_pairs(values, own_width)
 
         pair = shaped((2,) + block_shape, BF16)
-        if CFG["flags"]["join_y0"]:
-            mine, stream[0] = after(mine, stream[0])
-        if CFG["flags"]["join_zp0"]:
-            mine, zp_w[0] = after(mine, zp_w[0])
+        mine, stream[0] = after(mine, stream[0])
+        mine, zp_w[0] = after(mine, zp_w[0])
         plain, flipped = call(join_body, [pair, pair], mine, other)
-        if CFG["flags"]["own2_plain"]:
-            own_w[2], _ = after(own_w[2], plain)
+        own_w[2], _ = after(own_w[2], plain)
+        over_y(zp_w[0])
         over_y(own_w[2])
-        over_y(zp_w[0])
-        for k in range(1, count):
-            if k <= 2:
-                given[k], _ = after(given[k], plain)
-            else:
-                given[k], zp_w[k - 2] = after(given[k], zp_w[k - 2])
+        for k, first_done in ((1, sent), (2, plain)):
+            given[k], _ = after(given[k], first_done)
             zp_w[k] = swap(given[k], at_zp)
         near_rows = jnp.stack(
             [plain, swap(plain, at_x), swap(flipped, at_zp), swap(flipped, at_zp + at_x)]
         )
-        for at in (1, 2, 3):
-            if CFG["flags"][f"near_y{at}"]:
-                near_rows, stream[at] = after(near_rows, stream[at])
-        if CFG["flags"]["near_zp1"]:
-            near_rows, zp_w[1] = after(near_rows, zp_w[1])
+        near_rows, stream[1] = after(near_rows, stream[1])
         far_rows = swap(near_rows, at_core)
-        for at in (2,):
-            if CFG["flags"]["first_y2"]:
-                near_rows, stream[at] = after(near_rows, stream[at])
-        if CFG["flags"]["first_zp1"]:
-            near_rows, zp_w[1] = after(near_rows, zp_w[1])
+        near_rows, stream[3] = after(near_rows, stream[3])
+        near_rows, zp_w[1] = after(near_rows, zp_w[1])
         over_y(zp_w[1])
 
         slots = 16 * most
@@ -430,7 +411,7 @@
         pre, total = [None] * count, [None] * count
 
         def weights_of(k):
-            at = (k, k + 3) if k < 3 else (2 * k, 2 * k + 1)
+            at = ((0, 2), (1, 4), (3, 5))[k] if k < 3 else (2 * k, 2 * k + 1)
             return own_w[k], zp_w[k], stream[at[0]], stream[at[1]]
 
         def first(k, near_rows, far_rows):
@@ -441,7 +422,7 @@
                 near_rows,
                 far_rows,
                 *weights_of(k),
-                us=CFG["us"][0] * units // 256,
+                us=8 * units // 256,
             )
 
         def second(k):
@@ -460,7 +441,6 @@
                 swap(sent, at_zh),
                 *weights_of(k),
                 *held,
-                us=CFG["us"][1],
             )
 
         def held_back(values, firsts=(), seconds=()):
@@ -474,36 +454,47 @@
                 total[k] = [done.pop(0)]
             return values
 
-        def steps_of(names):
-            return [[k for kind, k in names if kind == want] for want in "FS"]
-
-        def emit_y(j):
-            k = j // 2
-            values = zp_w if (j % 2 or k < 3) else own_w
-            k = j - 3 if j < 6 else k
-            values[k] = held_back(values[k], *steps_of(CFG["y"][j]))
-            over_y(values[k])
-
-        pending = [5, 6, 7, 8, 9]
-        done_ops = []
-        while pending and not CFG["y"][pending[0]]:
-            emit_y(pending.pop(0))
-        for kind, k in CFG["order"]:
-            ties = steps_of(CFG["ties"].get((kind, k), []))
-            late = CFG["arrive"].get((kind, k), [])
-            values = near_rows if kind == "F" else pre[k][0]
-            if any(ties):
-                values = held_back(values, *ties)
-            for at in late:
-                values, stream[at] = after(values, stream[at])
-            if kind == "F":
-                first(k, values, far_rows)
-            else:
-                pre[k] = [values, pre[k][1]]
-                second(k)
-            done_ops.append((kind, k))
-            while pending and all(op in done_ops for op in CFG["y"][pending[0]]):
-                emit_y(pending.pop(0))
+        def first_after(k, *steps):
+            first(k, held_back(near_rows, *steps), far_rows)
+
+        def second_after(k, *steps):
+            pre[k] = [held_back(pre[k][0], *steps), pre[k][1]]
+            second(k)
+
+        def pair_exchange(k, *steps):
+            given[k] = held_back(given[k], *steps)
+            zp_w[k] = swap(given[k], at_zp)
+
+        def own_over_y(k, *steps):
+            own_w[k] = held_back(own_w[k], *steps)
+            over_y(own_w[k])
+
+        def pair_over_y(k, *steps):
+            zp_w[k] = held_back(zp_w[k], *steps)
+            over_y(zp_w[k])
+
+        first(0, near_rows, far_rows)
+        pair_exchange(3, [0])
+        pair_over_y(2, [0])
+        first_after(1, [0])
+        pair_exchange(4, [1])
+        own_over_y(3, [1])
+        pair_over_y(3, [1])
+        second_after(0, [1])
+        first_after(2, [1])
+        pair_exchange(5, [2])
+        own_over_y(4, [2])
+        pair_over_y(4, [2])
+        second_after(1, [2])
+        first_after(3, [], [0])
+        own_over_y(5, [3])
+        pair_over_y(5, [3])
+        second(2)
+        first_after(4, [3], [1])
+        second_after(3, [4])
+        first_after(5, [4], [3])
+        second_after(4, [5])
+        second(5)
         total = total[-1]
 
         def spread_body(keep_ref, recv_ref, own_ref, *outs):
@@ -566,8 +557,7 @@
                 route_experts,
                 route_gates,
                 scratch=[pltpu.VMEM((2, most, width), BF16)],
-                flops=4 * most * own_count * width,
-            )
+                )
         )
 
     return per_device

time: 158 us -> 151 us (0.956)
  waiting for transfers between devices: 83 us -> 65.2 us
  starting transfers between devices: 38.8 us -> 45.6 us
  Pallas kernels: 32.1 us -> 36.1 us
    ppermute x30 -> x34, waiting for transfers between devices: 83 us -> 65.2 us  [swap(): return lax.ppermute(values, ('fsdp', 'et'), pairs)]
    ppermute x30 -> x34, starting transfers between devices: 38.8 us -> 45.6 us  [swap(): return lax.ppermute(values, ('fsdp', 'et'), pairs)]
    pallas_call x15 -> x17, Pallas kernels: 20.6 us -> 22.8 us  [call(): pl.pallas_call(body, out_shape=list(outs), scratch_shapes=list(scratch),...]
    pallas_call x5 -> x6, Pallas kernels: 11.5 us -> 13.3 us  [weight_chunk(): pl.pallas_call(weight_chunk_body, out_shape=[out, out], grid_spec=pltpu.P...]
  transfers between devices with their start and end apart: 30 -> 34, of which waited for: 18 -> 19; matrix products, arithmetic and copies ran while one was open for 1% -> 1% of each run, Pallas kernels for 17% -> 21%
where the time goes in v7:
time: 151 us; the launch traced here: 150 us
  waiting for transfers between devices  65.2 us (43%)
  starting transfers between devices  45.6 us (30%)
  Pallas kernels  36.1 us (24%)
    ppermute x34, waiting for transfers between devices, swap(): return lax.ppermute(values, ('fsdp', 'et'), pairs)  65.2 us
    ppermute x34, starting transfers between devices, swap(): return lax.ppermute(values, ('fsdp', 'et'), pairs)  45.6 us
    pallas_call x17, Pallas kernels, call(): pl.pallas_call(body, out_shape=list(outs), scratch_shapes=list(scratch),...  22.8 us
    pallas_call x6, Pallas kernels, weight_chunk(): pl.pallas_call(weight_chunk_body, out_shape=[out, out], grid_spec=pltpu.P...  13.3 us
  transfers between devices with their start and end apart: 34, of which 19 were waited for; matrix products, arithmetic and copies ran while one was open for 1% of the time, Pallas kernels for 21%

profile of v7, /device:TPU:0, one launch (start us, length us, event | category | flops | bytes accessed | tf_op | source)
XLA Modules:
  0.0 150.4 jit_solution(11358177682964009453)
XLA Ops:
  0.7 2.1 %shard_map.87 = (bf16[3,384,128]{2,1,0:T(8,128)(2,1)}, bf16[3,384,128]{2,1,0:T(8,128)(2,1)}) custom-call(s32[1]{0:T(128)} %bitcast.low_ref, bf16[384,2048]{1,0:T(8,128)(2,1)} %refs_3_.11, bf16[384,2048]{1,0:T(8,128)(2,1)} %refs_4_.11, bf16[2048,384]{1,0:T(8,128)(2,1)} %refs_5_.11, bf16[384,2048]{1,0:T(8,128)(2,1)} %refs_3_.11, bf16[384,2048]{1,0:T(8,128)(2,1)} %refs_4_.11, ...), custom_call_target="tpu_custom_call" | custom-call | bytes 1024 | tf_op jit(solution)/shard_map/pallas_call | solution.py:250
  2.7 3.0 %collective-permute-start = (bf16[3,384,128]{2,1,0:T(8,128)(2,1)}, bf16[3,384,128]{2,1,0:T(8,128)(2,1)S(1)}, u32[]{:S(2)}, u32[]{:S(2)}) collective-permute-start(bf16[3,384,128]{2,1,0:T(8,128)(2,1)} %get-tuple-element.90.a_ref.refs_2_), channel_id=1, source_target_pairs={{0,4},{1,5},{2,6},{3,7},{4,0},{5,1},{6,2},{7,3},{8,12},{9,13},{10,... | collective-permute-start | bytes 884744 | tf_op jit(solution)/shard_map/ppermute | solution.py:268
  7.3 2.5 %shard_map.89 = (bf16[3,384,256]{2,1,0:T(8,128)(2,1)}, bf16[3,384,256]{2,1,0:T(8,128)(2,1)}) custom-call(s32[1]{0:T(128)} %bitcast.low_ref, bf16[384,2048]{1,0:T(8,128)(2,1)} %refs_3_.11, bf16[384,2048]{1,0:T(8,128)(2,1)} %refs_4_.11, bf16[2048,384]{1,0:T(8,128)(2,1)} %refs_5_.11, bf16[384,2048]{1,0:T(8,128)(2,1)} %refs_3_.11, bf16[384,2048]{1,0:T(8,128)(2,1)} %refs_4_.11, ...), custom_call_target="tpu_custom_call" | custom-call | bytes 1024 | tf_op jit(solution)/shard_map/pallas_call | solution.py:250
  11.1 2.7 %collective-permute-start.2 = (bf16[2,16,1536]{2,1,0:T(8,128)(2,1)S(1)}, bf16[2,16,1536]{2,1,0:T(8,128)(2,1)S(1)}, u32[]{:S(2)}, u32[]{:S(2)}) collective-permute-start(bf16[2,16,1536]{2,1,0:T(8,128)(2,1)S(1)} %get-tuple-element.94), channel_id=1, source_target_pairs={{0,16},{1,17},{2,18},{3,19},{4,20},{5,21},{6,22},{7,23},{8,24},{9,... | collective-permute-start | bytes 294920 | tf_op jit(solution)/shard_map/ppermute | solution.py:268
  22.7 2.5 %shard_map.90 = (bf16[3,384,256]{2,1,0:T(8,128)(2,1)}, bf16[3,384,256]{2,1,0:T(8,128)(2,1)}) custom-call(s32[1]{0:T(128)} %bitcast.low_ref, bf16[384,2048]{1,0:T(8,128)(2,1)} %refs_3_.11, bf16[384,2048]{1,0:T(8,128)(2,1)} %refs_4_.11, bf16[2048,384]{1,0:T(8,128)(2,1)} %refs_5_.11, bf16[384,2048]{1,0:T(8,128)(2,1)} %refs_3_.11, bf16[384,2048]{1,0:T(8,128)(2,1)} %refs_4_.11, ...), custom_call_target="tpu_custom_call" | custom-call | bytes 1024 | tf_op jit(solution)/shard_map/pallas_call | solution.py:250
  27.1 3.9 %collective-permute-done.5 = bf16[2,2,16,1536]{3,2,1,0:T(8,128)(2,1)} collective-permute-done((bf16[2,2,16,1536]{3,2,1,0:T(8,128)(2,1)S(1)}, bf16[2,2,16,1536]{3,2,1,0:T(8,128)(2,1)}, u32[]{:S(2)}, u32[]{:S(2)}) %collective-permute-start.5) | collective-permute-done | bytes 196640 | tf_op jit(solution)/shard_map/ppermute | solution.py:268
  32.3 2.3 %collective-permute-start.10 = (bf16[3,384,128]{2,1,0:T(8,128)(2,1)S(1)}, bf16[3,384,128]{2,1,0:T(8,128)(2,1)}, u32[]{:S(2)}, u32[]{:S(2)}) collective-permute-start(bf16[3,384,128]{2,1,0:T(8,128)(2,1)S(1)} %collective-permute-done.1.b_ref.refs_3_), channel_id=1, source_target_pairs={{0,4},{1,5},{2,6},{3,7},{4,0},{5,1},{6,2},{7,3},{8,12},{9,13},{10,... | collective-permute-start | bytes 884744 | tf_op jit(solution)/shard_map/ppermute | solution.py:268
  34.9 5.5 %collective-permute-done.7.c_ref.refs_4_ = bf16[3,384,256]{2,1,0:T(8,128)(2,1)S(1)} collective-permute-done((bf16[3,384,256]{2,1,0:T(8,128)(2,1)}, bf16[3,384,256]{2,1,0:T(8,128)(2,1)S(1)}, u32[]{:S(2)}, u32[]{:S(2)}) %collective-permute-start.7) | collective-permute-done | bytes 589856 | tf_op jit(solution)/shard_map/ppermute | solution.py:268
  40.4 3.3 %collective-permute-done.8.b_ref.refs_3_ = bf16[3,384,256]{2,1,0:T(8,128)(2,1)S(1)} collective-permute-done((bf16[3,384,256]{2,1,0:T(8,128)(2,1)}, bf16[3,384,256]{2,1,0:T(8,128)(2,1)S(1)}, u32[]{:S(2)}, u32[]{:S(2)}) %collective-permute-start.8) | collective-permute-done | bytes 589856 | tf_op jit(solution)/shard_map/ppermute | solution.py:268
  45.6 2.1 %shard_map.92 = (bf16[3,384,128]{2,1,0:T(8,128)(2,1)}, bf16[3,384,128]{2,1,0:T(8,128)(2,1)}) custom-call(s32[1]{0:T(128)} %bitcast.low_ref, bf16[384,2048]{1,0:T(8,128)(2,1)} %refs_3_.11, bf16[384,2048]{1,0:T(8,128)(2,1)} %refs_4_.11, bf16[2048,384]{1,0:T(8,128)(2,1)} %refs_5_.11, bf16[384,2048]{1,0:T(8,128)(2,1)} %refs_3_.11, bf16[384,2048]{1,0:T(8,128)(2,1)} %refs_4_.11, ...), custom_call_target="tpu_custom_call" | custom-call | bytes 1024 | tf_op jit(solution)/shard_map/pallas_call | solution.py:250
  47.7 2.1 %shard_map.93 = (bf16[3,384,128]{2,1,0:T(8,128)(2,1)}, bf16[3,384,128]{2,1,0:T(8,128)(2,1)}) custom-call(s32[1]{0:T(128)} %bitcast.low_ref, bf16[384,2048]{1,0:T(8,128)(2,1)} %refs_3_.11, bf16[384,2048]{1,0:T(8,128)(2,1)} %refs_4_.11, bf16[2048,384]{1,0:T(8,128)(2,1)} %refs_5_.11, bf16[384,2048]{1,0:T(8,128)(2,1)} %refs_3_.11, bf16[384,2048]{1,0:T(8,128)(2,1)} %refs_4_.11, ...), custom_call_target="tpu_custom_call" | custom-call | bytes 1024 | tf_op jit(solution)/shard_map/pallas_call | solution.py:250
  49.8 2.1 %shard_map.97 = (bf16[3,384,128]{2,1,0:T(8,128)(2,1)}, bf16[3,384,128]{2,1,0:T(8,128)(2,1)}) custom-call(s32[1]{0:T(128)} %bitcast.low_ref, bf16[384,2048]{1,0:T(8,128)(2,1)} %refs_3_.11, bf16[384,2048]{1,0:T(8,128)(2,1)} %refs_4_.11, bf16[2048,384]{1,0:T(8,128)(2,1)} %refs_5_.11, bf16[384,2048]{1,0:T(8,128)(2,1)} %refs_3_.11, bf16[384,2048]{1,0:T(8,128)(2,1)} %refs_4_.11, ...), custom_call_target="tpu_custom_call" | custom-call | bytes 1024 | tf_op jit(solution)/shard_map/pallas_call | solution.py:250
  52.9 2.0 %shard_map.91 = (f32[256,384]{1,0:T(8,128)S(1)}, bf16[256,384]{1,0:T(8,128)(2,1)S(1)}) custom-call(bf16[4,2,2,16,1536]{4,3,2,1,0:T(8,128)(2,1)S(1)} %pad_maximum_fusion.near_ref, bf16[4,2,2,16,1536]{4,3,2,1,0:T(8,128)(2,1)} %collective-permute-done.9.far_ref, bf16[3,384,128]{2,1,0:T(8,128)(2,1)S(1)} %copy-done.8, ...), custom_call_target="tpu_custom_call" | custom-call | flops 4000000000 | bytes 1024 | tf_op jit(solution)/shard_map/pallas_call | solution.py:191
  59.4 2.3 %shard_map.94 = (f32[256,768]{1,0:T(8,128)S(1)}, bf16[256,768]{1,0:T(8,128)(2,1)S(1)}) custom-call(bf16[4,2,2,16,1536]{4,3,2,1,0:T(8,128)(2,1)S(1)} %pad_maximum_fusion.near_ref, bf16[4,2,2,16,1536]{4,3,2,1,0:T(8,128)(2,1)} %collective-permute-done.9.far_ref, bf16[3,384,256]{2,1,0:T(8,128)(2,1)S(1)} %copy-done.2, ...), custom_call_target="tpu_custom_call" | custom-call | flops 8000000000 | bytes 1024 | tf_op jit(solution)/shard_map/pallas_call | solution.py:191
  61.7 2.4 %collective-permute-start.19 = (bf16[3,384,128]{2,1,0:T(8,128)(2,1)S(1)}, bf16[3,384,128]{2,1,0:T(8,128)(2,1)S(1)}, u32[]{:S(2)}, u32[]{:S(2)}) collective-permute-start(bf16[3,384,128]{2,1,0:T(8,128)(2,1)S(1)} %copy-done.16), channel_id=1, source_target_pairs={{0,8},{1,9},{2,10},{3,11},{4,12},{5,13},{6,14},{7,15},{8,0},{9,1},... | collective-permute-start | bytes 884744 | tf_op jit(solution)/shard_map/ppermute | solution.py:268
  65.6 3.4 %collective-permute-done.11.b_ref.refs_3_ = bf16[3,384,128]{2,1,0:T(8,128)(2,1)S(1)} collective-permute-done((bf16[3,384,128]{2,1,0:T(8,128)(2,1)S(1)}, bf16[3,384,128]{2,1,0:T(8,128)(2,1)S(1)}, u32[]{:S(2)}, u32[]{:S(2)}) %collective-permute-start.11) | collective-permute-done | bytes 294944 | tf_op jit(solution)/shard_map/ppermute | solution.py:268
  72.1 2.3 %shard_map.98 = (f32[256,768]{1,0:T(8,128)S(1)}, bf16[256,768]{1,0:T(8,128)(2,1)S(1)}) custom-call(bf16[4,2,2,16,1536]{4,3,2,1,0:T(8,128)(2,1)S(1)} %pad_maximum_fusion.near_ref, bf16[4,2,2,16,1536]{4,3,2,1,0:T(8,128)(2,1)} %collective-permute-done.9.far_ref, bf16[3,384,256]{2,1,0:T(8,128)(2,1)S(1)} %copy-done.3, ...), custom_call_target="tpu_custom_call" | custom-call | flops 8000000000 | bytes 1024 | tf_op jit(solution)/shard_map/pallas_call | solution.py:191
  75.3 2.7 %collective-permute-start.24 = (bf16[256,768]{1,0:T(8,128)(2,1)S(1)}, bf16[256,768]{1,0:T(8,128)(2,1)S(1)}, u32[]{:S(2)}, u32[]{:S(2)}) collective-permute-start(bf16[256,768]{1,0:T(8,128)(2,1)S(1)} %get-tuple-element.157), channel_id=1, source_target_pairs={{0,16},{1,17},{2,18},{3,19},{4,20},{5,21},{6,22},{7,23},{8,24},{9,... | collective-permute-start | bytes 1179656 | tf_op jit(solution)/shard_map/ppermute | solution.py:268
  81.0 3.7 %collective-permute-done.16.d_ref.refs_5_ = bf16[3,384,128]{2,1,0:T(8,128)(2,1)S(1)} collective-permute-done((bf16[3,384,128]{2,1,0:T(8,128)(2,1)S(1)}, bf16[3,384,128]{2,1,0:T(8,128)(2,1)S(1)}, u32[]{:S(2)}, u32[]{:S(2)}) %collective-permute-start.16) | collective-permute-done | bytes 294944 | tf_op jit(solution)/shard_map/ppermute | solution.py:268
  84.7 2.5 %collective-permute-start.21 = (bf16[3,384,128]{2,1,0:T(8,128)(2,1)S(1)}, bf16[3,384,128]{2,1,0:T(8,128)(2,1)S(1)}, u32[]{:S(2)}, u32[]{:S(2)}) collective-permute-start(bf16[3,384,128]{2,1,0:T(8,128)(2,1)S(1)} %copy-done.7), channel_id=1, source_target_pairs={{0,4},{1,5},{2,6},{3,7},{4,0},{5,1},{6,2},{7,3},{8,12},{9,13},{10,... | collective-permute-start | bytes 884744 | tf_op jit(solution)/shard_map/ppermute | solution.py:268
  89.1 6.1 %collective-permute-done.20.refs_1_ = bf16[256,768]{1,0:T(8,128)(2,1)S(1)} collective-permute-done((bf16[256,768]{1,0:T(8,128)(2,1)S(1)}, bf16[256,768]{1,0:T(8,128)(2,1)S(1)}, u32[]{:S(2)}, u32[]{:S(2)}) %collective-permute-start.20) | collective-permute-done | bytes 393248 | tf_op jit(solution)/shard_map/ppermute | solution.py:268
  96.2 2.1 %shard_map.99.refs_6_ = f32[2,256,1536]{2,1,0:T(8,128)S(1)} custom-call(f32[256,768]{1,0:T(8,128)S(1)} %get-tuple-element.147.refs_0_, bf16[256,768]{1,0:T(8,128)(2,1)S(1)} %collective-permute-done.20.refs_1_, bf16[3,384,256]{2,1,0:T(8,128)(2,1)S(1)} %copy-done.2, bf16[3,384,256]{2,1,0:T(8,128)(2,1)S(1)} %copy-done.5, ...), custom_call_target="tpu_custom_call" | custom-call | bytes 1024 | tf_op jit(solution)/shard_map/pallas_call | solution.py:191
  101.4 5.3 %collective-permute-done.24.refs_1_ = bf16[256,768]{1,0:T(8,128)(2,1)S(1)} collective-permute-done((bf16[256,768]{1,0:T(8,128)(2,1)S(1)}, bf16[256,768]{1,0:T(8,128)(2,1)S(1)}, u32[]{:S(2)}, u32[]{:S(2)}) %collective-permute-start.24) | collective-permute-done | bytes 393248 | tf_op jit(solution)/shard_map/ppermute | solution.py:268
  106.6 2.1 %shard_map.101.refs_6_ = f32[2,256,1536]{2,1,0:T(8,128)S(1)} custom-call(f32[256,768]{1,0:T(8,128)S(1)} %get-tuple-element.156.refs_0_, bf16[256,768]{1,0:T(8,128)(2,1)S(1)} %collective-permute-done.24.refs_1_, bf16[3,384,256]{2,1,0:T(8,128)(2,1)S(1)} %copy-done.3, bf16[3,384,256]{2,1,0:T(8,128)(2,1)} %collective-permute-done.12.b_ref.refs_3_, ...), custom_call_target="tpu_custom_call" | custom-call | bytes 1024 | tf_op jit(solution)/shard_map/pallas_call | solution.py:191
  111.5 3.0 %collective-permute-start.27 = (bf16[256,384]{1,0:T(8,128)(2,1)S(1)}, bf16[256,384]{1,0:T(8,128)(2,1)S(1)}, u32[]{:S(2)}, u32[]{:S(2)}) collective-permute-start(bf16[256,384]{1,0:T(8,128)(2,1)S(1)} %get-tuple-element.164), channel_id=1, source_target_pairs={{0,16},{1,17},{2,18},{3,19},{4,20},{5,21},{6,22},{7,23},{8,24},{9,... | collective-permute-start | bytes 589832 | tf_op jit(solution)/shard_map/ppermute | solution.py:268
  114.5 8.9 %collective-permute-done.28.refs_1_ = bf16[256,384]{1,0:T(8,128)(2,1)S(1)} collective-permute-done((bf16[256,384]{1,0:T(8,128)(2,1)S(1)}, bf16[256,384]{1,0:T(8,128)(2,1)S(1)}, u32[]{:S(2)}, u32[]{:S(2)}) %collective-permute-start.28) | collective-permute-done | bytes 196640 | tf_op jit(solution)/shard_map/ppermute | solution.py:268
  124.2 2.0 %collective-permute-done.27.refs_1_ = bf16[256,384]{1,0:T(8,128)(2,1)S(1)} collective-permute-done((bf16[256,384]{1,0:T(8,128)(2,1)S(1)}, bf16[256,384]{1,0:T(8,128)(2,1)S(1)}, u32[]{:S(2)}, u32[]{:S(2)}) %collective-permute-start.27) | collective-permute-done | bytes 196640 | tf_op jit(solution)/shard_map/ppermute | solution.py:268
  127.1 2.3 %collective-permute-done.29.recv_ref = bf16[4,2,2,16,1536]{4,3,2,1,0:T(8,128)(2,1)S(1)} collective-permute-done((bf16[4,2,2,16,1536]{4,3,2,1,0:T(8,128)(2,1)S(1)}, bf16[4,2,2,16,1536]{4,3,2,1,0:T(8,128)(2,1)S(1)}, u32[]{:S(2)}, u32[]{:S(2)}) %collective-permute-start.29) | collective-permute-done | bytes 786464 | tf_op jit(solution)/shard_map/ppermute | solution.py:268
  130.2 2.9 %collective-permute-start.32 = (bf16[2,2,16,1536]{3,2,1,0:T(8,128)(2,1)S(1)}, bf16[2,2,16,1536]{3,2,1,0:T(8,128)(2,1)S(1)}, u32[]{:S(2)}, u32[]{:S(2)}) collective-permute-start(bf16[2,2,16,1536]{3,2,1,0:T(8,128)(2,1)S(1)} %get-tuple-element.173), channel_id=1, source_target_pairs={{0,10},{1,11},{2,8},{3,9},{4,14},{5,15},{6,12},{7,13},{8,2},{9,3},... | collective-permute-start | bytes 589832 | tf_op jit(solution)/shard_map/ppermute | solution.py:268
  133.1 3.5 %collective-permute-done.30.x_ref = bf16[2,2,16,1536]{3,2,1,0:T(8,128)(2,1)S(1)} collective-permute-done((bf16[2,2,16,1536]{3,2,1,0:T(8,128)(2,1)S(1)}, bf16[2,2,16,1536]{3,2,1,0:T(8,128)(2,1)S(1)}, u32[]{:S(2)}, u32[]{:S(2)}) %collective-permute-start.30) | collective-permute-done | bytes 196640 | tf_op jit(solution)/shard_map/ppermute | solution.py:268
  138.0 4.0 %collective-permute-done.32.both_ref = bf16[2,2,16,1536]{3,2,1,0:T(8,128)(2,1)S(1)} collective-permute-done((bf16[2,2,16,1536]{3,2,1,0:T(8,128)(2,1)S(1)}, bf16[2,2,16,1536]{3,2,1,0:T(8,128)(2,1)S(1)}, u32[]{:S(2)}, u32[]{:S(2)}) %collective-permute-start.32) | collective-permute-done | bytes 196640 | tf_op jit(solution)/shard_map/ppermute | solution.py:268
  142.6 6.2 %collective-permute-done.33.other_ref = bf16[2,16,1536]{2,1,0:T(8,128)(2,1)S(1)} collective-permute-done((bf16[2,16,1536]{2,1,0:T(8,128)(2,1)S(1)}, bf16[2,16,1536]{2,1,0:T(8,128)(2,1)S(1)}, u32[]{:S(2)}, u32[]{:S(2)}) %collective-permute-start.33) | collective-permute-done | bytes 98336 | tf_op jit(solution)/shard_map/ppermute | solution.py:268
  (98 shorter events, 46.1 us)
Async XLA Ops:
  2.7 11.1 %collective-permute-start = (bf16[3,384,128]{2,1,0:T(8,128)(2,1)}, bf16[3,384,128]{2,1,0:T(8,128)(2,1)S(1)}, u32[]{:S(2)}, u32[]{:S(2)}) collective-permute-start(bf16[3,384,128]{2,1,0:T(8,128)(2,1)} %get-tuple-element.90.a_ref.refs_2_), channel_id=1, source_target_pairs={{0,4},{1,5},{2,6},{3,7},{4,0},{5,1},{6,2},{7,3},{8,12},{9,13},{10,... | collective-permute-start | bytes 884744 | tf_op jit(solution)/shard_map/ppermute | solution.py:268
  5.7 9.8 %collective-permute-start.1 = (bf16[3,384,128]{2,1,0:T(8,128)(2,1)}, bf16[3,384,128]{2,1,0:T(8,128)(2,1)S(1)}, u32[]{:S(2)}, u32[]{:S(2)}) collective-permute-start(bf16[3,384,128]{2,1,0:T(8,128)(2,1)} %get-tuple-element.92), channel_id=1, source_target_pairs={{0,8},{1,9},{2,10},{3,11},{4,12},{5,13},{6,14},{7,15},{8,0},{9,1},... | collective-permute-start | bytes 884744 | tf_op jit(solution)/shard_map/ppermute | solution.py:268
  9.8 22.4 %collective-permute-start.6 = (bf16[3,384,256]{2,1,0:T(8,128)(2,1)}, bf16[3,384,256]{2,1,0:T(8,128)(2,1)S(1)}, u32[]{:S(2)}, u32[]{:S(2)}) collective-permute-start(bf16[3,384,256]{2,1,0:T(8,128)(2,1)} %get-tuple-element.97.a_ref.refs_2_), channel_id=1, source_target_pairs={{0,4},{1,5},{2,6},{3,7},{4,0},{5,1},{6,2},{7,3},{8,12},{9,13},{10,... | collective-permute-start | bytes 1769480 | tf_op jit(solution)/shard_map/ppermute | solution.py:268
  17.5 7.7 %collective-permute-start.3 = (bf16[2,2,16,1536]{3,2,1,0:T(8,128)(2,1)S(1)}, bf16[2,2,16,1536]{3,2,1,0:T(8,128)(2,1)}, u32[]{:S(2)}, u32[]{:S(2)}) collective-permute-start(bf16[2,2,16,1536]{3,2,1,0:T(8,128)(2,1)S(1)} %get-tuple-element.95), channel_id=1, source_target_pairs={{0,2},{1,3},{2,0},{3,1},{4,6},{5,7},{6,4},{7,5},{8,10},{9,11},{10,... | collective-permute-start | bytes 589832 | tf_op jit(solution)/shard_map/ppermute | solution.py:268
  19.0 8.1 %collective-permute-start.4 = (bf16[2,2,16,1536]{3,2,1,0:T(8,128)(2,1)S(1)}, bf16[2,2,16,1536]{3,2,1,0:T(8,128)(2,1)}, u32[]{:S(2)}, u32[]{:S(2)}) collective-permute-start(bf16[2,2,16,1536]{3,2,1,0:T(8,128)(2,1)S(1)} %get-tuple-element.96), channel_id=1, source_target_pairs={{0,8},{1,9},{2,10},{3,11},{4,12},{5,13},{6,14},{7,15},{8,0},{9,1},... | collective-permute-start | bytes 589832 | tf_op jit(solution)/shard_map/ppermute | solution.py:268
  20.7 10.3 %collective-permute-start.5 = (bf16[2,2,16,1536]{3,2,1,0:T(8,128)(2,1)S(1)}, bf16[2,2,16,1536]{3,2,1,0:T(8,128)(2,1)}, u32[]{:S(2)}, u32[]{:S(2)}) collective-permute-start(bf16[2,2,16,1536]{3,2,1,0:T(8,128)(2,1)S(1)} %get-tuple-element.96), channel_id=1, source_target_pairs={{0,10},{1,11},{2,8},{3,9},{4,14},{5,15},{6,12},{7,13},{8,2},{9,3},... | collective-permute-start | bytes 589832 | tf_op jit(solution)/shard_map/ppermute | solution.py:268
  21.0 22.7 %collective-permute-start.8 = (bf16[3,384,256]{2,1,0:T(8,128)(2,1)}, bf16[3,384,256]{2,1,0:T(8,128)(2,1)S(1)}, u32[]{:S(2)}, u32[]{:S(2)}) collective-permute-start(bf16[3,384,256]{2,1,0:T(8,128)(2,1)} %get-tuple-element.103), channel_id=1, source_target_pairs={{0,8},{1,9},{2,10},{3,11},{4,12},{5,13},{6,14},{7,15},{8,0},{9,1},... | collective-permute-start | bytes 1769480 | tf_op jit(solution)/shard_map/ppermute | solution.py:268
  25.2 15.2 %collective-permute-start.7 = (bf16[3,384,256]{2,1,0:T(8,128)(2,1)}, bf16[3,384,256]{2,1,0:T(8,128)(2,1)S(1)}, u32[]{:S(2)}, u32[]{:S(2)}) collective-permute-start(bf16[3,384,256]{2,1,0:T(8,128)(2,1)} %get-tuple-element.100.a_ref.refs_2_), channel_id=1, source_target_pairs={{0,4},{1,5},{2,6},{3,7},{4,0},{5,1},{6,2},{7,3},{8,12},{9,13},{10,... | collective-permute-start | bytes 1769480 | tf_op jit(solution)/shard_map/ppermute | solution.py:268
  32.2 19.6 %collective-permute-start.9 = (bf16[4,2,2,16,1536]{4,3,2,1,0:T(8,128)(2,1)S(1)}, bf16[4,2,2,16,1536]{4,3,2,1,0:T(8,128)(2,1)}, u32[]{:S(2)}, u32[]{:S(2)}) collective-permute-start(bf16[4,2,2,16,1536]{4,3,2,1,0:T(8,128)(2,1)S(1)} %pad_maximum_fusion.near_ref), channel_id=1, source_target_pairs={{0,1},{1,0},{2,3},{3,2},{4,5},{5,4},{6,7},{7,6},{8,9},{9,8},{10,11... | collective-permute-start | bytes 2359304 | tf_op jit(solution)/shard_map/ppermute | solution.py:268
  32.3 19.6 %collective-permute-start.10 = (bf16[3,384,128]{2,1,0:T(8,128)(2,1)S(1)}, bf16[3,384,128]{2,1,0:T(8,128)(2,1)}, u32[]{:S(2)}, u32[]{:S(2)}) collective-permute-start(bf16[3,384,128]{2,1,0:T(8,128)(2,1)S(1)} %collective-permute-done.1.b_ref.refs_3_), channel_id=1, source_target_pairs={{0,4},{1,5},{2,6},{3,7},{4,0},{5,1},{6,2},{7,3},{8,12},{9,13},{10,... | collective-permute-start | bytes 884744 | tf_op jit(solution)/shard_map/ppermute | solution.py:268
  34.6 20.4 %collective-permute-start.12 = (bf16[3,384,256]{2,1,0:T(8,128)(2,1)}, bf16[3,384,256]{2,1,0:T(8,128)(2,1)}, u32[]{:S(2)}, u32[]{:S(2)}) collective-permute-start(bf16[3,384,256]{2,1,0:T(8,128)(2,1)} %get-tuple-element.114), channel_id=1, source_target_pairs={{0,8},{1,9},{2,10},{3,11},{4,12},{5,13},{6,14},{7,15},{8,0},{9,1},... | collective-permute-start | bytes 1769480 | tf_op jit(solution)/shard_map/ppermute | solution.py:268
  43.7 15.7 %collective-permute-start.13 = (bf16[3,384,256]{2,1,0:T(8,128)(2,1)S(1)}, bf16[3,384,256]{2,1,0:T(8,128)(2,1)}, u32[]{:S(2)}, u32[]{:S(2)}) collective-permute-start(bf16[3,384,256]{2,1,0:T(8,128)(2,1)S(1)} %collective-permute-done.8.b_ref.refs_3_), channel_id=1, source_target_pairs={{0,4},{1,5},{2,6},{3,7},{4,0},{5,1},{6,2},{7,3},{8,12},{9,13},{10,... | collective-permute-start | bytes 1769480 | tf_op jit(solution)/shard_map/ppermute | solution.py:268
  55.0 14.1 %collective-permute-start.11 = (bf16[3,384,128]{2,1,0:T(8,128)(2,1)S(1)}, bf16[3,384,128]{2,1,0:T(8,128)(2,1)S(1)}, u32[]{:S(2)}, u32[]{:S(2)}) collective-permute-start(bf16[3,384,128]{2,1,0:T(8,128)(2,1)S(1)} %copy-done.17), channel_id=1, source_target_pairs={{0,8},{1,9},{2,10},{3,11},{4,12},{5,13},{6,14},{7,15},{8,0},{9,1},... | collective-permute-start | bytes 884744 | tf_op jit(solution)/shard_map/ppermute | solution.py:268
  55.5 16.7 %collective-permute-start.17 = (bf16[3,384,256]{2,1,0:T(8,128)(2,1)}, bf16[3,384,256]{2,1,0:T(8,128)(2,1)S(1)}, u32[]{:S(2)}, u32[]{:S(2)}) collective-permute-start(bf16[3,384,256]{2,1,0:T(8,128)(2,1)} %collective-permute-done.12.b_ref.refs_3_), channel_id=1, source_target_pairs={{0,4},{1,5},{2,6},{3,7},{4,0},{5,1},{6,2},{7,3},{8,12},{9,13},{10,... | collective-permute-start | bytes 1769480 | tf_op jit(solution)/shard_map/ppermute | solution.py:268
  56.9 12.2 %collective-permute-start.14 = (bf16[256,384]{1,0:T(8,128)(2,1)S(1)}, bf16[256,384]{1,0:T(8,128)(2,1)S(1)}, u32[]{:S(2)}, u32[]{:S(2)}) collective-permute-start(bf16[256,384]{1,0:T(8,128)(2,1)S(1)} %get-tuple-element.125), channel_id=1, source_target_pairs={{0,16},{1,17},{2,18},{3,19},{4,20},{5,21},{6,22},{7,23},{8,24},{9,... | collective-permute-start | bytes 589832 | tf_op jit(solution)/shard_map/ppermute | solution.py:268
  61.7 13.5 %collective-permute-start.19 = (bf16[3,384,128]{2,1,0:T(8,128)(2,1)S(1)}, bf16[3,384,128]{2,1,0:T(8,128)(2,1)S(1)}, u32[]{:S(2)}, u32[]{:S(2)}) collective-permute-start(bf16[3,384,128]{2,1,0:T(8,128)(2,1)S(1)} %copy-done.16), channel_id=1, source_target_pairs={{0,8},{1,9},{2,10},{3,11},{4,12},{5,13},{6,14},{7,15},{8,0},{9,1},... | collective-permute-start | bytes 884744 | tf_op jit(solution)/shard_map/ppermute | solution.py:268
  64.2 15.0 %collective-permute-start.15 = (bf16[3,384,128]{2,1,0:T(8,128)(2,1)S(1)}, bf16[3,384,128]{2,1,0:T(8,128)(2,1)S(1)}, u32[]{:S(2)}, u32[]{:S(2)}) collective-permute-start(bf16[3,384,128]{2,1,0:T(8,128)(2,1)S(1)} %copy-done.12), channel_id=1, source_target_pairs={{0,4},{1,5},{2,6},{3,7},{4,0},{5,1},{6,2},{7,3},{8,12},{9,13},{10,... | collective-permute-start | bytes 884744 | tf_op jit(solution)/shard_map/ppermute | solution.py:268
  69.1 26.1 %collective-permute-start.20 = (bf16[256,768]{1,0:T(8,128)(2,1)S(1)}, bf16[256,768]{1,0:T(8,128)(2,1)S(1)}, u32[]{:S(2)}, u32[]{:S(2)}) collective-permute-start(bf16[256,768]{1,0:T(8,128)(2,1)S(1)} %get-tuple-element.148), channel_id=1, source_target_pairs={{0,16},{1,17},{2,18},{3,19},{4,20},{5,21},{6,22},{7,23},{8,24},{9,... | collective-permute-start | bytes 1179656 | tf_op jit(solution)/shard_map/ppermute | solution.py:268
  70.9 13.8 %collective-permute-start.16 = (bf16[3,384,128]{2,1,0:T(8,128)(2,1)S(1)}, bf16[3,384,128]{2,1,0:T(8,128)(2,1)S(1)}, u32[]{:S(2)}, u32[]{:S(2)}) collective-permute-start(bf16[3,384,128]{2,1,0:T(8,128)(2,1)S(1)} %collective-permute-done.11.b_ref.refs_3_), channel_id=1, source_target_pairs={{0,4},{1,5},{2,6},{3,7},{4,0},{5,1},{6,2},{7,3},{8,12},{9,13},{10,... | collective-permute-start | bytes 884744 | tf_op jit(solution)/shard_map/ppermute | solution.py:268
  75.3 31.4 %collective-permute-start.24 = (bf16[256,768]{1,0:T(8,128)(2,1)S(1)}, bf16[256,768]{1,0:T(8,128)(2,1)S(1)}, u32[]{:S(2)}, u32[]{:S(2)}) collective-permute-start(bf16[256,768]{1,0:T(8,128)(2,1)S(1)} %get-tuple-element.157), channel_id=1, source_target_pairs={{0,16},{1,17},{2,18},{3,19},{4,20},{5,21},{6,22},{7,23},{8,24},{9,... | collective-permute-start | bytes 1179656 | tf_op jit(solution)/shard_map/ppermute | solution.py:268
  78.0 20.3 %collective-permute-start.18 = (bf16[3,384,128]{2,1,0:T(8,128)(2,1)S(1)}, bf16[3,384,128]{2,1,0:T(8,128)(2,1)S(1)}, u32[]{:S(2)}, u32[]{:S(2)}) collective-permute-start(bf16[3,384,128]{2,1,0:T(8,128)(2,1)S(1)} %copy-done.15), channel_id=1, source_target_pairs={{0,8},{1,9},{2,10},{3,11},{4,12},{5,13},{6,14},{7,15},{8,0},{9,1},... | collective-permute-start | bytes 884744 | tf_op jit(solution)/shard_map/ppermute | solution.py:268
  79.2 19.2 %collective-permute-start.22 = (bf16[3,384,128]{2,1,0:T(8,128)(2,1)S(1)}, bf16[3,384,128]{2,1,0:T(8,128)(2,1)S(1)}, u32[]{:S(2)}, u32[]{:S(2)}) collective-permute-start(bf16[3,384,128]{2,1,0:T(8,128)(2,1)S(1)} %collective-permute-done.19.b_ref.refs_3_), channel_id=1, source_target_pairs={{0,4},{1,5},{2,6},{3,7},{4,0},{5,1},{6,2},{7,3},{8,12},{9,13},{10,... | collective-permute-start | bytes 884744 | tf_op jit(solution)/shard_map/ppermute | solution.py:268
  84.7 14.8 %collective-permute-start.21 = (bf16[3,384,128]{2,1,0:T(8,128)(2,1)S(1)}, bf16[3,384,128]{2,1,0:T(8,128)(2,1)S(1)}, u32[]{:S(2)}, u32[]{:S(2)}) collective-permute-start(bf16[3,384,128]{2,1,0:T(8,128)(2,1)S(1)} %copy-done.7), channel_id=1, source_target_pairs={{0,4},{1,5},{2,6},{3,7},{4,0},{5,1},{6,2},{7,3},{8,12},{9,13},{10,... | collective-permute-start | bytes 884744 | tf_op jit(solution)/shard_map/ppermute | solution.py:268
  95.2 14.4 %collective-permute-start.25 = (bf16[3,384,128]{2,1,0:T(8,128)(2,1)S(1)}, bf16[3,384,128]{2,1,0:T(8,128)(2,1)S(1)}, u32[]{:S(2)}, u32[]{:S(2)}) collective-permute-start(bf16[3,384,128]{2,1,0:T(8,128)(2,1)S(1)} %copy-done.6), channel_id=1, source_target_pairs={{0,4},{1,5},{2,6},{3,7},{4,0},{5,1},{6,2},{7,3},{8,12},{9,13},{10,... | collective-permute-start | bytes 884744 | tf_op jit(solution)/shard_map/ppermute | solution.py:268
  98.3 10.5 %collective-permute-start.23 = (bf16[256,384]{1,0:T(8,128)(2,1)S(1)}, bf16[256,384]{1,0:T(8,128)(2,1)S(1)}, u32[]{:S(2)}, u32[]{:S(2)}) collective-permute-start(bf16[256,384]{1,0:T(8,128)(2,1)S(1)} %get-tuple-element.155), channel_id=1, source_target_pairs={{0,16},{1,17},{2,18},{3,19},{4,20},{5,21},{6,22},{7,23},{8,24},{9,... | collective-permute-start | bytes 589832 | tf_op jit(solution)/shard_map/ppermute | solution.py:268
  98.4 11.3 %collective-permute-start.26 = (bf16[3,384,128]{2,1,0:T(8,128)(2,1)S(1)}, bf16[3,384,128]{2,1,0:T(8,128)(2,1)S(1)}, u32[]{:S(2)}, u32[]{:S(2)}) collective-permute-start(bf16[3,384,128]{2,1,0:T(8,128)(2,1)S(1)} %collective-permute-done.18.b_ref.refs_3_), channel_id=1, source_target_pairs={{0,4},{1,5},{2,6},{3,7},{4,0},{5,1},{6,2},{7,3},{8,12},{9,13},{10,... | collective-permute-start | bytes 884744 | tf_op jit(solution)/shard_map/ppermute | solution.py:268
  109.5 13.9 %collective-permute-start.28 = (bf16[256,384]{1,0:T(8,128)(2,1)S(1)}, bf16[256,384]{1,0:T(8,128)(2,1)S(1)}, u32[]{:S(2)}, u32[]{:S(2)}) collective-permute-start(bf16[256,384]{1,0:T(8,128)(2,1)S(1)} %get-tuple-element.166), channel_id=1, source_target_pairs={{0,16},{1,17},{2,18},{3,19},{4,20},{5,21},{6,22},{7,23},{8,24},{9,... | collective-permute-start | bytes 589832 | tf_op jit(solution)/shard_map/ppermute | solution.py:268
  111.5 14.7 %collective-permute-start.27 = (bf16[256,384]{1,0:T(8,128)(2,1)S(1)}, bf16[256,384]{1,0:T(8,128)(2,1)S(1)}, u32[]{:S(2)}, u32[]{:S(2)}) collective-permute-start(bf16[256,384]{1,0:T(8,128)(2,1)S(1)} %get-tuple-element.164), channel_id=1, source_target_pairs={{0,16},{1,17},{2,18},{3,19},{4,20},{5,21},{6,22},{7,23},{8,24},{9,... | collective-permute-start | bytes 589832 | tf_op jit(solution)/shard_map/ppermute | solution.py:268
  129.5 7.0 %collective-permute-start.30 = (bf16[2,2,16,1536]{3,2,1,0:T(8,128)(2,1)S(1)}, bf16[2,2,16,1536]{3,2,1,0:T(8,128)(2,1)S(1)}, u32[]{:S(2)}, u32[]{:S(2)}) collective-permute-start(bf16[2,2,16,1536]{3,2,1,0:T(8,128)(2,1)S(1)} %get-tuple-element.171), channel_id=1, source_target_pairs={{0,2},{1,3},{2,0},{3,1},{4,6},{5,7},{6,4},{7,5},{8,10},{9,11},{10,... | collective-permute-start | bytes 589832 | tf_op jit(solution)/shard_map/ppermute | solution.py:268
  130.2 7.8 %collective-permute-start.31 = (bf16[2,2,16,1536]{3,2,1,0:T(8,128)(2,1)S(1)}, bf16[2,2,16,1536]{3,2,1,0:T(8,128)(2,1)S(1)}, u32[]{:S(2)}, u32[]{:S(2)}) collective-permute-start(bf16[2,2,16,1536]{3,2,1,0:T(8,128)(2,1)S(1)} %get-tuple-element.172), channel_id=1, source_target_pairs={{0,8},{1,9},{2,10},{3,11},{4,12},{5,13},{6,14},{7,15},{8,0},{9,1},... | collective-permute-start | bytes 589832 | tf_op jit(solution)/shard_map/ppermute | solution.py:268
  130.2 11.7 %collective-permute-start.32 = (bf16[2,2,16,1536]{3,2,1,0:T(8,128)(2,1)S(1)}, bf16[2,2,16,1536]{3,2,1,0:T(8,128)(2,1)S(1)}, u32[]{:S(2)}, u32[]{:S(2)}) collective-permute-start(bf16[2,2,16,1536]{3,2,1,0:T(8,128)(2,1)S(1)} %get-tuple-element.173), channel_id=1, source_target_pairs={{0,10},{1,11},{2,8},{3,9},{4,14},{5,15},{6,12},{7,13},{8,2},{9,3},... | collective-permute-start | bytes 589832 | tf_op jit(solution)/shard_map/ppermute | solution.py:268
  142.0 6.8 %collective-permute-start.33 = (bf16[2,16,1536]{2,1,0:T(8,128)(2,1)S(1)}, bf16[2,16,1536]{2,1,0:T(8,128)(2,1)S(1)}, u32[]{:S(2)}, u32[]{:S(2)}) collective-permute-start(bf16[2,16,1536]{2,1,0:T(8,128)(2,1)S(1)} %get-tuple-element.175), channel_id=1, source_target_pairs={{0,16},{1,17},{2,18},{3,19},{4,20},{5,21},{6,22},{7,23},{8,24},{9,... | collective-permute-start | bytes 294920 | tf_op jit(solution)/shard_map/ppermute | solution.py:268
  (20 other events, 170.4 us)

commit v8 on v7

--- a/solution.py
+++ b/solution.py
@@ -260,6 +260,36 @@
     )(low, w_gate, w_up, w_down, w_gate, w_up, w_down)
 
 
+def weight_part_body(low_ref, gate, up, down, out):
+    out[0] = gate[...]
+    out[1] = up[...]
+    out[2] = down[...].T
+
+
+def weight_part(low, w_gate, w_up, w_down, lo, size, kept):
+    own_width, hidden_units = w_gate.shape
+    half = hidden_units // 2 // size
+
+    def block(low_ref):
+        return lo // size + half * (low_ref[0] if kept else 1 - low_ref[0])
+
+    across = pl.BlockSpec((own_width, size), lambda i, low_ref: (0, block(low_ref)))
+    down = pl.BlockSpec((size, own_width), lambda i, low_ref: (block(low_ref), 0))
+    out = shaped((3, own_width, size), BF16)
+    return pl.pallas_call(
+        weight_part_body,
+        out_shape=out,
+        grid_spec=pltpu.PrefetchScalarGridSpec(
+            num_scalar_prefetch=1,
+            grid=(1,),
+            in_specs=[across, across, down],
+            out_specs=pl.BlockSpec(out.shape, lambda i, low_ref: (0, 0, 0)),
+        ),
+        compiler_params=pltpu.CompilerParams(vmem_limit_bytes=60 * 1024 * 1024),
+        cost_estimate=pl.CostEstimate(flops=0, bytes_accessed=1024, transcendentals=0),
+    )(low, w_gate, w_up, w_down)
+
+
 def make_fused(n_fsdp, n_et):
     world = n_fsdp * n_et
 
@@ -290,6 +320,10 @@
             stream.append(swap(values, at_y))
 
         for k in range(count):
+            if k == 0:
+                own_w[0] = weight_part(low, w_gate, w_up, w_down, *chunks[0], True)
+                given[0] = weight_part(low, w_gate, w_up, w_down, *chunks[0], False)
+                continue
             own_w[k], given[k] = weight_chunk(low, w_gate, w_up, w_down, *chunks[k])
         over_y(own_w[0])
         zp_w[0] = swap(given[0], at_zp)

time: 151 us -> 155 us (1.026)
  waiting for transfers between devices: 65.2 us -> 67 us
  Pallas kernels: 36.1 us -> 37.7 us
    pallas_call x0 -> x2, Pallas kernels: none -> 3.61 us  [weight_part(): pl.pallas_call(weight_part_body, out_shape=out, grid_spec=pltpu.PrefetchS...]
    pallas_call x6 -> x5, Pallas kernels: 13.3 us -> 11.2 us  [weight_chunk(): pl.pallas_call(weight_chunk_body, out_shape=[out, out], grid_spec=pltpu.P...]
    ppermute x34, waiting for transfers between devices: 65.2 us -> 67 us  [swap(): return lax.ppermute(values, ('fsdp', 'et'), pairs)]
  transfers between devices with their start and end apart: 34 -> 34, of which waited for: 19 -> 18; matrix products, arithmetic and copies ran while one was open for 1% -> 1% of each run, Pallas kernels for 21% -> 22%
where the time goes in v8:
time: 155 us; the launch traced here: 154 us
  waiting for transfers between devices  67 us (43%)
  starting transfers between devices  45.1 us (29%)
  Pallas kernels  37.7 us (24%)
  local copies, waits for them, and re-layouts  2.04 us (1%)
    ppermute x34, waiting for transfers between devices, swap(): return lax.ppermute(values, ('fsdp', 'et'), pairs)  67 us
    ppermute x34, starting transfers between devices, swap(): return lax.ppermute(values, ('fsdp', 'et'), pairs)  45.1 us
    pallas_call x17, Pallas kernels, call(): pl.pallas_call(body, out_shape=list(outs), scratch_shapes=list(scratch),...  22.9 us
    pallas_call x5, Pallas kernels, weight_chunk(): pl.pallas_call(weight_chunk_body, out_shape=[out, out], grid_spec=pltpu.P...  11.2 us
    pallas_call x2, Pallas kernels, weight_part(): pl.pallas_call(weight_part_body, out_shape=out, grid_spec=pltpu.PrefetchS...  3.61 us
  transfers between devices with their start and end apart: 34, of which 18 were waited for; matrix products, arithmetic and copies ran while one was open for 1% of the time, Pallas kernels for 22%

profile of v8, /device:TPU:0, one launch (start us, length us, event | category | flops | bytes accessed | tf_op | source)
XLA Modules:
  0.0 154.1 jit_solution(6007515794734966701)
XLA Ops:
  2.5 3.0 %collective-permute-start = (bf16[3,384,128]{2,1,0:T(8,128)(2,1)}, bf16[3,384,128]{2,1,0:T(8,128)(2,1)S(1)}, u32[]{:S(2)}, u32[]{:S(2)}) collective-permute-start(bf16[3,384,128]{2,1,0:T(8,128)(2,1)} %shard_map.87.a_ref.refs_2_), channel_id=1, source_target_pairs={{0,4},{1,5},{2,6},{3,7},{4,0},{5,1},{6,2},{7,3},{8,12},{9,13},{10,... | collective-permute-start | bytes 884744 | tf_op jit(solution)/shard_map/ppermute | solution.py:298
  8.9 2.5 %shard_map.90 = (bf16[3,384,256]{2,1,0:T(8,128)(2,1)}, bf16[3,384,256]{2,1,0:T(8,128)(2,1)}) custom-call(s32[1]{0:T(128)} %bitcast.low_ref, bf16[384,2048]{1,0:T(8,128)(2,1)} %refs_3_.9, bf16[384,2048]{1,0:T(8,128)(2,1)} %refs_4_.9, bf16[2048,384]{1,0:T(8,128)(2,1)} %refs_5_.9, bf16[384,2048]{1,0:T(8,128)(2,1)} %refs_3_.9, bf16[384,2048]{1,0:T(8,128)(2,1)} %refs_4_.9, ...), custom_call_target="tpu_custom_call" | custom-call | bytes 1024 | tf_op jit(solution)/shard_map/pallas_call | solution.py:250
  12.7 2.7 %collective-permute-start.2 = (bf16[2,16,1536]{2,1,0:T(8,128)(2,1)S(1)}, bf16[2,16,1536]{2,1,0:T(8,128)(2,1)S(1)}, u32[]{:S(2)}, u32[]{:S(2)}) collective-permute-start(bf16[2,16,1536]{2,1,0:T(8,128)(2,1)S(1)} %get-tuple-element.90), channel_id=1, source_target_pairs={{0,16},{1,17},{2,18},{3,19},{4,20},{5,21},{6,22},{7,23},{8,24},{9,... | collective-permute-start | bytes 294920 | tf_op jit(solution)/shard_map/ppermute | solution.py:298
  24.3 2.5 %shard_map.91 = (bf16[3,384,256]{2,1,0:T(8,128)(2,1)}, bf16[3,384,256]{2,1,0:T(8,128)(2,1)}) custom-call(s32[1]{0:T(128)} %bitcast.low_ref, bf16[384,2048]{1,0:T(8,128)(2,1)} %refs_3_.9, bf16[384,2048]{1,0:T(8,128)(2,1)} %refs_4_.9, bf16[2048,384]{1,0:T(8,128)(2,1)} %refs_5_.9, bf16[384,2048]{1,0:T(8,128)(2,1)} %refs_3_.9, bf16[384,2048]{1,0:T(8,128)(2,1)} %refs_4_.9, ...), custom_call_target="tpu_custom_call" | custom-call | bytes 1024 | tf_op jit(solution)/shard_map/pallas_call | solution.py:250
  28.6 3.8 %collective-permute-done.5 = bf16[2,2,16,1536]{3,2,1,0:T(8,128)(2,1)S(1)} collective-permute-done((bf16[2,2,16,1536]{3,2,1,0:T(8,128)(2,1)S(1)}, bf16[2,2,16,1536]{3,2,1,0:T(8,128)(2,1)S(1)}, u32[]{:S(2)}, u32[]{:S(2)}) %collective-permute-start.5) | collective-permute-done | bytes 196640 | tf_op jit(solution)/shard_map/ppermute | solution.py:298
  34.4 2.3 %collective-permute-start.10 = (bf16[3,384,128]{2,1,0:T(8,128)(2,1)S(1)}, bf16[3,384,128]{2,1,0:T(8,128)(2,1)}, u32[]{:S(2)}, u32[]{:S(2)}) collective-permute-start(bf16[3,384,128]{2,1,0:T(8,128)(2,1)S(1)} %collective-permute-done.1.b_ref.refs_3_), channel_id=1, source_target_pairs={{0,4},{1,5},{2,6},{3,7},{4,0},{5,1},{6,2},{7,3},{8,12},{9,13},{10,... | collective-permute-start | bytes 884744 | tf_op jit(solution)/shard_map/ppermute | solution.py:298
  37.0 3.9 %collective-permute-done.7.c_ref.refs_4_ = bf16[3,384,256]{2,1,0:T(8,128)(2,1)S(1)} collective-permute-done((bf16[3,384,256]{2,1,0:T(8,128)(2,1)}, bf16[3,384,256]{2,1,0:T(8,128)(2,1)S(1)}, u32[]{:S(2)}, u32[]{:S(2)}) %collective-permute-start.7) | collective-permute-done | bytes 589856 | tf_op jit(solution)/shard_map/ppermute | solution.py:298
  40.9 3.9 %collective-permute-done.8.b_ref.refs_3_ = bf16[3,384,256]{2,1,0:T(8,128)(2,1)S(1)} collective-permute-done((bf16[3,384,256]{2,1,0:T(8,128)(2,1)}, bf16[3,384,256]{2,1,0:T(8,128)(2,1)S(1)}, u32[]{:S(2)}, u32[]{:S(2)}) %collective-permute-start.8) | collective-permute-done | bytes 589856 | tf_op jit(solution)/shard_map/ppermute | solution.py:298
  46.6 2.1 %shard_map.93 = (bf16[3,384,128]{2,1,0:T(8,128)(2,1)}, bf16[3,384,128]{2,1,0:T(8,128)(2,1)}) custom-call(s32[1]{0:T(128)} %bitcast.low_ref, bf16[384,2048]{1,0:T(8,128)(2,1)} %refs_3_.9, bf16[384,2048]{1,0:T(8,128)(2,1)} %refs_4_.9, bf16[2048,384]{1,0:T(8,128)(2,1)} %refs_5_.9, bf16[384,2048]{1,0:T(8,128)(2,1)} %refs_3_.9, bf16[384,2048]{1,0:T(8,128)(2,1)} %refs_4_.9, ...), custom_call_target="tpu_custom_call" | custom-call | bytes 1024 | tf_op jit(solution)/shard_map/pallas_call | solution.py:250
  48.7 2.1 %shard_map.94 = (bf16[3,384,128]{2,1,0:T(8,128)(2,1)}, bf16[3,384,128]{2,1,0:T(8,128)(2,1)}) custom-call(s32[1]{0:T(128)} %bitcast.low_ref, bf16[384,2048]{1,0:T(8,128)(2,1)} %refs_3_.9, bf16[384,2048]{1,0:T(8,128)(2,1)} %refs_4_.9, bf16[2048,384]{1,0:T(8,128)(2,1)} %refs_5_.9, bf16[384,2048]{1,0:T(8,128)(2,1)} %refs_3_.9, bf16[384,2048]{1,0:T(8,128)(2,1)} %refs_4_.9, ...), custom_call_target="tpu_custom_call" | custom-call | bytes 1024 | tf_op jit(solution)/shard_map/pallas_call | solution.py:250
  50.7 2.1 %shard_map.98 = (bf16[3,384,128]{2,1,0:T(8,128)(2,1)}, bf16[3,384,128]{2,1,0:T(8,128)(2,1)}) custom-call(s32[1]{0:T(128)} %bitcast.low_ref, bf16[384,2048]{1,0:T(8,128)(2,1)} %refs_3_.9, bf16[384,2048]{1,0:T(8,128)(2,1)} %refs_4_.9, bf16[2048,384]{1,0:T(8,128)(2,1)} %refs_5_.9, bf16[384,2048]{1,0:T(8,128)(2,1)} %refs_3_.9, bf16[384,2048]{1,0:T(8,128)(2,1)} %refs_4_.9, ...), custom_call_target="tpu_custom_call" | custom-call | bytes 1024 | tf_op jit(solution)/shard_map/pallas_call | solution.py:250
  53.9 2.0 %shard_map.92 = (f32[256,384]{1,0:T(8,128)S(1)}, bf16[256,384]{1,0:T(8,128)(2,1)S(1)}) custom-call(bf16[4,2,2,16,1536]{4,3,2,1,0:T(8,128)(2,1)S(1)} %pad_maximum_fusion.near_ref, bf16[4,2,2,16,1536]{4,3,2,1,0:T(8,128)(2,1)} %collective-permute-done.9.far_ref, bf16[3,384,128]{2,1,0:T(8,128)(2,1)S(1)} %copy-done, ...), custom_call_target="tpu_custom_call" | custom-call | flops 4000000000 | bytes 1024 | tf_op jit(solution)/shard_map/pallas_call | solution.py:191
  60.5 2.3 %shard_map.95 = (f32[256,768]{1,0:T(8,128)S(1)}, bf16[256,768]{1,0:T(8,128)(2,1)S(1)}) custom-call(bf16[4,2,2,16,1536]{4,3,2,1,0:T(8,128)(2,1)S(1)} %pad_maximum_fusion.near_ref, bf16[4,2,2,16,1536]{4,3,2,1,0:T(8,128)(2,1)} %collective-permute-done.9.far_ref, bf16[3,384,256]{2,1,0:T(8,128)(2,1)S(1)} %copy-done.3, ...), custom_call_target="tpu_custom_call" | custom-call | flops 8000000000 | bytes 1024 | tf_op jit(solution)/shard_map/pallas_call | solution.py:191
  63.1 2.3 %collective-permute-start.15 = (bf16[3,384,128]{2,1,0:T(8,128)(2,1)S(1)}, bf16[3,384,128]{2,1,0:T(8,128)(2,1)S(1)}, u32[]{:S(2)}, u32[]{:S(2)}) collective-permute-start(bf16[3,384,128]{2,1,0:T(8,128)(2,1)S(1)} %copy-done.12), channel_id=1, source_target_pairs={{0,4},{1,5},{2,6},{3,7},{4,0},{5,1},{6,2},{7,3},{8,12},{9,13},{10,... | collective-permute-start | bytes 884744 | tf_op jit(solution)/shard_map/ppermute | solution.py:298
  65.4 5.7 %collective-permute-done.11.b_ref.refs_3_ = bf16[3,384,128]{2,1,0:T(8,128)(2,1)S(1)} collective-permute-done((bf16[3,384,128]{2,1,0:T(8,128)(2,1)S(1)}, bf16[3,384,128]{2,1,0:T(8,128)(2,1)S(1)}, u32[]{:S(2)}, u32[]{:S(2)}) %collective-permute-start.11) | collective-permute-done | bytes 294944 | tf_op jit(solution)/shard_map/ppermute | solution.py:298
  71.1 2.4 %collective-permute-start.20 = (bf16[256,768]{1,0:T(8,128)(2,1)S(1)}, bf16[256,768]{1,0:T(8,128)(2,1)S(1)}, u32[]{:S(2)}, u32[]{:S(2)}) collective-permute-start(bf16[256,768]{1,0:T(8,128)(2,1)S(1)} %get-tuple-element.144), channel_id=1, source_target_pairs={{0,16},{1,17},{2,18},{3,19},{4,20},{5,21},{6,22},{7,23},{8,24},{9,... | collective-permute-start | bytes 1179656 | tf_op jit(solution)/shard_map/ppermute | solution.py:298
  75.4 2.3 %shard_map.99 = (f32[256,768]{1,0:T(8,128)S(1)}, bf16[256,768]{1,0:T(8,128)(2,1)S(1)}) custom-call(bf16[4,2,2,16,1536]{4,3,2,1,0:T(8,128)(2,1)S(1)} %pad_maximum_fusion.near_ref, bf16[4,2,2,16,1536]{4,3,2,1,0:T(8,128)(2,1)} %collective-permute-done.9.far_ref, bf16[3,384,256]{2,1,0:T(8,128)(2,1)S(1)} %copy-done.4, ...), custom_call_target="tpu_custom_call" | custom-call | flops 8000000000 | bytes 1024 | tf_op jit(solution)/shard_map/pallas_call | solution.py:191
  80.5 2.0 %collective-permute-start.22 = (bf16[3,384,128]{2,1,0:T(8,128)(2,1)S(1)}, bf16[3,384,128]{2,1,0:T(8,128)(2,1)S(1)}, u32[]{:S(2)}, u32[]{:S(2)}) collective-permute-start(bf16[3,384,128]{2,1,0:T(8,128)(2,1)S(1)} %collective-permute-done.19.b_ref.refs_3_), channel_id=1, source_target_pairs={{0,4},{1,5},{2,6},{3,7},{4,0},{5,1},{6,2},{7,3},{8,12},{9,13},{10,... | collective-permute-start | bytes 884744 | tf_op jit(solution)/shard_map/ppermute | solution.py:298
  82.5 3.6 %collective-permute-done.16.d_ref.refs_5_ = bf16[3,384,128]{2,1,0:T(8,128)(2,1)S(1)} collective-permute-done((bf16[3,384,128]{2,1,0:T(8,128)(2,1)S(1)}, bf16[3,384,128]{2,1,0:T(8,128)(2,1)S(1)}, u32[]{:S(2)}, u32[]{:S(2)}) %collective-permute-start.16) | collective-permute-done | bytes 294944 | tf_op jit(solution)/shard_map/ppermute | solution.py:298
  89.5 7.6 %collective-permute-done.20.refs_1_ = bf16[256,768]{1,0:T(8,128)(2,1)S(1)} collective-permute-done((bf16[256,768]{1,0:T(8,128)(2,1)S(1)}, bf16[256,768]{1,0:T(8,128)(2,1)S(1)}, u32[]{:S(2)}, u32[]{:S(2)}) %collective-permute-start.20) | collective-permute-done | bytes 393248 | tf_op jit(solution)/shard_map/ppermute | solution.py:298
  97.1 2.5 %collective-permute-start.25 = (bf16[3,384,128]{2,1,0:T(8,128)(2,1)S(1)}, bf16[3,384,128]{2,1,0:T(8,128)(2,1)S(1)}, u32[]{:S(2)}, u32[]{:S(2)}) collective-permute-start(bf16[3,384,128]{2,1,0:T(8,128)(2,1)S(1)} %copy-done.7), channel_id=1, source_target_pairs={{0,4},{1,5},{2,6},{3,7},{4,0},{5,1},{6,2},{7,3},{8,12},{9,13},{10,... | collective-permute-start | bytes 884744 | tf_op jit(solution)/shard_map/ppermute | solution.py:298
  99.6 2.1 %shard_map.100.refs_6_ = f32[2,256,1536]{2,1,0:T(8,128)S(1)} custom-call(f32[256,768]{1,0:T(8,128)S(1)} %get-tuple-element.143.refs_0_, bf16[256,768]{1,0:T(8,128)(2,1)S(1)} %collective-permute-done.20.refs_1_, bf16[3,384,256]{2,1,0:T(8,128)(2,1)S(1)} %copy-done.3, bf16[3,384,256]{2,1,0:T(8,128)(2,1)S(1)} %copy-done.6, ...), custom_call_target="tpu_custom_call" | custom-call | bytes 1024 | tf_op jit(solution)/shard_map/pallas_call | solution.py:191
  105.7 2.1 %shard_map.102.refs_6_ = f32[2,256,1536]{2,1,0:T(8,128)S(1)} custom-call(f32[256,768]{1,0:T(8,128)S(1)} %get-tuple-element.152.refs_0_, bf16[256,768]{1,0:T(8,128)(2,1)S(1)} %collective-permute-done.24.refs_1_, bf16[3,384,256]{2,1,0:T(8,128)(2,1)S(1)} %copy-done.4, bf16[3,384,256]{2,1,0:T(8,128)(2,1)} %collective-permute-done.12.b_ref.refs_3_, ...), custom_call_target="tpu_custom_call" | custom-call | bytes 1024 | tf_op jit(solution)/shard_map/pallas_call | solution.py:191
  107.8 8.5 %collective-permute-done.23.refs_1_ = bf16[256,384]{1,0:T(8,128)(2,1)S(1)} collective-permute-done((bf16[256,384]{1,0:T(8,128)(2,1)S(1)}, bf16[256,384]{1,0:T(8,128)(2,1)S(1)}, u32[]{:S(2)}, u32[]{:S(2)}) %collective-permute-start.23) | collective-permute-done | bytes 196640 | tf_op jit(solution)/shard_map/ppermute | solution.py:298
  119.0 3.0 %collective-permute-start.27 = (bf16[256,384]{1,0:T(8,128)(2,1)S(1)}, bf16[256,384]{1,0:T(8,128)(2,1)S(1)}, u32[]{:S(2)}, u32[]{:S(2)}) collective-permute-start(bf16[256,384]{1,0:T(8,128)(2,1)S(1)} %get-tuple-element.160), channel_id=1, source_target_pairs={{0,16},{1,17},{2,18},{3,19},{4,20},{5,21},{6,22},{7,23},{8,24},{9,... | collective-permute-start | bytes 589832 | tf_op jit(solution)/shard_map/ppermute | solution.py:298
  122.0 3.8 %collective-permute-done.28.refs_1_ = bf16[256,384]{1,0:T(8,128)(2,1)S(1)} collective-permute-done((bf16[256,384]{1,0:T(8,128)(2,1)S(1)}, bf16[256,384]{1,0:T(8,128)(2,1)S(1)}, u32[]{:S(2)}, u32[]{:S(2)}) %collective-permute-start.28) | collective-permute-done | bytes 196640 | tf_op jit(solution)/shard_map/ppermute | solution.py:298
  126.6 3.4 %collective-permute-done.27.refs_1_ = bf16[256,384]{1,0:T(8,128)(2,1)S(1)} collective-permute-done((bf16[256,384]{1,0:T(8,128)(2,1)S(1)}, bf16[256,384]{1,0:T(8,128)(2,1)S(1)}, u32[]{:S(2)}, u32[]{:S(2)}) %collective-permute-start.27) | collective-permute-done | bytes 196640 | tf_op jit(solution)/shard_map/ppermute | solution.py:298
  130.9 2.3 %collective-permute-done.29.recv_ref = bf16[4,2,2,16,1536]{4,3,2,1,0:T(8,128)(2,1)S(1)} collective-permute-done((bf16[4,2,2,16,1536]{4,3,2,1,0:T(8,128)(2,1)S(1)}, bf16[4,2,2,16,1536]{4,3,2,1,0:T(8,128)(2,1)S(1)}, u32[]{:S(2)}, u32[]{:S(2)}) %collective-permute-start.29) | collective-permute-done | bytes 786464 | tf_op jit(solution)/shard_map/ppermute | solution.py:298
  133.9 3.0 %collective-permute-start.32 = (bf16[2,2,16,1536]{3,2,1,0:T(8,128)(2,1)S(1)}, bf16[2,2,16,1536]{3,2,1,0:T(8,128)(2,1)S(1)}, u32[]{:S(2)}, u32[]{:S(2)}) collective-permute-start(bf16[2,2,16,1536]{3,2,1,0:T(8,128)(2,1)S(1)} %get-tuple-element.169), channel_id=1, source_target_pairs={{0,10},{1,11},{2,8},{3,9},{4,14},{5,15},{6,12},{7,13},{8,2},{9,3},... | collective-permute-start | bytes 589832 | tf_op jit(solution)/shard_map/ppermute | solution.py:298
  136.8 3.5 %collective-permute-done.30.x_ref = bf16[2,2,16,1536]{3,2,1,0:T(8,128)(2,1)S(1)} collective-permute-done((bf16[2,2,16,1536]{3,2,1,0:T(8,128)(2,1)S(1)}, bf16[2,2,16,1536]{3,2,1,0:T(8,128)(2,1)S(1)}, u32[]{:S(2)}, u32[]{:S(2)}) %collective-permute-start.30) | collective-permute-done | bytes 196640 | tf_op jit(solution)/shard_map/ppermute | solution.py:298
  141.2 4.5 %collective-permute-done.32.both_ref = bf16[2,2,16,1536]{3,2,1,0:T(8,128)(2,1)S(1)} collective-permute-done((bf16[2,2,16,1536]{3,2,1,0:T(8,128)(2,1)S(1)}, bf16[2,2,16,1536]{3,2,1,0:T(8,128)(2,1)S(1)}, u32[]{:S(2)}, u32[]{:S(2)}) %collective-permute-start.32) | collective-permute-done | bytes 196640 | tf_op jit(solution)/shard_map/ppermute | solution.py:298
  146.7 5.7 %collective-permute-done.33.other_ref = bf16[2,16,1536]{2,1,0:T(8,128)(2,1)S(1)} collective-permute-done((bf16[2,16,1536]{2,1,0:T(8,128)(2,1)S(1)}, bf16[2,16,1536]{2,1,0:T(8,128)(2,1)S(1)}, u32[]{:S(2)}, u32[]{:S(2)}) %collective-permute-start.33) | collective-permute-done | bytes 98336 | tf_op jit(solution)/shard_map/ppermute | solution.py:298
  (103 shorter events, 47.9 us)
Async XLA Ops:
  2.5 12.8 %collective-permute-start = (bf16[3,384,128]{2,1,0:T(8,128)(2,1)}, bf16[3,384,128]{2,1,0:T(8,128)(2,1)S(1)}, u32[]{:S(2)}, u32[]{:S(2)}) collective-permute-start(bf16[3,384,128]{2,1,0:T(8,128)(2,1)} %shard_map.87.a_ref.refs_2_), channel_id=1, source_target_pairs={{0,4},{1,5},{2,6},{3,7},{4,0},{5,1},{6,2},{7,3},{8,12},{9,13},{10,... | collective-permute-start | bytes 884744 | tf_op jit(solution)/shard_map/ppermute | solution.py:298
  7.2 9.8 %collective-permute-start.1 = (bf16[3,384,128]{2,1,0:T(8,128)(2,1)}, bf16[3,384,128]{2,1,0:T(8,128)(2,1)S(1)}, u32[]{:S(2)}, u32[]{:S(2)}) collective-permute-start(bf16[3,384,128]{2,1,0:T(8,128)(2,1)} %shard_map.88), channel_id=1, source_target_pairs={{0,8},{1,9},{2,10},{3,11},{4,12},{5,13},{6,14},{7,15},{8,0},{9,1},... | collective-permute-start | bytes 884744 | tf_op jit(solution)/shard_map/ppermute | solution.py:298
  11.4 23.0 %collective-permute-start.6 = (bf16[3,384,256]{2,1,0:T(8,128)(2,1)}, bf16[3,384,256]{2,1,0:T(8,128)(2,1)S(1)}, u32[]{:S(2)}, u32[]{:S(2)}) collective-permute-start(bf16[3,384,256]{2,1,0:T(8,128)(2,1)} %get-tuple-element.93.a_ref.refs_2_), channel_id=1, source_target_pairs={{0,4},{1,5},{2,6},{3,7},{4,0},{5,1},{6,2},{7,3},{8,12},{9,13},{10,... | collective-permute-start | bytes 1769480 | tf_op jit(solution)/shard_map/ppermute | solution.py:298
  19.0 7.7 %collective-permute-start.3 = (bf16[2,2,16,1536]{3,2,1,0:T(8,128)(2,1)S(1)}, bf16[2,2,16,1536]{3,2,1,0:T(8,128)(2,1)}, u32[]{:S(2)}, u32[]{:S(2)}) collective-permute-start(bf16[2,2,16,1536]{3,2,1,0:T(8,128)(2,1)S(1)} %get-tuple-element.91), channel_id=1, source_target_pairs={{0,2},{1,3},{2,0},{3,1},{4,6},{5,7},{6,4},{7,5},{8,10},{9,11},{10,... | collective-permute-start | bytes 589832 | tf_op jit(solution)/shard_map/ppermute | solution.py:298
  20.6 8.1 %collective-permute-start.4 = (bf16[2,2,16,1536]{3,2,1,0:T(8,128)(2,1)S(1)}, bf16[2,2,16,1536]{3,2,1,0:T(8,128)(2,1)S(1)}, u32[]{:S(2)}, u32[]{:S(2)}) collective-permute-start(bf16[2,2,16,1536]{3,2,1,0:T(8,128)(2,1)S(1)} %get-tuple-element.92), channel_id=1, source_target_pairs={{0,8},{1,9},{2,10},{3,11},{4,12},{5,13},{6,14},{7,15},{8,0},{9,1},... | collective-permute-start | bytes 589832 | tf_op jit(solution)/shard_map/ppermute | solution.py:298
  22.3 10.2 %collective-permute-start.5 = (bf16[2,2,16,1536]{3,2,1,0:T(8,128)(2,1)S(1)}, bf16[2,2,16,1536]{3,2,1,0:T(8,128)(2,1)S(1)}, u32[]{:S(2)}, u32[]{:S(2)}) collective-permute-start(bf16[2,2,16,1536]{3,2,1,0:T(8,128)(2,1)S(1)} %get-tuple-element.92), channel_id=1, source_target_pairs={{0,10},{1,11},{2,8},{3,9},{4,14},{5,15},{6,12},{7,13},{8,2},{9,3},... | collective-permute-start | bytes 589832 | tf_op jit(solution)/shard_map/ppermute | solution.py:298
  22.6 22.2 %collective-permute-start.8 = (bf16[3,384,256]{2,1,0:T(8,128)(2,1)}, bf16[3,384,256]{2,1,0:T(8,128)(2,1)S(1)}, u32[]{:S(2)}, u32[]{:S(2)}) collective-permute-start(bf16[3,384,256]{2,1,0:T(8,128)(2,1)} %get-tuple-element.99), channel_id=1, source_target_pairs={{0,8},{1,9},{2,10},{3,11},{4,12},{5,13},{6,14},{7,15},{8,0},{9,1},... | collective-permute-start | bytes 1769480 | tf_op jit(solution)/shard_map/ppermute | solution.py:298
  26.8 14.2 %collective-permute-start.7 = (bf16[3,384,256]{2,1,0:T(8,128)(2,1)}, bf16[3,384,256]{2,1,0:T(8,128)(2,1)S(1)}, u32[]{:S(2)}, u32[]{:S(2)}) collective-permute-start(bf16[3,384,256]{2,1,0:T(8,128)(2,1)} %get-tuple-element.96.a_ref.refs_2_), channel_id=1, source_target_pairs={{0,4},{1,5},{2,6},{3,7},{4,0},{5,1},{6,2},{7,3},{8,12},{9,13},{10,... | collective-permute-start | bytes 1769480 | tf_op jit(solution)/shard_map/ppermute | solution.py:298
  34.4 18.5 %collective-permute-start.9 = (bf16[4,2,2,16,1536]{4,3,2,1,0:T(8,128)(2,1)S(1)}, bf16[4,2,2,16,1536]{4,3,2,1,0:T(8,128)(2,1)}, u32[]{:S(2)}, u32[]{:S(2)}) collective-permute-start(bf16[4,2,2,16,1536]{4,3,2,1,0:T(8,128)(2,1)S(1)} %pad_maximum_fusion.near_ref), channel_id=1, source_target_pairs={{0,1},{1,0},{2,3},{3,2},{4,5},{5,4},{6,7},{7,6},{8,9},{9,8},{10,11... | collective-permute-start | bytes 2359304 | tf_op jit(solution)/shard_map/ppermute | solution.py:298
  34.4 18.4 %collective-permute-start.10 = (bf16[3,384,128]{2,1,0:T(8,128)(2,1)S(1)}, bf16[3,384,128]{2,1,0:T(8,128)(2,1)}, u32[]{:S(2)}, u32[]{:S(2)}) collective-permute-start(bf16[3,384,128]{2,1,0:T(8,128)(2,1)S(1)} %collective-permute-done.1.b_ref.refs_3_), channel_id=1, source_target_pairs={{0,4},{1,5},{2,6},{3,7},{4,0},{5,1},{6,2},{7,3},{8,12},{9,13},{10,... | collective-permute-start | bytes 884744 | tf_op jit(solution)/shard_map/ppermute | solution.py:298
  36.7 19.2 %collective-permute-start.12 = (bf16[3,384,256]{2,1,0:T(8,128)(2,1)}, bf16[3,384,256]{2,1,0:T(8,128)(2,1)}, u32[]{:S(2)}, u32[]{:S(2)}) collective-permute-start(bf16[3,384,256]{2,1,0:T(8,128)(2,1)} %get-tuple-element.110), channel_id=1, source_target_pairs={{0,8},{1,9},{2,10},{3,11},{4,12},{5,13},{6,14},{7,15},{8,0},{9,1},... | collective-permute-start | bytes 1769480 | tf_op jit(solution)/shard_map/ppermute | solution.py:298
  44.8 15.7 %collective-permute-start.13 = (bf16[3,384,256]{2,1,0:T(8,128)(2,1)S(1)}, bf16[3,384,256]{2,1,0:T(8,128)(2,1)}, u32[]{:S(2)}, u32[]{:S(2)}) collective-permute-start(bf16[3,384,256]{2,1,0:T(8,128)(2,1)S(1)} %collective-permute-done.8.b_ref.refs_3_), channel_id=1, source_target_pairs={{0,4},{1,5},{2,6},{3,7},{4,0},{5,1},{6,2},{7,3},{8,12},{9,13},{10,... | collective-permute-start | bytes 1769480 | tf_op jit(solution)/shard_map/ppermute | solution.py:298
  56.0 15.1 %collective-permute-start.11 = (bf16[3,384,128]{2,1,0:T(8,128)(2,1)S(1)}, bf16[3,384,128]{2,1,0:T(8,128)(2,1)S(1)}, u32[]{:S(2)}, u32[]{:S(2)}) collective-permute-start(bf16[3,384,128]{2,1,0:T(8,128)(2,1)S(1)} %copy-done.19), channel_id=1, source_target_pairs={{0,8},{1,9},{2,10},{3,11},{4,12},{5,13},{6,14},{7,15},{8,0},{9,1},... | collective-permute-start | bytes 884744 | tf_op jit(solution)/shard_map/ppermute | solution.py:298
  57.0 18.3 %collective-permute-start.17 = (bf16[3,384,256]{2,1,0:T(8,128)(2,1)}, bf16[3,384,256]{2,1,0:T(8,128)(2,1)S(1)}, u32[]{:S(2)}, u32[]{:S(2)}) collective-permute-start(bf16[3,384,256]{2,1,0:T(8,128)(2,1)} %collective-permute-done.12.b_ref.refs_3_), channel_id=1, source_target_pairs={{0,4},{1,5},{2,6},{3,7},{4,0},{5,1},{6,2},{7,3},{8,12},{9,13},{10,... | collective-permute-start | bytes 1769480 | tf_op jit(solution)/shard_map/ppermute | solution.py:298
  58.4 15.1 %collective-permute-start.14 = (bf16[256,384]{1,0:T(8,128)(2,1)S(1)}, bf16[256,384]{1,0:T(8,128)(2,1)S(1)}, u32[]{:S(2)}, u32[]{:S(2)}) collective-permute-start(bf16[256,384]{1,0:T(8,128)(2,1)S(1)} %get-tuple-element.121), channel_id=1, source_target_pairs={{0,16},{1,17},{2,18},{3,19},{4,20},{5,21},{6,22},{7,23},{8,24},{9,... | collective-permute-start | bytes 589832 | tf_op jit(solution)/shard_map/ppermute | solution.py:298
  62.8 14.9 %collective-permute-start.19 = (bf16[3,384,128]{2,1,0:T(8,128)(2,1)S(1)}, bf16[3,384,128]{2,1,0:T(8,128)(2,1)S(1)}, u32[]{:S(2)}, u32[]{:S(2)}) collective-permute-start(bf16[3,384,128]{2,1,0:T(8,128)(2,1)S(1)} %copy-done.18), channel_id=1, source_target_pairs={{0,8},{1,9},{2,10},{3,11},{4,12},{5,13},{6,14},{7,15},{8,0},{9,1},... | collective-permute-start | bytes 884744 | tf_op jit(solution)/shard_map/ppermute | solution.py:298
  63.1 17.4 %collective-permute-start.15 = (bf16[3,384,128]{2,1,0:T(8,128)(2,1)S(1)}, bf16[3,384,128]{2,1,0:T(8,128)(2,1)S(1)}, u32[]{:S(2)}, u32[]{:S(2)}) collective-permute-start(bf16[3,384,128]{2,1,0:T(8,128)(2,1)S(1)} %copy-done.12), channel_id=1, source_target_pairs={{0,4},{1,5},{2,6},{3,7},{4,0},{5,1},{6,2},{7,3},{8,12},{9,13},{10,... | collective-permute-start | bytes 884744 | tf_op jit(solution)/shard_map/ppermute | solution.py:298
  71.1 26.0 %collective-permute-start.20 = (bf16[256,768]{1,0:T(8,128)(2,1)S(1)}, bf16[256,768]{1,0:T(8,128)(2,1)S(1)}, u32[]{:S(2)}, u32[]{:S(2)}) collective-permute-start(bf16[256,768]{1,0:T(8,128)(2,1)S(1)} %get-tuple-element.144), channel_id=1, source_target_pairs={{0,16},{1,17},{2,18},{3,19},{4,20},{5,21},{6,22},{7,23},{8,24},{9,... | collective-permute-start | bytes 1179656 | tf_op jit(solution)/shard_map/ppermute | solution.py:298
  75.3 10.9 %collective-permute-start.16 = (bf16[3,384,128]{2,1,0:T(8,128)(2,1)S(1)}, bf16[3,384,128]{2,1,0:T(8,128)(2,1)S(1)}, u32[]{:S(2)}, u32[]{:S(2)}) collective-permute-start(bf16[3,384,128]{2,1,0:T(8,128)(2,1)S(1)} %collective-permute-done.11.b_ref.refs_3_), channel_id=1, source_target_pairs={{0,4},{1,5},{2,6},{3,7},{4,0},{5,1},{6,2},{7,3},{8,12},{9,13},{10,... | collective-permute-start | bytes 884744 | tf_op jit(solution)/shard_map/ppermute | solution.py:298
  77.7 28.0 %collective-permute-start.24 = (bf16[256,768]{1,0:T(8,128)(2,1)S(1)}, bf16[256,768]{1,0:T(8,128)(2,1)S(1)}, u32[]{:S(2)}, u32[]{:S(2)}) collective-permute-start(bf16[256,768]{1,0:T(8,128)(2,1)S(1)} %get-tuple-element.153), channel_id=1, source_target_pairs={{0,16},{1,17},{2,18},{3,19},{4,20},{5,21},{6,22},{7,23},{8,24},{9,... | collective-permute-start | bytes 1179656 | tf_op jit(solution)/shard_map/ppermute | solution.py:298
  79.2 22.4 %collective-permute-start.18 = (bf16[3,384,128]{2,1,0:T(8,128)(2,1)S(1)}, bf16[3,384,128]{2,1,0:T(8,128)(2,1)S(1)}, u32[]{:S(2)}, u32[]{:S(2)}) collective-permute-start(bf16[3,384,128]{2,1,0:T(8,128)(2,1)S(1)} %copy-done.17), channel_id=1, source_target_pairs={{0,8},{1,9},{2,10},{3,11},{4,12},{5,13},{6,14},{7,15},{8,0},{9,1},... | collective-permute-start | bytes 884744 | tf_op jit(solution)/shard_map/ppermute | solution.py:298
  80.5 21.2 %collective-permute-start.22 = (bf16[3,384,128]{2,1,0:T(8,128)(2,1)S(1)}, bf16[3,384,128]{2,1,0:T(8,128)(2,1)S(1)}, u32[]{:S(2)}, u32[]{:S(2)}) collective-permute-start(bf16[3,384,128]{2,1,0:T(8,128)(2,1)S(1)} %collective-permute-done.19.b_ref.refs_3_), channel_id=1, source_target_pairs={{0,4},{1,5},{2,6},{3,7},{4,0},{5,1},{6,2},{7,3},{8,12},{9,13},{10,... | collective-permute-start | bytes 884744 | tf_op jit(solution)/shard_map/ppermute | solution.py:298
  86.2 15.7 %collective-permute-start.21 = (bf16[3,384,128]{2,1,0:T(8,128)(2,1)S(1)}, bf16[3,384,128]{2,1,0:T(8,128)(2,1)S(1)}, u32[]{:S(2)}, u32[]{:S(2)}) collective-permute-start(bf16[3,384,128]{2,1,0:T(8,128)(2,1)S(1)} %copy-done.8), channel_id=1, source_target_pairs={{0,4},{1,5},{2,6},{3,7},{4,0},{5,1},{6,2},{7,3},{8,12},{9,13},{10,... | collective-permute-start | bytes 884744 | tf_op jit(solution)/shard_map/ppermute | solution.py:298
  97.1 20.0 %collective-permute-start.25 = (bf16[3,384,128]{2,1,0:T(8,128)(2,1)S(1)}, bf16[3,384,128]{2,1,0:T(8,128)(2,1)S(1)}, u32[]{:S(2)}, u32[]{:S(2)}) collective-permute-start(bf16[3,384,128]{2,1,0:T(8,128)(2,1)S(1)} %copy-done.7), channel_id=1, source_target_pairs={{0,4},{1,5},{2,6},{3,7},{4,0},{5,1},{6,2},{7,3},{8,12},{9,13},{10,... | collective-permute-start | bytes 884744 | tf_op jit(solution)/shard_map/ppermute | solution.py:298
  101.7 14.6 %collective-permute-start.23 = (bf16[256,384]{1,0:T(8,128)(2,1)S(1)}, bf16[256,384]{1,0:T(8,128)(2,1)S(1)}, u32[]{:S(2)}, u32[]{:S(2)}) collective-permute-start(bf16[256,384]{1,0:T(8,128)(2,1)S(1)} %get-tuple-element.151), channel_id=1, source_target_pairs={{0,16},{1,17},{2,18},{3,19},{4,20},{5,21},{6,22},{7,23},{8,24},{9,... | collective-permute-start | bytes 589832 | tf_op jit(solution)/shard_map/ppermute | solution.py:298
  101.7 15.4 %collective-permute-start.26 = (bf16[3,384,128]{2,1,0:T(8,128)(2,1)S(1)}, bf16[3,384,128]{2,1,0:T(8,128)(2,1)S(1)}, u32[]{:S(2)}, u32[]{:S(2)}) collective-permute-start(bf16[3,384,128]{2,1,0:T(8,128)(2,1)S(1)} %collective-permute-done.18.b_ref.refs_3_), channel_id=1, source_target_pairs={{0,4},{1,5},{2,6},{3,7},{4,0},{5,1},{6,2},{7,3},{8,12},{9,13},{10,... | collective-permute-start | bytes 884744 | tf_op jit(solution)/shard_map/ppermute | solution.py:298
  117.0 8.7 %collective-permute-start.28 = (bf16[256,384]{1,0:T(8,128)(2,1)S(1)}, bf16[256,384]{1,0:T(8,128)(2,1)S(1)}, u32[]{:S(2)}, u32[]{:S(2)}) collective-permute-start(bf16[256,384]{1,0:T(8,128)(2,1)S(1)} %get-tuple-element.162), channel_id=1, source_target_pairs={{0,16},{1,17},{2,18},{3,19},{4,20},{5,21},{6,22},{7,23},{8,24},{9,... | collective-permute-start | bytes 589832 | tf_op jit(solution)/shard_map/ppermute | solution.py:298
  119.0 11.0 %collective-permute-start.27 = (bf16[256,384]{1,0:T(8,128)(2,1)S(1)}, bf16[256,384]{1,0:T(8,128)(2,1)S(1)}, u32[]{:S(2)}, u32[]{:S(2)}) collective-permute-start(bf16[256,384]{1,0:T(8,128)(2,1)S(1)} %get-tuple-element.160), channel_id=1, source_target_pairs={{0,16},{1,17},{2,18},{3,19},{4,20},{5,21},{6,22},{7,23},{8,24},{9,... | collective-permute-start | bytes 589832 | tf_op jit(solution)/shard_map/ppermute | solution.py:298
  133.3 7.0 %collective-permute-start.30 = (bf16[2,2,16,1536]{3,2,1,0:T(8,128)(2,1)S(1)}, bf16[2,2,16,1536]{3,2,1,0:T(8,128)(2,1)S(1)}, u32[]{:S(2)}, u32[]{:S(2)}) collective-permute-start(bf16[2,2,16,1536]{3,2,1,0:T(8,128)(2,1)S(1)} %get-tuple-element.167), channel_id=1, source_target_pairs={{0,2},{1,3},{2,0},{3,1},{4,6},{5,7},{6,4},{7,5},{8,10},{9,11},{10,... | collective-permute-start | bytes 589832 | tf_op jit(solution)/shard_map/ppermute | solution.py:298
  133.4 7.8 %collective-permute-start.31 = (bf16[2,2,16,1536]{3,2,1,0:T(8,128)(2,1)S(1)}, bf16[2,2,16,1536]{3,2,1,0:T(8,128)(2,1)S(1)}, u32[]{:S(2)}, u32[]{:S(2)}) collective-permute-start(bf16[2,2,16,1536]{3,2,1,0:T(8,128)(2,1)S(1)} %get-tuple-element.168), channel_id=1, source_target_pairs={{0,8},{1,9},{2,10},{3,11},{4,12},{5,13},{6,14},{7,15},{8,0},{9,1},... | collective-permute-start | bytes 589832 | tf_op jit(solution)/shard_map/ppermute | solution.py:298
  133.9 11.8 %collective-permute-start.32 = (bf16[2,2,16,1536]{3,2,1,0:T(8,128)(2,1)S(1)}, bf16[2,2,16,1536]{3,2,1,0:T(8,128)(2,1)S(1)}, u32[]{:S(2)}, u32[]{:S(2)}) collective-permute-start(bf16[2,2,16,1536]{3,2,1,0:T(8,128)(2,1)S(1)} %get-tuple-element.169), channel_id=1, source_target_pairs={{0,10},{1,11},{2,8},{3,9},{4,14},{5,15},{6,12},{7,13},{8,2},{9,3},... | collective-permute-start | bytes 589832 | tf_op jit(solution)/shard_map/ppermute | solution.py:298
  145.8 6.7 %collective-permute-start.33 = (bf16[2,16,1536]{2,1,0:T(8,128)(2,1)S(1)}, bf16[2,16,1536]{2,1,0:T(8,128)(2,1)S(1)}, u32[]{:S(2)}, u32[]{:S(2)}) collective-permute-start(bf16[2,16,1536]{2,1,0:T(8,128)(2,1)S(1)} %get-tuple-element.171), channel_id=1, source_target_pairs={{0,16},{1,17},{2,18},{3,19},{4,20},{5,21},{6,22},{7,23},{8,24},{9,... | collective-permute-start | bytes 294920 | tf_op jit(solution)/shard_map/ppermute | solution.py:298
  (22 other events, 172.8 us)
